TPU v7x, 1024 devices: a whole 8x8x8 slice. The times are simulated.
1024 devices in a mesh: dom: 128 (over x, z, core), cls: 8 (over y).
Axes of the slice: x: 8, y: 8, z: 8, core: 2. Of those that a mesh axis runs over, the one named last changes fastest.
Arguments:
- tiles: bfloat16 [4096, 128, 128], P('dom'), may hold values from 0.0009994507 to 1
- tile_rows: int32 [4096], P('dom'), may hold values from 0 to 7
- tile_cols: int32 [4096], P('dom'), may hold values from 0 to 15
- send_lists: int32 [128, 4, 2], P('dom'), may hold values from 0 to 7
- seed_mask: int32 [131072], P('dom'), may hold values 0 or 1
- labels: float32 [131072, 1024], P('dom', 'cls'), may hold values from 0.1 to 10
Outputs:
- relabeled: float32 [131072, 1024], P('dom', 'cls')
All inputs are finite; a program needn't handle non-finite values. No bound on the sum of `seed_mask` on one device may be relied on, other than what follows from the above.
Results may differ from a plain program's by a relative error of at most 0.0003.
Values sent between devices are 32-bit elements; how exact they have to be, the bound alone decides.
No kernel may reach another device: no remote copies, remote signals or barrier semaphores. Data moves between devices by JAX's collectives and lax.ppermute only.
A program may use at most 32 MiB of HBM per device.

v0:
```python
import jax
import jax.numpy as jnp
from jax import lax
from jax.sharding import PartitionSpec as P

CLASSES = 1024
ITERS = 3


offsets_table = (1, 2, -1, -2)


def from_behind(value, axis, by):
    length = lax.axis_size(axis)
    return lax.ppermute(value, axis, [(i, (i + by) % length) for i in range(length)])


def fetch_direct(outgoing):
    received = []
    for position, offset in enumerate(offsets_table):
        received.append(from_behind(outgoing[position], "dom", offset))
    return jnp.stack(received)


def on_device(tiles, tile_rows, tile_cols, send_lists, seed_mask, labels):
    side = tiles.shape[1]
    block_count = labels.shape[0] // side
    class_share = labels.shape[1]
    blocks = labels.reshape(block_count, side, class_share)
    first_mass = lax.psum(jnp.sum(blocks, axis=2), "cls")
    seeded_prior = CLASSES * blocks / first_mass[:, :, None]
    seeded = seed_mask.reshape(block_count, side, 1).astype(jnp.float32)
    anchor = 64.0 * seeded * seeded_prior + 4.0
    weights = tiles.astype(jnp.float32)
    rows_onehot = (tile_rows[None, :] == jnp.arange(block_count, dtype=jnp.int32)[:, None]).astype(
        jnp.float32
    )
    send_rows = send_lists[0]
    ghost_count = send_rows.shape[1]
    current = seeded_prior
    for iteration in range(ITERS):
        outgoing = current[send_rows.reshape(-1)].reshape(4, ghost_count, side, class_share)
        ghosts = fetch_direct(outgoing)
        buffer = jnp.concatenate(
            [current, ghosts.reshape(4 * ghost_count, side, class_share)], axis=0
        )
        operand = buffer[tile_cols]
        products = jnp.einsum("tij,tjc->tic", weights, operand, precision=lax.Precision.HIGHEST)
        spread = jnp.einsum("bt,tic->bic", rows_onehot, products, precision=lax.Precision.HIGHEST)
        mixture = spread + anchor
        squared = mixture * mixture
        row_mass = lax.psum(jnp.sum(squared, axis=2), "cls")
        current = CLASSES * squared / row_mass[:, :, None]
    return current.reshape(block_count * side, class_share)


def solution(mesh):
    return jax.shard_map(
        on_device,
        mesh=mesh,
        in_specs=(
            P("dom", None, None),
            P("dom"),
            P("dom"),
            P("dom", None, None),
            P("dom"),
            P("dom", "cls"),
        ),
        out_specs=P("dom", "cls"),
        check_vma=False,
    )
```

profile of v0, /device:TPU:16, one launch (start us, length us, event | category | flops | bytes accessed | tf_op | source)
XLA Modules:
  0.0 218.4 jit_solution(5862734636167956620)
XLA Ops:
  0.0 0.9 copy.13
  0.9 0.1 reshape_squeeze.2
  1.0 1.2 fusion.35
  2.2 27.1 %psum.28 = f32[8,128]{1,0:T(8,128)S(1)} all-reduce(f32[8,128]{1,0:T(8,128)S(1)} %bitcast.82), channel_id=1, replica_groups=mesh['dom'=128,'cls'=8] {'cls'}, use_global_device_ids=true, to_apply=%region_1.0 | all-reduce | flops 1024 | bytes 8192 | tf_op jit(solution)/shard_map/psum | solution.py:30
  29.3 0.1 copy.11
  29.5 0.0 copy-start.3
  29.5 0.4 copy_divide_fusion
  29.8 0.1 copy.14
  29.9 0.6 gather_fusion
  30.6 1.9 collective-permute-start
  32.5 7.0 %collective-permute-start.2 = (f32[2,128,128]{2,1,0:T(8,128)S(1)}, f32[2,128,128]{2,1,0:T(8,128)S(1)}, u32[]{:S(2)}, u32[]{:S(2)}) collective-permute-start(f32[2,128,128]{2,1,0:T(8,128)S(1)} %get-tuple-element.14), channel_id=1, source_target_pairs={{0,1016},{8,0},{16,8},{24,16},{32,24},{40,32},{48,40},{56,48},{64,... | collective-permute-start | bytes 393224 | tf_op jit(solution)/shard_map/ppermute | solution.py:15
  39.5 1.9 collective-permute-start.1
  41.4 7.2 %collective-permute-start.3 = (f32[2,128,128]{2,1,0:T(8,128)S(1)}, f32[2,128,128]{2,1,0:T(8,128)S(1)}, u32[]{:S(2)}, u32[]{:S(2)}) collective-permute-start(f32[2,128,128]{2,1,0:T(8,128)S(1)} %get-tuple-element.16), channel_id=1, source_target_pairs={{0,1008},{8,1016},{16,0},{24,8},{32,16},{40,24},{48,32},{56,40},{6... | collective-permute-start | bytes 393224 | tf_op jit(solution)/shard_map/ppermute | solution.py:15
  48.7 0.1 copy.17
  48.8 0.0 collective-permute-done
  48.8 0.0 collective-permute-done.2
  48.8 0.8 collective-permute-done.1
  49.7 1.5 collective-permute-done.3
  51.2 0.4 copy.15
  51.6 0.1 pad_maximum_fusion
  51.7 0.3 copy.16
  52.0 2.0 gather_fusion.1
  54.0 4.8 %fusion.39 = f32[32,128,128]{2,1,0:T(8,128)} fusion(f32[32,128,128]{2,1,0:T(8,128)} %gather_fusion.1, bf16[32,128,128]{2,1,0:T(8,128)(2,1)S(1)} %copy-done), kind=kOutput, calls=%fused_computation.48 | convolution fusion | flops 805306368 | bytes 5242880 | tf_op jit(solution)/shard_map/tij,tjc->tic/dot_general | solution.py:48
  58.8 3.1 %copy.25 = f32[32,128,128]{1,0,2:T(8,128)} copy(f32[32,128,128]{2,1,0:T(8,128)} %fusion.39) | data formatting | bytes 4194304 | tf_op jit(solution)/shard_map/tij,tjc->tic/dot_general | solution.py:48
  61.9 2.5 %fusion.36 = (f32[8,128]{0,1:T(8,128)S(1)}, f32[8,128,128]{2,0,1:T(8,128)S(1)}) fusion(f32[8,128,128]{2,0,1:T(8,128)S(1)} %copy_divide_fusion, f32[8,128]{0,1:T(8,128)S(1)} %copy.17, f32[32,128,128]{1,0,2:T(8,128)} %copy.25, s32[32]{0:T(128)S(1)} %copy-done.1), kind=kOutput, calls=%fused_computation.45 | convolution fusion | flops 50986240 | bytes 3154048 | tf_op jit(solution)/shard_map/bt,tic->bic/dot_general | solution.py:49
  64.3 26.8 %psum.29 = f32[8,128]{0,1:T(8,128)S(1)} all-reduce(f32[8,128]{0,1:T(8,128)S(1)} %get-tuple-element.19), channel_id=1, replica_groups=mesh['dom'=128,'cls'=8] {'cls'}, use_global_device_ids=true, to_apply=%region_3.0 | all-reduce | flops 1024 | bytes 8192 | tf_op jit(solution)/shard_map/psum | solution.py:52
  91.2 0.2 multiply_divide_fusion.2
  91.4 0.1 copy.18
  91.5 0.6 gather_fusion.2
  92.1 1.9 collective-permute-start.4
  94.0 7.0 %collective-permute-start.6 = (f32[2,128,128]{2,1,0:T(8,128)S(1)}, f32[2,128,128]{2,1,0:T(8,128)S(1)}, u32[]{:S(2)}, u32[]{:S(2)}) collective-permute-start(f32[2,128,128]{2,1,0:T(8,128)S(1)} %get-tuple-element.10), channel_id=1, source_target_pairs={{0,1016},{8,0},{16,8},{24,16},{32,24},{40,32},{48,40},{56,48},{64,... | collective-permute-start | bytes 393224 | tf_op jit(solution)/shard_map/ppermute | solution.py:15
  101.0 1.9 collective-permute-start.5
  102.9 7.2 %collective-permute-start.7 = (f32[2,128,128]{2,1,0:T(8,128)S(1)}, f32[2,128,128]{2,1,0:T(8,128)S(1)}, u32[]{:S(2)}, u32[]{:S(2)}) collective-permute-start(f32[2,128,128]{2,1,0:T(8,128)S(1)} %get-tuple-element.12), channel_id=1, source_target_pairs={{0,1008},{8,1016},{16,0},{24,8},{32,16},{40,24},{48,32},{56,40},{6... | collective-permute-start | bytes 393224 | tf_op jit(solution)/shard_map/ppermute | solution.py:15
  110.2 0.0 collective-permute-done.4
  110.2 0.0 collective-permute-done.6
  110.2 1.0 collective-permute-done.5
  111.2 1.5 collective-permute-done.7
  112.7 0.4 copy.19
  113.2 0.1 pad_maximum_fusion.1
  113.2 0.3 copy.20
  113.6 2.0 gather_fusion.3
  115.6 4.8 %fusion.40 = f32[32,128,128]{2,1,0:T(8,128)} fusion(f32[32,128,128]{2,1,0:T(8,128)} %gather_fusion.3, bf16[32,128,128]{2,1,0:T(8,128)(2,1)S(1)} %copy-done), kind=kOutput, calls=%fused_computation.49 | convolution fusion | flops 805306368 | bytes 5242880 | tf_op jit(solution)/shard_map/tij,tjc->tic/dot_general | solution.py:48
  120.3 3.1 %copy.26 = f32[32,128,128]{1,0,2:T(8,128)} copy(f32[32,128,128]{2,1,0:T(8,128)} %fusion.40) | data formatting | bytes 4194304 | tf_op jit(solution)/shard_map/tij,tjc->tic/dot_general | solution.py:48
  123.4 2.5 %fusion.37 = (f32[8,128]{0,1:T(8,128)S(1)}, f32[8,128,128]{2,0,1:T(8,128)S(1)}) fusion(f32[8,128,128]{2,0,1:T(8,128)S(1)} %copy_divide_fusion, f32[8,128]{0,1:T(8,128)S(1)} %copy.17, f32[32,128,128]{1,0,2:T(8,128)} %copy.26, s32[32]{0:T(128)S(1)} %copy-done.1), kind=kOutput, calls=%fused_computation.46 | convolution fusion | flops 50986240 | bytes 3154048 | tf_op jit(solution)/shard_map/bt,tic->bic/dot_general | solution.py:49
  125.9 28.7 %psum.30 = f32[8,128]{0,1:T(8,128)S(1)} all-reduce(f32[8,128]{0,1:T(8,128)S(1)} %get-tuple-element.21), channel_id=1, replica_groups=mesh['dom'=128,'cls'=8] {'cls'}, use_global_device_ids=true, to_apply=%region_5.0 | all-reduce | flops 1024 | bytes 8192 | tf_op jit(solution)/shard_map/psum | solution.py:52
  154.6 0.2 multiply_divide_fusion.1
  154.8 0.1 copy.21
  154.9 0.6 gather_fusion.4
  155.6 1.9 collective-permute-start.8
  157.5 7.0 %collective-permute-start.10 = (f32[2,128,128]{2,1,0:T(8,128)S(1)}, f32[2,128,128]{2,1,0:T(8,128)S(1)}, u32[]{:S(2)}, u32[]{:S(2)}) collective-permute-start(f32[2,128,128]{2,1,0:T(8,128)S(1)} %get-tuple-element.6), channel_id=1, source_target_pairs={{0,1016},{8,0},{16,8},{24,16},{32,24},{40,32},{48,40},{56,48},{64,... | collective-permute-start | bytes 393224 | tf_op jit(solution)/shard_map/ppermute | solution.py:15
  164.5 1.9 collective-permute-start.9
  166.4 7.4 %collective-permute-start.11 = (f32[2,128,128]{2,1,0:T(8,128)S(1)}, f32[2,128,128]{2,1,0:T(8,128)S(1)}, u32[]{:S(2)}, u32[]{:S(2)}) collective-permute-start(f32[2,128,128]{2,1,0:T(8,128)S(1)} %get-tuple-element.8), channel_id=1, source_target_pairs={{0,1008},{8,1016},{16,0},{24,8},{32,16},{40,24},{48,32},{56,40},{6... | collective-permute-start | bytes 393224 | tf_op jit(solution)/shard_map/ppermute | solution.py:15
  173.9 0.8 collective-permute-done.9
  174.7 1.5 collective-permute-done.11
  176.2 0.4 copy.22
  176.6 0.1 pad_maximum_fusion.2
  176.7 0.3 copy.23
  177.0 2.0 gather_fusion.5
  179.0 4.8 %fusion.41 = f32[32,128,128]{2,1,0:T(8,128)} fusion(f32[32,128,128]{2,1,0:T(8,128)} %gather_fusion.5, bf16[32,128,128]{2,1,0:T(8,128)(2,1)S(1)} %copy-done), kind=kOutput, calls=%fused_computation.50 | convolution fusion | flops 805306368 | bytes 5242880 | tf_op jit(solution)/shard_map/tij,tjc->tic/dot_general | solution.py:48
  183.8 3.1 %copy.27 = f32[32,128,128]{1,0,2:T(8,128)} copy(f32[32,128,128]{2,1,0:T(8,128)} %fusion.41) | data formatting | bytes 4194304 | tf_op jit(solution)/shard_map/tij,tjc->tic/dot_general | solution.py:48
  186.9 2.5 %fusion.38 = (f32[8,128]{0,1:T(8,128)S(1)}, f32[8,128,128]{2,0,1:T(8,128)S(1)}) fusion(f32[8,128,128]{2,0,1:T(8,128)S(1)} %copy_divide_fusion, f32[8,128]{0,1:T(8,128)S(1)} %copy.17, f32[32,128,128]{1,0,2:T(8,128)} %copy.27, s32[32]{0:T(128)S(1)} %copy-done.1), kind=kOutput, calls=%fused_computation.47 | convolution fusion | flops 50986240 | bytes 3154048 | tf_op jit(solution)/shard_map/bt,tic->bic/dot_general | solution.py:49
  189.3 28.0 %psum.31 = f32[8,128]{0,1:T(8,128)S(1)} all-reduce(f32[8,128]{0,1:T(8,128)S(1)} %get-tuple-element.23), channel_id=1, replica_groups=mesh['dom'=128,'cls'=8] {'cls'}, use_global_device_ids=true, to_apply=%region_7.0 | all-reduce | flops 1024 | bytes 8192 | tf_op jit(solution)/shard_map/psum | solution.py:52
  217.3 0.2 multiply_divide_fusion
  217.5 0.9 copy.24
  (20 shorter events, 0.3 us)
Async XLA Ops:
  0.0 54.0 %copy-start = (bf16[32,128,128]{2,1,0:T(8,128)(2,1)S(1)}, bf16[32,128,128]{2,1,0:T(8,128)(2,1)}, u32[]{:S(2)}) copy-start(bf16[32,128,128]{2,1,0:T(8,128)(2,1)} %param.6) | copy-start | bytes 3145732
  29.5 19.2 %copy-start.2 = (s32[1024]{0:T(1024)S(1)}, s32[1024]{0:T(1024)}, u32[]{:S(2)}) copy-start(s32[1024]{0:T(1024)} %param.10) | copy-start | bytes 12292
  29.5 19.2 %copy-start.3 = (s32[32]{0:T(128)S(1)}, s32[32]{0:T(128)}, u32[]{:S(2)}) copy-start(s32[32]{0:T(128)} %param.8) | copy-start | bytes 388
  30.6 18.2 %collective-permute-start = (f32[2,128,128]{2,1,0:T(8,128)S(1)}, f32[2,128,128]{2,1,0:T(8,128)S(1)}, u32[]{:S(2)}, u32[]{:S(2)}) collective-permute-start(f32[2,128,128]{2,1,0:T(8,128)S(1)} %get-tuple-element.13), channel_id=1, source_target_pairs={{0,8},{8,16},{16,24},{24,32},{32,40},{40,48},{48,56},{56,64},{64,7... | collective-permute-start | bytes 393224 | tf_op jit(solution)/shard_map/ppermute | solution.py:15
  32.5 16.3 %collective-permute-start.2 = (f32[2,128,128]{2,1,0:T(8,128)S(1)}, f32[2,128,128]{2,1,0:T(8,128)S(1)}, u32[]{:S(2)}, u32[]{:S(2)}) collective-permute-start(f32[2,128,128]{2,1,0:T(8,128)S(1)} %get-tuple-element.14), channel_id=1, source_target_pairs={{0,1016},{8,0},{16,8},{24,16},{32,24},{40,32},{48,40},{56,48},{64,... | collective-permute-start | bytes 393224 | tf_op jit(solution)/shard_map/ppermute | solution.py:15
  39.5 10.2 %collective-permute-start.1 = (f32[2,128,128]{2,1,0:T(8,128)S(1)}, f32[2,128,128]{2,1,0:T(8,128)S(1)}, u32[]{:S(2)}, u32[]{:S(2)}) collective-permute-start(f32[2,128,128]{2,1,0:T(8,128)S(1)} %get-tuple-element.15), channel_id=1, source_target_pairs={{0,16},{8,24},{16,32},{24,40},{32,48},{40,56},{48,64},{56,72},{64,... | collective-permute-start | bytes 393224 | tf_op jit(solution)/shard_map/ppermute | solution.py:15
  41.4 9.7 %collective-permute-start.3 = (f32[2,128,128]{2,1,0:T(8,128)S(1)}, f32[2,128,128]{2,1,0:T(8,128)S(1)}, u32[]{:S(2)}, u32[]{:S(2)}) collective-permute-start(f32[2,128,128]{2,1,0:T(8,128)S(1)} %get-tuple-element.16), channel_id=1, source_target_pairs={{0,1008},{8,1016},{16,0},{24,8},{32,16},{40,24},{48,32},{56,40},{6... | collective-permute-start | bytes 393224 | tf_op jit(solution)/shard_map/ppermute | solution.py:15
  58.8 3.1 %copy-start.1 = (s32[32]{0:T(128)S(1)}, s32[32]{0:T(128)}, u32[]{:S(2)}) copy-start(s32[32]{0:T(128)} %param.7) | copy-start | bytes 388
  92.1 18.1 %collective-permute-start.4 = (f32[2,128,128]{2,1,0:T(8,128)S(1)}, f32[2,128,128]{2,1,0:T(8,128)S(1)}, u32[]{:S(2)}, u32[]{:S(2)}) collective-permute-start(f32[2,128,128]{2,1,0:T(8,128)S(1)} %get-tuple-element.9), channel_id=1, source_target_pairs={{0,8},{8,16},{16,24},{24,32},{32,40},{40,48},{48,56},{56,64},{64,7... | collective-permute-start | bytes 393224 | tf_op jit(solution)/shard_map/ppermute | solution.py:15
  94.0 16.2 %collective-permute-start.6 = (f32[2,128,128]{2,1,0:T(8,128)S(1)}, f32[2,128,128]{2,1,0:T(8,128)S(1)}, u32[]{:S(2)}, u32[]{:S(2)}) collective-permute-start(f32[2,128,128]{2,1,0:T(8,128)S(1)} %get-tuple-element.10), channel_id=1, source_target_pairs={{0,1016},{8,0},{16,8},{24,16},{32,24},{40,32},{48,40},{56,48},{64,... | collective-permute-start | bytes 393224 | tf_op jit(solution)/shard_map/ppermute | solution.py:15
  101.0 10.2 %collective-permute-start.5 = (f32[2,128,128]{2,1,0:T(8,128)S(1)}, f32[2,128,128]{2,1,0:T(8,128)S(1)}, u32[]{:S(2)}, u32[]{:S(2)}) collective-permute-start(f32[2,128,128]{2,1,0:T(8,128)S(1)} %get-tuple-element.11), channel_id=1, source_target_pairs={{0,16},{8,24},{16,32},{24,40},{32,48},{40,56},{48,64},{56,72},{64,... | collective-permute-start | bytes 393224 | tf_op jit(solution)/shard_map/ppermute | solution.py:15
  102.9 9.7 %collective-permute-start.7 = (f32[2,128,128]{2,1,0:T(8,128)S(1)}, f32[2,128,128]{2,1,0:T(8,128)S(1)}, u32[]{:S(2)}, u32[]{:S(2)}) collective-permute-start(f32[2,128,128]{2,1,0:T(8,128)S(1)} %get-tuple-element.12), channel_id=1, source_target_pairs={{0,1008},{8,1016},{16,0},{24,8},{32,16},{40,24},{48,32},{56,40},{6... | collective-permute-start | bytes 393224 | tf_op jit(solution)/shard_map/ppermute | solution.py:15
  155.6 18.3 %collective-permute-start.8 = (f32[2,128,128]{2,1,0:T(8,128)S(1)}, f32[2,128,128]{2,1,0:T(8,128)S(1)}, u32[]{:S(2)}, u32[]{:S(2)}) collective-permute-start(f32[2,128,128]{2,1,0:T(8,128)S(1)} %get-tuple-element.5), channel_id=1, source_target_pairs={{0,8},{8,16},{16,24},{24,32},{32,40},{40,48},{48,56},{56,64},{64,7... | collective-permute-start | bytes 393224 | tf_op jit(solution)/shard_map/ppermute | solution.py:15
  157.5 16.3 %collective-permute-start.10 = (f32[2,128,128]{2,1,0:T(8,128)S(1)}, f32[2,128,128]{2,1,0:T(8,128)S(1)}, u32[]{:S(2)}, u32[]{:S(2)}) collective-permute-start(f32[2,128,128]{2,1,0:T(8,128)S(1)} %get-tuple-element.6), channel_id=1, source_target_pairs={{0,1016},{8,0},{16,8},{24,16},{32,24},{40,32},{48,40},{56,48},{64,... | collective-permute-start | bytes 393224 | tf_op jit(solution)/shard_map/ppermute | solution.py:15
  164.5 10.2 %collective-permute-start.9 = (f32[2,128,128]{2,1,0:T(8,128)S(1)}, f32[2,128,128]{2,1,0:T(8,128)S(1)}, u32[]{:S(2)}, u32[]{:S(2)}) collective-permute-start(f32[2,128,128]{2,1,0:T(8,128)S(1)} %get-tuple-element.7), channel_id=1, source_target_pairs={{0,16},{8,24},{16,32},{24,40},{32,48},{40,56},{48,64},{56,72},{64,... | collective-permute-start | bytes 393224 | tf_op jit(solution)/shard_map/ppermute | solution.py:15
  166.4 9.7 %collective-permute-start.11 = (f32[2,128,128]{2,1,0:T(8,128)S(1)}, f32[2,128,128]{2,1,0:T(8,128)S(1)}, u32[]{:S(2)}, u32[]{:S(2)}) collective-permute-start(f32[2,128,128]{2,1,0:T(8,128)S(1)} %get-tuple-element.8), channel_id=1, source_target_pairs={{0,1008},{8,1016},{16,0},{24,8},{32,16},{40,24},{48,32},{56,40},{6... | collective-permute-start | bytes 393224 | tf_op jit(solution)/shard_map/ppermute | solution.py:15
where the time goes:
time: 219 us; the launch traced here: 218 us
  blocking collectives  111 us (51%)
  starting transfers between devices  54.3 us (25%)
  local copies, waits for them, and re-layouts  21.7 us (10%)
  matrix products  21.7 us (10%)
  waiting for transfers between devices  7.12 us (3%)
  other arithmetic  2.56 us (1%)
    psum x3, blocking collectives, on_device(): row_mass = lax.psum(jnp.sum(squared, axis=2), 'cls')  83.5 us
    ppermute x12, starting transfers between devices, from_behind(): lax.ppermute(value, axis, [(i, (i + by) % length) for i in range(length)])  54.3 us
    psum x1, blocking collectives, on_device(): first_mass = lax.psum(jnp.sum(blocks, axis=2), 'cls')  27.1 us
    dot_general x3, matrix products, on_device(): jnp.einsum('tij,tjc->tic', weights, operand, precision=lax.Precision.HIGH...  14.3 us
    dot_general x3, local copies, waits for them, and re-layouts, on_device(): jnp.einsum('tij,tjc->tic', weights, operand, precision=lax.Precision.HIGH...  9.29 us
    dot_general x3, matrix products, on_device(): jnp.einsum('bt,tic->bic', rows_onehot, products, precision=lax.Precision....  7.35 us
    ppermute x12, waiting for transfers between devices, from_behind(): lax.ppermute(value, axis, [(i, (i + by) % length) for i in range(length)])  7.12 us
    gather x3, local copies, waits for them, and re-layouts, on_device(): operand = buffer[tile_cols]  5.93 us
  transfers between devices with their start and end apart: 12, of which 6 were waited for; matrix products, arithmetic and copies ran while one was open for 0% of the time, Pallas kernels for 0%

commit v1 on v0

v1 whole, which is shorter than its diff:
```python
import jax
import jax.numpy as jnp
from jax import lax
from jax.experimental import pallas as pl
from jax.experimental.pallas import tpu as pltpu
from jax.sharding import PartitionSpec as P

CLASSES = 1024
ITERS = 3
SIDE = 128

VMEM = pl.BlockSpec(memory_space=pltpu.VMEM)
SMEM = pl.BlockSpec(memory_space=pltpu.SMEM)
F32 = jnp.float32
PARAMS = pltpu.CompilerParams(vmem_limit_bytes=16 * 1024 * 1024)


def shape(*dims):
    return jax.ShapeDtypeStruct(dims, F32)


def send_slot(position, odd):
    if position == 0:
        return 2 * odd
    if position == 1:
        return 2 - 2 * odd
    return 1 if position == 2 else 3


def buffer_block(col, odd):
    ghost = jnp.maximum(col - 8, 0)
    offset = lax.shift_right_logical(ghost, 1)
    near = jnp.where(offset == 0, 1 - odd, odd)
    pair = jnp.where(lax.rem(offset, 2) == 1, 2 + lax.shift_right_logical(offset, 1), near)
    return jnp.where(col < 8, col, 8 + 2 * pair + lax.rem(ghost, 2))


def parity():
    return lax.rem(lax.axis_index("dom"), 2)


def gather(source, send, outgoing):
    odd = parity()
    for position in range(4):
        slot = send_slot(position, odd)
        for within in range(2):
            outgoing[position][within] = source[send[0, slot, within]]


def lane_sums(block):
    return jnp.sum(jnp.transpose(block), axis=0, keepdims=True)


def first_kernel(labels, send, out0, out1, out2, out3, own):
    gather(labels, send, (out0, out1, out2, out3))
    for block in range(8):
        own[block : block + 1, :] = lane_sums(labels[block])


def mass_kernel(own, in0, in1, in2, in3, parts):
    rows = [own[...]]
    for pair in (in0, in1, in2, in3):
        for within in range(2):
            rows.append(lane_sums(pair[within]))
    partial = jnp.concatenate(rows, axis=0)
    for share in range(8):
        parts[share] = partial


def scales(parts, blocks):
    total = parts[0]
    for share in range(1, 8):
        total = total + parts[share]
    scale = CLASSES / total
    full = jnp.concatenate([scale, jnp.zeros((SIDE - blocks, SIDE), F32)], axis=0)
    return jnp.transpose(full)


def split(value):
    high = value.astype(jnp.bfloat16)
    low = (value - high.astype(F32)).astype(jnp.bfloat16)
    return high, low


def spread_kernel(first, *refs):
    if first:
        (tiles, rows, cols, send, mask, source, in0, in1, in2, in3, parts,
         anchor, squared, out0, out1, out2, out3, own, operand, products) = refs
    else:
        (tiles, rows, cols, send, anchor, source, in0, in1, in2, in3, parts,
         squared, out0, out1, out2, out3, own, operand, products) = refs
    scale = scales(parts, 16)
    if first:
        seeded = jnp.concatenate(
            [mask[...].astype(F32), jnp.zeros((SIDE - 8, SIDE), F32)], axis=0
        )
        seeded = 64.0 * jnp.transpose(seeded)
    received = (in0, in1, in2, in3)
    for block in range(16):
        if block < 8:
            value = source[block]
        else:
            value = received[(block - 8) // 2][(block - 8) % 2]
        value = value * scale[:, block : block + 1]
        if first and block < 8:
            anchor[block] = seeded[:, block : block + 1] * value + 4.0
        high, low = split(value)
        operand[block, :SIDE, :] = high
        operand[block, SIDE:, :] = low
    odd = parity()
    for tile in range(32):
        weights = tiles[tile]
        products[tile] = jnp.dot(
            jnp.concatenate([weights, weights], axis=1),
            operand[buffer_block(cols[tile], odd)],
            preferred_element_type=F32,
        )
    squared[...] = anchor[...]
    for tile in range(32):
        row = rows[tile]
        squared[row] = squared[row] + products[tile]
    for block in range(8):
        value = squared[block]
        value = value * value
        squared[block] = value
        own[block : block + 1, :] = lane_sums(value)
    gather(squared, send, (out0, out1, out2, out3))


def last_kernel(squared, parts, out):
    scale = scales(parts, 8)
    for block in range(8):
        out[block] = squared[block] * scale[:, block : block + 1]


def exchange(outgoing):
    count = lax.axis_size("dom")
    targets = (
        lambda i: i ^ 1,
        lambda i: ((i + 1) ^ 1) - 1,
        lambda i: i + 2,
        lambda i: i - 2,
    )
    received = []
    for pair, target in zip(outgoing, targets):
        received.append(
            lax.ppermute(pair, "dom", [(i, target(i) % count) for i in range(count)])
        )
    return received


def on_device(tiles, tile_rows, tile_cols, send_lists, seed_mask, labels):
    blocks = labels.reshape(8, SIDE, SIDE)
    mask = seed_mask.reshape(8, SIDE)
    pairs = [shape(2, SIDE, SIDE)] * 4
    *outgoing, own = pl.pallas_call(
        first_kernel,
        out_shape=pairs + [shape(8, SIDE)],
        in_specs=[VMEM, SMEM],
        out_specs=[VMEM] * 5,
        compiler_params=PARAMS,
    )(blocks, send_lists)
    source = blocks
    anchor = None
    for iteration in range(ITERS):
        first = iteration == 0
        received = exchange(outgoing)
        parts = pl.pallas_call(
            mass_kernel,
            out_shape=shape(8, 16, SIDE),
            in_specs=[VMEM] * 5,
            out_specs=VMEM,
            compiler_params=PARAMS,
        )(own, *received)
        parts = lax.all_to_all(parts, "cls", 0, 0)
        results = pl.pallas_call(
            lambda *refs, first=first: spread_kernel(first, *refs),
            out_shape=[shape(8, SIDE, SIDE)] * (2 if first else 1) + pairs + [shape(8, SIDE)],
            in_specs=[VMEM, SMEM, SMEM, SMEM] + [VMEM] * 7,
            out_specs=[VMEM] * (7 if first else 6),
            scratch_shapes=[
                pltpu.VMEM((16, 2 * SIDE, SIDE), jnp.bfloat16),
                pltpu.VMEM((32, SIDE, SIDE), F32),
            ],
            compiler_params=PARAMS,
        )(tiles, tile_rows, tile_cols, send_lists, mask if first else anchor, source, *received, parts)
        if first:
            anchor, *results = results
        source, *outgoing, own = results
    parts = lax.all_to_all(jnp.broadcast_to(own[None], (8, 8, SIDE)), "cls", 0, 0)
    out = pl.pallas_call(
        last_kernel,
        out_shape=shape(8, SIDE, SIDE),
        in_specs=[VMEM, VMEM],
        out_specs=VMEM,
        compiler_params=PARAMS,
    )(source, parts)
    return out.reshape(8 * SIDE, SIDE)


def solution(mesh):
    return jax.shard_map(
        on_device,
        mesh=mesh,
        in_specs=(
            P("dom", None, None),
            P("dom"),
            P("dom"),
            P("dom", None, None),
            P("dom"),
            P("dom", "cls"),
        ),
        out_specs=P("dom", "cls"),
        check_vma=False,
    )
```

time: 219 us -> 136 us (0.62)
  blocking collectives: 111 us -> 46.5 us
  matrix products: 21.7 us -> 0 us
  local copies, waits for them, and re-layouts: 21.7 us -> 3.61 us
  starting transfers between devices: 54.3 us -> 68.5 us
  Pallas kernels: 0 us -> 9.23 us
  other arithmetic: 2.56 us -> 0 us
    psum x4 -> x0, blocking collectives: 111 us -> none  [the longest x3 83.5 us: on_device(): row_mass = lax.psum(jnp.sum(squared, axis=2), 'cls')]
    all_to_all x0 -> x4, blocking collectives: none -> 46.5 us  [the longest x3 36.1 us: on_device(): parts = lax.all_to_all(parts, 'cls', 0, 0)]
    dot_general x6 -> x0, matrix products: 21.7 us -> none  [the longest x3 14.3 us: on_device(): jnp.einsum('tij,tjc->tic', weights, operand, precision=lax.Precision.HIGH...]
    ppermute x12, starting transfers between devices: 54.3 us -> 68.5 us  [exchange(): lax.ppermute(pair, 'dom', [(i, target(i) % count) for i in range(count)])]
    dot_general x3 -> x0, local copies, waits for them, and re-layouts: 9.29 us -> none  [on_device(): jnp.einsum('tij,tjc->tic', weights, operand, precision=lax.Precision.HIGH...]
    pallas_call x0 -> x8, Pallas kernels: none -> 9.23 us  [the longest x3 6.7 us: on_device(): pl.pallas_call(lambda *refs, first=first: spread_kernel(first, *refs), ou...]
    gather x6 -> x0, local copies, waits for them, and re-layouts: 7.67 us -> none  [the longest x3 5.93 us: on_device(): operand = buffer[tile_cols]]
    unnamed x9 -> x13, local copies, waits for them, and re-layouts: 0.87 us -> 3.61 us
where the time goes in v1:
time: 136 us
  starting transfers between devices  68.5 us (50%)
  blocking collectives  46.5 us (34%)
  Pallas kernels  9.23 us (7%)
  waiting for transfers between devices  7.45 us (5%)
  local copies, waits for them, and re-layouts  3.61 us (3%)
    ppermute x12, starting transfers between devices, exchange(): lax.ppermute(pair, 'dom', [(i, target(i) % count) for i in range(count)])  68.5 us
    all_to_all x3, blocking collectives, on_device(): parts = lax.all_to_all(parts, 'cls', 0, 0)  36.1 us
    all_to_all x1, blocking collectives, on_device(): lax.all_to_all(jnp.broadcast_to(own[None], (8, 8, SIDE)), 'cls', 0, 0)  10.4 us
    ppermute x12, waiting for transfers between devices, exchange(): lax.ppermute(pair, 'dom', [(i, target(i) % count) for i in range(count)])  7.45 us
    pallas_call x3, Pallas kernels, on_device(): pl.pallas_call(lambda *refs, first=first: spread_kernel(first, *refs), ou...  6.7 us
    unnamed x13, local copies, waits for them, and re-layouts  3.61 us
  transfers between devices with their start and end apart: 12, of which 6 were waited for; matrix products, arithmetic and copies ran while one was open for 0% of the time, Pallas kernels for 0%

profile of v1, /device:TPU:16, one launch (start us, length us, event | category | flops | bytes accessed | tf_op | source)
XLA Modules:
  0.0 135.5 jit_solution(1283648993084982653)
XLA Ops:
  0.0 0.0 copy-start
  0.0 0.9 copy.10.send.refs_3_
  0.9 0.0 copy-start.1
  0.9 1.0 copy-done.1
  1.9 0.8 shard_map.64
  2.7 1.9 %collective-permute-start = (f32[2,128,128]{2,1,0:T(8,128)S(1)}, f32[2,128,128]{2,1,0:T(8,128)S(1)}, u32[]{:S(2)}, u32[]{:S(2)}) collective-permute-start(f32[2,128,128]{2,1,0:T(8,128)S(1)} %get-tuple-element.25), channel_id=1, source_target_pairs={{0,8},{8,0},{16,24},{24,16},{32,40},{40,32},{48,56},{56,48},{64,72... | collective-permute-start | bytes 393224 | tf_op jit(solution)/shard_map/ppermute | solution.py:147
  4.6 19.7 %collective-permute-start.1 = (f32[2,128,128]{2,1,0:T(8,128)S(1)}, f32[2,128,128]{2,1,0:T(8,128)S(1)}, u32[]{:S(2)}, u32[]{:S(2)}) collective-permute-start(f32[2,128,128]{2,1,0:T(8,128)S(1)} %get-tuple-element.26), channel_id=1, source_target_pairs={{0,1016},{8,16},{16,8},{24,32},{32,24},{40,48},{48,40},{56,64},{64... | collective-permute-start | bytes 393224 | tf_op jit(solution)/shard_map/ppermute | solution.py:147
  24.3 1.9 %collective-permute-start.2 = (f32[2,128,128]{2,1,0:T(8,128)S(1)}, f32[2,128,128]{2,1,0:T(8,128)S(1)}, u32[]{:S(2)}, u32[]{:S(2)}) collective-permute-start(f32[2,128,128]{2,1,0:T(8,128)S(1)} %get-tuple-element.27), channel_id=1, source_target_pairs={{0,16},{8,24},{16,32},{24,40},{32,48},{40,56},{48,64},{56,72},{64,... | collective-permute-start | bytes 393224 | tf_op jit(solution)/shard_map/ppermute | solution.py:147
  26.3 7.2 %collective-permute-start.3 = (f32[2,128,128]{2,1,0:T(8,128)S(1)}, f32[2,128,128]{2,1,0:T(8,128)S(1)}, u32[]{:S(2)}, u32[]{:S(2)}) collective-permute-start(f32[2,128,128]{2,1,0:T(8,128)S(1)} %get-tuple-element.28), channel_id=1, source_target_pairs={{0,1008},{8,1016},{16,0},{24,8},{32,16},{40,24},{48,32},{56,40},{6... | collective-permute-start | bytes 393224 | tf_op jit(solution)/shard_map/ppermute | solution.py:147
  33.5 0.0 collective-permute-done.in0.refs_6_
  33.5 0.0 collective-permute-done.1.in1.refs_7_
  33.5 1.0 collective-permute-done.2.in2.refs_8_
  34.5 1.5 %collective-permute-done.3.in3.refs_9_ = f32[2,128,128]{2,1,0:T(8,128)S(1)} collective-permute-done((f32[2,128,128]{2,1,0:T(8,128)S(1)}, f32[2,128,128]{2,1,0:T(8,128)S(1)}, u32[]{:S(2)}, u32[]{:S(2)}) %collective-permute-start.3) | collective-permute-done | bytes 131104 | tf_op jit(solution)/shard_map/ppermute | solution.py:147
  36.0 0.2 shard_map.65
  36.2 0.0 copy-start.5
  36.2 14.6 %all_to_all.20.refs_10_ = f32[8,16,128]{2,1,0:T(8,128)S(1)} all-to-all(f32[8,16,128]{2,1,0:T(8,128)S(1)} %shard_map.65), channel_id=1, replica_groups=mesh['dom'=128,'cls'=8] {'cls'}, dimensions={0} | all-to-all | bytes 131072 | tf_op jit(solution)/shard_map/all_to_all | solution.py:175
  50.8 0.0 copy-start.3
  50.9 0.0 copy-start.4
  50.9 0.0 copy-done
  50.9 0.0 copy-done.5
  50.9 0.6 copy-done.3
  51.5 0.0 copy-done.4
  51.5 0.0 copy-start.2
  51.5 1.0 copy-done.2
  52.6 2.0 %shard_map.66 = (f32[8,128,128]{2,1,0:T(8,128)S(1)}, f32[8,128,128]{2,1,0:T(8,128)S(1)}, f32[2,128,128]{2,1,0:T(8,128)S(1)}, f32[2,128,128]{2,1,0:T(8,128)S(1)},...) custom-call(bf16[32,128,128]{2,1,0:T(8,128)(2,1)S(1)} %copy-done, s32[32]{0:T(128)S(1)} %copy-done.3, ...), custom_call_target="tpu_custom_call" | custom-call | tf_op jit(solution)/shard_map/pallas_call | solution.py:176
  54.6 1.9 %collective-permute-start.4 = (f32[2,128,128]{2,1,0:T(8,128)S(1)}, f32[2,128,128]{2,1,0:T(8,128)S(1)}, u32[]{:S(2)}, u32[]{:S(2)}) collective-permute-start(f32[2,128,128]{2,1,0:T(8,128)S(1)} %get-tuple-element.32), channel_id=1, source_target_pairs={{0,8},{8,0},{16,24},{24,16},{32,40},{40,32},{48,56},{56,48},{64,72... | collective-permute-start | bytes 393224 | tf_op jit(solution)/shard_map/ppermute | solution.py:147
  56.5 7.8 %collective-permute-start.5 = (f32[2,128,128]{2,1,0:T(8,128)S(1)}, f32[2,128,128]{2,1,0:T(8,128)S(1)}, u32[]{:S(2)}, u32[]{:S(2)}) collective-permute-start(f32[2,128,128]{2,1,0:T(8,128)S(1)} %get-tuple-element.33), channel_id=1, source_target_pairs={{0,1016},{8,16},{16,8},{24,32},{32,24},{40,48},{48,40},{56,64},{64... | collective-permute-start | bytes 393224 | tf_op jit(solution)/shard_map/ppermute | solution.py:147
  64.3 1.9 %collective-permute-start.6 = (f32[2,128,128]{2,1,0:T(8,128)S(1)}, f32[2,128,128]{2,1,0:T(8,128)S(1)}, u32[]{:S(2)}, u32[]{:S(2)}) collective-permute-start(f32[2,128,128]{2,1,0:T(8,128)S(1)} %get-tuple-element.34), channel_id=1, source_target_pairs={{0,16},{8,24},{16,32},{24,40},{32,48},{40,56},{48,64},{56,72},{64,... | collective-permute-start | bytes 393224 | tf_op jit(solution)/shard_map/ppermute | solution.py:147
  66.2 7.2 %collective-permute-start.7 = (f32[2,128,128]{2,1,0:T(8,128)S(1)}, f32[2,128,128]{2,1,0:T(8,128)S(1)}, u32[]{:S(2)}, u32[]{:S(2)}) collective-permute-start(f32[2,128,128]{2,1,0:T(8,128)S(1)} %get-tuple-element.35), channel_id=1, source_target_pairs={{0,1008},{8,1016},{16,0},{24,8},{32,16},{40,24},{48,32},{56,40},{6... | collective-permute-start | bytes 393224 | tf_op jit(solution)/shard_map/ppermute | solution.py:147
  73.5 0.0 collective-permute-done.4.in0.refs_6_
  73.5 0.0 collective-permute-done.5.in1.refs_7_
  73.5 1.0 collective-permute-done.6.in2.refs_8_
  74.5 1.5 %collective-permute-done.7.in3.refs_9_ = f32[2,128,128]{2,1,0:T(8,128)S(1)} collective-permute-done((f32[2,128,128]{2,1,0:T(8,128)S(1)}, f32[2,128,128]{2,1,0:T(8,128)S(1)}, u32[]{:S(2)}, u32[]{:S(2)}) %collective-permute-start.7) | collective-permute-done | bytes 131104 | tf_op jit(solution)/shard_map/ppermute | solution.py:147
  76.0 0.2 shard_map.67
  76.2 10.8 %all_to_all.21.refs_10_ = f32[8,16,128]{2,1,0:T(8,128)S(1)} all-to-all(f32[8,16,128]{2,1,0:T(8,128)S(1)} %shard_map.67), channel_id=1, replica_groups=mesh['dom'=128,'cls'=8] {'cls'}, dimensions={0} | all-to-all | bytes 131072 | tf_op jit(solution)/shard_map/all_to_all | solution.py:175
  86.9 2.0 %shard_map.68 = (f32[8,128,128]{2,1,0:T(8,128)S(1)}, f32[2,128,128]{2,1,0:T(8,128)S(1)}, f32[2,128,128]{2,1,0:T(8,128)S(1)}, f32[2,128,128]{2,1,0:T(8,128)S(1)},...) custom-call(bf16[32,128,128]{2,1,0:T(8,128)(2,1)S(1)} %copy-done, s32[32]{0:T(128)S(1)} %copy-done.3, s32[32]{0:T(128)S(1)} %copy-done.4, ...), custom_call_target="tpu_custom_call" | custom-call | tf_op jit(solution)/shard_map/pallas_call | solution.py:176
  88.9 1.9 %collective-permute-start.8 = (f32[2,128,128]{2,1,0:T(8,128)S(1)}, f32[2,128,128]{2,1,0:T(8,128)S(1)}, u32[]{:S(2)}, u32[]{:S(2)}) collective-permute-start(f32[2,128,128]{2,1,0:T(8,128)S(1)} %get-tuple-element.38), channel_id=1, source_target_pairs={{0,8},{8,0},{16,24},{24,16},{32,40},{40,32},{48,56},{56,48},{64,72... | collective-permute-start | bytes 393224 | tf_op jit(solution)/shard_map/ppermute | solution.py:147
  90.9 7.8 %collective-permute-start.9 = (f32[2,128,128]{2,1,0:T(8,128)S(1)}, f32[2,128,128]{2,1,0:T(8,128)S(1)}, u32[]{:S(2)}, u32[]{:S(2)}) collective-permute-start(f32[2,128,128]{2,1,0:T(8,128)S(1)} %get-tuple-element.39), channel_id=1, source_target_pairs={{0,1016},{8,16},{16,8},{24,32},{32,24},{40,48},{48,40},{56,64},{64... | collective-permute-start | bytes 393224 | tf_op jit(solution)/shard_map/ppermute | solution.py:147
  98.7 1.9 %collective-permute-start.10 = (f32[2,128,128]{2,1,0:T(8,128)S(1)}, f32[2,128,128]{2,1,0:T(8,128)S(1)}, u32[]{:S(2)}, u32[]{:S(2)}) collective-permute-start(f32[2,128,128]{2,1,0:T(8,128)S(1)} %get-tuple-element.40), channel_id=1, source_target_pairs={{0,16},{8,24},{16,32},{24,40},{32,48},{40,56},{48,64},{56,72},{64,... | collective-permute-start | bytes 393224 | tf_op jit(solution)/shard_map/ppermute | solution.py:147
  100.6 7.2 %collective-permute-start.11 = (f32[2,128,128]{2,1,0:T(8,128)S(1)}, f32[2,128,128]{2,1,0:T(8,128)S(1)}, u32[]{:S(2)}, u32[]{:S(2)}) collective-permute-start(f32[2,128,128]{2,1,0:T(8,128)S(1)} %get-tuple-element.41), channel_id=1, source_target_pairs={{0,1008},{8,1016},{16,0},{24,8},{32,16},{40,24},{48,32},{56,40},{6... | collective-permute-start | bytes 393224 | tf_op jit(solution)/shard_map/ppermute | solution.py:147
  107.8 0.0 collective-permute-done.8.in0.refs_6_
  107.9 0.0 collective-permute-done.9.in1.refs_7_
  107.9 1.0 collective-permute-done.10.in2.refs_8_
  108.8 1.5 %collective-permute-done.11.in3.refs_9_ = f32[2,128,128]{2,1,0:T(8,128)S(1)} collective-permute-done((f32[2,128,128]{2,1,0:T(8,128)S(1)}, f32[2,128,128]{2,1,0:T(8,128)S(1)}, u32[]{:S(2)}, u32[]{:S(2)}) %collective-permute-start.11) | collective-permute-done | bytes 131104 | tf_op jit(solution)/shard_map/ppermute | solution.py:147
  110.3 0.2 shard_map.69
  110.6 10.8 %all_to_all.22.refs_10_ = f32[8,16,128]{2,1,0:T(8,128)S(1)} all-to-all(f32[8,16,128]{2,1,0:T(8,128)S(1)} %shard_map.69), channel_id=1, replica_groups=mesh['dom'=128,'cls'=8] {'cls'}, dimensions={0} | all-to-all | bytes 131072 | tf_op jit(solution)/shard_map/all_to_all | solution.py:175
  121.3 2.7 %shard_map.70 = (f32[8,128,128]{2,1,0:T(8,128)S(1)}, f32[2,128,128]{2,1,0:T(8,128)}, f32[2,128,128]{2,1,0:T(8,128)}, f32[2,128,128]{2,1,0:T(8,128)}, f32[2,128,128]{2,1,0:T(8,128)}, /*index=5*/f32[8,128]{1,0:T(8,128)S(1)}) custom-call(bf16[32,128,128]{2,1,0:T(8,128)(2,1)S(1)} %copy-done, s32[32]{0:T(128)S(1)} %copy-done.3, s32[32]{0:T(128)S(1)} %copy-done.4, ...), custom_call_target="tpu_custom_call" | custom-call | tf_op jit(solution)/shard_map/pallas_call | solution.py:176
  124.0 10.4 %all_to_all.23.parts = f32[8,8,128]{2,1,0:T(8,128)S(1)} all-to-all(f32[8,8,128]{2,1,0:T(8,128)S(1)} %broadcast_in_dim.2), channel_id=1, replica_groups=mesh['dom'=128,'cls'=8] {'cls'}, dimensions={0} | all-to-all | bytes 65536 | tf_op jit(solution)/shard_map/all_to_all | solution.py:190
  134.4 1.1 shard_map.71
  (1 shorter events, 0.0 us)
Async XLA Ops:
  0.0 50.9 %copy-start = (bf16[32,128,128]{2,1,0:T(8,128)(2,1)S(1)}, bf16[32,128,128]{2,1,0:T(8,128)(2,1)}, u32[]{:S(2)}) copy-start(bf16[32,128,128]{2,1,0:T(8,128)(2,1)} %refs_0_.5) | copy-start | bytes 3145732
  0.9 1.0 copy-start.1
  2.7 30.8 %collective-permute-start = (f32[2,128,128]{2,1,0:T(8,128)S(1)}, f32[2,128,128]{2,1,0:T(8,128)S(1)}, u32[]{:S(2)}, u32[]{:S(2)}) collective-permute-start(f32[2,128,128]{2,1,0:T(8,128)S(1)} %get-tuple-element.25), channel_id=1, source_target_pairs={{0,8},{8,0},{16,24},{24,16},{32,40},{40,32},{48,56},{56,48},{64,72... | collective-permute-start | bytes 393224 | tf_op jit(solution)/shard_map/ppermute | solution.py:147
  4.6 28.9 %collective-permute-start.1 = (f32[2,128,128]{2,1,0:T(8,128)S(1)}, f32[2,128,128]{2,1,0:T(8,128)S(1)}, u32[]{:S(2)}, u32[]{:S(2)}) collective-permute-start(f32[2,128,128]{2,1,0:T(8,128)S(1)} %get-tuple-element.26), channel_id=1, source_target_pairs={{0,1016},{8,16},{16,8},{24,32},{32,24},{40,48},{48,40},{56,64},{64... | collective-permute-start | bytes 393224 | tf_op jit(solution)/shard_map/ppermute | solution.py:147
  24.3 10.2 %collective-permute-start.2 = (f32[2,128,128]{2,1,0:T(8,128)S(1)}, f32[2,128,128]{2,1,0:T(8,128)S(1)}, u32[]{:S(2)}, u32[]{:S(2)}) collective-permute-start(f32[2,128,128]{2,1,0:T(8,128)S(1)} %get-tuple-element.27), channel_id=1, source_target_pairs={{0,16},{8,24},{16,32},{24,40},{32,48},{40,56},{48,64},{56,72},{64,... | collective-permute-start | bytes 393224 | tf_op jit(solution)/shard_map/ppermute | solution.py:147
  26.3 9.7 %collective-permute-start.3 = (f32[2,128,128]{2,1,0:T(8,128)S(1)}, f32[2,128,128]{2,1,0:T(8,128)S(1)}, u32[]{:S(2)}, u32[]{:S(2)}) collective-permute-start(f32[2,128,128]{2,1,0:T(8,128)S(1)} %get-tuple-element.28), channel_id=1, source_target_pairs={{0,1008},{8,1016},{16,0},{24,8},{32,16},{40,24},{48,32},{56,40},{6... | collective-permute-start | bytes 393224 | tf_op jit(solution)/shard_map/ppermute | solution.py:147
  36.2 14.6 %copy-start.5 = (s32[1024]{0:T(1024)S(1)}, s32[1024]{0:T(1024)}, u32[]{:S(2)}) copy-start(s32[1024]{0:T(1024)} %param.10) | copy-start | bytes 12292
  50.8 0.7 copy-start.3
  50.9 0.7 copy-start.4
  51.5 1.0 copy-start.2
  54.6 18.9 %collective-permute-start.4 = (f32[2,128,128]{2,1,0:T(8,128)S(1)}, f32[2,128,128]{2,1,0:T(8,128)S(1)}, u32[]{:S(2)}, u32[]{:S(2)}) collective-permute-start(f32[2,128,128]{2,1,0:T(8,128)S(1)} %get-tuple-element.32), channel_id=1, source_target_pairs={{0,8},{8,0},{16,24},{24,16},{32,40},{40,32},{48,56},{56,48},{64,72... | collective-permute-start | bytes 393224 | tf_op jit(solution)/shard_map/ppermute | solution.py:147
  56.5 17.0 %collective-permute-start.5 = (f32[2,128,128]{2,1,0:T(8,128)S(1)}, f32[2,128,128]{2,1,0:T(8,128)S(1)}, u32[]{:S(2)}, u32[]{:S(2)}) collective-permute-start(f32[2,128,128]{2,1,0:T(8,128)S(1)} %get-tuple-element.33), channel_id=1, source_target_pairs={{0,1016},{8,16},{16,8},{24,32},{32,24},{40,48},{48,40},{56,64},{64... | collective-permute-start | bytes 393224 | tf_op jit(solution)/shard_map/ppermute | solution.py:147
  64.3 10.2 %collective-permute-start.6 = (f32[2,128,128]{2,1,0:T(8,128)S(1)}, f32[2,128,128]{2,1,0:T(8,128)S(1)}, u32[]{:S(2)}, u32[]{:S(2)}) collective-permute-start(f32[2,128,128]{2,1,0:T(8,128)S(1)} %get-tuple-element.34), channel_id=1, source_target_pairs={{0,16},{8,24},{16,32},{24,40},{32,48},{40,56},{48,64},{56,72},{64,... | collective-permute-start | bytes 393224 | tf_op jit(solution)/shard_map/ppermute | solution.py:147
  66.2 9.7 %collective-permute-start.7 = (f32[2,128,128]{2,1,0:T(8,128)S(1)}, f32[2,128,128]{2,1,0:T(8,128)S(1)}, u32[]{:S(2)}, u32[]{:S(2)}) collective-permute-start(f32[2,128,128]{2,1,0:T(8,128)S(1)} %get-tuple-element.35), channel_id=1, source_target_pairs={{0,1008},{8,1016},{16,0},{24,8},{32,16},{40,24},{48,32},{56,40},{6... | collective-permute-start | bytes 393224 | tf_op jit(solution)/shard_map/ppermute | solution.py:147
  88.9 18.9 %collective-permute-start.8 = (f32[2,128,128]{2,1,0:T(8,128)S(1)}, f32[2,128,128]{2,1,0:T(8,128)S(1)}, u32[]{:S(2)}, u32[]{:S(2)}) collective-permute-start(f32[2,128,128]{2,1,0:T(8,128)S(1)} %get-tuple-element.38), channel_id=1, source_target_pairs={{0,8},{8,0},{16,24},{24,16},{32,40},{40,32},{48,56},{56,48},{64,72... | collective-permute-start | bytes 393224 | tf_op jit(solution)/shard_map/ppermute | solution.py:147
  90.9 17.0 %collective-permute-start.9 = (f32[2,128,128]{2,1,0:T(8,128)S(1)}, f32[2,128,128]{2,1,0:T(8,128)S(1)}, u32[]{:S(2)}, u32[]{:S(2)}) collective-permute-start(f32[2,128,128]{2,1,0:T(8,128)S(1)} %get-tuple-element.39), channel_id=1, source_target_pairs={{0,1016},{8,16},{16,8},{24,32},{32,24},{40,48},{48,40},{56,64},{64... | collective-permute-start | bytes 393224 | tf_op jit(solution)/shard_map/ppermute | solution.py:147
  98.7 10.2 %collective-permute-start.10 = (f32[2,128,128]{2,1,0:T(8,128)S(1)}, f32[2,128,128]{2,1,0:T(8,128)S(1)}, u32[]{:S(2)}, u32[]{:S(2)}) collective-permute-start(f32[2,128,128]{2,1,0:T(8,128)S(1)} %get-tuple-element.40), channel_id=1, source_target_pairs={{0,16},{8,24},{16,32},{24,40},{32,48},{40,56},{48,64},{56,72},{64,... | collective-permute-start | bytes 393224 | tf_op jit(solution)/shard_map/ppermute | solution.py:147
  100.6 9.7 %collective-permute-start.11 = (f32[2,128,128]{2,1,0:T(8,128)S(1)}, f32[2,128,128]{2,1,0:T(8,128)S(1)}, u32[]{:S(2)}, u32[]{:S(2)}) collective-permute-start(f32[2,128,128]{2,1,0:T(8,128)S(1)} %get-tuple-element.41), channel_id=1, source_target_pairs={{0,1008},{8,1016},{16,0},{24,8},{32,16},{40,24},{48,32},{56,40},{6... | collective-permute-start | bytes 393224 | tf_op jit(solution)/shard_map/ppermute | solution.py:147

commit v2 on v1

v2 whole, which is shorter than its diff:
```python
import jax
import jax.numpy as jnp
from jax import lax
from jax.experimental import pallas as pl
from jax.experimental.pallas import tpu as pltpu
from jax.sharding import Mesh
from jax.sharding import PartitionSpec as P

CLASSES = 1024
ITERS = 3
SIDE = 128

VMEM = pl.BlockSpec(memory_space=pltpu.VMEM)
SMEM = pl.BlockSpec(memory_space=pltpu.SMEM)
F32 = jnp.float32
PARAMS = pltpu.CompilerParams(vmem_limit_bytes=16 * 1024 * 1024)


def shape(*dims):
    return jax.ShapeDtypeStruct(dims, F32)


def shift_right(value, by):
    return lax.shift_right_logical(value, by)


def gather(source, send, out0, out1):
    odd = lax.rem(lax.axis_index("chip"), 2)
    for out, behind in ((out0, odd), (out1, 1 - odd)):
        for part in range(2):
            slot = 2 * behind + 1 - part
            for within in range(2):
                out[2 * part + within] = source[send[0, slot, within]]


def operand_block(col):
    odd = lax.rem(lax.axis_index("chip"), 2)
    core = lax.axis_index("core")
    ghost = jnp.maximum(col - 8, 0)
    offset = shift_right(ghost, 1)
    half = shift_right(offset, 1)
    near = half ^ (1 - core)
    far = 2 + (half ^ (1 - odd))
    pair = jnp.where(lax.rem(offset, 2) == 1, far, near)
    return jnp.where(col < 8, col, 8 + 2 * pair + lax.rem(ghost, 2))


def lane_sums(block):
    return jnp.sum(jnp.transpose(block), axis=0, keepdims=True)


def first_kernel(labels, rows, cols, send, mask, kept, out0, out1, own):
    gather(labels, send, out0, out1)
    for block in range(8):
        kept[block] = labels[block]
        own[block : block + 1, :] = lane_sums(labels[block])


def mass_kernel(send, source, own, in0, in1, parts, relay, rows):
    odd = lax.rem(lax.axis_index("chip"), 2)
    core = lax.axis_index("core")
    rows[0:8, :] = own[...]
    for within in range(2):
        block = send[0, 2 * core, within]
        relay[within] = source[block]
        rows[12 + within : 13 + within, :] = own[pl.ds(block, 1), :]
        rows[8 + within : 9 + within, :] = lane_sums(in0[within])
        rows[10 + within : 11 + within, :] = lane_sums(in1[within])

    def pass_on(received):
        for within in range(2):
            value = received[2 + within]
            relay[2 + within] = value
            rows[14 + within : 15 + within, :] = lane_sums(value)

    pl.when(odd == core)(lambda: pass_on(in0))
    pl.when(odd != core)(lambda: pass_on(in1))
    partial = rows[...]
    for share in range(16):
        parts[share] = partial


def scales(total, blocks):
    scale = CLASSES / total
    full = jnp.concatenate([scale, jnp.zeros((SIDE - blocks, SIDE), F32)], axis=0)
    return jnp.transpose(full)


def total_of(parts, core):
    total = parts[8 * core]
    for share in range(1, 8):
        total = total + parts[8 * core + share]
    return total


def split(value):
    high = value.astype(jnp.bfloat16)
    low = (value - high.astype(F32)).astype(jnp.bfloat16)
    return high, low


def spread_kernel(first, last, *refs):
    refs = list(refs)
    tiles, rows, cols, send, mask, source, in0, in1, near, parts = refs[:10]
    refs = refs[10:]
    anchor = refs.pop(0) if first else mask
    squared = refs.pop(0)
    if last:
        own_parts, operand, products = refs
    else:
        out0, out1, own, operand, products = refs
    core = lax.axis_index("core")
    mine = total_of(parts, core)
    mate = total_of(parts, 1 - core)
    scale = scales(jnp.concatenate([mine[0:8], mate[12:16], mine[8:12]], axis=0), 16)
    if first:
        seeded = jnp.concatenate(
            [mask[...].astype(F32), jnp.zeros((SIDE - 8, SIDE), F32)], axis=0
        )
        seeded = 64.0 * jnp.transpose(seeded)
    blocks = [(source, block) for block in range(8)]
    blocks += [(near, block) for block in range(4)]
    blocks += [(in0, 0), (in0, 1), (in1, 0), (in1, 1)]
    for block, (ref, place) in enumerate(blocks):
        value = ref[place] * scale[:, block : block + 1]
        if first and block < 8:
            anchor[block] = seeded[:, block : block + 1] * value + 4.0
        high, low = split(value)
        operand[block, :SIDE, :] = high
        operand[block, SIDE:, :] = low
    for tile in range(32):
        weights = tiles[tile]
        products[tile] = jnp.dot(
            jnp.concatenate([weights, weights], axis=1),
            operand[operand_block(cols[tile])],
            preferred_element_type=F32,
        )
    squared[...] = anchor[...]
    for tile in range(32):
        row = rows[tile]
        squared[row] = squared[row] + products[tile]
    sums = []
    for block in range(8):
        value = squared[block]
        value = value * value
        squared[block] = value
        sums.append(lane_sums(value))
    sums = jnp.concatenate(sums, axis=0)
    if last:
        for share in range(8):
            own_parts[share] = sums
    else:
        own[...] = sums
        gather(squared, send, out0, out1)


def last_kernel(squared, parts, out):
    scale = scales(total_of(parts, 0), 8)
    for block in range(8):
        out[block] = squared[block] * scale[:, block : block + 1]


def on_device(tiles, tile_rows, tile_cols, send_lists, seed_mask, labels):
    chips = lax.axis_size("chip")
    first_swap = [(i, i ^ 1) for i in range(chips)]
    second_swap = [(i, (((i + 1) ^ 1) - 1) % chips) for i in range(chips)]
    blocks = labels.reshape(8, SIDE, SIDE)
    mask = seed_mask.reshape(8, SIDE)
    own_shape = shape(8, SIDE, SIDE)
    swap_shape = shape(4, SIDE, SIDE)
    source, out0, out1, own = pl.pallas_call(
        first_kernel,
        out_shape=[own_shape, swap_shape, swap_shape, shape(8, SIDE)],
        in_specs=[VMEM, SMEM, SMEM, SMEM, VMEM],
        out_specs=[VMEM] * 4,
        compiler_params=PARAMS,
    )(blocks, tile_rows, tile_cols, send_lists, mask)
    anchor = None
    for iteration in range(ITERS):
        first = iteration == 0
        last = iteration == ITERS - 1
        in0 = lax.ppermute(out0, "chip", first_swap)
        in1 = lax.ppermute(out1, "chip", second_swap)
        parts, relay = pl.pallas_call(
            mass_kernel,
            out_shape=[shape(16, 16, SIDE), swap_shape],
            in_specs=[SMEM] + [VMEM] * 4,
            out_specs=[VMEM, VMEM],
            scratch_shapes=[pltpu.VMEM((16, SIDE), F32)],
            compiler_params=PARAMS,
        )(send_lists, source, own, in0, in1)
        near = lax.ppermute(relay, "core", [(0, 1), (1, 0)])
        parts = lax.all_to_all(parts, ("core", "cls"), 0, 0)
        out_shape = [own_shape] * (2 if first else 1)
        out_shape += [shape(8, 8, SIDE)] if last else [swap_shape, swap_shape, shape(8, SIDE)]
        results = pl.pallas_call(
            lambda *refs, first=first, last=last: spread_kernel(first, last, *refs),
            out_shape=out_shape,
            in_specs=[VMEM, SMEM, SMEM, SMEM] + [VMEM] * 6,
            out_specs=[VMEM] * len(out_shape),
            scratch_shapes=[
                pltpu.VMEM((16, 2 * SIDE, SIDE), jnp.bfloat16),
                pltpu.VMEM((32, SIDE, SIDE), F32),
            ],
            compiler_params=PARAMS,
        )(tiles, tile_rows, tile_cols, send_lists, mask if first else anchor, source, in0, in1, near, parts)
        if first:
            anchor, *results = results
        if last:
            source, parts = results
        else:
            source, out0, out1, own = results
    parts = lax.all_to_all(parts, "cls", 0, 0)
    out = pl.pallas_call(
        last_kernel,
        out_shape=own_shape,
        in_specs=[VMEM, VMEM],
        out_specs=VMEM,
        compiler_params=PARAMS,
    )(source, parts)
    return out.reshape(8 * SIDE, SIDE)


def solution(mesh):
    split_mesh = Mesh(
        mesh.devices.reshape(mesh.shape["dom"] // 2, 2, mesh.shape["cls"]), ("chip", "core", "cls")
    )
    dom = ("chip", "core")
    return jax.shard_map(
        on_device,
        mesh=split_mesh,
        in_specs=(P(dom, None, None), P(dom), P(dom), P(dom, None, None), P(dom), P(dom, "cls")),
        out_specs=P(dom, "cls"),
        check_vma=False,
    )
```

time: 136 us -> 129 us (0.949)
  the two profiles are of different devices: /device:TPU:16 before, /device:TPU:1 now
where the time goes in v2:
time: 129 us; the launch traced here: 128 us
  starting transfers between devices  50.9 us (39%)
  blocking collectives  47.1 us (37%)
  waiting for transfers between devices  15.8 us (12%)
  Pallas kernels  10.4 us (8%)
  local copies, waits for them, and re-layouts  3.91 us (3%)
    all_to_all x3, blocking collectives, on_device(): parts = lax.all_to_all(parts, ('core', 'cls'), 0, 0)  36.9 us
    ppermute x3, starting transfers between devices, on_device(): in1 = lax.ppermute(out1, 'chip', second_swap)  29.8 us
    ppermute x3, waiting for transfers between devices, on_device(): in1 = lax.ppermute(out1, 'chip', second_swap)  15.8 us
    ppermute x3, starting transfers between devices, on_device(): near = lax.ppermute(relay, 'core', [(0, 1), (1, 0)])  11.5 us
    all_to_all x1, blocking collectives, on_device(): parts = lax.all_to_all(parts, 'cls', 0, 0)  10.2 us
    ppermute x3, starting transfers between devices, on_device(): in0 = lax.ppermute(out0, 'chip', first_swap)  9.58 us
    pallas_call x3, Pallas kernels, on_device(): pl.pallas_call(lambda *refs, first=first, last=last: spread_kernel(first,...  6.07 us
    unnamed x15, local copies, waits for them, and re-layouts  3.91 us
  transfers between devices with their start and end apart: 9, of which 3 were waited for; matrix products, arithmetic and copies ran while one was open for 0% of the time, Pallas kernels for 0%

profile of v2, /device:TPU:1, one launch (start us, length us, event | category | flops | bytes accessed | tf_op | source)
XLA Modules:
  0.0 128.3 jit_solution(9664106510348635192)
XLA Ops:
  0.0 0.0 copy-start
  0.0 0.9 copy.13.send.refs_3_
  0.9 0.0 copy-start.1
  0.9 1.0 copy-done.1
  1.9 0.0 copy-start.2
  1.9 0.7 copy-done.2
  2.6 0.0 copy-start.4
  2.6 0.7 copy-done.4
  3.2 0.0 copy-start.5
  3.2 0.7 copy-done.5
  3.9 0.8 shard_map.64
  4.7 5.7 %collective-permute-start = (f32[4,128,128]{2,1,0:T(8,128)S(1)}, f32[4,128,128]{2,1,0:T(8,128)S(1)}, u32[]{:S(2)}, u32[]{:S(2)}) collective-permute-start(f32[4,128,128]{2,1,0:T(8,128)S(1)} %get-tuple-element.27), channel_id=1, source_target_pairs={{0,16},{16,0},{32,48},{48,32},{64,80},{80,64},{96,112},{112,96},{1... | collective-permute-start | bytes 786440 | tf_op jit(solution)/shard_map/ppermute | solution.py:182
  10.4 16.4 %collective-permute-start.1 = (f32[4,128,128]{2,1,0:T(8,128)S(1)}, f32[4,128,128]{2,1,0:T(8,128)S(1)}, u32[]{:S(2)}, u32[]{:S(2)}) collective-permute-start(f32[4,128,128]{2,1,0:T(8,128)S(1)} %get-tuple-element.28), channel_id=1, source_target_pairs={{0,1008},{16,32},{32,16},{48,64},{64,48},{80,96},{96,80},{112,128}... | collective-permute-start | bytes 786440 | tf_op jit(solution)/shard_map/ppermute | solution.py:183
  26.8 0.0 collective-permute-done.in0.refs_6_
  26.8 5.7 %collective-permute-done.1.in1.refs_7_ = f32[4,128,128]{2,1,0:T(8,128)S(1)} collective-permute-done((f32[4,128,128]{2,1,0:T(8,128)S(1)}, f32[4,128,128]{2,1,0:T(8,128)S(1)}, u32[]{:S(2)}, u32[]{:S(2)}) %collective-permute-start.1) | collective-permute-done | bytes 262176 | tf_op jit(solution)/shard_map/ppermute | solution.py:183
  32.5 0.8 shard_map.65
  33.3 3.4 %collective-permute-start.2 = (f32[4,128,128]{2,1,0:T(8,128)S(1)}, f32[4,128,128]{2,1,0:T(8,128)S(1)}, u32[]{:S(2)}, u32[]{:S(2)}) collective-permute-start(f32[4,128,128]{2,1,0:T(8,128)S(1)} %get-tuple-element.30), channel_id=1, source_target_pairs={{0,8},{8,0},{1,9},{9,1},{2,10},{10,2},{3,11},{11,3},{4,12},{12,4},... | collective-permute-start | bytes 786440 | tf_op jit(solution)/shard_map/ppermute | solution.py:192
  36.8 0.0 copy-start.3
  36.8 0.0 copy-start.6
  36.8 14.8 %all_to_all.20.refs_9_ = f32[16,16,128]{2,1,0:T(8,128)S(1)} all-to-all(f32[16,16,128]{2,1,0:T(8,128)S(1)} %get-tuple-element.31), channel_id=1, replica_groups=mesh['chip'=64,'core'=2,'cls'=8] {'core','cls'}, dimensions={0} | all-to-all | bytes 262144 | tf_op jit(solution)/shard_map/all_to_all | solution.py:193
  51.6 0.0 collective-permute-done.2.refs_8_
  51.6 0.0 copy-done
  51.6 0.0 copy-done.3
  51.6 0.0 copy-done.6
  51.6 2.1 %shard_map.66 = (f32[8,128,128]{2,1,0:T(8,128)S(1)}, f32[8,128,128]{2,1,0:T(8,128)S(1)}, f32[4,128,128]{2,1,0:T(8,128)S(1)}, f32[4,128,128]{2,1,0:T(8,128)S(1)}, f32[8,128]{1,0:T(8,128)S(1)}) custom-call(bf16[32,128,128]{2,1,0:T(8,128)(2,1)S(1)} %copy-done, s32[32]{0:T(128)S(1)} %copy-done.4, s32[32]{0:T(128)S(1)} %copy-done.6, ...), custom_call_target="tpu_custom_call" | custom-call | tf_op jit(solution)/shard_map/pallas_call | solution.py:196
  53.6 1.9 %collective-permute-start.3 = (f32[4,128,128]{2,1,0:T(8,128)S(1)}, f32[4,128,128]{2,1,0:T(8,128)S(1)}, u32[]{:S(2)}, u32[]{:S(2)}) collective-permute-start(f32[4,128,128]{2,1,0:T(8,128)S(1)} %get-tuple-element.34), channel_id=1, source_target_pairs={{0,16},{16,0},{32,48},{48,32},{64,80},{80,64},{96,112},{112,96},{1... | collective-permute-start | bytes 786440 | tf_op jit(solution)/shard_map/ppermute | solution.py:182
  55.6 6.7 %collective-permute-start.4 = (f32[4,128,128]{2,1,0:T(8,128)S(1)}, f32[4,128,128]{2,1,0:T(8,128)S(1)}, u32[]{:S(2)}, u32[]{:S(2)}) collective-permute-start(f32[4,128,128]{2,1,0:T(8,128)S(1)} %get-tuple-element.35), channel_id=1, source_target_pairs={{0,1008},{16,32},{32,16},{48,64},{64,48},{80,96},{96,80},{112,128}... | collective-permute-start | bytes 786440 | tf_op jit(solution)/shard_map/ppermute | solution.py:183
  62.3 0.0 collective-permute-done.3.in0.refs_6_
  62.3 5.1 %collective-permute-done.4.in1.refs_7_ = f32[4,128,128]{2,1,0:T(8,128)S(1)} collective-permute-done((f32[4,128,128]{2,1,0:T(8,128)S(1)}, f32[4,128,128]{2,1,0:T(8,128)S(1)}, u32[]{:S(2)}, u32[]{:S(2)}) %collective-permute-start.4) | collective-permute-done | bytes 262176 | tf_op jit(solution)/shard_map/ppermute | solution.py:183
  67.3 0.8 shard_map.67
  68.2 4.1 %collective-permute-start.5 = (f32[4,128,128]{2,1,0:T(8,128)S(1)}, f32[4,128,128]{2,1,0:T(8,128)S(1)}, u32[]{:S(2)}, u32[]{:S(2)}) collective-permute-start(f32[4,128,128]{2,1,0:T(8,128)S(1)} %get-tuple-element.37), channel_id=1, source_target_pairs={{0,8},{8,0},{1,9},{9,1},{2,10},{10,2},{3,11},{11,3},{4,12},{12,4},... | collective-permute-start | bytes 786440 | tf_op jit(solution)/shard_map/ppermute | solution.py:192
  72.2 11.0 %all_to_all.21.refs_9_ = f32[16,16,128]{2,1,0:T(8,128)S(1)} all-to-all(f32[16,16,128]{2,1,0:T(8,128)S(1)} %get-tuple-element.38), channel_id=1, replica_groups=mesh['chip'=64,'core'=2,'cls'=8] {'core','cls'}, dimensions={0} | all-to-all | bytes 262144 | tf_op jit(solution)/shard_map/all_to_all | solution.py:193
  83.3 0.0 collective-permute-done.5.refs_8_
  83.3 2.0 %shard_map.68 = (f32[8,128,128]{2,1,0:T(8,128)S(1)}, f32[4,128,128]{2,1,0:T(8,128)S(1)}, f32[4,128,128]{2,1,0:T(8,128)S(1)}, f32[8,128]{1,0:T(8,128)S(1)}) custom-call(bf16[32,128,128]{2,1,0:T(8,128)(2,1)S(1)} %copy-done, s32[32]{0:T(128)S(1)} %copy-done.4, s32[32]{0:T(128)S(1)} %copy-done.6, s32[1,4,2]{2,1,0:T(4,128)S(1)} %copy.13.send.refs_3_, ...), custom_call_target="tpu_custom_call" | custom-call | tf_op jit(solution)/shard_map/pallas_call | solution.py:196
  85.3 1.9 %collective-permute-start.6 = (f32[4,128,128]{2,1,0:T(8,128)S(1)}, f32[4,128,128]{2,1,0:T(8,128)S(1)}, u32[]{:S(2)}, u32[]{:S(2)}) collective-permute-start(f32[4,128,128]{2,1,0:T(8,128)S(1)} %get-tuple-element.40), channel_id=1, source_target_pairs={{0,16},{16,0},{32,48},{48,32},{64,80},{80,64},{96,112},{112,96},{1... | collective-permute-start | bytes 786440 | tf_op jit(solution)/shard_map/ppermute | solution.py:182
  87.2 6.7 %collective-permute-start.7 = (f32[4,128,128]{2,1,0:T(8,128)S(1)}, f32[4,128,128]{2,1,0:T(8,128)S(1)}, u32[]{:S(2)}, u32[]{:S(2)}) collective-permute-start(f32[4,128,128]{2,1,0:T(8,128)S(1)} %get-tuple-element.41), channel_id=1, source_target_pairs={{0,1008},{16,32},{32,16},{48,64},{64,48},{80,96},{96,80},{112,128}... | collective-permute-start | bytes 786440 | tf_op jit(solution)/shard_map/ppermute | solution.py:183
  93.9 0.0 collective-permute-done.6.in0.refs_6_
  94.0 5.1 %collective-permute-done.7.in1.refs_7_ = f32[4,128,128]{2,1,0:T(8,128)S(1)} collective-permute-done((f32[4,128,128]{2,1,0:T(8,128)S(1)}, f32[4,128,128]{2,1,0:T(8,128)S(1)}, u32[]{:S(2)}, u32[]{:S(2)}) %collective-permute-start.7) | collective-permute-done | bytes 262176 | tf_op jit(solution)/shard_map/ppermute | solution.py:183
  99.0 0.8 shard_map.69
  99.8 4.1 %collective-permute-start.8 = (f32[4,128,128]{2,1,0:T(8,128)S(1)}, f32[4,128,128]{2,1,0:T(8,128)S(1)}, u32[]{:S(2)}, u32[]{:S(2)}) collective-permute-start(f32[4,128,128]{2,1,0:T(8,128)S(1)} %get-tuple-element.43), channel_id=1, source_target_pairs={{0,8},{8,0},{1,9},{9,1},{2,10},{10,2},{3,11},{11,3},{4,12},{12,4},... | collective-permute-start | bytes 786440 | tf_op jit(solution)/shard_map/ppermute | solution.py:192
  103.9 11.0 %all_to_all.22.refs_9_ = f32[16,16,128]{2,1,0:T(8,128)S(1)} all-to-all(f32[16,16,128]{2,1,0:T(8,128)S(1)} %get-tuple-element.44), channel_id=1, replica_groups=mesh['chip'=64,'core'=2,'cls'=8] {'core','cls'}, dimensions={0} | all-to-all | bytes 262144 | tf_op jit(solution)/shard_map/all_to_all | solution.py:193
  115.0 0.0 collective-permute-done.8.refs_8_
  115.0 2.0 %shard_map.70 = (f32[8,128,128]{2,1,0:T(8,128)S(1)}, f32[8,8,128]{2,1,0:T(8,128)S(1)}) custom-call(bf16[32,128,128]{2,1,0:T(8,128)(2,1)S(1)} %copy-done, s32[32]{0:T(128)S(1)} %copy-done.4, s32[32]{0:T(128)S(1)} %copy-done.6, s32[1,4,2]{2,1,0:T(4,128)S(1)} %copy.13.send.refs_3_, f32[8,128,128]{2,1,0:T(8,128)S(1)} %get-tuple-element.32.refs_4_, ...), custom_call_target="tpu_custom_call" | custom-call | tf_op jit(solution)/shard_map/pallas_call | solution.py:196
  117.0 10.2 %all_to_all.23.parts = f32[8,8,128]{2,1,0:T(8,128)S(1)} all-to-all(f32[8,8,128]{2,1,0:T(8,128)S(1)} %get-tuple-element.46), channel_id=1, replica_groups=mesh['chip'=64,'core'=2,'cls'=8] {'cls'}, dimensions={0} | all-to-all | bytes 65536 | tf_op jit(solution)/shard_map/all_to_all | solution.py:213
  127.2 1.1 shard_map.71
Async XLA Ops:
  0.0 51.6 %copy-start = (bf16[32,128,128]{2,1,0:T(8,128)(2,1)S(1)}, bf16[32,128,128]{2,1,0:T(8,128)(2,1)}, u32[]{:S(2)}) copy-start(bf16[32,128,128]{2,1,0:T(8,128)(2,1)} %refs_0_.5) | copy-start | bytes 3145732
  0.9 1.0 copy-start.1
  1.9 0.7 copy-start.2
  2.6 0.7 copy-start.4
  3.2 0.7 copy-start.5
  4.7 22.1 %collective-permute-start = (f32[4,128,128]{2,1,0:T(8,128)S(1)}, f32[4,128,128]{2,1,0:T(8,128)S(1)}, u32[]{:S(2)}, u32[]{:S(2)}) collective-permute-start(f32[4,128,128]{2,1,0:T(8,128)S(1)} %get-tuple-element.27), channel_id=1, source_target_pairs={{0,16},{16,0},{32,48},{48,32},{64,80},{80,64},{96,112},{112,96},{1... | collective-permute-start | bytes 786440 | tf_op jit(solution)/shard_map/ppermute | solution.py:182
  10.4 22.1 %collective-permute-start.1 = (f32[4,128,128]{2,1,0:T(8,128)S(1)}, f32[4,128,128]{2,1,0:T(8,128)S(1)}, u32[]{:S(2)}, u32[]{:S(2)}) collective-permute-start(f32[4,128,128]{2,1,0:T(8,128)S(1)} %get-tuple-element.28), channel_id=1, source_target_pairs={{0,1008},{16,32},{32,16},{48,64},{64,48},{80,96},{96,80},{112,128}... | collective-permute-start | bytes 786440 | tf_op jit(solution)/shard_map/ppermute | solution.py:183
  33.3 18.2 %collective-permute-start.2 = (f32[4,128,128]{2,1,0:T(8,128)S(1)}, f32[4,128,128]{2,1,0:T(8,128)S(1)}, u32[]{:S(2)}, u32[]{:S(2)}) collective-permute-start(f32[4,128,128]{2,1,0:T(8,128)S(1)} %get-tuple-element.30), channel_id=1, source_target_pairs={{0,8},{8,0},{1,9},{9,1},{2,10},{10,2},{3,11},{11,3},{4,12},{12,4},... | collective-permute-start | bytes 786440 | tf_op jit(solution)/shard_map/ppermute | solution.py:192
  36.8 14.8 %copy-start.3 = (s32[1024]{0:T(1024)S(1)}, s32[1024]{0:T(1024)}, u32[]{:S(2)}) copy-start(s32[1024]{0:T(1024)} %param.10) | copy-start | bytes 12292
  36.8 14.8 %copy-start.6 = (s32[32]{0:T(128)S(1)}, s32[32]{0:T(128)}, u32[]{:S(2)}) copy-start(s32[32]{0:T(128)} %refs_2_.5) | copy-start | bytes 388
  53.6 8.6 %collective-permute-start.3 = (f32[4,128,128]{2,1,0:T(8,128)S(1)}, f32[4,128,128]{2,1,0:T(8,128)S(1)}, u32[]{:S(2)}, u32[]{:S(2)}) collective-permute-start(f32[4,128,128]{2,1,0:T(8,128)S(1)} %get-tuple-element.34), channel_id=1, source_target_pairs={{0,16},{16,0},{32,48},{48,32},{64,80},{80,64},{96,112},{112,96},{1... | collective-permute-start | bytes 786440 | tf_op jit(solution)/shard_map/ppermute | solution.py:182
  55.6 11.8 %collective-permute-start.4 = (f32[4,128,128]{2,1,0:T(8,128)S(1)}, f32[4,128,128]{2,1,0:T(8,128)S(1)}, u32[]{:S(2)}, u32[]{:S(2)}) collective-permute-start(f32[4,128,128]{2,1,0:T(8,128)S(1)} %get-tuple-element.35), channel_id=1, source_target_pairs={{0,1008},{16,32},{32,16},{48,64},{64,48},{80,96},{96,80},{112,128}... | collective-permute-start | bytes 786440 | tf_op jit(solution)/shard_map/ppermute | solution.py:183
  68.2 15.1 %collective-permute-start.5 = (f32[4,128,128]{2,1,0:T(8,128)S(1)}, f32[4,128,128]{2,1,0:T(8,128)S(1)}, u32[]{:S(2)}, u32[]{:S(2)}) collective-permute-start(f32[4,128,128]{2,1,0:T(8,128)S(1)} %get-tuple-element.37), channel_id=1, source_target_pairs={{0,8},{8,0},{1,9},{9,1},{2,10},{10,2},{3,11},{11,3},{4,12},{12,4},... | collective-permute-start | bytes 786440 | tf_op jit(solution)/shard_map/ppermute | solution.py:192
  85.3 8.6 %collective-permute-start.6 = (f32[4,128,128]{2,1,0:T(8,128)S(1)}, f32[4,128,128]{2,1,0:T(8,128)S(1)}, u32[]{:S(2)}, u32[]{:S(2)}) collective-permute-start(f32[4,128,128]{2,1,0:T(8,128)S(1)} %get-tuple-element.40), channel_id=1, source_target_pairs={{0,16},{16,0},{32,48},{48,32},{64,80},{80,64},{96,112},{112,96},{1... | collective-permute-start | bytes 786440 | tf_op jit(solution)/shard_map/ppermute | solution.py:182
  87.2 11.8 %collective-permute-start.7 = (f32[4,128,128]{2,1,0:T(8,128)S(1)}, f32[4,128,128]{2,1,0:T(8,128)S(1)}, u32[]{:S(2)}, u32[]{:S(2)}) collective-permute-start(f32[4,128,128]{2,1,0:T(8,128)S(1)} %get-tuple-element.41), channel_id=1, source_target_pairs={{0,1008},{16,32},{32,16},{48,64},{64,48},{80,96},{96,80},{112,128}... | collective-permute-start | bytes 786440 | tf_op jit(solution)/shard_map/ppermute | solution.py:183
  99.8 15.1 %collective-permute-start.8 = (f32[4,128,128]{2,1,0:T(8,128)S(1)}, f32[4,128,128]{2,1,0:T(8,128)S(1)}, u32[]{:S(2)}, u32[]{:S(2)}) collective-permute-start(f32[4,128,128]{2,1,0:T(8,128)S(1)} %get-tuple-element.43), channel_id=1, source_target_pairs={{0,8},{8,0},{1,9},{9,1},{2,10},{10,2},{3,11},{11,3},{4,12},{12,4},... | collective-permute-start | bytes 786440 | tf_op jit(solution)/shard_map/ppermute | solution.py:192

commit v3 on v2

--- a/solution.py
+++ b/solution.py
@@ -24,13 +24,17 @@
     return lax.shift_right_logical(value, by)
 
 
-def gather(source, send, out0, out1):
-    odd = lax.rem(lax.axis_index("chip"), 2)
-    for out, behind in ((out0, odd), (out1, 1 - odd)):
+def sent_blocks(send, outs):
+    odd = lax.rem(lax.axis_index("chip"), 2)
+    for out, behind in zip(outs, (odd, 1 - odd)):
         for part in range(2):
-            slot = 2 * behind + 1 - part
             for within in range(2):
-                out[2 * part + within] = source[send[0, slot, within]]
+                yield out, 2 * part + within, send[0, within, 2 * behind + 1 - part]
+
+
+def gather(source, send, outs):
+    for out, place, block in sent_blocks(send, outs):
+        out[place] = source[block]
 
 
 def operand_block(col):
@@ -49,35 +53,60 @@
     return jnp.sum(jnp.transpose(block), axis=0, keepdims=True)
 
 
-def first_kernel(labels, rows, cols, send, mask, kept, out0, out1, own):
-    gather(labels, send, out0, out1)
-    for block in range(8):
-        kept[block] = labels[block]
-        own[block : block + 1, :] = lane_sums(labels[block])
-
-
-def mass_kernel(send, source, own, in0, in1, parts, relay, rows):
-    odd = lax.rem(lax.axis_index("chip"), 2)
-    core = lax.axis_index("core")
-    rows[0:8, :] = own[...]
-    for within in range(2):
-        block = send[0, 2 * core, within]
-        relay[within] = source[block]
-        rows[12 + within : 13 + within, :] = own[pl.ds(block, 1), :]
-        rows[8 + within : 9 + within, :] = lane_sums(in0[within])
-        rows[10 + within : 11 + within, :] = lane_sums(in1[within])
-
-    def pass_on(received):
+def fetch_kernel(labels, send, out0, out1, sems):
+    copies = []
+    for number, (out, place, block) in enumerate(sent_blocks(send, (out0, out1))):
+        copy = pltpu.make_async_copy(labels.at[block], out.at[place], sems.at[number])
+        copy.start()
+        copies.append(copy)
+    for copy in copies:
+        copy.wait()
+
+
+def fill_parts(sums, send, parts, rows):
+    rows[0:8, :] = sums
+    rows[8:16, :] = jnp.zeros((8, SIDE), F32)
+    for half in range(2):
         for within in range(2):
-            value = received[2 + within]
-            relay[2 + within] = value
-            rows[14 + within : 15 + within, :] = lane_sums(value)
-
-    pl.when(odd == core)(lambda: pass_on(in0))
-    pl.when(odd != core)(lambda: pass_on(in1))
+            place = 8 + 2 * half + within
+            rows[place : place + 1, :] = rows[pl.ds(send[0, within, 2 * half], 1), :]
     partial = rows[...]
     for share in range(16):
         parts[share] = partial
+
+
+def first_kernel(labels, rows, cols, send, mask, kept, parts, scratch):
+    sums = []
+    for block in range(8):
+        value = labels[block]
+        kept[block] = value
+        sums.append(lane_sums(value))
+    fill_parts(jnp.concatenate(sums, axis=0), send, parts, scratch)
+
+
+def mass_kernel(parts, send, source, in0, in1, known, mass0, mass1, relay):
+    odd = lax.rem(lax.axis_index("chip"), 2)
+    core = lax.axis_index("core")
+    mine = total_of(parts, core)
+    mate = total_of(parts, 1 - core)
+    known[0:8, :] = mine[0:8]
+    known[8:10, :] = jnp.where(core == 0, mate[10:12], mate[8:10])
+    known[10:16, :] = jnp.ones((6, SIDE), F32)
+    for out, behind in ((mass0, odd), (mass1, 1 - odd)):
+        for within in range(2):
+            block = send[0, within, 2 * behind + 1]
+            out[within : within + 1, :] = known[pl.ds(block, 1), :]
+        out[2:4, :] = jnp.where(behind == 0, mate[8:10], mate[10:12])
+        out[4:8, :] = jnp.ones((4, SIDE), F32)
+    for within in range(2):
+        relay[within] = source[send[0, within, 2 * core]]
+
+    def pass_on(received):
+        for within in range(2):
+            relay[2 + within] = received[2 + within]
+
+    pl.when(odd == core)(lambda: pass_on(in0))
+    pl.when(odd != core)(lambda: pass_on(in1))
 
 
 def scales(total, blocks):
@@ -101,18 +130,19 @@
 
 def spread_kernel(first, last, *refs):
     refs = list(refs)
-    tiles, rows, cols, send, mask, source, in0, in1, near, parts = refs[:10]
-    refs = refs[10:]
+    tiles, rows, cols, send, mask, source, in0, in1, near, known, mass0, mass1 = refs[:12]
+    refs = refs[12:]
     anchor = refs.pop(0) if first else mask
     squared = refs.pop(0)
     if last:
-        own_parts, operand, products = refs
+        parts, operand, products = refs
     else:
-        out0, out1, own, operand, products = refs
+        out0, out1, parts, operand, products, scratch = refs
+    odd = lax.rem(lax.axis_index("chip"), 2)
     core = lax.axis_index("core")
-    mine = total_of(parts, core)
-    mate = total_of(parts, 1 - core)
-    scale = scales(jnp.concatenate([mine[0:8], mate[12:16], mine[8:12]], axis=0), 16)
+    relayed = jnp.where(odd != core, mass0[2:4, :], mass1[2:4, :])
+    total = jnp.concatenate([known[0:10, :], relayed, mass0[0:2, :], mass1[0:2, :]], axis=0)
+    scale = scales(total, 16)
     if first:
         seeded = jnp.concatenate(
             [mask[...].astype(F32), jnp.zeros((SIDE - 8, SIDE), F32)], axis=0
@@ -148,10 +178,10 @@
     sums = jnp.concatenate(sums, axis=0)
     if last:
         for share in range(8):
-            own_parts[share] = sums
+            parts[share] = sums
     else:
-        own[...] = sums
-        gather(squared, send, out0, out1)
+        gather(squared, send, (out0, out1))
+        fill_parts(sums, send, parts, scratch)
 
 
 def last_kernel(squared, parts, out):
@@ -164,16 +194,30 @@
     chips = lax.axis_size("chip")
     first_swap = [(i, i ^ 1) for i in range(chips)]
     second_swap = [(i, (((i + 1) ^ 1) - 1) % chips) for i in range(chips)]
+    send_lists = jnp.transpose(send_lists, (0, 2, 1))
     blocks = labels.reshape(8, SIDE, SIDE)
     mask = seed_mask.reshape(8, SIDE)
     own_shape = shape(8, SIDE, SIDE)
     swap_shape = shape(4, SIDE, SIDE)
-    source, out0, out1, own = pl.pallas_call(
+    parts_shape = shape(16, 16, SIDE)
+    rows_scratch = pltpu.VMEM((16, SIDE), F32)
+    out0, out1 = pl.pallas_call(
+        fetch_kernel,
+        out_shape=[swap_shape, swap_shape],
+        in_specs=[pl.BlockSpec(memory_space=pltpu.HBM), SMEM],
+        out_specs=[VMEM] * 2,
+        scratch_shapes=[pltpu.SemaphoreType.DMA((8,))],
+        compiler_params=PARAMS,
+        cost_estimate=pl.CostEstimate(flops=0, bytes_accessed=1 << 19, transcendentals=0),
+    )(blocks, send_lists)
+    source, parts = pl.pallas_call(
         first_kernel,
-        out_shape=[own_shape, swap_shape, swap_shape, shape(8, SIDE)],
+        out_shape=[own_shape, parts_shape],
         in_specs=[VMEM, SMEM, SMEM, SMEM, VMEM],
-        out_specs=[VMEM] * 4,
+        out_specs=[VMEM] * 2,
+        scratch_shapes=[rows_scratch],
         compiler_params=PARAMS,
+        cost_estimate=pl.CostEstimate(flops=1 << 20, bytes_accessed=1 << 20, transcendentals=0),
     )(blocks, tile_rows, tile_cols, send_lists, mask)
     anchor = None
     for iteration in range(ITERS):
@@ -181,35 +225,41 @@
         last = iteration == ITERS - 1
         in0 = lax.ppermute(out0, "chip", first_swap)
         in1 = lax.ppermute(out1, "chip", second_swap)
-        parts, relay = pl.pallas_call(
+        parts = lax.all_to_all(parts, ("core", "cls"), 0, 0)
+        known, mass0, mass1, relay = pl.pallas_call(
             mass_kernel,
-            out_shape=[shape(16, 16, SIDE), swap_shape],
-            in_specs=[SMEM] + [VMEM] * 4,
-            out_specs=[VMEM, VMEM],
-            scratch_shapes=[pltpu.VMEM((16, SIDE), F32)],
+            out_shape=[shape(16, SIDE), shape(8, SIDE), shape(8, SIDE), swap_shape],
+            in_specs=[VMEM, SMEM] + [VMEM] * 3,
+            out_specs=[VMEM] * 4,
             compiler_params=PARAMS,
-        )(send_lists, source, own, in0, in1)
+        )(parts, send_lists, source, in0, in1)
         near = lax.ppermute(relay, "core", [(0, 1), (1, 0)])
-        parts = lax.all_to_all(parts, ("core", "cls"), 0, 0)
+        mass0 = lax.ppermute(mass0, "chip", first_swap)
+        mass1 = lax.ppermute(mass1, "chip", second_swap)
         out_shape = [own_shape] * (2 if first else 1)
-        out_shape += [shape(8, 8, SIDE)] if last else [swap_shape, swap_shape, shape(8, SIDE)]
+        out_shape += [shape(8, 8, SIDE)] if last else [swap_shape, swap_shape, parts_shape]
         results = pl.pallas_call(
             lambda *refs, first=first, last=last: spread_kernel(first, last, *refs),
             out_shape=out_shape,
-            in_specs=[VMEM, SMEM, SMEM, SMEM] + [VMEM] * 6,
+            in_specs=[VMEM, SMEM, SMEM, SMEM] + [VMEM] * 8,
             out_specs=[VMEM] * len(out_shape),
             scratch_shapes=[
                 pltpu.VMEM((16, 2 * SIDE, SIDE), jnp.bfloat16),
                 pltpu.VMEM((32, SIDE, SIDE), F32),
-            ],
+            ]
+            + ([] if last else [rows_scratch]),
             compiler_params=PARAMS,
-        )(tiles, tile_rows, tile_cols, send_lists, mask if first else anchor, source, in0, in1, near, parts)
+            cost_estimate=pl.CostEstimate(flops=1 << 28, bytes_accessed=1 << 22, transcendentals=0),
+        )(
+            tiles, tile_rows, tile_cols, send_lists, mask if first else anchor, source,
+            in0, in1, near, known, mass0, mass1,
+        )
         if first:
             anchor, *results = results
         if last:
             source, parts = results
         else:
-            source, out0, out1, own = results
+            source, out0, out1, parts = results
     parts = lax.all_to_all(parts, "cls", 0, 0)
     out = pl.pallas_call(
         last_kernel,

time: 129 us -> 135 us (1.047)
  starting transfers between devices: 50.9 us -> 61.7 us
  waiting for transfers between devices: 15.8 us -> 11 us
  local copies, waits for them, and re-layouts: 3.91 us -> 1.74 us
  blocking collectives: 47.1 us -> 49 us
    ppermute x0 -> x6, starting transfers between devices: none -> 17.7 us  [the longest x3 12 us: on_device(): mass1 = lax.ppermute(mass1, 'chip', second_swap)]
    ppermute x3, waiting for transfers between devices: 15.8 us -> 0.01 us  [on_device(): in1 = lax.ppermute(out1, 'chip', second_swap)]
    ppermute x0 -> x6, waiting for transfers between devices: none -> 11 us  [the longest x3 11 us: on_device(): mass1 = lax.ppermute(mass1, 'chip', second_swap)]
    ppermute x3, starting transfers between devices: 29.8 us -> 24.7 us  [on_device(): in1 = lax.ppermute(out1, 'chip', second_swap)]
    all_to_all x3, blocking collectives: 36.9 us -> 39.4 us  [on_device(): parts = lax.all_to_all(parts, ('core', 'cls'), 0, 0)]
    unnamed x15 -> x12, local copies, waits for them, and re-layouts: 3.91 us -> 1.74 us
    ppermute x3, starting transfers between devices: 11.5 us -> 9.57 us  [on_device(): near = lax.ppermute(relay, 'core', [(0, 1), (1, 0)])]
    pallas_call x4 -> x5, Pallas kernels: 3.24 us -> 3.93 us  [the longest x3 1.78 us: on_device(): pl.pallas_call(mass_kernel, out_shape=[shape(16, SIDE), shape(8, SIDE), s...]
  transfers between devices with their start and end apart: 9 -> 15, of which waited for: 3 -> 3; matrix products, arithmetic and copies ran while one was open for 0% -> 0% of each run, Pallas kernels for 0% -> 1%
where the time goes in v3:
time: 135 us
  starting transfers between devices  61.7 us (46%)
  blocking collectives  49 us (36%)
  Pallas kernels  11.1 us (8%)
  waiting for transfers between devices  11 us (8%)
  local copies, waits for them, and re-layouts  1.74 us (1%)
    all_to_all x3, blocking collectives, on_device(): parts = lax.all_to_all(parts, ('core', 'cls'), 0, 0)  39.4 us
    ppermute x3, starting transfers between devices, on_device(): in1 = lax.ppermute(out1, 'chip', second_swap)  24.7 us
    ppermute x3, starting transfers between devices, on_device(): mass1 = lax.ppermute(mass1, 'chip', second_swap)  12 us
    ppermute x3, waiting for transfers between devices, on_device(): mass1 = lax.ppermute(mass1, 'chip', second_swap)  11 us
    ppermute x3, starting transfers between devices, on_device(): in0 = lax.ppermute(out0, 'chip', first_swap)  9.71 us
    all_to_all x1, blocking collectives, on_device(): parts = lax.all_to_all(parts, 'cls', 0, 0)  9.61 us
    ppermute x3, starting transfers between devices, on_device(): near = lax.ppermute(relay, 'core', [(0, 1), (1, 0)])  9.57 us
    pallas_call x3, Pallas kernels, on_device(): pl.pallas_call(lambda *refs, first=first, last=last: spread_kernel(first,...  6.02 us
  transfers between devices with their start and end apart: 15, of which 3 were waited for; matrix products, arithmetic and copies ran while one was open for 0% of the time, Pallas kernels for 1%

profile of v3, /device:TPU:1, one launch (start us, length us, event | category | flops | bytes accessed | tf_op | source)
XLA Modules:
  0.0 134.8 jit_solution(10132597301868571771)
XLA Ops:
  0.0 0.0 copy-start.2
  0.0 0.7 copy-done.2
  0.7 0.0 copy-start.1
  0.7 1.0 copy-done.1
  1.7 0.0 copy-start.3
  1.7 0.0 copy-start.4
  1.7 0.0 copy-start.5
  1.7 1.4 %shard_map.65 = (f32[4,128,128]{2,1,0:T(8,128)S(1)}, f32[4,128,128]{2,1,0:T(8,128)S(1)}) custom-call(f32[8,128,128]{2,1,0:T(8,128)S(1)} %bitcast.4, s32[1,2,4]{2,1,0:T(2,128)S(1)} %bitcast.6), custom_call_target="tpu_custom_call" | custom-call | bytes 524288 | tf_op jit(solution)/shard_map/pallas_call | solution.py:204
  3.1 0.0 copy-start
  3.1 5.9 %collective-permute-start = (f32[4,128,128]{2,1,0:T(8,128)S(1)}, f32[4,128,128]{2,1,0:T(8,128)S(1)}, u32[]{:S(2)}, u32[]{:S(2)}) collective-permute-start(f32[4,128,128]{2,1,0:T(8,128)S(1)} %get-tuple-element.33), channel_id=1, source_target_pairs={{0,16},{16,0},{32,48},{48,32},{64,80},{80,64},{96,112},{112,96},{1... | collective-permute-start | bytes 786440 | tf_op jit(solution)/shard_map/ppermute | solution.py:226
  9.0 16.4 %collective-permute-start.1 = (f32[4,128,128]{2,1,0:T(8,128)S(1)}, f32[4,128,128]{2,1,0:T(8,128)S(1)}, u32[]{:S(2)}, u32[]{:S(2)}) collective-permute-start(f32[4,128,128]{2,1,0:T(8,128)S(1)} %get-tuple-element.34), channel_id=1, source_target_pairs={{0,1008},{16,32},{32,16},{48,64},{64,48},{80,96},{96,80},{112,128}... | collective-permute-start | bytes 786440 | tf_op jit(solution)/shard_map/ppermute | solution.py:227
  25.3 0.0 copy-done.3
  25.4 0.0 copy-done.4
  25.4 0.0 copy-done.5
  25.4 0.8 shard_map.64
  26.2 15.6 %all_to_all.20.parts = f32[16,16,128]{2,1,0:T(8,128)S(1)} all-to-all(f32[16,16,128]{2,1,0:T(8,128)S(1)} %get-tuple-element.35), channel_id=1, replica_groups=mesh['chip'=64,'core'=2,'cls'=8] {'core','cls'}, dimensions={0} | all-to-all | bytes 262144 | tf_op jit(solution)/shard_map/all_to_all | solution.py:228
  41.8 0.0 collective-permute-done.in0.refs_6_
  41.8 0.0 collective-permute-done.1.in1.refs_7_
  41.8 0.6 shard_map.66
  42.4 3.2 %collective-permute-start.2 = (f32[4,128,128]{2,1,0:T(8,128)S(1)}, f32[4,128,128]{2,1,0:T(8,128)S(1)}, u32[]{:S(2)}, u32[]{:S(2)}) collective-permute-start(f32[4,128,128]{2,1,0:T(8,128)S(1)} %get-tuple-element.36), channel_id=1, source_target_pairs={{0,8},{8,0},{1,9},{9,1},{2,10},{10,2},{3,11},{11,3},{4,12},{12,4},... | collective-permute-start | bytes 786440 | tf_op jit(solution)/shard_map/ppermute | solution.py:236
  45.6 1.9 %collective-permute-start.3 = (f32[8,128]{1,0:T(8,128)S(1)}, f32[8,128]{1,0:T(8,128)S(1)}, u32[]{:S(2)}, u32[]{:S(2)}) collective-permute-start(f32[8,128]{1,0:T(8,128)S(1)} %get-tuple-element.38), channel_id=1, source_target_pairs={{0,16},{16,0},{32,48},{48,32},{64,80},{80,64},{96,112},{112,96},{1... | collective-permute-start | bytes 12296 | tf_op jit(solution)/shard_map/ppermute | solution.py:237
  47.5 3.4 %collective-permute-start.4 = (f32[8,128]{1,0:T(8,128)S(1)}, f32[8,128]{1,0:T(8,128)S(1)}, u32[]{:S(2)}, u32[]{:S(2)}) collective-permute-start(f32[8,128]{1,0:T(8,128)S(1)} %get-tuple-element.39), channel_id=1, source_target_pairs={{0,1008},{16,32},{32,16},{48,64},{64,48},{80,96},{96,80},{112,128}... | collective-permute-start | bytes 12296 | tf_op jit(solution)/shard_map/ppermute | solution.py:238
  50.9 0.0 collective-permute-done.3.refs_10_
  50.9 4.3 %collective-permute-done.4.refs_11_ = f32[8,128]{1,0:T(8,128)S(1)} collective-permute-done((f32[8,128]{1,0:T(8,128)S(1)}, f32[8,128]{1,0:T(8,128)S(1)}, u32[]{:S(2)}, u32[]{:S(2)}) %collective-permute-start.4) | collective-permute-done | bytes 4128 | tf_op jit(solution)/shard_map/ppermute | solution.py:238
  55.2 0.0 collective-permute-done.2.refs_8_
  55.2 0.0 copy-done
  55.2 2.0 %shard_map.67 = (f32[8,128,128]{2,1,0:T(8,128)S(1)}, f32[8,128,128]{2,1,0:T(8,128)S(1)}, f32[4,128,128]{2,1,0:T(8,128)S(1)}, f32[4,128,128]{2,1,0:T(8,128)S(1)}, f32[16,16,128]{2,1,0:T(8,128)S(1)}) custom-call(bf16[32,128,128]{2,1,0:T(8,128)(2,1)S(1)} %copy-done, s32[32]{0:T(128)S(1)} %copy-done.4, s32[32]{0:T(128)S(1)} %copy-done.5, ...), custom_call_target="tpu_custom_call" | custom-call | flops 268435456 | bytes 4194304 | tf_op jit(solution)/shard_map/pallas_call | solution.py:241
  57.2 1.9 %collective-permute-start.5 = (f32[4,128,128]{2,1,0:T(8,128)S(1)}, f32[4,128,128]{2,1,0:T(8,128)S(1)}, u32[]{:S(2)}, u32[]{:S(2)}) collective-permute-start(f32[4,128,128]{2,1,0:T(8,128)S(1)} %get-tuple-element.42), channel_id=1, source_target_pairs={{0,16},{16,0},{32,48},{48,32},{64,80},{80,64},{96,112},{112,96},{1... | collective-permute-start | bytes 786440 | tf_op jit(solution)/shard_map/ppermute | solution.py:226
  59.2 3.4 %collective-permute-start.6 = (f32[4,128,128]{2,1,0:T(8,128)S(1)}, f32[4,128,128]{2,1,0:T(8,128)S(1)}, u32[]{:S(2)}, u32[]{:S(2)}) collective-permute-start(f32[4,128,128]{2,1,0:T(8,128)S(1)} %get-tuple-element.43), channel_id=1, source_target_pairs={{0,1008},{16,32},{32,16},{48,64},{64,48},{80,96},{96,80},{112,128}... | collective-permute-start | bytes 786440 | tf_op jit(solution)/shard_map/ppermute | solution.py:227
  62.5 12.0 %all_to_all.21.parts = f32[16,16,128]{2,1,0:T(8,128)S(1)} all-to-all(f32[16,16,128]{2,1,0:T(8,128)S(1)} %get-tuple-element.44), channel_id=1, replica_groups=mesh['chip'=64,'core'=2,'cls'=8] {'core','cls'}, dimensions={0} | all-to-all | bytes 262144 | tf_op jit(solution)/shard_map/all_to_all | solution.py:228
  74.6 0.0 collective-permute-done.5.in0.refs_6_
  74.6 0.0 collective-permute-done.6.in1.refs_7_
  74.6 0.6 shard_map.68
  75.2 3.2 %collective-permute-start.7 = (f32[4,128,128]{2,1,0:T(8,128)S(1)}, f32[4,128,128]{2,1,0:T(8,128)S(1)}, u32[]{:S(2)}, u32[]{:S(2)}) collective-permute-start(f32[4,128,128]{2,1,0:T(8,128)S(1)} %get-tuple-element.45), channel_id=1, source_target_pairs={{0,8},{8,0},{1,9},{9,1},{2,10},{10,2},{3,11},{11,3},{4,12},{12,4},... | collective-permute-start | bytes 786440 | tf_op jit(solution)/shard_map/ppermute | solution.py:236
  78.4 1.9 %collective-permute-start.8 = (f32[8,128]{1,0:T(8,128)S(1)}, f32[8,128]{1,0:T(8,128)S(1)}, u32[]{:S(2)}, u32[]{:S(2)}) collective-permute-start(f32[8,128]{1,0:T(8,128)S(1)} %get-tuple-element.47), channel_id=1, source_target_pairs={{0,16},{16,0},{32,48},{48,32},{64,80},{80,64},{96,112},{112,96},{1... | collective-permute-start | bytes 12296 | tf_op jit(solution)/shard_map/ppermute | solution.py:237
  80.3 5.0 %collective-permute-start.9 = (f32[8,128]{1,0:T(8,128)S(1)}, f32[8,128]{1,0:T(8,128)S(1)}, u32[]{:S(2)}, u32[]{:S(2)}) collective-permute-start(f32[8,128]{1,0:T(8,128)S(1)} %get-tuple-element.48), channel_id=1, source_target_pairs={{0,1008},{16,32},{32,16},{48,64},{64,48},{80,96},{96,80},{112,128}... | collective-permute-start | bytes 12296 | tf_op jit(solution)/shard_map/ppermute | solution.py:238
  85.3 0.0 collective-permute-done.8.refs_10_
  85.3 2.7 %collective-permute-done.9.refs_11_ = f32[8,128]{1,0:T(8,128)S(1)} collective-permute-done((f32[8,128]{1,0:T(8,128)S(1)}, f32[8,128]{1,0:T(8,128)S(1)}, u32[]{:S(2)}, u32[]{:S(2)}) %collective-permute-start.9) | collective-permute-done | bytes 4128 | tf_op jit(solution)/shard_map/ppermute | solution.py:238
  88.0 0.0 collective-permute-done.7.refs_8_
  88.0 2.0 %shard_map.69 = (f32[8,128,128]{2,1,0:T(8,128)S(1)}, f32[4,128,128]{2,1,0:T(8,128)S(1)}, f32[4,128,128]{2,1,0:T(8,128)S(1)}, f32[16,16,128]{2,1,0:T(8,128)S(1)}) custom-call(bf16[32,128,128]{2,1,0:T(8,128)(2,1)S(1)} %copy-done, s32[32]{0:T(128)S(1)} %copy-done.4, s32[32]{0:T(128)S(1)} %copy-done.5, s32[1,2,4]{2,1,0:T(2,128)S(1)} %bitcast.11, ...), custom_call_target="tpu_custom_call" | custom-call | flops 268435456 | bytes 4194304 | tf_op jit(solution)/shard_map/pallas_call | solution.py:241
  90.0 1.9 %collective-permute-start.10 = (f32[4,128,128]{2,1,0:T(8,128)S(1)}, f32[4,128,128]{2,1,0:T(8,128)S(1)}, u32[]{:S(2)}, u32[]{:S(2)}) collective-permute-start(f32[4,128,128]{2,1,0:T(8,128)S(1)} %get-tuple-element.50), channel_id=1, source_target_pairs={{0,16},{16,0},{32,48},{48,32},{64,80},{80,64},{96,112},{112,96},{1... | collective-permute-start | bytes 786440 | tf_op jit(solution)/shard_map/ppermute | solution.py:226
  91.9 5.0 %collective-permute-start.11 = (f32[4,128,128]{2,1,0:T(8,128)S(1)}, f32[4,128,128]{2,1,0:T(8,128)S(1)}, u32[]{:S(2)}, u32[]{:S(2)}) collective-permute-start(f32[4,128,128]{2,1,0:T(8,128)S(1)} %get-tuple-element.51), channel_id=1, source_target_pairs={{0,1008},{16,32},{32,16},{48,64},{64,48},{80,96},{96,80},{112,128}... | collective-permute-start | bytes 786440 | tf_op jit(solution)/shard_map/ppermute | solution.py:227
  96.9 11.8 %all_to_all.22.parts = f32[16,16,128]{2,1,0:T(8,128)S(1)} all-to-all(f32[16,16,128]{2,1,0:T(8,128)S(1)} %get-tuple-element.52), channel_id=1, replica_groups=mesh['chip'=64,'core'=2,'cls'=8] {'core','cls'}, dimensions={0} | all-to-all | bytes 262144 | tf_op jit(solution)/shard_map/all_to_all | solution.py:228
  108.6 0.0 collective-permute-done.10.in0.refs_6_
  108.6 0.0 collective-permute-done.11.in1.refs_7_
  108.6 0.6 shard_map.70
  109.2 3.2 %collective-permute-start.12 = (f32[4,128,128]{2,1,0:T(8,128)S(1)}, f32[4,128,128]{2,1,0:T(8,128)S(1)}, u32[]{:S(2)}, u32[]{:S(2)}) collective-permute-start(f32[4,128,128]{2,1,0:T(8,128)S(1)} %get-tuple-element.53), channel_id=1, source_target_pairs={{0,8},{8,0},{1,9},{9,1},{2,10},{10,2},{3,11},{11,3},{4,12},{12,4},... | collective-permute-start | bytes 786440 | tf_op jit(solution)/shard_map/ppermute | solution.py:236
  112.4 1.9 %collective-permute-start.13 = (f32[8,128]{1,0:T(8,128)S(1)}, f32[8,128]{1,0:T(8,128)S(1)}, u32[]{:S(2)}, u32[]{:S(2)}) collective-permute-start(f32[8,128]{1,0:T(8,128)S(1)} %get-tuple-element.55), channel_id=1, source_target_pairs={{0,16},{16,0},{32,48},{48,32},{64,80},{80,64},{96,112},{112,96},{1... | collective-permute-start | bytes 12296 | tf_op jit(solution)/shard_map/ppermute | solution.py:237
  114.3 3.6 %collective-permute-start.14 = (f32[8,128]{1,0:T(8,128)S(1)}, f32[8,128]{1,0:T(8,128)S(1)}, u32[]{:S(2)}, u32[]{:S(2)}) collective-permute-start(f32[8,128]{1,0:T(8,128)S(1)} %get-tuple-element.56), channel_id=1, source_target_pairs={{0,1008},{16,32},{32,16},{48,64},{64,48},{80,96},{96,80},{112,128}... | collective-permute-start | bytes 12296 | tf_op jit(solution)/shard_map/ppermute | solution.py:238
  118.0 0.0 collective-permute-done.13.refs_10_
  118.0 4.0 %collective-permute-done.14.refs_11_ = f32[8,128]{1,0:T(8,128)S(1)} collective-permute-done((f32[8,128]{1,0:T(8,128)S(1)}, f32[8,128]{1,0:T(8,128)S(1)}, u32[]{:S(2)}, u32[]{:S(2)}) %collective-permute-start.14) | collective-permute-done | bytes 4128 | tf_op jit(solution)/shard_map/ppermute | solution.py:238
  122.0 0.0 collective-permute-done.12.refs_8_
  122.0 2.0 %shard_map.71 = (f32[8,128,128]{2,1,0:T(8,128)S(1)}, f32[8,8,128]{2,1,0:T(8,128)S(1)}) custom-call(bf16[32,128,128]{2,1,0:T(8,128)(2,1)S(1)} %copy-done, s32[32]{0:T(128)S(1)} %copy-done.4, s32[32]{0:T(128)S(1)} %copy-done.5, s32[1,2,4]{2,1,0:T(2,128)S(1)} %bitcast.13, f32[8,128,128]{2,1,0:T(8,128)S(1)} %get-tuple-element.40.refs_4_, ...), custom_call_target="tpu_custom_call" | custom-call | flops 268435456 | bytes 4194304 | tf_op jit(solution)/shard_map/pallas_call | solution.py:241
  124.0 9.6 %all_to_all.23.parts = f32[8,8,128]{2,1,0:T(8,128)S(1)} all-to-all(f32[8,8,128]{2,1,0:T(8,128)S(1)} %get-tuple-element.58), channel_id=1, replica_groups=mesh['chip'=64,'core'=2,'cls'=8] {'cls'}, dimensions={0} | all-to-all | bytes 65536 | tf_op jit(solution)/shard_map/all_to_all | solution.py:263
  133.6 1.1 shard_map.72
Async XLA Ops:
  0.0 0.7 copy-start.2
  0.7 1.0 copy-start.1
  1.7 23.6 %copy-start.3 = (s32[1024]{0:T(1024)S(1)}, s32[1024]{0:T(1024)}, u32[]{:S(2)}) copy-start(s32[1024]{0:T(1024)} %param.10) | copy-start | bytes 12292
  1.7 23.6 %copy-start.4 = (s32[32]{0:T(128)S(1)}, s32[32]{0:T(128)}, u32[]{:S(2)}) copy-start(s32[32]{0:T(128)} %refs_1_.5) | copy-start | bytes 388
  1.7 23.6 %copy-start.5 = (s32[32]{0:T(128)S(1)}, s32[32]{0:T(128)}, u32[]{:S(2)}) copy-start(s32[32]{0:T(128)} %refs_2_.5) | copy-start | bytes 388
  3.1 52.1 %copy-start = (bf16[32,128,128]{2,1,0:T(8,128)(2,1)S(1)}, bf16[32,128,128]{2,1,0:T(8,128)(2,1)}, u32[]{:S(2)}) copy-start(bf16[32,128,128]{2,1,0:T(8,128)(2,1)} %refs_0_.5) | copy-start | bytes 3145732
  3.1 38.7 %collective-permute-start = (f32[4,128,128]{2,1,0:T(8,128)S(1)}, f32[4,128,128]{2,1,0:T(8,128)S(1)}, u32[]{:S(2)}, u32[]{:S(2)}) collective-permute-start(f32[4,128,128]{2,1,0:T(8,128)S(1)} %get-tuple-element.33), channel_id=1, source_target_pairs={{0,16},{16,0},{32,48},{48,32},{64,80},{80,64},{96,112},{112,96},{1... | collective-permute-start | bytes 786440 | tf_op jit(solution)/shard_map/ppermute | solution.py:226
  9.0 32.8 %collective-permute-start.1 = (f32[4,128,128]{2,1,0:T(8,128)S(1)}, f32[4,128,128]{2,1,0:T(8,128)S(1)}, u32[]{:S(2)}, u32[]{:S(2)}) collective-permute-start(f32[4,128,128]{2,1,0:T(8,128)S(1)} %get-tuple-element.34), channel_id=1, source_target_pairs={{0,1008},{16,32},{32,16},{48,64},{64,48},{80,96},{96,80},{112,128}... | collective-permute-start | bytes 786440 | tf_op jit(solution)/shard_map/ppermute | solution.py:227
  42.4 12.8 %collective-permute-start.2 = (f32[4,128,128]{2,1,0:T(8,128)S(1)}, f32[4,128,128]{2,1,0:T(8,128)S(1)}, u32[]{:S(2)}, u32[]{:S(2)}) collective-permute-start(f32[4,128,128]{2,1,0:T(8,128)S(1)} %get-tuple-element.36), channel_id=1, source_target_pairs={{0,8},{8,0},{1,9},{9,1},{2,10},{10,2},{3,11},{11,3},{4,12},{12,4},... | collective-permute-start | bytes 786440 | tf_op jit(solution)/shard_map/ppermute | solution.py:236
  45.6 5.3 %collective-permute-start.3 = (f32[8,128]{1,0:T(8,128)S(1)}, f32[8,128]{1,0:T(8,128)S(1)}, u32[]{:S(2)}, u32[]{:S(2)}) collective-permute-start(f32[8,128]{1,0:T(8,128)S(1)} %get-tuple-element.38), channel_id=1, source_target_pairs={{0,16},{16,0},{32,48},{48,32},{64,80},{80,64},{96,112},{112,96},{1... | collective-permute-start | bytes 12296 | tf_op jit(solution)/shard_map/ppermute | solution.py:237
  47.5 7.7 %collective-permute-start.4 = (f32[8,128]{1,0:T(8,128)S(1)}, f32[8,128]{1,0:T(8,128)S(1)}, u32[]{:S(2)}, u32[]{:S(2)}) collective-permute-start(f32[8,128]{1,0:T(8,128)S(1)} %get-tuple-element.39), channel_id=1, source_target_pairs={{0,1008},{16,32},{32,16},{48,64},{64,48},{80,96},{96,80},{112,128}... | collective-permute-start | bytes 12296 | tf_op jit(solution)/shard_map/ppermute | solution.py:238
  57.2 17.3 %collective-permute-start.5 = (f32[4,128,128]{2,1,0:T(8,128)S(1)}, f32[4,128,128]{2,1,0:T(8,128)S(1)}, u32[]{:S(2)}, u32[]{:S(2)}) collective-permute-start(f32[4,128,128]{2,1,0:T(8,128)S(1)} %get-tuple-element.42), channel_id=1, source_target_pairs={{0,16},{16,0},{32,48},{48,32},{64,80},{80,64},{96,112},{112,96},{1... | collective-permute-start | bytes 786440 | tf_op jit(solution)/shard_map/ppermute | solution.py:226
  59.2 15.4 %collective-permute-start.6 = (f32[4,128,128]{2,1,0:T(8,128)S(1)}, f32[4,128,128]{2,1,0:T(8,128)S(1)}, u32[]{:S(2)}, u32[]{:S(2)}) collective-permute-start(f32[4,128,128]{2,1,0:T(8,128)S(1)} %get-tuple-element.43), channel_id=1, source_target_pairs={{0,1008},{16,32},{32,16},{48,64},{64,48},{80,96},{96,80},{112,128}... | collective-permute-start | bytes 786440 | tf_op jit(solution)/shard_map/ppermute | solution.py:227
  75.2 12.8 %collective-permute-start.7 = (f32[4,128,128]{2,1,0:T(8,128)S(1)}, f32[4,128,128]{2,1,0:T(8,128)S(1)}, u32[]{:S(2)}, u32[]{:S(2)}) collective-permute-start(f32[4,128,128]{2,1,0:T(8,128)S(1)} %get-tuple-element.45), channel_id=1, source_target_pairs={{0,8},{8,0},{1,9},{9,1},{2,10},{10,2},{3,11},{11,3},{4,12},{12,4},... | collective-permute-start | bytes 786440 | tf_op jit(solution)/shard_map/ppermute | solution.py:236
  78.4 6.9 %collective-permute-start.8 = (f32[8,128]{1,0:T(8,128)S(1)}, f32[8,128]{1,0:T(8,128)S(1)}, u32[]{:S(2)}, u32[]{:S(2)}) collective-permute-start(f32[8,128]{1,0:T(8,128)S(1)} %get-tuple-element.47), channel_id=1, source_target_pairs={{0,16},{16,0},{32,48},{48,32},{64,80},{80,64},{96,112},{112,96},{1... | collective-permute-start | bytes 12296 | tf_op jit(solution)/shard_map/ppermute | solution.py:237
  80.3 7.7 %collective-permute-start.9 = (f32[8,128]{1,0:T(8,128)S(1)}, f32[8,128]{1,0:T(8,128)S(1)}, u32[]{:S(2)}, u32[]{:S(2)}) collective-permute-start(f32[8,128]{1,0:T(8,128)S(1)} %get-tuple-element.48), channel_id=1, source_target_pairs={{0,1008},{16,32},{32,16},{48,64},{64,48},{80,96},{96,80},{112,128}... | collective-permute-start | bytes 12296 | tf_op jit(solution)/shard_map/ppermute | solution.py:238
  90.0 18.6 %collective-permute-start.10 = (f32[4,128,128]{2,1,0:T(8,128)S(1)}, f32[4,128,128]{2,1,0:T(8,128)S(1)}, u32[]{:S(2)}, u32[]{:S(2)}) collective-permute-start(f32[4,128,128]{2,1,0:T(8,128)S(1)} %get-tuple-element.50), channel_id=1, source_target_pairs={{0,16},{16,0},{32,48},{48,32},{64,80},{80,64},{96,112},{112,96},{1... | collective-permute-start | bytes 786440 | tf_op jit(solution)/shard_map/ppermute | solution.py:226
  91.9 16.7 %collective-permute-start.11 = (f32[4,128,128]{2,1,0:T(8,128)S(1)}, f32[4,128,128]{2,1,0:T(8,128)S(1)}, u32[]{:S(2)}, u32[]{:S(2)}) collective-permute-start(f32[4,128,128]{2,1,0:T(8,128)S(1)} %get-tuple-element.51), channel_id=1, source_target_pairs={{0,1008},{16,32},{32,16},{48,64},{64,48},{80,96},{96,80},{112,128}... | collective-permute-start | bytes 786440 | tf_op jit(solution)/shard_map/ppermute | solution.py:227
  109.2 12.8 %collective-permute-start.12 = (f32[4,128,128]{2,1,0:T(8,128)S(1)}, f32[4,128,128]{2,1,0:T(8,128)S(1)}, u32[]{:S(2)}, u32[]{:S(2)}) collective-permute-start(f32[4,128,128]{2,1,0:T(8,128)S(1)} %get-tuple-element.53), channel_id=1, source_target_pairs={{0,8},{8,0},{1,9},{9,1},{2,10},{10,2},{3,11},{11,3},{4,12},{12,4},... | collective-permute-start | bytes 786440 | tf_op jit(solution)/shard_map/ppermute | solution.py:236
  112.4 5.6 %collective-permute-start.13 = (f32[8,128]{1,0:T(8,128)S(1)}, f32[8,128]{1,0:T(8,128)S(1)}, u32[]{:S(2)}, u32[]{:S(2)}) collective-permute-start(f32[8,128]{1,0:T(8,128)S(1)} %get-tuple-element.55), channel_id=1, source_target_pairs={{0,16},{16,0},{32,48},{48,32},{64,80},{80,64},{96,112},{112,96},{1... | collective-permute-start | bytes 12296 | tf_op jit(solution)/shard_map/ppermute | solution.py:237
  114.3 7.7 %collective-permute-start.14 = (f32[8,128]{1,0:T(8,128)S(1)}, f32[8,128]{1,0:T(8,128)S(1)}, u32[]{:S(2)}, u32[]{:S(2)}) collective-permute-start(f32[8,128]{1,0:T(8,128)S(1)} %get-tuple-element.56), channel_id=1, source_target_pairs={{0,1008},{16,32},{32,16},{48,64},{64,48},{80,96},{96,80},{112,128}... | collective-permute-start | bytes 12296 | tf_op jit(solution)/shard_map/ppermute | solution.py:238

commit v4 on v2

v4 whole, which is shorter than its diff:
```python
import jax
import jax.numpy as jnp
from jax import lax
from jax.experimental import pallas as pl
from jax.experimental.pallas import tpu as pltpu
from jax.sharding import Mesh
from jax.sharding import PartitionSpec as P

CLASSES = 1024
ITERS = 3
SIDE = 128

VMEM = pl.BlockSpec(memory_space=pltpu.VMEM)
SMEM = pl.BlockSpec(memory_space=pltpu.SMEM)
HBM = pl.BlockSpec(memory_space=pltpu.HBM)
F32 = jnp.float32
PARAMS = pltpu.CompilerParams(vmem_limit_bytes=16 * 1024 * 1024)


def shape(*dims):
    return jax.ShapeDtypeStruct(dims, F32)


def shift_right(value, by):
    return lax.shift_right_logical(value, by)


def previous_first():
    return 1 - lax.rem(lax.axis_index("chip"), 2)


def plan_entries(rows, cols, send):
    core = lax.axis_index("core")
    for tile in range(32):
        yield rows[tile]
    for tile in range(32):
        col = cols[tile]
        ghost = jnp.maximum(col - 8, 0)
        offset = shift_right(ghost, 1)
        half = shift_right(offset, 1)
        near = half ^ (1 - core)
        far = 2 + (half ^ (1 - previous_first()))
        pair = jnp.where(lax.rem(offset, 2) == 1, far, near)
        yield jnp.where(col < 8, col, 8 + 2 * pair + lax.rem(ghost, 2))
    for offset in range(4):
        for within in range(2):
            yield send[0, within, offset]


def row_block(plan, tile):
    return plan[tile]


def operand_block(plan, tile):
    return plan[32 + tile]


def sent_block(plan, offset, within):
    return plan[64 + 2 * offset + within]


def block_at(ref, place):
    return ref[SIDE * place : SIDE * (place + 1), :]


def fill_swaps(source, sums, plan, outs):
    previous = previous_first()
    for out, behind in zip(outs, (previous, 1 - previous)):
        out[4 * SIDE + 4 :, :] = jnp.zeros((4, SIDE), F32)
        for part in range(2):
            for within in range(2):
                place = 2 * part + within
                block = sent_block(plan, 2 * behind + 1 - part, within)
                out[SIDE * place : SIDE * (place + 1), :] = source[block]
                out[4 * SIDE + place : 4 * SIDE + place + 1, :] = sums[pl.ds(block, 1), :]


def lane_sums(block):
    return jnp.sum(jnp.transpose(block), axis=0, keepdims=True)


def first_kernel(labels, rows, cols, send, mask, kept, mask_kept, plan, out0, out1, own, *scratch):
    rows_here, cols_here, send_here, sems = scratch
    pairs = [(rows, rows_here), (cols, cols_here), (send, send_here)]
    pairs += [(labels.at[block], kept.at[block]) for block in range(8)]
    pairs += [(mask, mask_kept)]
    copies = []
    for number, (here, there) in enumerate(pairs):
        copy = pltpu.make_async_copy(here, there, sems.at[number])
        copy.start()
        copies.append(copy)
    for copy in copies[:3]:
        copy.wait()
    for place, entry in enumerate(plan_entries(rows_here, cols_here, send_here)):
        plan[place] = entry
    for block in range(8):
        copies[3 + block].wait()
        own[block : block + 1, :] = lane_sums(kept[block])
    fill_swaps(kept, own, plan, (out0, out1))
    copies[11].wait()


def mass_kernel(plan, source, own, in0, in1, parts, relay, rows):
    previous = previous_first()
    core = lax.axis_index("core")
    rows[0:8, :] = own[...]
    rows[8:10, :] = in0[4 * SIDE : 4 * SIDE + 2, :]
    rows[10:12, :] = in1[4 * SIDE : 4 * SIDE + 2, :]
    for within in range(2):
        block = sent_block(plan, 2 * core, within)
        relay[within] = source[block]
        rows[12 + within : 13 + within, :] = own[pl.ds(block, 1), :]

    def pass_on(received):
        for within in range(2):
            relay[2 + within] = block_at(received, 2 + within)
        rows[14:16, :] = received[4 * SIDE + 2 : 4 * SIDE + 4, :]

    pl.when(previous == core)(lambda: pass_on(in0))
    pl.when(previous != core)(lambda: pass_on(in1))
    partial = rows[...]
    for share in range(16):
        parts[share] = partial


def scales(total, blocks):
    scale = CLASSES / total
    full = jnp.concatenate([scale, jnp.zeros((SIDE - blocks, SIDE), F32)], axis=0)
    return jnp.transpose(full)


def total_of(parts, core):
    total = parts[8 * core]
    for share in range(1, 8):
        total = total + parts[8 * core + share]
    return total


def split(value):
    high = value.astype(jnp.bfloat16)
    low = (value - high.astype(F32)).astype(jnp.bfloat16)
    return high, low


def spread_kernel(first, last, *refs):
    refs = list(refs)
    tiles, plan, mask, source, in0, in1, near, parts = refs[:8]
    refs = refs[8:]
    anchor = refs.pop(0) if first else mask
    squared = refs.pop(0)
    if last:
        own_parts, operand, products = refs
    else:
        out0, out1, own, operand, products = refs
    core = lax.axis_index("core")
    mine = total_of(parts, core)
    mate = total_of(parts, 1 - core)
    scale = scales(jnp.concatenate([mine[0:8], mate[12:16], mine[8:12]], axis=0), 16)
    if first:
        seeded = jnp.concatenate(
            [mask[...].astype(F32), jnp.zeros((SIDE - 8, SIDE), F32)], axis=0
        )
        seeded = 64.0 * jnp.transpose(seeded)
    for block in range(16):
        if block < 8:
            value = source[block]
        elif block < 12:
            value = near[block - 8]
        else:
            value = block_at(in0 if block < 14 else in1, block % 2)
        value = value * scale[:, block : block + 1]
        if first and block < 8:
            anchor[block] = seeded[:, block : block + 1] * value + 4.0
        high, low = split(value)
        operand[block, :SIDE, :] = high
        operand[block, SIDE:, :] = low
    for tile in range(32):
        weights = tiles[tile]
        products[tile] = jnp.dot(
            jnp.concatenate([weights, weights], axis=1),
            operand[operand_block(plan, tile)],
            preferred_element_type=F32,
        )
    squared[...] = anchor[...]
    for tile in range(32):
        row = row_block(plan, tile)
        squared[row] = squared[row] + products[tile]
    sums = []
    for block in range(8):
        value = squared[block]
        value = value * value
        squared[block] = value
        sums.append(lane_sums(value))
    sums = jnp.concatenate(sums, axis=0)
    if last:
        for share in range(8):
            own_parts[share] = sums
    else:
        own[...] = sums
        fill_swaps(squared, own, plan, (out0, out1))


def last_kernel(squared, parts, out):
    scale = scales(total_of(parts, 0), 8)
    for block in range(8):
        out[block] = squared[block] * scale[:, block : block + 1]


def on_device(tiles, tile_rows, tile_cols, send_lists, seed_mask, labels):
    chips = lax.axis_size("chip")
    swap0 = [(i, (((i + 1) ^ 1) - 1) % chips) for i in range(chips)]
    swap1 = [(i, i ^ 1) for i in range(chips)]
    send_lists = jnp.transpose(send_lists, (0, 2, 1))
    blocks = labels.reshape(8, SIDE, SIDE)
    mask = seed_mask.reshape(8, SIDE)
    own_shape = shape(8, SIDE, SIDE)
    swap_shape = shape(4 * SIDE + 8, SIDE)
    source, mask, plan, out0, out1, own = pl.pallas_call(
        first_kernel,
        out_shape=[
            own_shape,
            jax.ShapeDtypeStruct((8, SIDE), jnp.int32),
            jax.ShapeDtypeStruct((72,), jnp.int32),
            swap_shape,
            swap_shape,
            shape(8, SIDE),
        ],
        in_specs=[HBM] * 5,
        out_specs=[VMEM, VMEM, SMEM, VMEM, VMEM, VMEM],
        scratch_shapes=[
            pltpu.SMEM((32,), jnp.int32),
            pltpu.SMEM((32,), jnp.int32),
            pltpu.SMEM((1, 2, 4), jnp.int32),
            pltpu.SemaphoreType.DMA((12,)),
        ],
        compiler_params=PARAMS,
    )(*[
        pltpu.with_memory_space_constraint(value, pltpu.HBM)
        for value in (blocks, tile_rows, tile_cols, send_lists, mask)
    ])
    anchor = None
    for iteration in range(ITERS):
        first = iteration == 0
        last = iteration == ITERS - 1
        in0 = lax.ppermute(out0, "chip", swap0)
        in1 = lax.ppermute(out1, "chip", swap1)
        parts, relay = pl.pallas_call(
            mass_kernel,
            out_shape=[shape(16, 16, SIDE), shape(4, SIDE, SIDE)],
            in_specs=[SMEM] + [VMEM] * 4,
            out_specs=[VMEM, VMEM],
            scratch_shapes=[pltpu.VMEM((16, SIDE), F32)],
            compiler_params=PARAMS,
        )(plan, source, own, in0, in1)
        near = lax.ppermute(relay, "core", [(0, 1), (1, 0)])
        parts = lax.all_to_all(parts, ("core", "cls"), 0, 0)
        out_shape = [own_shape] * (2 if first else 1)
        out_shape += [shape(8, 8, SIDE)] if last else [swap_shape, swap_shape, shape(8, SIDE)]
        results = pl.pallas_call(
            lambda *refs, first=first, last=last: spread_kernel(first, last, *refs),
            out_shape=out_shape,
            in_specs=[VMEM, SMEM] + [VMEM] * 6,
            out_specs=[VMEM] * len(out_shape),
            scratch_shapes=[
                pltpu.VMEM((16, 2 * SIDE, SIDE), jnp.bfloat16),
                pltpu.VMEM((32, SIDE, SIDE), F32),
            ],
            compiler_params=PARAMS,
        )(tiles, plan, mask if first else anchor, source, in0, in1, near, parts)
        if first:
            anchor, *results = results
        if last:
            source, parts = results
        else:
            source, out0, out1, own = results
    parts = lax.all_to_all(parts, "cls", 0, 0)
    out = pl.pallas_call(
        last_kernel,
        out_shape=own_shape,
        in_specs=[VMEM, VMEM],
        out_specs=VMEM,
        compiler_params=PARAMS,
    )(source, parts)
    return out.reshape(8 * SIDE, SIDE)


def solution(mesh):
    split_mesh = Mesh(
        mesh.devices.reshape(mesh.shape["dom"] // 2, 2, mesh.shape["cls"]), ("chip", "core", "cls")
    )
    dom = ("chip", "core")
    return jax.shard_map(
        on_device,
        mesh=split_mesh,
        in_specs=(P(dom, None, None), P(dom), P(dom), P(dom, None, None), P(dom), P(dom, "cls")),
        out_specs=P(dom, "cls"),
        check_vma=False,
    )
```

time: 129 us -> 126 us (0.977)
  starting transfers between devices: 50.9 us -> 46.8 us
  waiting for transfers between devices: 15.8 us -> 19.8 us
  local copies, waits for them, and re-layouts: 3.91 us -> 0.01 us
    ppermute x6, starting transfers between devices: 39.3 us -> 34.5 us  [the longest x3 28.8 us: on_device(): in0 = lax.ppermute(out0, 'chip', swap0)]
    ppermute x6, waiting for transfers between devices: 15.8 us -> 19.8 us  [the longest x3 15 us: on_device(): in0 = lax.ppermute(out0, 'chip', swap0)]
    unnamed x15 -> x2, local copies, waits for them, and re-layouts: 3.91 us -> 0.01 us
  transfers between devices with their start and end apart: 9 -> 9, of which waited for: 3 -> 5; matrix products, arithmetic and copies ran while one was open for 0% -> 0% of each run, Pallas kernels for 0% -> 0%
where the time goes in v4:
time: 126 us; the launch traced here: 125 us
  blocking collectives  47.1 us (37%)
  starting transfers between devices  46.8 us (37%)
  waiting for transfers between devices  19.8 us (16%)
  Pallas kernels  11.5 us (9%)
    all_to_all x3, blocking collectives, on_device(): parts = lax.all_to_all(parts, ('core', 'cls'), 0, 0)  36.9 us
    ppermute x3, starting transfers between devices, on_device(): in0 = lax.ppermute(out0, 'chip', swap0)  28.8 us
    ppermute x3, waiting for transfers between devices, on_device(): in0 = lax.ppermute(out0, 'chip', swap0)  15 us
    ppermute x3, starting transfers between devices, on_device(): near = lax.ppermute(relay, 'core', [(0, 1), (1, 0)])  12.3 us
    all_to_all x1, blocking collectives, on_device(): parts = lax.all_to_all(parts, 'cls', 0, 0)  10.2 us
    pallas_call x3, Pallas kernels, on_device(): pl.pallas_call(lambda *refs, first=first, last=last: spread_kernel(first,...  6.01 us
    ppermute x3, starting transfers between devices, on_device(): in1 = lax.ppermute(out1, 'chip', swap1)  5.76 us
    ppermute x3, waiting for transfers between devices, on_device(): in1 = lax.ppermute(out1, 'chip', swap1)  4.74 us
  transfers between devices with their start and end apart: 9, of which 5 were waited for; matrix products, arithmetic and copies ran while one was open for 0% of the time, Pallas kernels for 0%

profile of v4, /device:TPU:1, one launch (start us, length us, event | category | flops | bytes accessed | tf_op | source)
XLA Modules:
  0.0 125.3 jit_solution(7205634294409602001)
XLA Ops:
  0.0 0.0 copy-start
  0.0 2.6 %shard_map.64 = (f32[8,128,128]{2,1,0:T(8,128)S(1)}, s32[8,128]{1,0:T(8,128)S(1)}, s32[72]{0:T(128)S(1)}, f32[520,128]{1,0:T(8,128)S(1)}, f32[520,128]{1,0:T(8,128)S(1)}, /*index=5*/f32[8,128]{1,0:T(8,128)S(1)}) custom-call(f32[8,128,128]{2,1,0:T(8,128)} %bitcast.4, s32[32]{0:T(128)} %rows.1, s32[32]{0:T(128)} %cols.1, s32[1,2,4]{2,1,0:T(2,128)} %bitcast.6, ...), custom_call_target="tpu_custom_call" | custom-call | tf_op jit(solution)/shard_map/pallas_call | solution.py:218
  2.6 20.2 %collective-permute-start = (f32[520,128]{1,0:T(8,128)S(1)}, f32[520,128]{1,0:T(8,128)S(1)}, u32[]{:S(2)}, u32[]{:S(2)}) collective-permute-start(f32[520,128]{1,0:T(8,128)S(1)} %get-tuple-element.31), channel_id=1, source_target_pairs={{0,1008},{16,32},{32,16},{48,64},{64,48},{80,96},{96,80},{112,128}... | collective-permute-start | bytes 798728 | tf_op jit(solution)/shard_map/ppermute | solution.py:245
  22.8 1.9 %collective-permute-start.1 = (f32[520,128]{1,0:T(8,128)S(1)}, f32[520,128]{1,0:T(8,128)S(1)}, u32[]{:S(2)}, u32[]{:S(2)}) collective-permute-start(f32[520,128]{1,0:T(8,128)S(1)} %get-tuple-element.32), channel_id=1, source_target_pairs={{0,16},{16,0},{32,48},{48,32},{64,80},{80,64},{96,112},{112,96},{1... | collective-permute-start | bytes 798728 | tf_op jit(solution)/shard_map/ppermute | solution.py:246
  24.7 3.9 %collective-permute-done.in0.refs_4_ = f32[520,128]{1,0:T(8,128)S(1)} collective-permute-done((f32[520,128]{1,0:T(8,128)S(1)}, f32[520,128]{1,0:T(8,128)S(1)}, u32[]{:S(2)}, u32[]{:S(2)}) %collective-permute-start) | collective-permute-done | bytes 266272 | tf_op jit(solution)/shard_map/ppermute | solution.py:245
  28.6 3.0 %collective-permute-done.1.in1.refs_5_ = f32[520,128]{1,0:T(8,128)S(1)} collective-permute-done((f32[520,128]{1,0:T(8,128)S(1)}, f32[520,128]{1,0:T(8,128)S(1)}, u32[]{:S(2)}, u32[]{:S(2)}) %collective-permute-start.1) | collective-permute-done | bytes 266272 | tf_op jit(solution)/shard_map/ppermute | solution.py:246
  31.6 0.6 shard_map.65
  32.2 3.8 %collective-permute-start.2 = (f32[4,128,128]{2,1,0:T(8,128)S(1)}, f32[4,128,128]{2,1,0:T(8,128)S(1)}, u32[]{:S(2)}, u32[]{:S(2)}) collective-permute-start(f32[4,128,128]{2,1,0:T(8,128)S(1)} %get-tuple-element.34), channel_id=1, source_target_pairs={{0,8},{8,0},{1,9},{9,1},{2,10},{10,2},{3,11},{11,3},{4,12},{12,4},... | collective-permute-start | bytes 786440 | tf_op jit(solution)/shard_map/ppermute | solution.py:255
  36.0 14.8 %all_to_all.20.refs_7_ = f32[16,16,128]{2,1,0:T(8,128)S(1)} all-to-all(f32[16,16,128]{2,1,0:T(8,128)S(1)} %get-tuple-element.35), channel_id=1, replica_groups=mesh['chip'=64,'core'=2,'cls'=8] {'core','cls'}, dimensions={0} | all-to-all | bytes 262144 | tf_op jit(solution)/shard_map/all_to_all | solution.py:256
  50.8 0.0 collective-permute-done.2.refs_6_
  50.8 0.0 copy-done
  50.8 2.0 %shard_map.66 = (f32[8,128,128]{2,1,0:T(8,128)S(1)}, f32[8,128,128]{2,1,0:T(8,128)S(1)}, f32[520,128]{1,0:T(8,128)S(1)}, f32[520,128]{1,0:T(8,128)S(1)}, f32[8,128]{1,0:T(8,128)S(1)}) custom-call(bf16[32,128,128]{2,1,0:T(8,128)(2,1)S(1)} %copy-done, s32[72]{0:T(128)S(1)} %get-tuple-element.28.plan.refs_1_, s32[8,128]{1,0:T(8,128)S(1)} %get-tuple-element.29.refs_2_, ...), custom_call_target="tpu_custom_call" | custom-call | tf_op jit(solution)/shard_map/pallas_call | solution.py:259
  52.8 3.3 %collective-permute-start.3 = (f32[520,128]{1,0:T(8,128)S(1)}, f32[520,128]{1,0:T(8,128)S(1)}, u32[]{:S(2)}, u32[]{:S(2)}) collective-permute-start(f32[520,128]{1,0:T(8,128)S(1)} %get-tuple-element.38), channel_id=1, source_target_pairs={{0,1008},{16,32},{32,16},{48,64},{64,48},{80,96},{96,80},{112,128}... | collective-permute-start | bytes 798728 | tf_op jit(solution)/shard_map/ppermute | solution.py:245
  56.1 1.9 %collective-permute-start.4 = (f32[520,128]{1,0:T(8,128)S(1)}, f32[520,128]{1,0:T(8,128)S(1)}, u32[]{:S(2)}, u32[]{:S(2)}) collective-permute-start(f32[520,128]{1,0:T(8,128)S(1)} %get-tuple-element.39), channel_id=1, source_target_pairs={{0,16},{16,0},{32,48},{48,32},{64,80},{80,64},{96,112},{112,96},{1... | collective-permute-start | bytes 798728 | tf_op jit(solution)/shard_map/ppermute | solution.py:246
  58.1 6.6 %collective-permute-done.3.in0.refs_4_ = f32[520,128]{1,0:T(8,128)S(1)} collective-permute-done((f32[520,128]{1,0:T(8,128)S(1)}, f32[520,128]{1,0:T(8,128)S(1)}, u32[]{:S(2)}, u32[]{:S(2)}) %collective-permute-start.3) | collective-permute-done | bytes 266272 | tf_op jit(solution)/shard_map/ppermute | solution.py:245
  64.6 0.0 collective-permute-done.4.in1.refs_5_
  64.6 0.6 shard_map.67
  65.2 4.1 %collective-permute-start.5 = (f32[4,128,128]{2,1,0:T(8,128)S(1)}, f32[4,128,128]{2,1,0:T(8,128)S(1)}, u32[]{:S(2)}, u32[]{:S(2)}) collective-permute-start(f32[4,128,128]{2,1,0:T(8,128)S(1)} %get-tuple-element.41), channel_id=1, source_target_pairs={{0,8},{8,0},{1,9},{9,1},{2,10},{10,2},{3,11},{11,3},{4,12},{12,4},... | collective-permute-start | bytes 786440 | tf_op jit(solution)/shard_map/ppermute | solution.py:255
  69.4 11.0 %all_to_all.21.refs_7_ = f32[16,16,128]{2,1,0:T(8,128)S(1)} all-to-all(f32[16,16,128]{2,1,0:T(8,128)S(1)} %get-tuple-element.42), channel_id=1, replica_groups=mesh['chip'=64,'core'=2,'cls'=8] {'core','cls'}, dimensions={0} | all-to-all | bytes 262144 | tf_op jit(solution)/shard_map/all_to_all | solution.py:256
  80.4 0.0 collective-permute-done.5.refs_6_
  80.4 2.0 %shard_map.68 = (f32[8,128,128]{2,1,0:T(8,128)S(1)}, f32[520,128]{1,0:T(8,128)S(1)}, f32[520,128]{1,0:T(8,128)S(1)}, f32[8,128]{1,0:T(8,128)S(1)}) custom-call(bf16[32,128,128]{2,1,0:T(8,128)(2,1)S(1)} %copy-done, s32[72]{0:T(128)S(1)} %get-tuple-element.28.plan.refs_1_, f32[8,128,128]{2,1,0:T(8,128)S(1)} %get-tuple-element.36.refs_2_, ...), custom_call_target="tpu_custom_call" | custom-call | tf_op jit(solution)/shard_map/pallas_call | solution.py:259
  82.4 5.3 %collective-permute-start.6 = (f32[520,128]{1,0:T(8,128)S(1)}, f32[520,128]{1,0:T(8,128)S(1)}, u32[]{:S(2)}, u32[]{:S(2)}) collective-permute-start(f32[520,128]{1,0:T(8,128)S(1)} %get-tuple-element.44), channel_id=1, source_target_pairs={{0,1008},{16,32},{32,16},{48,64},{64,48},{80,96},{96,80},{112,128}... | collective-permute-start | bytes 798728 | tf_op jit(solution)/shard_map/ppermute | solution.py:245
  87.7 1.9 %collective-permute-start.7 = (f32[520,128]{1,0:T(8,128)S(1)}, f32[520,128]{1,0:T(8,128)S(1)}, u32[]{:S(2)}, u32[]{:S(2)}) collective-permute-start(f32[520,128]{1,0:T(8,128)S(1)} %get-tuple-element.45), channel_id=1, source_target_pairs={{0,16},{16,0},{32,48},{48,32},{64,80},{80,64},{96,112},{112,96},{1... | collective-permute-start | bytes 798728 | tf_op jit(solution)/shard_map/ppermute | solution.py:246
  89.6 4.6 %collective-permute-done.6.in0.refs_4_ = f32[520,128]{1,0:T(8,128)S(1)} collective-permute-done((f32[520,128]{1,0:T(8,128)S(1)}, f32[520,128]{1,0:T(8,128)S(1)}, u32[]{:S(2)}, u32[]{:S(2)}) %collective-permute-start.6) | collective-permute-done | bytes 266272 | tf_op jit(solution)/shard_map/ppermute | solution.py:245
  94.2 1.7 %collective-permute-done.7.in1.refs_5_ = f32[520,128]{1,0:T(8,128)S(1)} collective-permute-done((f32[520,128]{1,0:T(8,128)S(1)}, f32[520,128]{1,0:T(8,128)S(1)}, u32[]{:S(2)}, u32[]{:S(2)}) %collective-permute-start.7) | collective-permute-done | bytes 266272 | tf_op jit(solution)/shard_map/ppermute | solution.py:246
  95.9 0.6 shard_map.69
  96.5 4.4 %collective-permute-start.8 = (f32[4,128,128]{2,1,0:T(8,128)S(1)}, f32[4,128,128]{2,1,0:T(8,128)S(1)}, u32[]{:S(2)}, u32[]{:S(2)}) collective-permute-start(f32[4,128,128]{2,1,0:T(8,128)S(1)} %get-tuple-element.47), channel_id=1, source_target_pairs={{0,8},{8,0},{1,9},{9,1},{2,10},{10,2},{3,11},{11,3},{4,12},{12,4},... | collective-permute-start | bytes 786440 | tf_op jit(solution)/shard_map/ppermute | solution.py:255
  100.9 11.0 %all_to_all.22.refs_7_ = f32[16,16,128]{2,1,0:T(8,128)S(1)} all-to-all(f32[16,16,128]{2,1,0:T(8,128)S(1)} %get-tuple-element.48), channel_id=1, replica_groups=mesh['chip'=64,'core'=2,'cls'=8] {'core','cls'}, dimensions={0} | all-to-all | bytes 262144 | tf_op jit(solution)/shard_map/all_to_all | solution.py:256
  112.0 0.0 collective-permute-done.8.refs_6_
  112.0 2.0 %shard_map.70 = (f32[8,128,128]{2,1,0:T(8,128)S(1)}, f32[8,8,128]{2,1,0:T(8,128)S(1)}) custom-call(bf16[32,128,128]{2,1,0:T(8,128)(2,1)S(1)} %copy-done, s32[72]{0:T(128)S(1)} %get-tuple-element.28.plan.refs_1_, f32[8,128,128]{2,1,0:T(8,128)S(1)} %get-tuple-element.36.refs_2_, f32[8,128,128]{2,1,0:T(8,128)S(1)} %get-tuple-element.43.source.refs_3_, ...), custom_call_target="tpu_custom_call" | custom-call | tf_op jit(solution)/shard_map/pallas_call | solution.py:259
  114.0 10.2 %all_to_all.23.parts = f32[8,8,128]{2,1,0:T(8,128)S(1)} all-to-all(f32[8,8,128]{2,1,0:T(8,128)S(1)} %get-tuple-element.50), channel_id=1, replica_groups=mesh['chip'=64,'core'=2,'cls'=8] {'cls'}, dimensions={0} | all-to-all | bytes 65536 | tf_op jit(solution)/shard_map/all_to_all | solution.py:276
  124.2 1.1 shard_map.71
Async XLA Ops:
  0.0 50.8 %copy-start = (bf16[32,128,128]{2,1,0:T(8,128)(2,1)S(1)}, bf16[32,128,128]{2,1,0:T(8,128)(2,1)}, u32[]{:S(2)}) copy-start(bf16[32,128,128]{2,1,0:T(8,128)(2,1)} %refs_0_.5) | copy-start | bytes 3145732
  2.6 26.0 %collective-permute-start = (f32[520,128]{1,0:T(8,128)S(1)}, f32[520,128]{1,0:T(8,128)S(1)}, u32[]{:S(2)}, u32[]{:S(2)}) collective-permute-start(f32[520,128]{1,0:T(8,128)S(1)} %get-tuple-element.31), channel_id=1, source_target_pairs={{0,1008},{16,32},{32,16},{48,64},{64,48},{80,96},{96,80},{112,128}... | collective-permute-start | bytes 798728 | tf_op jit(solution)/shard_map/ppermute | solution.py:245
  22.8 8.8 %collective-permute-start.1 = (f32[520,128]{1,0:T(8,128)S(1)}, f32[520,128]{1,0:T(8,128)S(1)}, u32[]{:S(2)}, u32[]{:S(2)}) collective-permute-start(f32[520,128]{1,0:T(8,128)S(1)} %get-tuple-element.32), channel_id=1, source_target_pairs={{0,16},{16,0},{32,48},{48,32},{64,80},{80,64},{96,112},{112,96},{1... | collective-permute-start | bytes 798728 | tf_op jit(solution)/shard_map/ppermute | solution.py:246
  32.2 18.6 %collective-permute-start.2 = (f32[4,128,128]{2,1,0:T(8,128)S(1)}, f32[4,128,128]{2,1,0:T(8,128)S(1)}, u32[]{:S(2)}, u32[]{:S(2)}) collective-permute-start(f32[4,128,128]{2,1,0:T(8,128)S(1)} %get-tuple-element.34), channel_id=1, source_target_pairs={{0,8},{8,0},{1,9},{9,1},{2,10},{10,2},{3,11},{11,3},{4,12},{12,4},... | collective-permute-start | bytes 786440 | tf_op jit(solution)/shard_map/ppermute | solution.py:255
  52.8 11.8 %collective-permute-start.3 = (f32[520,128]{1,0:T(8,128)S(1)}, f32[520,128]{1,0:T(8,128)S(1)}, u32[]{:S(2)}, u32[]{:S(2)}) collective-permute-start(f32[520,128]{1,0:T(8,128)S(1)} %get-tuple-element.38), channel_id=1, source_target_pairs={{0,1008},{16,32},{32,16},{48,64},{64,48},{80,96},{96,80},{112,128}... | collective-permute-start | bytes 798728 | tf_op jit(solution)/shard_map/ppermute | solution.py:245
  56.1 8.5 %collective-permute-start.4 = (f32[520,128]{1,0:T(8,128)S(1)}, f32[520,128]{1,0:T(8,128)S(1)}, u32[]{:S(2)}, u32[]{:S(2)}) collective-permute-start(f32[520,128]{1,0:T(8,128)S(1)} %get-tuple-element.39), channel_id=1, source_target_pairs={{0,16},{16,0},{32,48},{48,32},{64,80},{80,64},{96,112},{112,96},{1... | collective-permute-start | bytes 798728 | tf_op jit(solution)/shard_map/ppermute | solution.py:246
  65.2 15.2 %collective-permute-start.5 = (f32[4,128,128]{2,1,0:T(8,128)S(1)}, f32[4,128,128]{2,1,0:T(8,128)S(1)}, u32[]{:S(2)}, u32[]{:S(2)}) collective-permute-start(f32[4,128,128]{2,1,0:T(8,128)S(1)} %get-tuple-element.41), channel_id=1, source_target_pairs={{0,8},{8,0},{1,9},{9,1},{2,10},{10,2},{3,11},{11,3},{4,12},{12,4},... | collective-permute-start | bytes 786440 | tf_op jit(solution)/shard_map/ppermute | solution.py:255
  82.4 11.8 %collective-permute-start.6 = (f32[520,128]{1,0:T(8,128)S(1)}, f32[520,128]{1,0:T(8,128)S(1)}, u32[]{:S(2)}, u32[]{:S(2)}) collective-permute-start(f32[520,128]{1,0:T(8,128)S(1)} %get-tuple-element.44), channel_id=1, source_target_pairs={{0,1008},{16,32},{32,16},{48,64},{64,48},{80,96},{96,80},{112,128}... | collective-permute-start | bytes 798728 | tf_op jit(solution)/shard_map/ppermute | solution.py:245
  87.7 8.2 %collective-permute-start.7 = (f32[520,128]{1,0:T(8,128)S(1)}, f32[520,128]{1,0:T(8,128)S(1)}, u32[]{:S(2)}, u32[]{:S(2)}) collective-permute-start(f32[520,128]{1,0:T(8,128)S(1)} %get-tuple-element.45), channel_id=1, source_target_pairs={{0,16},{16,0},{32,48},{48,32},{64,80},{80,64},{96,112},{112,96},{1... | collective-permute-start | bytes 798728 | tf_op jit(solution)/shard_map/ppermute | solution.py:246
  96.5 15.4 %collective-permute-start.8 = (f32[4,128,128]{2,1,0:T(8,128)S(1)}, f32[4,128,128]{2,1,0:T(8,128)S(1)}, u32[]{:S(2)}, u32[]{:S(2)}) collective-permute-start(f32[4,128,128]{2,1,0:T(8,128)S(1)} %get-tuple-element.47), channel_id=1, source_target_pairs={{0,8},{8,0},{1,9},{9,1},{2,10},{10,2},{3,11},{11,3},{4,12},{12,4},... | collective-permute-start | bytes 786440 | tf_op jit(solution)/shard_map/ppermute | solution.py:255

commit v5 on v4

v5 whole, which is shorter than its diff:
```python
import functools

import jax
import jax.numpy as jnp
from jax import lax
from jax.experimental import pallas as pl
from jax.experimental.pallas import tpu as pltpu
from jax.sharding import Mesh
from jax.sharding import PartitionSpec as P

CLASSES = 1024
ITERS = 3
SIDE = 128

VMEM = pl.BlockSpec(memory_space=pltpu.VMEM)
SMEM = pl.BlockSpec(memory_space=pltpu.SMEM)
HBM = pl.BlockSpec(memory_space=pltpu.HBM)
F32 = jnp.float32
PARAMS = pltpu.CompilerParams(vmem_limit_bytes=16 * 1024 * 1024)


def shape(*dims):
    return jax.ShapeDtypeStruct(dims, F32)


def shift_right(value, by):
    return lax.shift_right_logical(value, by)


def plan_entries(rows, cols, send):
    core = lax.axis_index("core")
    for tile in range(32):
        yield rows[tile]
    for tile in range(32):
        col = cols[tile]
        ghost = jnp.maximum(col - 8, 0)
        offset = shift_right(ghost, 1)
        half = shift_right(offset, 1)
        pair = jnp.where(lax.rem(offset, 2) == 1, 2 + (half ^ (1 - core)), half ^ core)
        yield jnp.where(col < 8, col, 8 + 2 * pair + lax.rem(ghost, 2))
    for offset in range(4):
        for within in range(2):
            yield send[0, within, offset]


def row_block(plan, tile):
    return plan[tile]


def operand_block(plan, tile):
    return plan[32 + tile]


def sent_block(plan, offset, within):
    return plan[64 + 2 * offset + within]


def block_at(ref, place):
    return ref[SIDE * place : SIDE * (place + 1), :]


def fill_swaps(source, sums, block_of, wide, narrow):
    core = lax.axis_index("core")
    for out, offsets in ((wide, (2 - 2 * core, 3 - 2 * core)), (narrow, (1 + 2 * core,))):
        count = 2 * len(offsets)
        out[count * SIDE + count :, :] = jnp.zeros((8 - count, SIDE), F32)
        for part, offset in enumerate(offsets):
            for within in range(2):
                place = 2 * part + within
                block = block_of(offset, within)
                out[SIDE * place : SIDE * (place + 1), :] = source[block]
                out[count * SIDE + place : count * SIDE + place + 1, :] = sums[pl.ds(block, 1), :]


def lane_sums(block):
    return jnp.sum(jnp.transpose(block), axis=0, keepdims=True)


def copy_all(pairs, sems):
    copies = []
    for number, (here, there) in enumerate(pairs):
        copy = pltpu.make_async_copy(here, there, sems.at[number])
        copy.start()
        copies.append(copy)
    return copies


def first_kernel(labels, send, kept, wide, narrow, own, send_here, sems):
    pairs = [(labels.at[block], kept.at[block]) for block in range(8)]
    copies = copy_all([(send, send_here)] + pairs, sems)
    for block in range(8):
        copies[1 + block].wait()
        own[block : block + 1, :] = lane_sums(kept[block])
    copies[0].wait()
    fill_swaps(kept, own, lambda offset, within: send_here[0, within, offset], wide, narrow)


def plan_kernel(rows, cols, send, mask, plan, mask_kept, rows_here, cols_here, send_here, sems):
    copies = copy_all([(rows, rows_here), (cols, cols_here), (send, send_here), (mask, mask_kept)], sems)
    for copy in copies:
        copy.wait()
    for place, entry in enumerate(plan_entries(rows_here, cols_here, send_here)):
        plan[place] = entry


def mass_kernel(plan, source, own, wide, narrow, parts, relay, rows):
    core = lax.axis_index("core")
    rows[0:8, :] = own[...]
    rows[8:10, :] = wide[4 * SIDE : 4 * SIDE + 2, :]
    rows[12:14, :] = wide[4 * SIDE + 2 : 4 * SIDE + 4, :]
    rows[14:16, :] = narrow[2 * SIDE : 2 * SIDE + 2, :]
    for within in range(2):
        block = sent_block(plan, 2 * core, within)
        rows[10 + within : 11 + within, :] = own[pl.ds(block, 1), :]
        relay[within] = source[block]
        relay[2 + within] = block_at(wide, 2 + within)
        relay[4 + within] = block_at(narrow, within)
    partial = rows[...]
    for share in range(16):
        parts[share] = partial


def scales(total, blocks):
    scale = CLASSES / total
    full = jnp.concatenate([scale, jnp.zeros((SIDE - blocks, SIDE), F32)], axis=0)
    return jnp.transpose(full)


def total_of(parts, core):
    total = parts[8 * core]
    for share in range(1, 8):
        total = total + parts[8 * core + share]
    return total


def split(value):
    high = value.astype(jnp.bfloat16)
    low = (value - high.astype(F32)).astype(jnp.bfloat16)
    return high, low


def spread_kernel(first, last, *refs):
    refs = list(refs)
    tiles, plan, mask, source, wide, relay, parts = refs[:7]
    refs = refs[7:]
    anchor = refs.pop(0) if first else mask
    squared = refs.pop(0)
    if last:
        own_parts, operand, products = refs
    else:
        wide_out, narrow_out, own, operand, products = refs
    core = lax.axis_index("core")
    mine = total_of(parts, core)
    mate = total_of(parts, 1 - core)
    scale = scales(jnp.concatenate([mine[0:10], mate[10:16]], axis=0), 16)
    if first:
        seeded = jnp.concatenate(
            [mask[...].astype(F32), jnp.zeros((SIDE - 8, SIDE), F32)], axis=0
        )
        seeded = 64.0 * jnp.transpose(seeded)
    for block in range(16):
        if block < 8:
            value = source[block]
        elif block < 10:
            value = block_at(wide, block - 8)
        else:
            value = relay[block - 10]
        value = value * scale[:, block : block + 1]
        if first and block < 8:
            anchor[block] = seeded[:, block : block + 1] * value + 4.0
        high, low = split(value)
        operand[block, :SIDE, :] = high
        operand[block, SIDE:, :] = low
    for tile in range(32):
        weights = tiles[tile]
        products[tile] = jnp.dot(
            jnp.concatenate([weights, weights], axis=1),
            operand[operand_block(plan, tile)],
            preferred_element_type=F32,
        )
    squared[...] = anchor[...]
    for tile in range(32):
        row = row_block(plan, tile)
        squared[row] = squared[row] + products[tile]
    sums = []
    for block in range(8):
        value = squared[block]
        value = value * value
        squared[block] = value
        sums.append(lane_sums(value))
    sums = jnp.concatenate(sums, axis=0)
    if last:
        for share in range(8):
            own_parts[share] = sums
    else:
        own[...] = sums
        block_of = functools.partial(sent_block, plan)
        fill_swaps(squared, own, block_of, wide_out, narrow_out)


def last_kernel(squared, parts, out, scaled, sems):
    scale = scales(total_of(parts, 0), 8)
    copies = []
    for block in range(8):
        scaled[block] = squared[block] * scale[:, block : block + 1]
        copy = pltpu.make_async_copy(scaled.at[block], out.at[block], sems.at[block])
        copy.start()
        copies.append(copy)
    for copy in copies:
        copy.wait()


def on_device(tiles, tile_rows, tile_cols, send_lists, seed_mask, labels):
    dom = ("chip", "core")
    count = 2 * lax.axis_size("chip")
    adjacent = [(i, (i + (1 if i % 2 else -1)) % count) for i in range(count)]
    three_away = [(i, (i + (-3 if i % 2 else 3)) % count) for i in range(count)]
    send_lists = jnp.transpose(send_lists, (0, 2, 1))
    own_shape = shape(8, SIDE, SIDE)
    swap_shapes = [shape(4 * SIDE + 8, SIDE), shape(2 * SIDE + 8, SIDE), shape(8, SIDE)]
    blocks, tile_rows, tile_cols, send_lists, mask = [
        pltpu.with_memory_space_constraint(value, pltpu.HBM)
        for value in (
            labels.reshape(8, SIDE, SIDE),
            tile_rows,
            tile_cols,
            send_lists,
            seed_mask.reshape(8, SIDE),
        )
    ]
    send_scratch = pltpu.SMEM((1, 2, 4), jnp.int32)
    source, wide, narrow, own = pl.pallas_call(
        first_kernel,
        out_shape=[own_shape] + swap_shapes,
        in_specs=[HBM] * 2,
        out_specs=[VMEM] * 4,
        scratch_shapes=[send_scratch, pltpu.SemaphoreType.DMA((9,))],
        compiler_params=PARAMS,
        cost_estimate=pl.CostEstimate(flops=1 << 20, bytes_accessed=1 << 20, transcendentals=0),
    )(blocks, send_lists)
    plan, mask = pl.pallas_call(
        plan_kernel,
        out_shape=[
            jax.ShapeDtypeStruct((72,), jnp.int32),
            jax.ShapeDtypeStruct((8, SIDE), jnp.int32),
        ],
        in_specs=[HBM] * 4,
        out_specs=[SMEM, VMEM],
        scratch_shapes=[
            pltpu.SMEM((32,), jnp.int32),
            pltpu.SMEM((32,), jnp.int32),
            send_scratch,
            pltpu.SemaphoreType.DMA((4,)),
        ],
        compiler_params=PARAMS,
        cost_estimate=pl.CostEstimate(flops=1 << 20, bytes_accessed=1 << 20, transcendentals=0),
    )(tile_rows, tile_cols, send_lists, mask)
    anchor = None
    for iteration in range(ITERS):
        first = iteration == 0
        last = iteration == ITERS - 1
        wide = lax.ppermute(wide, dom, adjacent)
        narrow = lax.ppermute(narrow, dom, three_away)
        parts, relay = pl.pallas_call(
            mass_kernel,
            out_shape=[shape(16, 16, SIDE), shape(6, SIDE, SIDE)],
            in_specs=[SMEM] + [VMEM] * 4,
            out_specs=[VMEM, VMEM],
            scratch_shapes=[pltpu.VMEM((16, SIDE), F32)],
            compiler_params=PARAMS,
        )(plan, source, own, wide, narrow)
        relay = lax.ppermute(relay, "core", [(0, 1), (1, 0)])
        parts = lax.all_to_all(parts, ("core", "cls"), 0, 0)
        out_shape = [own_shape] * (2 if first else 1)
        out_shape += [shape(8, 8, SIDE)] if last else swap_shapes
        results = pl.pallas_call(
            lambda *refs, first=first, last=last: spread_kernel(first, last, *refs),
            out_shape=out_shape,
            in_specs=[VMEM, SMEM] + [VMEM] * 5,
            out_specs=[VMEM] * len(out_shape),
            scratch_shapes=[
                pltpu.VMEM((16, 2 * SIDE, SIDE), jnp.bfloat16),
                pltpu.VMEM((32, SIDE, SIDE), F32),
            ],
            compiler_params=PARAMS,
        )(tiles, plan, mask if first else anchor, source, wide, relay, parts)
        if first:
            anchor, *results = results
        if last:
            source, parts = results
        else:
            source, wide, narrow, own = results
    parts = lax.all_to_all(parts, "cls", 0, 0)
    out = pl.pallas_call(
        last_kernel,
        out_shape=own_shape,
        in_specs=[VMEM, VMEM],
        out_specs=HBM,
        scratch_shapes=[pltpu.VMEM((8, SIDE, SIDE), F32), pltpu.SemaphoreType.DMA((8,))],
        compiler_params=PARAMS,
    )(source, parts)
    return out.reshape(8 * SIDE, SIDE)


def solution(mesh):
    split_mesh = Mesh(
        mesh.devices.reshape(mesh.shape["dom"] // 2, 2, mesh.shape["cls"]), ("chip", "core", "cls")
    )
    dom = ("chip", "core")
    return jax.shard_map(
        on_device,
        mesh=split_mesh,
        in_specs=(P(dom, None, None), P(dom), P(dom), P(dom, None, None), P(dom), P(dom, "cls")),
        out_specs=P(dom, "cls"),
        check_vma=False,
    )
```

time: 126 us -> 117 us (0.929)
  waiting for transfers between devices: 19.8 us -> 8.84 us
  starting transfers between devices: 46.8 us -> 48.6 us
    ppermute x9, waiting for transfers between devices: 19.8 us -> 8.84 us  [the longest x3 8.82 us: on_device(): narrow = lax.ppermute(narrow, dom, three_away)]
    ppermute x9, starting transfers between devices: 46.8 us -> 48.6 us  [the longest x3 29.3 us: on_device(): narrow = lax.ppermute(narrow, dom, three_away)]
    pallas_call x4 -> x5, Pallas kernels: 4.37 us -> 5.2 us  [the longest x1 1.92 us: on_device(): pl.pallas_call(first_kernel, out_shape=[own_shape] + swap_shapes, in_spec...]
  transfers between devices with their start and end apart: 9 -> 9, of which waited for: 5 -> 3; matrix products, arithmetic and copies ran while one was open for 0% -> 0% of each run, Pallas kernels for 0% -> 1%
where the time goes in v5:
time: 117 us
  starting transfers between devices  48.6 us (42%)
  blocking collectives  47.1 us (40%)
  Pallas kernels  12.3 us (11%)
  waiting for transfers between devices  8.84 us (8%)
    all_to_all x3, blocking collectives, on_device(): parts = lax.all_to_all(parts, ('core', 'cls'), 0, 0)  36.9 us
    ppermute x3, starting transfers between devices, on_device(): narrow = lax.ppermute(narrow, dom, three_away)  29.3 us
    ppermute x3, starting transfers between devices, on_device(): wide = lax.ppermute(wide, dom, adjacent)  12.5 us
    all_to_all x1, blocking collectives, on_device(): parts = lax.all_to_all(parts, 'cls', 0, 0)  10.2 us
    ppermute x3, waiting for transfers between devices, on_device(): narrow = lax.ppermute(narrow, dom, three_away)  8.82 us
    ppermute x3, starting transfers between devices, on_device(): relay = lax.ppermute(relay, 'core', [(0, 1), (1, 0)])  6.87 us
    pallas_call x3, Pallas kernels, on_device(): pl.pallas_call(lambda *refs, first=first, last=last: spread_kernel(first,...  5.98 us
  transfers between devices with their start and end apart: 9, of which 3 were waited for; matrix products, arithmetic and copies ran while one was open for 0% of the time, Pallas kernels for 1%

profile of v5, /device:TPU:1, one launch (start us, length us, event | category | flops | bytes accessed | tf_op | source)
XLA Modules:
  0.0 116.9 jit_solution(10527112234349917095)
XLA Ops:
  0.0 0.0 copy-start
  0.0 1.9 %shard_map.65 = (f32[8,128,128]{2,1,0:T(8,128)S(1)}, f32[520,128]{1,0:T(8,128)S(1)}, f32[264,128]{1,0:T(8,128)S(1)}, f32[8,128]{1,0:T(8,128)S(1)}) custom-call(f32[8,128,128]{2,1,0:T(8,128)} %bitcast.4, s32[1,2,4]{2,1,0:T(2,128)} %bitcast.5), custom_call_target="tpu_custom_call" | custom-call | flops 1048576 | bytes 1048576 | tf_op jit(solution)/shard_map/pallas_call | solution.py:232
  1.9 6.3 %collective-permute-start = (f32[520,128]{1,0:T(8,128)S(1)}, f32[520,128]{1,0:T(8,128)S(1)}, u32[]{:S(2)}, u32[]{:S(2)}) collective-permute-start(f32[520,128]{1,0:T(8,128)S(1)} %get-tuple-element.31), channel_id=1, source_target_pairs={{0,1016},{8,16},{16,8},{24,32},{32,24},{40,48},{48,40},{56,64},{64... | collective-permute-start | bytes 798728 | tf_op jit(solution)/shard_map/ppermute | solution.py:262
  8.2 16.4 %collective-permute-start.1 = (f32[264,128]{1,0:T(8,128)S(1)}, f32[264,128]{1,0:T(8,128)S(1)}, u32[]{:S(2)}, u32[]{:S(2)}) collective-permute-start(f32[264,128]{1,0:T(8,128)S(1)} %get-tuple-element.33), channel_id=1, source_target_pairs={{0,24},{8,1008},{16,40},{24,0},{32,56},{40,16},{48,72},{56,32},{64... | collective-permute-start | bytes 405512 | tf_op jit(solution)/shard_map/ppermute | solution.py:263
  24.6 1.5 %shard_map.64 = (s32[72]{0:T(128)S(1)}, s32[8,128]{1,0:T(8,128)S(1)}) custom-call(s32[32]{0:T(128)} %rows.1, s32[32]{0:T(128)} %cols.1, s32[1,2,4]{2,1,0:T(2,128)} %bitcast.6, s32[8,128]{1,0:T(8,128)} %bitcast.7), custom_call_target="tpu_custom_call" | custom-call | flops 1048576 | bytes 1048576 | tf_op jit(solution)/shard_map/pallas_call | solution.py:241
  26.2 1.8 %collective-permute-done.1.narrow = f32[264,128]{1,0:T(8,128)S(1)} collective-permute-done((f32[264,128]{1,0:T(8,128)S(1)}, f32[264,128]{1,0:T(8,128)S(1)}, u32[]{:S(2)}, u32[]{:S(2)}) %collective-permute-start.1) | collective-permute-done | bytes 135200 | tf_op jit(solution)/shard_map/ppermute | solution.py:263
  27.9 0.0 collective-permute-done.wide.refs_4_
  27.9 0.6 shard_map.66
  28.5 2.8 %collective-permute-start.2 = (f32[6,128,128]{2,1,0:T(8,128)S(1)}, f32[6,128,128]{2,1,0:T(8,128)S(1)}, u32[]{:S(2)}, u32[]{:S(2)}) collective-permute-start(f32[6,128,128]{2,1,0:T(8,128)S(1)} %get-tuple-element.34), channel_id=1, source_target_pairs={{0,8},{8,0},{1,9},{9,1},{2,10},{10,2},{3,11},{11,3},{4,12},{12,4},... | collective-permute-start | bytes 1179656 | tf_op jit(solution)/shard_map/ppermute | solution.py:272
  31.3 14.8 %all_to_all.20.refs_6_ = f32[16,16,128]{2,1,0:T(8,128)S(1)} all-to-all(f32[16,16,128]{2,1,0:T(8,128)S(1)} %get-tuple-element.35), channel_id=1, replica_groups=mesh['chip'=64,'core'=2,'cls'=8] {'core','cls'}, dimensions={0} | all-to-all | bytes 262144 | tf_op jit(solution)/shard_map/all_to_all | solution.py:273
  46.1 0.0 collective-permute-done.2.refs_5_
  46.1 0.0 copy-done
  46.1 2.0 %shard_map.67 = (f32[8,128,128]{2,1,0:T(8,128)S(1)}, f32[8,128,128]{2,1,0:T(8,128)S(1)}, f32[520,128]{1,0:T(8,128)S(1)}, f32[264,128]{1,0:T(8,128)S(1)}, f32[8,128]{1,0:T(8,128)S(1)}) custom-call(bf16[32,128,128]{2,1,0:T(8,128)(2,1)S(1)} %copy-done, s32[72]{0:T(128)S(1)} %get-tuple-element.28.plan.refs_1_, s32[8,128]{1,0:T(8,128)S(1)} %get-tuple-element.29.refs_2_, ...), custom_call_target="tpu_custom_call" | custom-call | tf_op jit(solution)/shard_map/pallas_call | solution.py:276
  48.1 3.1 %collective-permute-start.3 = (f32[520,128]{1,0:T(8,128)S(1)}, f32[520,128]{1,0:T(8,128)S(1)}, u32[]{:S(2)}, u32[]{:S(2)}) collective-permute-start(f32[520,128]{1,0:T(8,128)S(1)} %get-tuple-element.38), channel_id=1, source_target_pairs={{0,1016},{8,16},{16,8},{24,32},{32,24},{40,48},{48,40},{56,64},{64... | collective-permute-start | bytes 798728 | tf_op jit(solution)/shard_map/ppermute | solution.py:262
  51.2 6.5 %collective-permute-start.4 = (f32[264,128]{1,0:T(8,128)S(1)}, f32[264,128]{1,0:T(8,128)S(1)}, u32[]{:S(2)}, u32[]{:S(2)}) collective-permute-start(f32[264,128]{1,0:T(8,128)S(1)} %get-tuple-element.40), channel_id=1, source_target_pairs={{0,24},{8,1008},{16,40},{24,0},{32,56},{40,16},{48,72},{56,32},{64... | collective-permute-start | bytes 405512 | tf_op jit(solution)/shard_map/ppermute | solution.py:263
  57.7 3.5 %collective-permute-done.4.narrow = f32[264,128]{1,0:T(8,128)S(1)} collective-permute-done((f32[264,128]{1,0:T(8,128)S(1)}, f32[264,128]{1,0:T(8,128)S(1)}, u32[]{:S(2)}, u32[]{:S(2)}) %collective-permute-start.4) | collective-permute-done | bytes 135200 | tf_op jit(solution)/shard_map/ppermute | solution.py:263
  61.2 0.0 collective-permute-done.3.wide.refs_4_
  61.2 0.6 shard_map.68
  61.8 2.0 %collective-permute-start.5 = (f32[6,128,128]{2,1,0:T(8,128)S(1)}, f32[6,128,128]{2,1,0:T(8,128)S(1)}, u32[]{:S(2)}, u32[]{:S(2)}) collective-permute-start(f32[6,128,128]{2,1,0:T(8,128)S(1)} %get-tuple-element.41), channel_id=1, source_target_pairs={{0,8},{8,0},{1,9},{9,1},{2,10},{10,2},{3,11},{11,3},{4,12},{12,4},... | collective-permute-start | bytes 1179656 | tf_op jit(solution)/shard_map/ppermute | solution.py:272
  63.8 11.0 %all_to_all.21.refs_6_ = f32[16,16,128]{2,1,0:T(8,128)S(1)} all-to-all(f32[16,16,128]{2,1,0:T(8,128)S(1)} %get-tuple-element.42), channel_id=1, replica_groups=mesh['chip'=64,'core'=2,'cls'=8] {'core','cls'}, dimensions={0} | all-to-all | bytes 262144 | tf_op jit(solution)/shard_map/all_to_all | solution.py:273
  74.9 0.0 collective-permute-done.5.refs_5_
  74.9 2.0 %shard_map.69 = (f32[8,128,128]{2,1,0:T(8,128)S(1)}, f32[520,128]{1,0:T(8,128)S(1)}, f32[264,128]{1,0:T(8,128)S(1)}, f32[8,128]{1,0:T(8,128)S(1)}) custom-call(bf16[32,128,128]{2,1,0:T(8,128)(2,1)S(1)} %copy-done, s32[72]{0:T(128)S(1)} %get-tuple-element.28.plan.refs_1_, f32[8,128,128]{2,1,0:T(8,128)S(1)} %get-tuple-element.36.refs_2_, ...), custom_call_target="tpu_custom_call" | custom-call | tf_op jit(solution)/shard_map/pallas_call | solution.py:276
  76.9 3.1 %collective-permute-start.6 = (f32[520,128]{1,0:T(8,128)S(1)}, f32[520,128]{1,0:T(8,128)S(1)}, u32[]{:S(2)}, u32[]{:S(2)}) collective-permute-start(f32[520,128]{1,0:T(8,128)S(1)} %get-tuple-element.44), channel_id=1, source_target_pairs={{0,1016},{8,16},{16,8},{24,32},{32,24},{40,48},{48,40},{56,64},{64... | collective-permute-start | bytes 798728 | tf_op jit(solution)/shard_map/ppermute | solution.py:262
  80.0 6.5 %collective-permute-start.7 = (f32[264,128]{1,0:T(8,128)S(1)}, f32[264,128]{1,0:T(8,128)S(1)}, u32[]{:S(2)}, u32[]{:S(2)}) collective-permute-start(f32[264,128]{1,0:T(8,128)S(1)} %get-tuple-element.46), channel_id=1, source_target_pairs={{0,24},{8,1008},{16,40},{24,0},{32,56},{40,16},{48,72},{56,32},{64... | collective-permute-start | bytes 405512 | tf_op jit(solution)/shard_map/ppermute | solution.py:263
  86.4 3.5 %collective-permute-done.7.narrow = f32[264,128]{1,0:T(8,128)S(1)} collective-permute-done((f32[264,128]{1,0:T(8,128)S(1)}, f32[264,128]{1,0:T(8,128)S(1)}, u32[]{:S(2)}, u32[]{:S(2)}) %collective-permute-start.7) | collective-permute-done | bytes 135200 | tf_op jit(solution)/shard_map/ppermute | solution.py:263
  90.0 0.0 collective-permute-done.6.wide.refs_4_
  90.0 0.6 shard_map.70
  90.6 2.0 %collective-permute-start.8 = (f32[6,128,128]{2,1,0:T(8,128)S(1)}, f32[6,128,128]{2,1,0:T(8,128)S(1)}, u32[]{:S(2)}, u32[]{:S(2)}) collective-permute-start(f32[6,128,128]{2,1,0:T(8,128)S(1)} %get-tuple-element.47), channel_id=1, source_target_pairs={{0,8},{8,0},{1,9},{9,1},{2,10},{10,2},{3,11},{11,3},{4,12},{12,4},... | collective-permute-start | bytes 1179656 | tf_op jit(solution)/shard_map/ppermute | solution.py:272
  92.6 11.0 %all_to_all.22.refs_6_ = f32[16,16,128]{2,1,0:T(8,128)S(1)} all-to-all(f32[16,16,128]{2,1,0:T(8,128)S(1)} %get-tuple-element.48), channel_id=1, replica_groups=mesh['chip'=64,'core'=2,'cls'=8] {'core','cls'}, dimensions={0} | all-to-all | bytes 262144 | tf_op jit(solution)/shard_map/all_to_all | solution.py:273
  103.6 0.0 collective-permute-done.8.refs_5_
  103.6 2.0 %shard_map.71 = (f32[8,128,128]{2,1,0:T(8,128)S(1)}, f32[8,8,128]{2,1,0:T(8,128)S(1)}) custom-call(bf16[32,128,128]{2,1,0:T(8,128)(2,1)S(1)} %copy-done, s32[72]{0:T(128)S(1)} %get-tuple-element.28.plan.refs_1_, f32[8,128,128]{2,1,0:T(8,128)S(1)} %get-tuple-element.36.refs_2_, f32[8,128,128]{2,1,0:T(8,128)S(1)} %get-tuple-element.43.source.refs_3_, ...), custom_call_target="tpu_custom_call" | custom-call | tf_op jit(solution)/shard_map/pallas_call | solution.py:276
  105.6 10.2 %all_to_all.23.parts = f32[8,8,128]{2,1,0:T(8,128)S(1)} all-to-all(f32[8,8,128]{2,1,0:T(8,128)S(1)} %get-tuple-element.50), channel_id=1, replica_groups=mesh['chip'=64,'core'=2,'cls'=8] {'cls'}, dimensions={0} | all-to-all | bytes 65536 | tf_op jit(solution)/shard_map/all_to_all | solution.py:293
  115.8 1.1 shard_map.72
Async XLA Ops:
  0.0 46.1 %copy-start = (bf16[32,128,128]{2,1,0:T(8,128)(2,1)S(1)}, bf16[32,128,128]{2,1,0:T(8,128)(2,1)}, u32[]{:S(2)}) copy-start(bf16[32,128,128]{2,1,0:T(8,128)(2,1)} %refs_0_.5) | copy-start | bytes 3145732
  1.9 26.0 %collective-permute-start = (f32[520,128]{1,0:T(8,128)S(1)}, f32[520,128]{1,0:T(8,128)S(1)}, u32[]{:S(2)}, u32[]{:S(2)}) collective-permute-start(f32[520,128]{1,0:T(8,128)S(1)} %get-tuple-element.31), channel_id=1, source_target_pairs={{0,1016},{8,16},{16,8},{24,32},{32,24},{40,48},{48,40},{56,64},{64... | collective-permute-start | bytes 798728 | tf_op jit(solution)/shard_map/ppermute | solution.py:262
  8.2 19.7 %collective-permute-start.1 = (f32[264,128]{1,0:T(8,128)S(1)}, f32[264,128]{1,0:T(8,128)S(1)}, u32[]{:S(2)}, u32[]{:S(2)}) collective-permute-start(f32[264,128]{1,0:T(8,128)S(1)} %get-tuple-element.33), channel_id=1, source_target_pairs={{0,24},{8,1008},{16,40},{24,0},{32,56},{40,16},{48,72},{56,32},{64... | collective-permute-start | bytes 405512 | tf_op jit(solution)/shard_map/ppermute | solution.py:263
  28.5 17.6 %collective-permute-start.2 = (f32[6,128,128]{2,1,0:T(8,128)S(1)}, f32[6,128,128]{2,1,0:T(8,128)S(1)}, u32[]{:S(2)}, u32[]{:S(2)}) collective-permute-start(f32[6,128,128]{2,1,0:T(8,128)S(1)} %get-tuple-element.34), channel_id=1, source_target_pairs={{0,8},{8,0},{1,9},{9,1},{2,10},{10,2},{3,11},{11,3},{4,12},{12,4},... | collective-permute-start | bytes 1179656 | tf_op jit(solution)/shard_map/ppermute | solution.py:272
  48.1 13.1 %collective-permute-start.3 = (f32[520,128]{1,0:T(8,128)S(1)}, f32[520,128]{1,0:T(8,128)S(1)}, u32[]{:S(2)}, u32[]{:S(2)}) collective-permute-start(f32[520,128]{1,0:T(8,128)S(1)} %get-tuple-element.38), channel_id=1, source_target_pairs={{0,1016},{8,16},{16,8},{24,32},{32,24},{40,48},{48,40},{56,64},{64... | collective-permute-start | bytes 798728 | tf_op jit(solution)/shard_map/ppermute | solution.py:262
  51.2 10.0 %collective-permute-start.4 = (f32[264,128]{1,0:T(8,128)S(1)}, f32[264,128]{1,0:T(8,128)S(1)}, u32[]{:S(2)}, u32[]{:S(2)}) collective-permute-start(f32[264,128]{1,0:T(8,128)S(1)} %get-tuple-element.40), channel_id=1, source_target_pairs={{0,24},{8,1008},{16,40},{24,0},{32,56},{40,16},{48,72},{56,32},{64... | collective-permute-start | bytes 405512 | tf_op jit(solution)/shard_map/ppermute | solution.py:263
  61.8 13.1 %collective-permute-start.5 = (f32[6,128,128]{2,1,0:T(8,128)S(1)}, f32[6,128,128]{2,1,0:T(8,128)S(1)}, u32[]{:S(2)}, u32[]{:S(2)}) collective-permute-start(f32[6,128,128]{2,1,0:T(8,128)S(1)} %get-tuple-element.41), channel_id=1, source_target_pairs={{0,8},{8,0},{1,9},{9,1},{2,10},{10,2},{3,11},{11,3},{4,12},{12,4},... | collective-permute-start | bytes 1179656 | tf_op jit(solution)/shard_map/ppermute | solution.py:272
  76.9 13.1 %collective-permute-start.6 = (f32[520,128]{1,0:T(8,128)S(1)}, f32[520,128]{1,0:T(8,128)S(1)}, u32[]{:S(2)}, u32[]{:S(2)}) collective-permute-start(f32[520,128]{1,0:T(8,128)S(1)} %get-tuple-element.44), channel_id=1, source_target_pairs={{0,1016},{8,16},{16,8},{24,32},{32,24},{40,48},{48,40},{56,64},{64... | collective-permute-start | bytes 798728 | tf_op jit(solution)/shard_map/ppermute | solution.py:262
  80.0 10.0 %collective-permute-start.7 = (f32[264,128]{1,0:T(8,128)S(1)}, f32[264,128]{1,0:T(8,128)S(1)}, u32[]{:S(2)}, u32[]{:S(2)}) collective-permute-start(f32[264,128]{1,0:T(8,128)S(1)} %get-tuple-element.46), channel_id=1, source_target_pairs={{0,24},{8,1008},{16,40},{24,0},{32,56},{40,16},{48,72},{56,32},{64... | collective-permute-start | bytes 405512 | tf_op jit(solution)/shard_map/ppermute | solution.py:263
  90.6 13.1 %collective-permute-start.8 = (f32[6,128,128]{2,1,0:T(8,128)S(1)}, f32[6,128,128]{2,1,0:T(8,128)S(1)}, u32[]{:S(2)}, u32[]{:S(2)}) collective-permute-start(f32[6,128,128]{2,1,0:T(8,128)S(1)} %get-tuple-element.47), channel_id=1, source_target_pairs={{0,8},{8,0},{1,9},{9,1},{2,10},{10,2},{3,11},{11,3},{4,12},{12,4},... | collective-permute-start | bytes 1179656 | tf_op jit(solution)/shard_map/ppermute | solution.py:272

commit v6 on v5

--- a/solution.py
+++ b/solution.py
@@ -59,8 +59,14 @@
     return ref[SIDE * place : SIDE * (place + 1), :]
 
 
-def fill_swaps(source, sums, block_of, wide, narrow):
+def fill_swaps(source, sums, block_of, wide, narrow, near, rows):
     core = lax.axis_index("core")
+    rows[0:8, :] = sums
+    rows[8:16, :] = jnp.zeros((8, SIDE), F32)
+    for within in range(2):
+        block = block_of(2 * core, within)
+        near[within] = source[block]
+        rows[10 + within : 11 + within, :] = rows[pl.ds(block, 1), :]
     for out, offsets in ((wide, (2 - 2 * core, 3 - 2 * core)), (narrow, (1 + 2 * core,))):
         count = 2 * len(offsets)
         out[count * SIDE + count :, :] = jnp.zeros((8 - count, SIDE), F32)
@@ -69,7 +75,7 @@
                 place = 2 * part + within
                 block = block_of(offset, within)
                 out[SIDE * place : SIDE * (place + 1), :] = source[block]
-                out[count * SIDE + place : count * SIDE + place + 1, :] = sums[pl.ds(block, 1), :]
+                out[count * SIDE + place : count * SIDE + place + 1, :] = rows[pl.ds(block, 1), :]
 
 
 def lane_sums(block):
@@ -85,14 +91,16 @@
     return copies
 
 
-def first_kernel(labels, send, kept, wide, narrow, own, send_here, sems):
+def first_kernel(labels, send, kept, wide, narrow, near, rows, send_here, sems):
     pairs = [(labels.at[block], kept.at[block]) for block in range(8)]
     copies = copy_all([(send, send_here)] + pairs, sems)
+    sums = []
     for block in range(8):
         copies[1 + block].wait()
-        own[block : block + 1, :] = lane_sums(kept[block])
+        sums.append(lane_sums(kept[block]))
     copies[0].wait()
-    fill_swaps(kept, own, lambda offset, within: send_here[0, within, offset], wide, narrow)
+    block_of = lambda offset, within: send_here[0, within, offset]
+    fill_swaps(kept, jnp.concatenate(sums, axis=0), block_of, wide, narrow, near, rows)
 
 
 def plan_kernel(rows, cols, send, mask, plan, mask_kept, rows_here, cols_here, send_here, sems):
@@ -103,16 +111,13 @@
         plan[place] = entry
 
 
-def mass_kernel(plan, source, own, wide, narrow, parts, relay, rows):
-    core = lax.axis_index("core")
-    rows[0:8, :] = own[...]
+def mass_kernel(sums, near, wide, narrow, plan, parts, relay, rows):
+    rows[...] = sums[...]
     rows[8:10, :] = wide[4 * SIDE : 4 * SIDE + 2, :]
     rows[12:14, :] = wide[4 * SIDE + 2 : 4 * SIDE + 4, :]
     rows[14:16, :] = narrow[2 * SIDE : 2 * SIDE + 2, :]
     for within in range(2):
-        block = sent_block(plan, 2 * core, within)
-        rows[10 + within : 11 + within, :] = own[pl.ds(block, 1), :]
-        relay[within] = source[block]
+        relay[within] = near[within]
         relay[2 + within] = block_at(wide, 2 + within)
         relay[4 + within] = block_at(narrow, within)
     partial = rows[...]
@@ -146,9 +151,12 @@
     anchor = refs.pop(0) if first else mask
     squared = refs.pop(0)
     if last:
-        own_parts, operand, products = refs
+        own_parts, *refs = refs
     else:
-        wide_out, narrow_out, own, operand, products = refs
+        wide_out, narrow_out, near_out, rows_out, *refs = refs
+    operand, products, plan_here, plan_sem = refs
+    plan_copy = pltpu.make_async_copy(plan, plan_here, plan_sem)
+    plan_copy.start()
     core = lax.axis_index("core")
     mine = total_of(parts, core)
     mate = total_of(parts, 1 - core)
@@ -171,6 +179,8 @@
         high, low = split(value)
         operand[block, :SIDE, :] = high
         operand[block, SIDE:, :] = low
+    plan_copy.wait()
+    plan = plan_here
     for tile in range(32):
         weights = tiles[tile]
         products[tile] = jnp.dot(
@@ -193,9 +203,8 @@
         for share in range(8):
             own_parts[share] = sums
     else:
-        own[...] = sums
         block_of = functools.partial(sent_block, plan)
-        fill_swaps(squared, own, block_of, wide_out, narrow_out)
+        fill_swaps(squared, sums, block_of, wide_out, narrow_out, near_out, rows_out)
 
 
 def last_kernel(squared, parts, out, scaled, sems):
@@ -217,7 +226,12 @@
     three_away = [(i, (i + (-3 if i % 2 else 3)) % count) for i in range(count)]
     send_lists = jnp.transpose(send_lists, (0, 2, 1))
     own_shape = shape(8, SIDE, SIDE)
-    swap_shapes = [shape(4 * SIDE + 8, SIDE), shape(2 * SIDE + 8, SIDE), shape(8, SIDE)]
+    sent_shapes = [
+        shape(4 * SIDE + 8, SIDE),
+        shape(2 * SIDE + 8, SIDE),
+        shape(2, SIDE, SIDE),
+        shape(16, SIDE),
+    ]
     blocks, tile_rows, tile_cols, send_lists, mask = [
         pltpu.with_memory_space_constraint(value, pltpu.HBM)
         for value in (
@@ -229,11 +243,11 @@
         )
     ]
     send_scratch = pltpu.SMEM((1, 2, 4), jnp.int32)
-    source, wide, narrow, own = pl.pallas_call(
+    source, wide, narrow, near, rows = pl.pallas_call(
         first_kernel,
-        out_shape=[own_shape] + swap_shapes,
+        out_shape=[own_shape] + sent_shapes,
         in_specs=[HBM] * 2,
-        out_specs=[VMEM] * 4,
+        out_specs=[VMEM] * 5,
         scratch_shapes=[send_scratch, pltpu.SemaphoreType.DMA((9,))],
         compiler_params=PARAMS,
         cost_estimate=pl.CostEstimate(flops=1 << 20, bytes_accessed=1 << 20, transcendentals=0),
@@ -264,23 +278,25 @@
         parts, relay = pl.pallas_call(
             mass_kernel,
             out_shape=[shape(16, 16, SIDE), shape(6, SIDE, SIDE)],
-            in_specs=[SMEM] + [VMEM] * 4,
+            in_specs=[VMEM] * 5,
             out_specs=[VMEM, VMEM],
             scratch_shapes=[pltpu.VMEM((16, SIDE), F32)],
             compiler_params=PARAMS,
-        )(plan, source, own, wide, narrow)
+        )(rows, near, wide, narrow, plan)
         relay = lax.ppermute(relay, "core", [(0, 1), (1, 0)])
         parts = lax.all_to_all(parts, ("core", "cls"), 0, 0)
         out_shape = [own_shape] * (2 if first else 1)
-        out_shape += [shape(8, 8, SIDE)] if last else swap_shapes
+        out_shape += [shape(8, 8, SIDE)] if last else sent_shapes
         results = pl.pallas_call(
             lambda *refs, first=first, last=last: spread_kernel(first, last, *refs),
             out_shape=out_shape,
-            in_specs=[VMEM, SMEM] + [VMEM] * 5,
+            in_specs=[VMEM] * 7,
             out_specs=[VMEM] * len(out_shape),
             scratch_shapes=[
                 pltpu.VMEM((16, 2 * SIDE, SIDE), jnp.bfloat16),
                 pltpu.VMEM((32, SIDE, SIDE), F32),
+                pltpu.SMEM((72,), jnp.int32),
+                pltpu.SemaphoreType.DMA,
             ],
             compiler_params=PARAMS,
         )(tiles, plan, mask if first else anchor, source, wide, relay, parts)
@@ -289,7 +305,7 @@
         if last:
             source, parts = results
         else:
-            source, wide, narrow, own = results
+            source, wide, narrow, near, rows = results
     parts = lax.all_to_all(parts, "cls", 0, 0)
     out = pl.pallas_call(
         last_kernel,

time: 117 us -> 115 us (0.983)
  Pallas kernels: 12.3 us -> 10.1 us
    pallas_call x3, Pallas kernels: 1.74 us -> 0.11 us  [on_device(): pl.pallas_call(mass_kernel, out_shape=[shape(16, 16, SIDE), shape(6, SIDE...]
where the time goes in v6:
time: 115 us
  starting transfers between devices  48.6 us (42%)
  blocking collectives  47.1 us (41%)
  Pallas kernels  10.1 us (9%)
  waiting for transfers between devices  8.84 us (8%)
    all_to_all x3, blocking collectives, on_device(): parts = lax.all_to_all(parts, ('core', 'cls'), 0, 0)  36.9 us
    ppermute x3, starting transfers between devices, on_device(): narrow = lax.ppermute(narrow, dom, three_away)  29.3 us
    ppermute x3, starting transfers between devices, on_device(): wide = lax.ppermute(wide, dom, adjacent)  12.5 us
    all_to_all x1, blocking collectives, on_device(): parts = lax.all_to_all(parts, 'cls', 0, 0)  10.2 us
    ppermute x3, waiting for transfers between devices, on_device(): narrow = lax.ppermute(narrow, dom, three_away)  8.82 us
    ppermute x3, starting transfers between devices, on_device(): relay = lax.ppermute(relay, 'core', [(0, 1), (1, 0)])  6.87 us
    pallas_call x3, Pallas kernels, on_device(): pl.pallas_call(lambda *refs, first=first, last=last: spread_kernel(first,...  5.41 us
  transfers between devices with their start and end apart: 9, of which 3 were waited for; matrix products, arithmetic and copies ran while one was open for 0% of the time, Pallas kernels for 1%

profile of v6, /device:TPU:1, one launch (start us, length us, event | category | flops | bytes accessed | tf_op | source)
XLA Modules:
  0.0 114.7 jit_solution(1319723026705837116)
XLA Ops:
  0.0 0.0 copy-start
  0.0 1.9 %shard_map.65 = (f32[8,128,128]{2,1,0:T(8,128)S(1)}, f32[520,128]{1,0:T(8,128)S(1)}, f32[264,128]{1,0:T(8,128)S(1)}, f32[2,128,128]{2,1,0:T(8,128)S(1)}, f32[16,128]{1,0:T(8,128)S(1)}) custom-call(f32[8,128,128]{2,1,0:T(8,128)} %bitcast.4, s32[1,2,4]{2,1,0:T(2,128)} %bitcast.5), custom_call_target="tpu_custom_call" | custom-call | flops 1048576 | bytes 1048576 | tf_op jit(solution)/shard_map/pallas_call | solution.py:246
  1.9 6.3 %collective-permute-start = (f32[520,128]{1,0:T(8,128)S(1)}, f32[520,128]{1,0:T(8,128)S(1)}, u32[]{:S(2)}, u32[]{:S(2)}) collective-permute-start(f32[520,128]{1,0:T(8,128)S(1)} %get-tuple-element.34), channel_id=1, source_target_pairs={{0,1016},{8,16},{16,8},{24,32},{32,24},{40,48},{48,40},{56,64},{64... | collective-permute-start | bytes 798728 | tf_op jit(solution)/shard_map/ppermute | solution.py:276
  8.2 16.4 %collective-permute-start.1 = (f32[264,128]{1,0:T(8,128)S(1)}, f32[264,128]{1,0:T(8,128)S(1)}, u32[]{:S(2)}, u32[]{:S(2)}) collective-permute-start(f32[264,128]{1,0:T(8,128)S(1)} %get-tuple-element.37), channel_id=1, source_target_pairs={{0,24},{8,1008},{16,40},{24,0},{32,56},{40,16},{48,72},{56,32},{64... | collective-permute-start | bytes 405512 | tf_op jit(solution)/shard_map/ppermute | solution.py:277
  24.6 1.5 %shard_map.64 = (s32[72]{0:T(128)S(1)}, s32[8,128]{1,0:T(8,128)S(1)}) custom-call(s32[32]{0:T(128)} %rows.1, s32[32]{0:T(128)} %cols.1, s32[1,2,4]{2,1,0:T(2,128)} %bitcast.6, s32[8,128]{1,0:T(8,128)} %bitcast.7), custom_call_target="tpu_custom_call" | custom-call | flops 1048576 | bytes 1048576 | tf_op jit(solution)/shard_map/pallas_call | solution.py:255
  26.2 1.8 %collective-permute-done.1.narrow = f32[264,128]{1,0:T(8,128)S(1)} collective-permute-done((f32[264,128]{1,0:T(8,128)S(1)}, f32[264,128]{1,0:T(8,128)S(1)}, u32[]{:S(2)}, u32[]{:S(2)}) %collective-permute-start.1) | collective-permute-done | bytes 135200 | tf_op jit(solution)/shard_map/ppermute | solution.py:277
  27.9 0.0 collective-permute-done.wide.refs_4_
  27.9 2.8 %collective-permute-start.2 = (f32[6,128,128]{2,1,0:T(8,128)S(1)}, f32[6,128,128]{2,1,0:T(8,128)S(1)}, u32[]{:S(2)}, u32[]{:S(2)}) collective-permute-start(f32[6,128,128]{2,1,0:T(8,128)S(1)} %get-tuple-element.38), channel_id=1, source_target_pairs={{0,8},{8,0},{1,9},{9,1},{2,10},{10,2},{3,11},{11,3},{4,12},{12,4},... | collective-permute-start | bytes 1179656 | tf_op jit(solution)/shard_map/ppermute | solution.py:286
  30.8 14.8 %all_to_all.20.refs_6_ = f32[16,16,128]{2,1,0:T(8,128)S(1)} all-to-all(f32[16,16,128]{2,1,0:T(8,128)S(1)} %get-tuple-element.39), channel_id=1, replica_groups=mesh['chip'=64,'core'=2,'cls'=8] {'core','cls'}, dimensions={0} | all-to-all | bytes 262144 | tf_op jit(solution)/shard_map/all_to_all | solution.py:287
  45.6 0.0 collective-permute-done.2.refs_5_
  45.6 0.0 copy-done
  45.6 2.0 %shard_map.67 = (f32[8,128,128]{2,1,0:T(8,128)S(1)}, f32[8,128,128]{2,1,0:T(8,128)S(1)}, f32[520,128]{1,0:T(8,128)S(1)}, f32[264,128]{1,0:T(8,128)S(1)}, f32[2,1...) custom-call(bf16[32,128,128]{2,1,0:T(8,128)(2,1)S(1)} %copy-done, s32[72]{0:T(128)S(1)} %get-tuple-element.31.plan.refs_1_, ...), custom_call_target="tpu_custom_call" | custom-call | tf_op jit(solution)/shard_map/pallas_call | solution.py:290
  47.6 3.1 %collective-permute-start.3 = (f32[520,128]{1,0:T(8,128)S(1)}, f32[520,128]{1,0:T(8,128)S(1)}, u32[]{:S(2)}, u32[]{:S(2)}) collective-permute-start(f32[520,128]{1,0:T(8,128)S(1)} %get-tuple-element.42), channel_id=1, source_target_pairs={{0,1016},{8,16},{16,8},{24,32},{32,24},{40,48},{48,40},{56,64},{64... | collective-permute-start | bytes 798728 | tf_op jit(solution)/shard_map/ppermute | solution.py:276
  50.7 6.5 %collective-permute-start.4 = (f32[264,128]{1,0:T(8,128)S(1)}, f32[264,128]{1,0:T(8,128)S(1)}, u32[]{:S(2)}, u32[]{:S(2)}) collective-permute-start(f32[264,128]{1,0:T(8,128)S(1)} %get-tuple-element.45), channel_id=1, source_target_pairs={{0,24},{8,1008},{16,40},{24,0},{32,56},{40,16},{48,72},{56,32},{64... | collective-permute-start | bytes 405512 | tf_op jit(solution)/shard_map/ppermute | solution.py:277
  57.2 3.5 %collective-permute-done.4.narrow = f32[264,128]{1,0:T(8,128)S(1)} collective-permute-done((f32[264,128]{1,0:T(8,128)S(1)}, f32[264,128]{1,0:T(8,128)S(1)}, u32[]{:S(2)}, u32[]{:S(2)}) %collective-permute-start.4) | collective-permute-done | bytes 135200 | tf_op jit(solution)/shard_map/ppermute | solution.py:277
  60.7 0.0 collective-permute-done.3.wide.refs_4_
  60.8 2.0 %collective-permute-start.5 = (f32[6,128,128]{2,1,0:T(8,128)S(1)}, f32[6,128,128]{2,1,0:T(8,128)S(1)}, u32[]{:S(2)}, u32[]{:S(2)}) collective-permute-start(f32[6,128,128]{2,1,0:T(8,128)S(1)} %get-tuple-element.46), channel_id=1, source_target_pairs={{0,8},{8,0},{1,9},{9,1},{2,10},{10,2},{3,11},{11,3},{4,12},{12,4},... | collective-permute-start | bytes 1179656 | tf_op jit(solution)/shard_map/ppermute | solution.py:286
  62.8 11.0 %all_to_all.21.refs_6_ = f32[16,16,128]{2,1,0:T(8,128)S(1)} all-to-all(f32[16,16,128]{2,1,0:T(8,128)S(1)} %get-tuple-element.47), channel_id=1, replica_groups=mesh['chip'=64,'core'=2,'cls'=8] {'core','cls'}, dimensions={0} | all-to-all | bytes 262144 | tf_op jit(solution)/shard_map/all_to_all | solution.py:287
  73.8 0.0 collective-permute-done.5.refs_5_
  73.8 1.9 %shard_map.69 = (f32[8,128,128]{2,1,0:T(8,128)S(1)}, f32[520,128]{1,0:T(8,128)S(1)}, f32[264,128]{1,0:T(8,128)S(1)}, f32[2,128,128]{2,1,0:T(8,128)S(1)}, f32[16,128]{1,0:T(8,128)S(1)}) custom-call(bf16[32,128,128]{2,1,0:T(8,128)(2,1)S(1)} %copy-done, s32[72]{0:T(128)S(1)} %get-tuple-element.31.plan.refs_1_, f32[8,128,128]{2,1,0:T(8,128)S(1)} %get-tuple-element.40.refs_2_, ...), custom_call_target="tpu_custom_call" | custom-call | tf_op jit(solution)/shard_map/pallas_call | solution.py:290
  75.7 3.1 %collective-permute-start.6 = (f32[520,128]{1,0:T(8,128)S(1)}, f32[520,128]{1,0:T(8,128)S(1)}, u32[]{:S(2)}, u32[]{:S(2)}) collective-permute-start(f32[520,128]{1,0:T(8,128)S(1)} %get-tuple-element.49), channel_id=1, source_target_pairs={{0,1016},{8,16},{16,8},{24,32},{32,24},{40,48},{48,40},{56,64},{64... | collective-permute-start | bytes 798728 | tf_op jit(solution)/shard_map/ppermute | solution.py:276
  78.8 6.5 %collective-permute-start.7 = (f32[264,128]{1,0:T(8,128)S(1)}, f32[264,128]{1,0:T(8,128)S(1)}, u32[]{:S(2)}, u32[]{:S(2)}) collective-permute-start(f32[264,128]{1,0:T(8,128)S(1)} %get-tuple-element.52), channel_id=1, source_target_pairs={{0,24},{8,1008},{16,40},{24,0},{32,56},{40,16},{48,72},{56,32},{64... | collective-permute-start | bytes 405512 | tf_op jit(solution)/shard_map/ppermute | solution.py:277
  85.3 3.5 %collective-permute-done.7.narrow = f32[264,128]{1,0:T(8,128)S(1)} collective-permute-done((f32[264,128]{1,0:T(8,128)S(1)}, f32[264,128]{1,0:T(8,128)S(1)}, u32[]{:S(2)}, u32[]{:S(2)}) %collective-permute-start.7) | collective-permute-done | bytes 135200 | tf_op jit(solution)/shard_map/ppermute | solution.py:277
  88.8 0.0 collective-permute-done.6.wide.refs_4_
  88.8 2.0 %collective-permute-start.8 = (f32[6,128,128]{2,1,0:T(8,128)S(1)}, f32[6,128,128]{2,1,0:T(8,128)S(1)}, u32[]{:S(2)}, u32[]{:S(2)}) collective-permute-start(f32[6,128,128]{2,1,0:T(8,128)S(1)} %get-tuple-element.53), channel_id=1, source_target_pairs={{0,8},{8,0},{1,9},{9,1},{2,10},{10,2},{3,11},{11,3},{4,12},{12,4},... | collective-permute-start | bytes 1179656 | tf_op jit(solution)/shard_map/ppermute | solution.py:286
  90.9 11.0 %all_to_all.22.refs_6_ = f32[16,16,128]{2,1,0:T(8,128)S(1)} all-to-all(f32[16,16,128]{2,1,0:T(8,128)S(1)} %get-tuple-element.54), channel_id=1, replica_groups=mesh['chip'=64,'core'=2,'cls'=8] {'core','cls'}, dimensions={0} | all-to-all | bytes 262144 | tf_op jit(solution)/shard_map/all_to_all | solution.py:287
  101.9 0.0 collective-permute-done.8.refs_5_
  101.9 1.5 %shard_map.71 = (f32[8,128,128]{2,1,0:T(8,128)S(1)}, f32[8,8,128]{2,1,0:T(8,128)S(1)}) custom-call(bf16[32,128,128]{2,1,0:T(8,128)(2,1)S(1)} %copy-done, s32[72]{0:T(128)S(1)} %get-tuple-element.31.plan.refs_1_, f32[8,128,128]{2,1,0:T(8,128)S(1)} %get-tuple-element.40.refs_2_, f32[8,128,128]{2,1,0:T(8,128)S(1)} %get-tuple-element.48.refs_3_, ...), custom_call_target="tpu_custom_call" | custom-call | tf_op jit(solution)/shard_map/pallas_call | solution.py:290
  103.4 10.2 %all_to_all.23.parts = f32[8,8,128]{2,1,0:T(8,128)S(1)} all-to-all(f32[8,8,128]{2,1,0:T(8,128)S(1)} %get-tuple-element.56), channel_id=1, replica_groups=mesh['chip'=64,'core'=2,'cls'=8] {'cls'}, dimensions={0} | all-to-all | bytes 65536 | tf_op jit(solution)/shard_map/all_to_all | solution.py:309
  113.6 1.1 shard_map.72
  (3 shorter events, 0.1 us)
Async XLA Ops:
  0.0 45.6 %copy-start = (bf16[32,128,128]{2,1,0:T(8,128)(2,1)S(1)}, bf16[32,128,128]{2,1,0:T(8,128)(2,1)}, u32[]{:S(2)}) copy-start(bf16[32,128,128]{2,1,0:T(8,128)(2,1)} %refs_0_.5) | copy-start | bytes 3145732
  1.9 26.0 %collective-permute-start = (f32[520,128]{1,0:T(8,128)S(1)}, f32[520,128]{1,0:T(8,128)S(1)}, u32[]{:S(2)}, u32[]{:S(2)}) collective-permute-start(f32[520,128]{1,0:T(8,128)S(1)} %get-tuple-element.34), channel_id=1, source_target_pairs={{0,1016},{8,16},{16,8},{24,32},{32,24},{40,48},{48,40},{56,64},{64... | collective-permute-start | bytes 798728 | tf_op jit(solution)/shard_map/ppermute | solution.py:276
  8.2 19.7 %collective-permute-start.1 = (f32[264,128]{1,0:T(8,128)S(1)}, f32[264,128]{1,0:T(8,128)S(1)}, u32[]{:S(2)}, u32[]{:S(2)}) collective-permute-start(f32[264,128]{1,0:T(8,128)S(1)} %get-tuple-element.37), channel_id=1, source_target_pairs={{0,24},{8,1008},{16,40},{24,0},{32,56},{40,16},{48,72},{56,32},{64... | collective-permute-start | bytes 405512 | tf_op jit(solution)/shard_map/ppermute | solution.py:277
  27.9 17.6 %collective-permute-start.2 = (f32[6,128,128]{2,1,0:T(8,128)S(1)}, f32[6,128,128]{2,1,0:T(8,128)S(1)}, u32[]{:S(2)}, u32[]{:S(2)}) collective-permute-start(f32[6,128,128]{2,1,0:T(8,128)S(1)} %get-tuple-element.38), channel_id=1, source_target_pairs={{0,8},{8,0},{1,9},{9,1},{2,10},{10,2},{3,11},{11,3},{4,12},{12,4},... | collective-permute-start | bytes 1179656 | tf_op jit(solution)/shard_map/ppermute | solution.py:286
  47.6 13.1 %collective-permute-start.3 = (f32[520,128]{1,0:T(8,128)S(1)}, f32[520,128]{1,0:T(8,128)S(1)}, u32[]{:S(2)}, u32[]{:S(2)}) collective-permute-start(f32[520,128]{1,0:T(8,128)S(1)} %get-tuple-element.42), channel_id=1, source_target_pairs={{0,1016},{8,16},{16,8},{24,32},{32,24},{40,48},{48,40},{56,64},{64... | collective-permute-start | bytes 798728 | tf_op jit(solution)/shard_map/ppermute | solution.py:276
  50.7 10.0 %collective-permute-start.4 = (f32[264,128]{1,0:T(8,128)S(1)}, f32[264,128]{1,0:T(8,128)S(1)}, u32[]{:S(2)}, u32[]{:S(2)}) collective-permute-start(f32[264,128]{1,0:T(8,128)S(1)} %get-tuple-element.45), channel_id=1, source_target_pairs={{0,24},{8,1008},{16,40},{24,0},{32,56},{40,16},{48,72},{56,32},{64... | collective-permute-start | bytes 405512 | tf_op jit(solution)/shard_map/ppermute | solution.py:277
  60.8 13.1 %collective-permute-start.5 = (f32[6,128,128]{2,1,0:T(8,128)S(1)}, f32[6,128,128]{2,1,0:T(8,128)S(1)}, u32[]{:S(2)}, u32[]{:S(2)}) collective-permute-start(f32[6,128,128]{2,1,0:T(8,128)S(1)} %get-tuple-element.46), channel_id=1, source_target_pairs={{0,8},{8,0},{1,9},{9,1},{2,10},{10,2},{3,11},{11,3},{4,12},{12,4},... | collective-permute-start | bytes 1179656 | tf_op jit(solution)/shard_map/ppermute | solution.py:286
  75.7 13.1 %collective-permute-start.6 = (f32[520,128]{1,0:T(8,128)S(1)}, f32[520,128]{1,0:T(8,128)S(1)}, u32[]{:S(2)}, u32[]{:S(2)}) collective-permute-start(f32[520,128]{1,0:T(8,128)S(1)} %get-tuple-element.49), channel_id=1, source_target_pairs={{0,1016},{8,16},{16,8},{24,32},{32,24},{40,48},{48,40},{56,64},{64... | collective-permute-start | bytes 798728 | tf_op jit(solution)/shard_map/ppermute | solution.py:276
  78.8 10.0 %collective-permute-start.7 = (f32[264,128]{1,0:T(8,128)S(1)}, f32[264,128]{1,0:T(8,128)S(1)}, u32[]{:S(2)}, u32[]{:S(2)}) collective-permute-start(f32[264,128]{1,0:T(8,128)S(1)} %get-tuple-element.52), channel_id=1, source_target_pairs={{0,24},{8,1008},{16,40},{24,0},{32,56},{40,16},{48,72},{56,32},{64... | collective-permute-start | bytes 405512 | tf_op jit(solution)/shard_map/ppermute | solution.py:277
  88.8 13.1 %collective-permute-start.8 = (f32[6,128,128]{2,1,0:T(8,128)S(1)}, f32[6,128,128]{2,1,0:T(8,128)S(1)}, u32[]{:S(2)}, u32[]{:S(2)}) collective-permute-start(f32[6,128,128]{2,1,0:T(8,128)S(1)} %get-tuple-element.53), channel_id=1, source_target_pairs={{0,8},{8,0},{1,9},{9,1},{2,10},{10,2},{3,11},{11,3},{4,12},{12,4},... | collective-permute-start | bytes 1179656 | tf_op jit(solution)/shard_map/ppermute | solution.py:286

commit v7 on v6

--- a/solution.py
+++ b/solution.py
@@ -29,6 +29,7 @@
 
 def plan_entries(rows, cols, send):
     core = lax.axis_index("core")
+    odd = lax.rem(lax.axis_index("chip"), 2)
     for tile in range(32):
         yield rows[tile]
     for tile in range(32):
@@ -36,7 +37,7 @@
         ghost = jnp.maximum(col - 8, 0)
         offset = shift_right(ghost, 1)
         half = shift_right(offset, 1)
-        pair = jnp.where(lax.rem(offset, 2) == 1, 2 + (half ^ (1 - core)), half ^ core)
+        pair = jnp.where(lax.rem(offset, 2) == 1, 2 * (half ^ odd), 1 + 2 * (half ^ core))
         yield jnp.where(col < 8, col, 8 + 2 * pair + lax.rem(ghost, 2))
     for offset in range(4):
         for within in range(2):
@@ -59,23 +60,16 @@
     return ref[SIDE * place : SIDE * (place + 1), :]
 
 
-def fill_swaps(source, sums, block_of, wide, narrow, near, rows):
+def fill_swaps(source, sums, block_of, outs, rows):
     core = lax.axis_index("core")
+    odd = lax.rem(lax.axis_index("chip"), 2)
     rows[0:8, :] = sums
-    rows[8:16, :] = jnp.zeros((8, SIDE), F32)
-    for within in range(2):
-        block = block_of(2 * core, within)
-        near[within] = source[block]
-        rows[10 + within : 11 + within, :] = rows[pl.ds(block, 1), :]
-    for out, offsets in ((wide, (2 - 2 * core, 3 - 2 * core)), (narrow, (1 + 2 * core,))):
-        count = 2 * len(offsets)
-        out[count * SIDE + count :, :] = jnp.zeros((8 - count, SIDE), F32)
-        for part, offset in enumerate(offsets):
-            for within in range(2):
-                place = 2 * part + within
-                block = block_of(offset, within)
-                out[SIDE * place : SIDE * (place + 1), :] = source[block]
-                out[count * SIDE + place : count * SIDE + place + 1, :] = rows[pl.ds(block, 1), :]
+    for out, offset in zip(outs, (3 - 2 * odd, 2 - 2 * core, 1 + 2 * odd, 2 * core)):
+        out[2 * SIDE + 2 :, :] = jnp.zeros((6, SIDE), F32)
+        for within in range(2):
+            block = block_of(offset, within)
+            out[SIDE * within : SIDE * (within + 1), :] = source[block]
+            out[2 * SIDE + within : 2 * SIDE + within + 1, :] = rows[pl.ds(block, 1), :]
 
 
 def lane_sums(block):
@@ -91,7 +85,7 @@
     return copies
 
 
-def first_kernel(labels, send, kept, wide, narrow, near, rows, send_here, sems):
+def first_kernel(labels, send, kept, out0, out1, out2, out3, rows, send_here, sems):
     pairs = [(labels.at[block], kept.at[block]) for block in range(8)]
     copies = copy_all([(send, send_here)] + pairs, sems)
     sums = []
@@ -100,7 +94,7 @@
         sums.append(lane_sums(kept[block]))
     copies[0].wait()
     block_of = lambda offset, within: send_here[0, within, offset]
-    fill_swaps(kept, jnp.concatenate(sums, axis=0), block_of, wide, narrow, near, rows)
+    fill_swaps(kept, jnp.concatenate(sums, axis=0), block_of, (out0, out1, out2, out3), rows)
 
 
 def plan_kernel(rows, cols, send, mask, plan, mask_kept, rows_here, cols_here, send_here, sems):
@@ -111,17 +105,10 @@
         plan[place] = entry
 
 
-def mass_kernel(sums, near, wide, narrow, plan, parts, relay, rows):
-    rows[...] = sums[...]
-    rows[8:10, :] = wide[4 * SIDE : 4 * SIDE + 2, :]
-    rows[12:14, :] = wide[4 * SIDE + 2 : 4 * SIDE + 4, :]
-    rows[14:16, :] = narrow[2 * SIDE : 2 * SIDE + 2, :]
-    for within in range(2):
-        relay[within] = near[within]
-        relay[2 + within] = block_at(wide, 2 + within)
-        relay[4 + within] = block_at(narrow, within)
-    partial = rows[...]
-    for share in range(16):
+def mass_kernel(sums, in0, in1, in2, in3, plan, parts):
+    received = [ref[2 * SIDE : 2 * SIDE + 2, :] for ref in (in0, in1, in2, in3)]
+    partial = jnp.concatenate([sums[...]] + received, axis=0)
+    for share in range(8):
         parts[share] = partial
 
 
@@ -131,10 +118,10 @@
     return jnp.transpose(full)
 
 
-def total_of(parts, core):
-    total = parts[8 * core]
+def total_of(parts):
+    total = parts[0]
     for share in range(1, 8):
-        total = total + parts[8 * core + share]
+        total = total + parts[share]
     return total
 
 
@@ -146,21 +133,21 @@
 
 def spread_kernel(first, last, *refs):
     refs = list(refs)
-    tiles, plan, mask, source, wide, relay, parts = refs[:7]
-    refs = refs[7:]
+    tiles, plan, mask, source = refs[:4]
+    received = refs[4:8]
+    parts = refs[8]
+    refs = refs[9:]
     anchor = refs.pop(0) if first else mask
     squared = refs.pop(0)
     if last:
         own_parts, *refs = refs
     else:
-        wide_out, narrow_out, near_out, rows_out, *refs = refs
+        *outs, rows_out = refs[:5]
+        refs = refs[5:]
     operand, products, plan_here, plan_sem = refs
     plan_copy = pltpu.make_async_copy(plan, plan_here, plan_sem)
     plan_copy.start()
-    core = lax.axis_index("core")
-    mine = total_of(parts, core)
-    mate = total_of(parts, 1 - core)
-    scale = scales(jnp.concatenate([mine[0:10], mate[10:16]], axis=0), 16)
+    scale = scales(total_of(parts), 16)
     if first:
         seeded = jnp.concatenate(
             [mask[...].astype(F32), jnp.zeros((SIDE - 8, SIDE), F32)], axis=0
@@ -169,10 +156,8 @@
     for block in range(16):
         if block < 8:
             value = source[block]
-        elif block < 10:
-            value = block_at(wide, block - 8)
         else:
-            value = relay[block - 10]
+            value = block_at(received[(block - 8) // 2], block % 2)
         value = value * scale[:, block : block + 1]
         if first and block < 8:
             anchor[block] = seeded[:, block : block + 1] * value + 4.0
@@ -204,11 +189,11 @@
             own_parts[share] = sums
     else:
         block_of = functools.partial(sent_block, plan)
-        fill_swaps(squared, sums, block_of, wide_out, narrow_out, near_out, rows_out)
+        fill_swaps(squared, sums, block_of, outs, rows_out)
 
 
 def last_kernel(squared, parts, out, scaled, sems):
-    scale = scales(total_of(parts, 0), 8)
+    scale = scales(total_of(parts), 8)
     copies = []
     for block in range(8):
         scaled[block] = squared[block] * scale[:, block : block + 1]
@@ -222,16 +207,15 @@
 def on_device(tiles, tile_rows, tile_cols, send_lists, seed_mask, labels):
     dom = ("chip", "core")
     count = 2 * lax.axis_size("chip")
-    adjacent = [(i, (i + (1 if i % 2 else -1)) % count) for i in range(count)]
-    three_away = [(i, (i + (-3 if i % 2 else 3)) % count) for i in range(count)]
+    swaps = [
+        [(i, (i + (2 if i // 2 % 2 else -2)) % count) for i in range(count)],
+        [(i, (i + (1 if i % 2 else -1)) % count) for i in range(count)],
+        [(i, (i + (-2 if i // 2 % 2 else 2)) % count) for i in range(count)],
+        [(i, i ^ 1) for i in range(count)],
+    ]
     send_lists = jnp.transpose(send_lists, (0, 2, 1))
     own_shape = shape(8, SIDE, SIDE)
-    sent_shapes = [
-        shape(4 * SIDE + 8, SIDE),
-        shape(2 * SIDE + 8, SIDE),
-        shape(2, SIDE, SIDE),
-        shape(16, SIDE),
-    ]
+    sent_shapes = [shape(2 * SIDE + 8, SIDE)] * 4 + [shape(8, SIDE)]
     blocks, tile_rows, tile_cols, send_lists, mask = [
         pltpu.with_memory_space_constraint(value, pltpu.HBM)
         for value in (
@@ -243,11 +227,11 @@
         )
     ]
     send_scratch = pltpu.SMEM((1, 2, 4), jnp.int32)
-    source, wide, narrow, near, rows = pl.pallas_call(
+    source, *outs, rows = pl.pallas_call(
         first_kernel,
         out_shape=[own_shape] + sent_shapes,
         in_specs=[HBM] * 2,
-        out_specs=[VMEM] * 5,
+        out_specs=[VMEM] * 6,
         scratch_shapes=[send_scratch, pltpu.SemaphoreType.DMA((9,))],
         compiler_params=PARAMS,
         cost_estimate=pl.CostEstimate(flops=1 << 20, bytes_accessed=1 << 20, transcendentals=0),
@@ -273,24 +257,21 @@
     for iteration in range(ITERS):
         first = iteration == 0
         last = iteration == ITERS - 1
-        wide = lax.ppermute(wide, dom, adjacent)
-        narrow = lax.ppermute(narrow, dom, three_away)
-        parts, relay = pl.pallas_call(
+        received = [lax.ppermute(out, dom, swap) for out, swap in zip(outs, swaps)]
+        parts = pl.pallas_call(
             mass_kernel,
-            out_shape=[shape(16, 16, SIDE), shape(6, SIDE, SIDE)],
-            in_specs=[VMEM] * 5,
-            out_specs=[VMEM, VMEM],
-            scratch_shapes=[pltpu.VMEM((16, SIDE), F32)],
+            out_shape=shape(8, 16, SIDE),
+            in_specs=[VMEM] * 6,
+            out_specs=VMEM,
             compiler_params=PARAMS,
-        )(rows, near, wide, narrow, plan)
-        relay = lax.ppermute(relay, "core", [(0, 1), (1, 0)])
-        parts = lax.all_to_all(parts, ("core", "cls"), 0, 0)
+        )(rows, *received, plan)
+        parts = lax.all_to_all(parts, "cls", 0, 0)
         out_shape = [own_shape] * (2 if first else 1)
         out_shape += [shape(8, 8, SIDE)] if last else sent_shapes
         results = pl.pallas_call(
             lambda *refs, first=first, last=last: spread_kernel(first, last, *refs),
             out_shape=out_shape,
-            in_specs=[VMEM] * 7,
+            in_specs=[VMEM] * 9,
             out_specs=[VMEM] * len(out_shape),
             scratch_shapes=[
                 pltpu.VMEM((16, 2 * SIDE, SIDE), jnp.bfloat16),
@@ -299,13 +280,13 @@
                 pltpu.SemaphoreType.DMA,
             ],
             compiler_params=PARAMS,
-        )(tiles, plan, mask if first else anchor, source, wide, relay, parts)
+        )(tiles, plan, mask if first else anchor, source, *received, parts)
         if first:
             anchor, *results = results
         if last:
             source, parts = results
         else:
-            source, wide, narrow, near, rows = results
+            source, *outs, rows = results
     parts = lax.all_to_all(parts, "cls", 0, 0)
     out = pl.pallas_call(
         last_kernel,

time: 115 us -> 114 us (level); the launches traced: 115 us -> 112 us
  starting transfers between devices: 48.6 us -> 57.7 us
  waiting for transfers between devices: 8.84 us -> 1.91 us
  blocking collectives: 47.1 us -> 42.8 us
    all_to_all x3 -> x0, blocking collectives: 36.9 us -> none  [on_device(): parts = lax.all_to_all(parts, ('core', 'cls'), 0, 0)]
    all_to_all x1 -> x4, blocking collectives: 10.2 us -> 42.8 us  [on_device(): parts = lax.all_to_all(parts, 'cls', 0, 0)]
    ppermute x9 -> x12, starting transfers between devices: 48.6 us -> 57.7 us  [on_device(): received = [lax.ppermute(out, dom, swap) for out, swap in zip(outs, swaps)]]
    ppermute x9 -> x12, waiting for transfers between devices: 8.84 us -> 1.91 us  [on_device(): received = [lax.ppermute(out, dom, swap) for out, swap in zip(outs, swaps)]]
  transfers between devices with their start and end apart: 9 -> 12, of which waited for: 3 -> 3; matrix products, arithmetic and copies ran while one was open for 0% -> 0% of each run, Pallas kernels for 1% -> 1%
where the time goes in v7:
time: 114 us; the launch traced here: 112 us
  starting transfers between devices  57.7 us (51%)
  blocking collectives  42.8 us (38%)
  Pallas kernels  9.71 us (9%)
  waiting for transfers between devices  1.91 us (2%)
    ppermute x12, starting transfers between devices, on_device(): received = [lax.ppermute(out, dom, swap) for out, swap in zip(outs, swaps)]  57.7 us
    all_to_all x4, blocking collectives, on_device(): parts = lax.all_to_all(parts, 'cls', 0, 0)  42.8 us
    pallas_call x3, Pallas kernels, on_device(): pl.pallas_call(lambda *refs, first=first, last=last: spread_kernel(first,...  5.1 us
  transfers between devices with their start and end apart: 12, of which 3 were waited for; matrix products, arithmetic and copies ran while one was open for 0% of the time, Pallas kernels for 1%

profile of v7, /device:TPU:1, one launch (start us, length us, event | category | flops | bytes accessed | tf_op | source)
XLA Modules:
  0.0 112.4 jit_solution(7134591677694907913)
XLA Ops:
  0.0 0.0 copy-start
  0.0 1.9 %shard_map.65 = (f32[8,128,128]{2,1,0:T(8,128)S(1)}, f32[264,128]{1,0:T(8,128)S(1)}, f32[264,128]{1,0:T(8,128)S(1)}, f32[264,128]{1,0:T(8,128)S(1)}, f32[264,128]{1,0:T(8,128)S(1)}, /*index=5*/f32[8,128]{1,0:T(8,128)S(1)}) custom-call(f32[8,128,128]{2,1,0:T(8,128)} %bitcast.4, s32[1,2,4]{2,1,0:T(2,128)} %bitcast.5), custom_call_target="tpu_custom_call" | custom-call | flops 1048576 | bytes 1048576 | tf_op jit(solution)/shard_map/pallas_call | solution.py:230
  1.9 20.2 %collective-permute-start = (f32[264,128]{1,0:T(8,128)S(1)}, f32[264,128]{1,0:T(8,128)S(1)}, u32[]{:S(2)}, u32[]{:S(2)}) collective-permute-start(f32[264,128]{1,0:T(8,128)S(1)} %get-tuple-element.31), channel_id=1, source_target_pairs={{0,1008},{8,1016},{16,32},{24,40},{32,16},{40,24},{48,64},{56,72},... | collective-permute-start | bytes 405512 | tf_op jit(solution)/shard_map/ppermute | solution.py:260
  22.1 1.9 %collective-permute-start.1 = (f32[264,128]{1,0:T(8,128)S(1)}, f32[264,128]{1,0:T(8,128)S(1)}, u32[]{:S(2)}, u32[]{:S(2)}) collective-permute-start(f32[264,128]{1,0:T(8,128)S(1)} %get-tuple-element.32), channel_id=1, source_target_pairs={{0,1016},{8,16},{16,8},{24,32},{32,24},{40,48},{48,40},{56,64},{64... | collective-permute-start | bytes 405512 | tf_op jit(solution)/shard_map/ppermute | solution.py:260
  24.0 1.9 %collective-permute-start.2 = (f32[264,128]{1,0:T(8,128)S(1)}, f32[264,128]{1,0:T(8,128)S(1)}, u32[]{:S(2)}, u32[]{:S(2)}) collective-permute-start(f32[264,128]{1,0:T(8,128)S(1)} %get-tuple-element.33), channel_id=1, source_target_pairs={{0,16},{8,24},{16,0},{24,8},{32,48},{40,56},{48,32},{56,40},{64,80... | collective-permute-start | bytes 405512 | tf_op jit(solution)/shard_map/ppermute | solution.py:260
  26.0 4.0 %collective-permute-start.3 = (f32[264,128]{1,0:T(8,128)S(1)}, f32[264,128]{1,0:T(8,128)S(1)}, u32[]{:S(2)}, u32[]{:S(2)}) collective-permute-start(f32[264,128]{1,0:T(8,128)S(1)} %get-tuple-element.34), channel_id=1, source_target_pairs={{0,8},{8,0},{16,24},{24,16},{32,40},{40,32},{48,56},{56,48},{64,72... | collective-permute-start | bytes 405512 | tf_op jit(solution)/shard_map/ppermute | solution.py:260
  30.0 1.6 %shard_map.64 = (s32[72]{0:T(128)S(1)}, s32[8,128]{1,0:T(8,128)S(1)}) custom-call(s32[32]{0:T(128)} %rows.1, s32[32]{0:T(128)} %cols.1, s32[1,2,4]{2,1,0:T(2,128)} %bitcast.6, s32[8,128]{1,0:T(8,128)} %bitcast.7), custom_call_target="tpu_custom_call" | custom-call | flops 1048576 | bytes 1048576 | tf_op jit(solution)/shard_map/pallas_call | solution.py:239
  31.6 0.0 collective-permute-done.in0.refs_4_
  31.6 0.0 collective-permute-done.1.in1.refs_5_
  31.6 0.0 collective-permute-done.2.in2.refs_6_
  31.6 0.0 collective-permute-done.3.in3.refs_7_
  31.6 14.3 %all_to_all.20.refs_8_ = f32[8,16,128]{2,1,0:T(8,128)S(1)} all-to-all(f32[8,16,128]{2,1,0:T(8,128)S(1)} %shard_map.66), channel_id=1, replica_groups=mesh['chip'=64,'core'=2,'cls'=8] {'cls'}, dimensions={0} | all-to-all | bytes 131072 | tf_op jit(solution)/shard_map/all_to_all | solution.py:268
  45.9 0.0 copy-done
  45.9 2.1 %shard_map.67 = (f32[8,128,128]{2,1,0:T(8,128)S(1)}, f32[8,128,128]{2,1,0:T(8,128)S(1)}, f32[264,128]{1,0:T(8,128)S(1)}, f32[264,128]{1,0:T(8,128)S(1)}, f32[264...) custom-call(bf16[32,128,128]{2,1,0:T(8,128)(2,1)S(1)} %copy-done, ...), custom_call_target="tpu_custom_call" | custom-call | tf_op jit(solution)/shard_map/pallas_call | solution.py:271
  48.0 5.7 %collective-permute-start.4 = (f32[264,128]{1,0:T(8,128)S(1)}, f32[264,128]{1,0:T(8,128)S(1)}, u32[]{:S(2)}, u32[]{:S(2)}) collective-permute-start(f32[264,128]{1,0:T(8,128)S(1)} %get-tuple-element.38), channel_id=1, source_target_pairs={{0,1008},{8,1016},{16,32},{24,40},{32,16},{40,24},{48,64},{56,72},... | collective-permute-start | bytes 405512 | tf_op jit(solution)/shard_map/ppermute | solution.py:260
  53.7 1.9 %collective-permute-start.5 = (f32[264,128]{1,0:T(8,128)S(1)}, f32[264,128]{1,0:T(8,128)S(1)}, u32[]{:S(2)}, u32[]{:S(2)}) collective-permute-start(f32[264,128]{1,0:T(8,128)S(1)} %get-tuple-element.39), channel_id=1, source_target_pairs={{0,1016},{8,16},{16,8},{24,32},{32,24},{40,48},{48,40},{56,64},{64... | collective-permute-start | bytes 405512 | tf_op jit(solution)/shard_map/ppermute | solution.py:260
  55.6 2.4 %collective-permute-start.6 = (f32[264,128]{1,0:T(8,128)S(1)}, f32[264,128]{1,0:T(8,128)S(1)}, u32[]{:S(2)}, u32[]{:S(2)}) collective-permute-start(f32[264,128]{1,0:T(8,128)S(1)} %get-tuple-element.40), channel_id=1, source_target_pairs={{0,16},{8,24},{16,0},{24,8},{32,48},{40,56},{48,32},{56,40},{64,80... | collective-permute-start | bytes 405512 | tf_op jit(solution)/shard_map/ppermute | solution.py:260
  58.0 3.6 %collective-permute-start.7 = (f32[264,128]{1,0:T(8,128)S(1)}, f32[264,128]{1,0:T(8,128)S(1)}, u32[]{:S(2)}, u32[]{:S(2)}) collective-permute-start(f32[264,128]{1,0:T(8,128)S(1)} %get-tuple-element.41), channel_id=1, source_target_pairs={{0,8},{8,0},{16,24},{24,16},{32,40},{40,32},{48,56},{56,48},{64,72... | collective-permute-start | bytes 405512 | tf_op jit(solution)/shard_map/ppermute | solution.py:260
  61.6 0.0 collective-permute-done.4.in0.refs_4_
  61.6 0.0 collective-permute-done.5.in1.refs_5_
  61.6 0.0 collective-permute-done.6.in2.refs_6_
  61.6 0.9 collective-permute-done.7.in3.refs_7_
  62.6 9.7 %all_to_all.21.refs_8_ = f32[8,16,128]{2,1,0:T(8,128)S(1)} all-to-all(f32[8,16,128]{2,1,0:T(8,128)S(1)} %shard_map.68), channel_id=1, replica_groups=mesh['chip'=64,'core'=2,'cls'=8] {'cls'}, dimensions={0} | all-to-all | bytes 131072 | tf_op jit(solution)/shard_map/all_to_all | solution.py:268
  72.3 1.5 %shard_map.69 = (f32[8,128,128]{2,1,0:T(8,128)S(1)}, f32[264,128]{1,0:T(8,128)S(1)}, f32[264,128]{1,0:T(8,128)S(1)}, f32[264,128]{1,0:T(8,128)S(1)}, f32[264,128]{1,0:T(8,128)S(1)}, /*index=5*/f32[8,128]{1,0:T(8,128)S(1)}) custom-call(bf16[32,128,128]{2,1,0:T(8,128)(2,1)S(1)} %copy-done, s32[72]{0:T(128)S(1)} %get-tuple-element.28.plan.refs_1_, ...), custom_call_target="tpu_custom_call" | custom-call | tf_op jit(solution)/shard_map/pallas_call | solution.py:271
  73.8 8.2 %collective-permute-start.8 = (f32[264,128]{1,0:T(8,128)S(1)}, f32[264,128]{1,0:T(8,128)S(1)}, u32[]{:S(2)}, u32[]{:S(2)}) collective-permute-start(f32[264,128]{1,0:T(8,128)S(1)} %get-tuple-element.44), channel_id=1, source_target_pairs={{0,1008},{8,1016},{16,32},{24,40},{32,16},{40,24},{48,64},{56,72},... | collective-permute-start | bytes 405512 | tf_op jit(solution)/shard_map/ppermute | solution.py:260
  82.0 1.9 %collective-permute-start.9 = (f32[264,128]{1,0:T(8,128)S(1)}, f32[264,128]{1,0:T(8,128)S(1)}, u32[]{:S(2)}, u32[]{:S(2)}) collective-permute-start(f32[264,128]{1,0:T(8,128)S(1)} %get-tuple-element.45), channel_id=1, source_target_pairs={{0,1016},{8,16},{16,8},{24,32},{32,24},{40,48},{48,40},{56,64},{64... | collective-permute-start | bytes 405512 | tf_op jit(solution)/shard_map/ppermute | solution.py:260
  84.0 1.9 %collective-permute-start.10 = (f32[264,128]{1,0:T(8,128)S(1)}, f32[264,128]{1,0:T(8,128)S(1)}, u32[]{:S(2)}, u32[]{:S(2)}) collective-permute-start(f32[264,128]{1,0:T(8,128)S(1)} %get-tuple-element.46), channel_id=1, source_target_pairs={{0,16},{8,24},{16,0},{24,8},{32,48},{40,56},{48,32},{56,40},{64,80... | collective-permute-start | bytes 405512 | tf_op jit(solution)/shard_map/ppermute | solution.py:260
  85.9 4.0 %collective-permute-start.11 = (f32[264,128]{1,0:T(8,128)S(1)}, f32[264,128]{1,0:T(8,128)S(1)}, u32[]{:S(2)}, u32[]{:S(2)}) collective-permute-start(f32[264,128]{1,0:T(8,128)S(1)} %get-tuple-element.47), channel_id=1, source_target_pairs={{0,8},{8,0},{16,24},{24,16},{32,40},{40,32},{48,56},{56,48},{64,72... | collective-permute-start | bytes 405512 | tf_op jit(solution)/shard_map/ppermute | solution.py:260
  89.9 0.0 collective-permute-done.8.in0.refs_4_
  89.9 0.0 collective-permute-done.9.in1.refs_5_
  90.0 0.6 collective-permute-done.10.in2.refs_6_
  90.5 0.4 collective-permute-done.11.in3.refs_7_
  90.9 9.6 %all_to_all.22.refs_8_ = f32[8,16,128]{2,1,0:T(8,128)S(1)} all-to-all(f32[8,16,128]{2,1,0:T(8,128)S(1)} %shard_map.70), channel_id=1, replica_groups=mesh['chip'=64,'core'=2,'cls'=8] {'cls'}, dimensions={0} | all-to-all | bytes 131072 | tf_op jit(solution)/shard_map/all_to_all | solution.py:268
  100.5 1.5 %shard_map.71 = (f32[8,128,128]{2,1,0:T(8,128)S(1)}, f32[8,8,128]{2,1,0:T(8,128)S(1)}) custom-call(bf16[32,128,128]{2,1,0:T(8,128)(2,1)S(1)} %copy-done, s32[72]{0:T(128)S(1)} %get-tuple-element.28.plan.refs_1_, f32[8,128,128]{2,1,0:T(8,128)S(1)} %get-tuple-element.36.refs_2_, f32[8,128,128]{2,1,0:T(8,128)S(1)} %get-tuple-element.43.refs_3_, ...), custom_call_target="tpu_custom_call" | custom-call | tf_op jit(solution)/shard_map/pallas_call | solution.py:271
  102.0 9.2 %all_to_all.23.parts = f32[8,8,128]{2,1,0:T(8,128)S(1)} all-to-all(f32[8,8,128]{2,1,0:T(8,128)S(1)} %get-tuple-element.50), channel_id=1, replica_groups=mesh['chip'=64,'core'=2,'cls'=8] {'cls'}, dimensions={0} | all-to-all | bytes 65536 | tf_op jit(solution)/shard_map/all_to_all | solution.py:290
  111.3 1.1 shard_map.72
  (3 shorter events, 0.0 us)
Async XLA Ops:
  0.0 45.9 %copy-start = (bf16[32,128,128]{2,1,0:T(8,128)(2,1)S(1)}, bf16[32,128,128]{2,1,0:T(8,128)(2,1)}, u32[]{:S(2)}) copy-start(bf16[32,128,128]{2,1,0:T(8,128)(2,1)} %refs_0_.5) | copy-start | bytes 3145732
  1.9 29.6 %collective-permute-start = (f32[264,128]{1,0:T(8,128)S(1)}, f32[264,128]{1,0:T(8,128)S(1)}, u32[]{:S(2)}, u32[]{:S(2)}) collective-permute-start(f32[264,128]{1,0:T(8,128)S(1)} %get-tuple-element.31), channel_id=1, source_target_pairs={{0,1008},{8,1016},{16,32},{24,40},{32,16},{40,24},{48,64},{56,72},... | collective-permute-start | bytes 405512 | tf_op jit(solution)/shard_map/ppermute | solution.py:260
  22.1 9.5 %collective-permute-start.1 = (f32[264,128]{1,0:T(8,128)S(1)}, f32[264,128]{1,0:T(8,128)S(1)}, u32[]{:S(2)}, u32[]{:S(2)}) collective-permute-start(f32[264,128]{1,0:T(8,128)S(1)} %get-tuple-element.32), channel_id=1, source_target_pairs={{0,1016},{8,16},{16,8},{24,32},{32,24},{40,48},{48,40},{56,64},{64... | collective-permute-start | bytes 405512 | tf_op jit(solution)/shard_map/ppermute | solution.py:260
  24.0 7.6 %collective-permute-start.2 = (f32[264,128]{1,0:T(8,128)S(1)}, f32[264,128]{1,0:T(8,128)S(1)}, u32[]{:S(2)}, u32[]{:S(2)}) collective-permute-start(f32[264,128]{1,0:T(8,128)S(1)} %get-tuple-element.33), channel_id=1, source_target_pairs={{0,16},{8,24},{16,0},{24,8},{32,48},{40,56},{48,32},{56,40},{64,80... | collective-permute-start | bytes 405512 | tf_op jit(solution)/shard_map/ppermute | solution.py:260
  26.0 5.6 %collective-permute-start.3 = (f32[264,128]{1,0:T(8,128)S(1)}, f32[264,128]{1,0:T(8,128)S(1)}, u32[]{:S(2)}, u32[]{:S(2)}) collective-permute-start(f32[264,128]{1,0:T(8,128)S(1)} %get-tuple-element.34), channel_id=1, source_target_pairs={{0,8},{8,0},{16,24},{24,16},{32,40},{40,32},{48,56},{56,48},{64,72... | collective-permute-start | bytes 405512 | tf_op jit(solution)/shard_map/ppermute | solution.py:260
  48.0 13.6 %collective-permute-start.4 = (f32[264,128]{1,0:T(8,128)S(1)}, f32[264,128]{1,0:T(8,128)S(1)}, u32[]{:S(2)}, u32[]{:S(2)}) collective-permute-start(f32[264,128]{1,0:T(8,128)S(1)} %get-tuple-element.38), channel_id=1, source_target_pairs={{0,1008},{8,1016},{16,32},{24,40},{32,16},{40,24},{48,64},{56,72},... | collective-permute-start | bytes 405512 | tf_op jit(solution)/shard_map/ppermute | solution.py:260
  53.7 7.9 %collective-permute-start.5 = (f32[264,128]{1,0:T(8,128)S(1)}, f32[264,128]{1,0:T(8,128)S(1)}, u32[]{:S(2)}, u32[]{:S(2)}) collective-permute-start(f32[264,128]{1,0:T(8,128)S(1)} %get-tuple-element.39), channel_id=1, source_target_pairs={{0,1016},{8,16},{16,8},{24,32},{32,24},{40,48},{48,40},{56,64},{64... | collective-permute-start | bytes 405512 | tf_op jit(solution)/shard_map/ppermute | solution.py:260
  55.6 6.0 %collective-permute-start.6 = (f32[264,128]{1,0:T(8,128)S(1)}, f32[264,128]{1,0:T(8,128)S(1)}, u32[]{:S(2)}, u32[]{:S(2)}) collective-permute-start(f32[264,128]{1,0:T(8,128)S(1)} %get-tuple-element.40), channel_id=1, source_target_pairs={{0,16},{8,24},{16,0},{24,8},{32,48},{40,56},{48,32},{56,40},{64,80... | collective-permute-start | bytes 405512 | tf_op jit(solution)/shard_map/ppermute | solution.py:260
  58.0 4.6 %collective-permute-start.7 = (f32[264,128]{1,0:T(8,128)S(1)}, f32[264,128]{1,0:T(8,128)S(1)}, u32[]{:S(2)}, u32[]{:S(2)}) collective-permute-start(f32[264,128]{1,0:T(8,128)S(1)} %get-tuple-element.41), channel_id=1, source_target_pairs={{0,8},{8,0},{16,24},{24,16},{32,40},{40,32},{48,56},{56,48},{64,72... | collective-permute-start | bytes 405512 | tf_op jit(solution)/shard_map/ppermute | solution.py:260
  73.8 16.1 %collective-permute-start.8 = (f32[264,128]{1,0:T(8,128)S(1)}, f32[264,128]{1,0:T(8,128)S(1)}, u32[]{:S(2)}, u32[]{:S(2)}) collective-permute-start(f32[264,128]{1,0:T(8,128)S(1)} %get-tuple-element.44), channel_id=1, source_target_pairs={{0,1008},{8,1016},{16,32},{24,40},{32,16},{40,24},{48,64},{56,72},... | collective-permute-start | bytes 405512 | tf_op jit(solution)/shard_map/ppermute | solution.py:260
  82.0 7.9 %collective-permute-start.9 = (f32[264,128]{1,0:T(8,128)S(1)}, f32[264,128]{1,0:T(8,128)S(1)}, u32[]{:S(2)}, u32[]{:S(2)}) collective-permute-start(f32[264,128]{1,0:T(8,128)S(1)} %get-tuple-element.45), channel_id=1, source_target_pairs={{0,1016},{8,16},{16,8},{24,32},{32,24},{40,48},{48,40},{56,64},{64... | collective-permute-start | bytes 405512 | tf_op jit(solution)/shard_map/ppermute | solution.py:260
  84.0 6.5 %collective-permute-start.10 = (f32[264,128]{1,0:T(8,128)S(1)}, f32[264,128]{1,0:T(8,128)S(1)}, u32[]{:S(2)}, u32[]{:S(2)}) collective-permute-start(f32[264,128]{1,0:T(8,128)S(1)} %get-tuple-element.46), channel_id=1, source_target_pairs={{0,16},{8,24},{16,0},{24,8},{32,48},{40,56},{48,32},{56,40},{64,80... | collective-permute-start | bytes 405512 | tf_op jit(solution)/shard_map/ppermute | solution.py:260
  85.9 5.0 %collective-permute-start.11 = (f32[264,128]{1,0:T(8,128)S(1)}, f32[264,128]{1,0:T(8,128)S(1)}, u32[]{:S(2)}, u32[]{:S(2)}) collective-permute-start(f32[264,128]{1,0:T(8,128)S(1)} %get-tuple-element.47), channel_id=1, source_target_pairs={{0,8},{8,0},{16,24},{24,16},{32,40},{40,32},{48,56},{56,48},{64,72... | collective-permute-start | bytes 405512 | tf_op jit(solution)/shard_map/ppermute | solution.py:260

commit v8 on v7

v8 whole, which is shorter than its diff:
```python
import jax
import jax.numpy as jnp
from jax import lax
from jax.experimental import pallas as pl
from jax.experimental.pallas import tpu as pltpu
from jax.sharding import Mesh
from jax.sharding import PartitionSpec as P

CLASSES = 1024
ITERS = 3
SIDE = 128

VMEM = pl.BlockSpec(memory_space=pltpu.VMEM)
SMEM = pl.BlockSpec(memory_space=pltpu.SMEM)
HBM = pl.BlockSpec(memory_space=pltpu.HBM)
F32 = jnp.float32
PARAMS = pltpu.CompilerParams(vmem_limit_bytes=16 * 1024 * 1024)


def shape(*dims):
    return jax.ShapeDtypeStruct(dims, F32)


def shift_right(value, by):
    return lax.shift_right_logical(value, by)


def operand_block(col):
    odd = lax.rem(lax.axis_index("chip"), 2)
    core = lax.axis_index("core")
    ghost = jnp.maximum(col - 8, 0)
    offset = shift_right(ghost, 1)
    half = shift_right(offset, 1)
    pair = jnp.where(lax.rem(offset, 2) == 1, half ^ odd, 2 + (half ^ core))
    return jnp.where(col < 8, col, 8 + 2 * pair + lax.rem(ghost, 2))


def block_at(ref, place):
    return ref[SIDE * place : SIDE * (place + 1), :]


def fill_swaps(source, sums, send, outs, rows):
    core = lax.axis_index("core")
    odd = lax.rem(lax.axis_index("chip"), 2)
    rows[0:8, :] = sums
    for out, offset in zip(outs, (3 - 2 * odd, 1 + 2 * odd, 2 - 2 * core, 2 * core)):
        out[2 * SIDE + 2 :, :] = jnp.zeros((6, SIDE), F32)
        for within in range(2):
            block = send[0, within, offset]
            out[SIDE * within : SIDE * (within + 1), :] = source[block]
            out[2 * SIDE + within : 2 * SIDE + within + 1, :] = rows[pl.ds(block, 1), :]


def lane_sums(block):
    return jnp.sum(jnp.transpose(block), axis=0, keepdims=True)


def copy_all(pairs, sems):
    copies = []
    for number, (here, there) in enumerate(pairs):
        copy = pltpu.make_async_copy(here, there, sems.at[number])
        copy.start()
        copies.append(copy)
    return copies


def first_kernel(labels, send, rows, cols, mask, kept, send_kept, rows_kept, cols_kept, mask_kept, *refs):
    *outs, sums_out, send_here, sems = refs
    pairs = [(send, send_here)]
    pairs += [(labels.at[block], kept.at[block]) for block in range(8)]
    pairs += [(send, send_kept), (rows, rows_kept), (cols, cols_kept), (mask, mask_kept)]
    copies = copy_all(pairs, sems)
    sums = []
    for block in range(8):
        copies[1 + block].wait()
        sums.append(lane_sums(kept[block]))
    copies[0].wait()
    fill_swaps(kept, jnp.concatenate(sums, axis=0), send_here, outs, sums_out)
    for copy in copies[9:]:
        copy.wait()


def mass_kernel(sums, in0, in1, in2, in3, parts):
    received = [ref[2 * SIDE : 2 * SIDE + 2, :] for ref in (in0, in1, in2, in3)]
    partial = jnp.concatenate([sums[...]] + received, axis=0)
    for share in range(8):
        parts[share] = partial


def scales(total, blocks):
    scale = CLASSES / total
    full = jnp.concatenate([scale, jnp.zeros((SIDE - blocks, SIDE), F32)], axis=0)
    return jnp.transpose(full)


def total_of(parts):
    total = parts[0]
    for share in range(1, 8):
        total = total + parts[share]
    return total


def split(value):
    high = value.astype(jnp.bfloat16)
    low = (value - high.astype(F32)).astype(jnp.bfloat16)
    return high, low


def spread_kernel(first, last, *refs):
    refs = list(refs)
    tiles, *indices = refs[:4]
    mask, source, *received = refs[4:10]
    parts = refs[10]
    refs = refs[11:]
    anchor = refs.pop(0) if first else mask
    squared = refs.pop(0)
    if last:
        own_parts, *refs = refs
    else:
        *outs, rows_out = refs[:5]
        refs = refs[5:]
    operand, products, send, rows, cols, sems = refs
    copies = copy_all(list(zip(indices, (send, rows, cols))), sems)
    scale = scales(total_of(parts), 16)
    if first:
        seeded = jnp.concatenate(
            [mask[...].astype(F32), jnp.zeros((SIDE - 8, SIDE), F32)], axis=0
        )
        seeded = 64.0 * jnp.transpose(seeded)
    for block in range(16):
        if block < 8:
            value = source[block]
        else:
            value = block_at(received[(block - 8) // 2], block % 2)
        value = value * scale[:, block : block + 1]
        if first and block < 8:
            anchor[block] = seeded[:, block : block + 1] * value + 4.0
        high, low = split(value)
        operand[block, :SIDE, :] = high
        operand[block, SIDE:, :] = low
    for copy in copies:
        copy.wait()
    for tile in range(32):
        weights = tiles[tile]
        products[tile] = jnp.dot(
            jnp.concatenate([weights, weights], axis=1),
            operand[operand_block(cols[tile])],
            preferred_element_type=F32,
        )
    squared[...] = anchor[...]
    for tile in range(32):
        row = rows[tile]
        squared[row] = squared[row] + products[tile]
    sums = []
    for block in range(8):
        value = squared[block]
        value = value * value
        squared[block] = value
        sums.append(lane_sums(value))
    sums = jnp.concatenate(sums, axis=0)
    if last:
        for share in range(8):
            own_parts[share] = sums
    else:
        fill_swaps(squared, sums, send, outs, rows_out)


def last_kernel(squared, parts, out, scaled, sems):
    scale = scales(total_of(parts), 8)
    copies = []
    for block in range(8):
        scaled[block] = squared[block] * scale[:, block : block + 1]
        copy = pltpu.make_async_copy(scaled.at[block], out.at[block], sems.at[block])
        copy.start()
        copies.append(copy)
    for copy in copies:
        copy.wait()


def on_device(tiles, tile_rows, tile_cols, send_lists, seed_mask, labels):
    dom = ("chip", "core")
    count = 2 * lax.axis_size("chip")
    swaps = [
        [(i, (i + (2 if i // 2 % 2 else -2)) % count) for i in range(count)],
        [(i, (i + (-2 if i // 2 % 2 else 2)) % count) for i in range(count)],
        [(i, (i + (1 if i % 2 else -1)) % count) for i in range(count)],
        [(i, i ^ 1) for i in range(count)],
    ]
    send_lists = jnp.transpose(send_lists, (0, 2, 1))
    own_shape = shape(8, SIDE, SIDE)
    sent_shapes = [shape(2 * SIDE + 8, SIDE)] * 4 + [shape(8, SIDE)]
    blocks, tile_rows, tile_cols, send_lists, mask = [
        pltpu.with_memory_space_constraint(value, pltpu.HBM)
        for value in (
            labels.reshape(8, SIDE, SIDE),
            tile_rows,
            tile_cols,
            send_lists,
            seed_mask.reshape(8, SIDE),
        )
    ]
    index_shapes = [(1, 2, 4), (32,), (32,)]
    index_scratch = [pltpu.SMEM(dims, jnp.int32) for dims in index_shapes]
    source, send_lists, tile_rows, tile_cols, mask, *outs, rows = pl.pallas_call(
        first_kernel,
        out_shape=[own_shape]
        + [jax.ShapeDtypeStruct(dims, jnp.int32) for dims in index_shapes + [(8, SIDE)]]
        + sent_shapes,
        in_specs=[HBM] * 5,
        out_specs=[VMEM] * 10,
        scratch_shapes=index_scratch[:1] + [pltpu.SemaphoreType.DMA((13,))],
        compiler_params=PARAMS,
        cost_estimate=pl.CostEstimate(flops=1 << 20, bytes_accessed=1 << 20, transcendentals=0),
    )(blocks, send_lists, tile_rows, tile_cols, mask)
    anchor = None
    for iteration in range(ITERS):
        first = iteration == 0
        last = iteration == ITERS - 1
        received = [lax.ppermute(out, dom, swap) for out, swap in zip(outs, swaps)]
        parts = pl.pallas_call(
            mass_kernel,
            out_shape=shape(8, 16, SIDE),
            in_specs=[VMEM] * 5,
            out_specs=VMEM,
            compiler_params=PARAMS,
        )(rows, *received)
        parts = lax.all_to_all(parts, "cls", 0, 0)
        out_shape = [own_shape] * (2 if first else 1)
        out_shape += [shape(8, 8, SIDE)] if last else sent_shapes
        results = pl.pallas_call(
            lambda *refs, first=first, last=last: spread_kernel(first, last, *refs),
            out_shape=out_shape,
            in_specs=[VMEM] * 11,
            out_specs=[VMEM] * len(out_shape),
            scratch_shapes=[
                pltpu.VMEM((16, 2 * SIDE, SIDE), jnp.bfloat16),
                pltpu.VMEM((32, SIDE, SIDE), F32),
            ]
            + index_scratch
            + [pltpu.SemaphoreType.DMA((3,))],
            compiler_params=PARAMS,
        )(
            tiles, send_lists, tile_rows, tile_cols, mask if first else anchor, source,
            *received, parts,
        )
        if first:
            anchor, *results = results
        if last:
            source, parts = results
        else:
            source, *outs, rows = results
    parts = lax.all_to_all(parts, "cls", 0, 0)
    out = pl.pallas_call(
        last_kernel,
        out_shape=own_shape,
        in_specs=[VMEM, VMEM],
        out_specs=HBM,
        scratch_shapes=[pltpu.VMEM((8, SIDE, SIDE), F32), pltpu.SemaphoreType.DMA((8,))],
        compiler_params=PARAMS,
    )(source, parts)
    return out.reshape(8 * SIDE, SIDE)


def solution(mesh):
    split_mesh = Mesh(
        mesh.devices.reshape(mesh.shape["dom"] // 2, 2, mesh.shape["cls"]), ("chip", "core", "cls")
    )
    dom = ("chip", "core")
    return jax.shard_map(
        on_device,
        mesh=split_mesh,
        in_specs=(P(dom, None, None), P(dom), P(dom), P(dom, None, None), P(dom), P(dom, "cls")),
        out_specs=P(dom, "cls"),
        check_vma=False,
    )
```

time: 114 us -> 116 us (1.018)
  the two profiles are of different devices: /device:TPU:1 before, /device:TPU:16 now
where the time goes in v8:
time: 116 us
  starting transfers between devices  49.2 us (42%)
  blocking collectives  46.5 us (40%)
  waiting for transfers between devices  11 us (9%)
  Pallas kernels  8.63 us (7%)
    ppermute x12, starting transfers between devices, on_device(): received = [lax.ppermute(out, dom, swap) for out, swap in zip(outs, swaps)]  49.2 us
    all_to_all x4, blocking collectives, on_device(): parts = lax.all_to_all(parts, 'cls', 0, 0)  46.5 us
    ppermute x12, waiting for transfers between devices, on_device(): received = [lax.ppermute(out, dom, swap) for out, swap in zip(outs, swaps)]  11 us
    pallas_call x3, Pallas kernels, on_device(): pl.pallas_call(lambda *refs, first=first, last=last: spread_kernel(first,...  5.53 us
  transfers between devices with their start and end apart: 12, of which 3 were waited for; matrix products, arithmetic and copies ran while one was open for 0% of the time, Pallas kernels for 0%

profile of v8, /device:TPU:16, one launch (start us, length us, event | category | flops | bytes accessed | tf_op | source)
XLA Modules:
  0.0 115.5 jit_solution(11885047347051495864)
XLA Ops:
  0.0 0.0 copy-start
  0.0 2.0 %shard_map.64 = (f32[8,128,128]{2,1,0:T(8,128)S(1)}, s32[1,2,4]{2,1,0:T(2,128)S(1)}, s32[32]{0:T(128)S(1)}, s32[32]{0:T(128)S(1)}, s32[8,128]{1,0:T(8,128)S(1)},...) custom-call(f32[8,128,128]{2,1,0:T(8,128)} %bitcast.4, ...), custom_call_target="tpu_custom_call" | custom-call | flops 1048576 | bytes 1048576 | tf_op jit(solution)/shard_map/pallas_call | solution.py:204
  2.0 19.6 %collective-permute-start = (f32[264,128]{1,0:T(8,128)S(1)}, f32[264,128]{1,0:T(8,128)S(1)}, u32[]{:S(2)}, u32[]{:S(2)}) collective-permute-start(f32[264,128]{1,0:T(8,128)S(1)} %get-tuple-element.35), channel_id=1, source_target_pairs={{0,1008},{8,1016},{16,32},{24,40},{32,16},{40,24},{48,64},{56,72},... | collective-permute-start | bytes 405512 | tf_op jit(solution)/shard_map/ppermute | solution.py:219
  21.6 1.9 %collective-permute-start.1 = (f32[264,128]{1,0:T(8,128)S(1)}, f32[264,128]{1,0:T(8,128)S(1)}, u32[]{:S(2)}, u32[]{:S(2)}) collective-permute-start(f32[264,128]{1,0:T(8,128)S(1)} %get-tuple-element.36), channel_id=1, source_target_pairs={{0,16},{8,24},{16,0},{24,8},{32,48},{40,56},{48,32},{56,40},{64,80... | collective-permute-start | bytes 405512 | tf_op jit(solution)/shard_map/ppermute | solution.py:219
  23.5 1.9 %collective-permute-start.2 = (f32[264,128]{1,0:T(8,128)S(1)}, f32[264,128]{1,0:T(8,128)S(1)}, u32[]{:S(2)}, u32[]{:S(2)}) collective-permute-start(f32[264,128]{1,0:T(8,128)S(1)} %get-tuple-element.37), channel_id=1, source_target_pairs={{0,1016},{8,16},{16,8},{24,32},{32,24},{40,48},{48,40},{56,64},{64... | collective-permute-start | bytes 405512 | tf_op jit(solution)/shard_map/ppermute | solution.py:219
  25.5 4.0 %collective-permute-start.3 = (f32[264,128]{1,0:T(8,128)S(1)}, f32[264,128]{1,0:T(8,128)S(1)}, u32[]{:S(2)}, u32[]{:S(2)}) collective-permute-start(f32[264,128]{1,0:T(8,128)S(1)} %get-tuple-element.38), channel_id=1, source_target_pairs={{0,8},{8,0},{16,24},{24,16},{32,40},{40,32},{48,56},{56,48},{64,72... | collective-permute-start | bytes 405512 | tf_op jit(solution)/shard_map/ppermute | solution.py:219
  29.5 0.0 collective-permute-done.in0.refs_6_
  29.5 0.0 collective-permute-done.1.in1.refs_7_
  29.5 3.7 %collective-permute-done.2.in2.refs_8_ = f32[264,128]{1,0:T(8,128)S(1)} collective-permute-done((f32[264,128]{1,0:T(8,128)S(1)}, f32[264,128]{1,0:T(8,128)S(1)}, u32[]{:S(2)}, u32[]{:S(2)}) %collective-permute-start.2) | collective-permute-done | bytes 135200 | tf_op jit(solution)/shard_map/ppermute | solution.py:219
  33.2 0.0 collective-permute-done.3.in3.refs_9_
  33.2 14.6 %all_to_all.20.refs_10_ = f32[8,16,128]{2,1,0:T(8,128)S(1)} all-to-all(f32[8,16,128]{2,1,0:T(8,128)S(1)} %shard_map.65), channel_id=1, replica_groups=mesh['chip'=64,'core'=2,'cls'=8] {'cls'}, dimensions={0} | all-to-all | bytes 131072 | tf_op jit(solution)/shard_map/all_to_all | solution.py:227
  47.8 0.0 copy-done
  47.8 2.0 %shard_map.66 = (f32[8,128,128]{2,1,0:T(8,128)S(1)}, f32[8,128,128]{2,1,0:T(8,128)S(1)}, f32[264,128]{1,0:T(8,128)S(1)}, f32[264,128]{1,0:T(8,128)S(1)}, f32[264...) custom-call(bf16[32,128,128]{2,1,0:T(8,128)(2,1)S(1)} %copy-done, ...), custom_call_target="tpu_custom_call" | custom-call | tf_op jit(solution)/shard_map/pallas_call | solution.py:230
  49.8 2.5 %collective-permute-start.4 = (f32[264,128]{1,0:T(8,128)S(1)}, f32[264,128]{1,0:T(8,128)S(1)}, u32[]{:S(2)}, u32[]{:S(2)}) collective-permute-start(f32[264,128]{1,0:T(8,128)S(1)} %get-tuple-element.42), channel_id=1, source_target_pairs={{0,1008},{8,1016},{16,32},{24,40},{32,16},{40,24},{48,64},{56,72},... | collective-permute-start | bytes 405512 | tf_op jit(solution)/shard_map/ppermute | solution.py:219
  52.4 1.9 %collective-permute-start.5 = (f32[264,128]{1,0:T(8,128)S(1)}, f32[264,128]{1,0:T(8,128)S(1)}, u32[]{:S(2)}, u32[]{:S(2)}) collective-permute-start(f32[264,128]{1,0:T(8,128)S(1)} %get-tuple-element.43), channel_id=1, source_target_pairs={{0,16},{8,24},{16,0},{24,8},{32,48},{40,56},{48,32},{56,40},{64,80... | collective-permute-start | bytes 405512 | tf_op jit(solution)/shard_map/ppermute | solution.py:219
  54.3 2.3 %collective-permute-start.6 = (f32[264,128]{1,0:T(8,128)S(1)}, f32[264,128]{1,0:T(8,128)S(1)}, u32[]{:S(2)}, u32[]{:S(2)}) collective-permute-start(f32[264,128]{1,0:T(8,128)S(1)} %get-tuple-element.44), channel_id=1, source_target_pairs={{0,1016},{8,16},{16,8},{24,32},{32,24},{40,48},{48,40},{56,64},{64... | collective-permute-start | bytes 405512 | tf_op jit(solution)/shard_map/ppermute | solution.py:219
  56.6 3.7 %collective-permute-start.7 = (f32[264,128]{1,0:T(8,128)S(1)}, f32[264,128]{1,0:T(8,128)S(1)}, u32[]{:S(2)}, u32[]{:S(2)}) collective-permute-start(f32[264,128]{1,0:T(8,128)S(1)} %get-tuple-element.45), channel_id=1, source_target_pairs={{0,8},{8,0},{16,24},{24,16},{32,40},{40,32},{48,56},{56,48},{64,72... | collective-permute-start | bytes 405512 | tf_op jit(solution)/shard_map/ppermute | solution.py:219
  60.3 0.0 collective-permute-done.4.in0.refs_6_
  60.3 0.0 collective-permute-done.5.in1.refs_7_
  60.3 3.7 %collective-permute-done.6.in2.refs_8_ = f32[264,128]{1,0:T(8,128)S(1)} collective-permute-done((f32[264,128]{1,0:T(8,128)S(1)}, f32[264,128]{1,0:T(8,128)S(1)}, u32[]{:S(2)}, u32[]{:S(2)}) %collective-permute-start.6) | collective-permute-done | bytes 135200 | tf_op jit(solution)/shard_map/ppermute | solution.py:219
  63.9 0.0 collective-permute-done.7.in3.refs_9_
  64.0 10.8 %all_to_all.21.refs_10_ = f32[8,16,128]{2,1,0:T(8,128)S(1)} all-to-all(f32[8,16,128]{2,1,0:T(8,128)S(1)} %shard_map.67), channel_id=1, replica_groups=mesh['chip'=64,'core'=2,'cls'=8] {'cls'}, dimensions={0} | all-to-all | bytes 131072 | tf_op jit(solution)/shard_map/all_to_all | solution.py:227
  74.7 1.9 %shard_map.68 = (f32[8,128,128]{2,1,0:T(8,128)S(1)}, f32[264,128]{1,0:T(8,128)S(1)}, f32[264,128]{1,0:T(8,128)S(1)}, f32[264,128]{1,0:T(8,128)S(1)}, f32[264,128]{1,0:T(8,128)S(1)}, /*index=5*/f32[8,128]{1,0:T(8,128)S(1)}) custom-call(bf16[32,128,128]{2,1,0:T(8,128)(2,1)S(1)} %copy-done, s32[1,2,4]{2,1,0:T(2,128)S(1)} %get-tuple-element.30.refs_1_, ...), custom_call_target="tpu_custom_call" | custom-call | tf_op jit(solution)/shard_map/pallas_call | solution.py:230
  76.7 3.4 %collective-permute-start.8 = (f32[264,128]{1,0:T(8,128)S(1)}, f32[264,128]{1,0:T(8,128)S(1)}, u32[]{:S(2)}, u32[]{:S(2)}) collective-permute-start(f32[264,128]{1,0:T(8,128)S(1)} %get-tuple-element.48), channel_id=1, source_target_pairs={{0,1008},{8,1016},{16,32},{24,40},{32,16},{40,24},{48,64},{56,72},... | collective-permute-start | bytes 405512 | tf_op jit(solution)/shard_map/ppermute | solution.py:219
  80.1 1.9 %collective-permute-start.9 = (f32[264,128]{1,0:T(8,128)S(1)}, f32[264,128]{1,0:T(8,128)S(1)}, u32[]{:S(2)}, u32[]{:S(2)}) collective-permute-start(f32[264,128]{1,0:T(8,128)S(1)} %get-tuple-element.49), channel_id=1, source_target_pairs={{0,16},{8,24},{16,0},{24,8},{32,48},{40,56},{48,32},{56,40},{64,80... | collective-permute-start | bytes 405512 | tf_op jit(solution)/shard_map/ppermute | solution.py:219
  82.0 2.8 %collective-permute-start.10 = (f32[264,128]{1,0:T(8,128)S(1)}, f32[264,128]{1,0:T(8,128)S(1)}, u32[]{:S(2)}, u32[]{:S(2)}) collective-permute-start(f32[264,128]{1,0:T(8,128)S(1)} %get-tuple-element.50), channel_id=1, source_target_pairs={{0,1016},{8,16},{16,8},{24,32},{32,24},{40,48},{48,40},{56,64},{64... | collective-permute-start | bytes 405512 | tf_op jit(solution)/shard_map/ppermute | solution.py:219
  84.8 3.2 %collective-permute-start.11 = (f32[264,128]{1,0:T(8,128)S(1)}, f32[264,128]{1,0:T(8,128)S(1)}, u32[]{:S(2)}, u32[]{:S(2)}) collective-permute-start(f32[264,128]{1,0:T(8,128)S(1)} %get-tuple-element.51), channel_id=1, source_target_pairs={{0,8},{8,0},{16,24},{24,16},{32,40},{40,32},{48,56},{56,48},{64,72... | collective-permute-start | bytes 405512 | tf_op jit(solution)/shard_map/ppermute | solution.py:219
  88.0 0.0 collective-permute-done.8.in0.refs_6_
  88.0 0.0 collective-permute-done.9.in1.refs_7_
  88.0 3.7 %collective-permute-done.10.in2.refs_8_ = f32[264,128]{1,0:T(8,128)S(1)} collective-permute-done((f32[264,128]{1,0:T(8,128)S(1)}, f32[264,128]{1,0:T(8,128)S(1)}, u32[]{:S(2)}, u32[]{:S(2)}) %collective-permute-start.10) | collective-permute-done | bytes 135200 | tf_op jit(solution)/shard_map/ppermute | solution.py:219
  91.7 0.0 collective-permute-done.11.in3.refs_9_
  91.7 10.7 %all_to_all.22.refs_10_ = f32[8,16,128]{2,1,0:T(8,128)S(1)} all-to-all(f32[8,16,128]{2,1,0:T(8,128)S(1)} %shard_map.69), channel_id=1, replica_groups=mesh['chip'=64,'core'=2,'cls'=8] {'cls'}, dimensions={0} | all-to-all | bytes 131072 | tf_op jit(solution)/shard_map/all_to_all | solution.py:227
  102.4 1.6 %shard_map.70 = (f32[8,128,128]{2,1,0:T(8,128)S(1)}, f32[8,8,128]{2,1,0:T(8,128)S(1)}) custom-call(bf16[32,128,128]{2,1,0:T(8,128)(2,1)S(1)} %copy-done, s32[1,2,4]{2,1,0:T(2,128)S(1)} %get-tuple-element.30.refs_1_, s32[32]{0:T(128)S(1)} %get-tuple-element.31.refs_2_, s32[32]{0:T(128)S(1)} %get-tuple-element.32.refs_3_, ...), custom_call_target="tpu_custom_call" | custom-call | tf_op jit(solution)/shard_map/pallas_call | solution.py:230
  104.0 10.4 %all_to_all.23.parts = f32[8,8,128]{2,1,0:T(8,128)S(1)} all-to-all(f32[8,8,128]{2,1,0:T(8,128)S(1)} %get-tuple-element.54), channel_id=1, replica_groups=mesh['chip'=64,'core'=2,'cls'=8] {'cls'}, dimensions={0} | all-to-all | bytes 65536 | tf_op jit(solution)/shard_map/all_to_all | solution.py:252
  114.4 1.1 shard_map.71
  (3 shorter events, 0.0 us)
Async XLA Ops:
  0.0 47.8 %copy-start = (bf16[32,128,128]{2,1,0:T(8,128)(2,1)S(1)}, bf16[32,128,128]{2,1,0:T(8,128)(2,1)}, u32[]{:S(2)}) copy-start(bf16[32,128,128]{2,1,0:T(8,128)(2,1)} %refs_0_.5) | copy-start | bytes 3145732
  2.0 27.5 %collective-permute-start = (f32[264,128]{1,0:T(8,128)S(1)}, f32[264,128]{1,0:T(8,128)S(1)}, u32[]{:S(2)}, u32[]{:S(2)}) collective-permute-start(f32[264,128]{1,0:T(8,128)S(1)} %get-tuple-element.35), channel_id=1, source_target_pairs={{0,1008},{8,1016},{16,32},{24,40},{32,16},{40,24},{48,64},{56,72},... | collective-permute-start | bytes 405512 | tf_op jit(solution)/shard_map/ppermute | solution.py:219
  21.6 7.9 %collective-permute-start.1 = (f32[264,128]{1,0:T(8,128)S(1)}, f32[264,128]{1,0:T(8,128)S(1)}, u32[]{:S(2)}, u32[]{:S(2)}) collective-permute-start(f32[264,128]{1,0:T(8,128)S(1)} %get-tuple-element.36), channel_id=1, source_target_pairs={{0,16},{8,24},{16,0},{24,8},{32,48},{40,56},{48,32},{56,40},{64,80... | collective-permute-start | bytes 405512 | tf_op jit(solution)/shard_map/ppermute | solution.py:219
  23.5 9.7 %collective-permute-start.2 = (f32[264,128]{1,0:T(8,128)S(1)}, f32[264,128]{1,0:T(8,128)S(1)}, u32[]{:S(2)}, u32[]{:S(2)}) collective-permute-start(f32[264,128]{1,0:T(8,128)S(1)} %get-tuple-element.37), channel_id=1, source_target_pairs={{0,1016},{8,16},{16,8},{24,32},{32,24},{40,48},{48,40},{56,64},{64... | collective-permute-start | bytes 405512 | tf_op jit(solution)/shard_map/ppermute | solution.py:219
  25.5 7.7 %collective-permute-start.3 = (f32[264,128]{1,0:T(8,128)S(1)}, f32[264,128]{1,0:T(8,128)S(1)}, u32[]{:S(2)}, u32[]{:S(2)}) collective-permute-start(f32[264,128]{1,0:T(8,128)S(1)} %get-tuple-element.38), channel_id=1, source_target_pairs={{0,8},{8,0},{16,24},{24,16},{32,40},{40,32},{48,56},{56,48},{64,72... | collective-permute-start | bytes 405512 | tf_op jit(solution)/shard_map/ppermute | solution.py:219
  49.8 10.4 %collective-permute-start.4 = (f32[264,128]{1,0:T(8,128)S(1)}, f32[264,128]{1,0:T(8,128)S(1)}, u32[]{:S(2)}, u32[]{:S(2)}) collective-permute-start(f32[264,128]{1,0:T(8,128)S(1)} %get-tuple-element.42), channel_id=1, source_target_pairs={{0,1008},{8,1016},{16,32},{24,40},{32,16},{40,24},{48,64},{56,72},... | collective-permute-start | bytes 405512 | tf_op jit(solution)/shard_map/ppermute | solution.py:219
  52.4 7.9 %collective-permute-start.5 = (f32[264,128]{1,0:T(8,128)S(1)}, f32[264,128]{1,0:T(8,128)S(1)}, u32[]{:S(2)}, u32[]{:S(2)}) collective-permute-start(f32[264,128]{1,0:T(8,128)S(1)} %get-tuple-element.43), channel_id=1, source_target_pairs={{0,16},{8,24},{16,0},{24,8},{32,48},{40,56},{48,32},{56,40},{64,80... | collective-permute-start | bytes 405512 | tf_op jit(solution)/shard_map/ppermute | solution.py:219
  54.3 9.7 %collective-permute-start.6 = (f32[264,128]{1,0:T(8,128)S(1)}, f32[264,128]{1,0:T(8,128)S(1)}, u32[]{:S(2)}, u32[]{:S(2)}) collective-permute-start(f32[264,128]{1,0:T(8,128)S(1)} %get-tuple-element.44), channel_id=1, source_target_pairs={{0,1016},{8,16},{16,8},{24,32},{32,24},{40,48},{48,40},{56,64},{64... | collective-permute-start | bytes 405512 | tf_op jit(solution)/shard_map/ppermute | solution.py:219
  56.6 7.4 %collective-permute-start.7 = (f32[264,128]{1,0:T(8,128)S(1)}, f32[264,128]{1,0:T(8,128)S(1)}, u32[]{:S(2)}, u32[]{:S(2)}) collective-permute-start(f32[264,128]{1,0:T(8,128)S(1)} %get-tuple-element.45), channel_id=1, source_target_pairs={{0,8},{8,0},{16,24},{24,16},{32,40},{40,32},{48,56},{56,48},{64,72... | collective-permute-start | bytes 405512 | tf_op jit(solution)/shard_map/ppermute | solution.py:219
  76.7 11.3 %collective-permute-start.8 = (f32[264,128]{1,0:T(8,128)S(1)}, f32[264,128]{1,0:T(8,128)S(1)}, u32[]{:S(2)}, u32[]{:S(2)}) collective-permute-start(f32[264,128]{1,0:T(8,128)S(1)} %get-tuple-element.48), channel_id=1, source_target_pairs={{0,1008},{8,1016},{16,32},{24,40},{32,16},{40,24},{48,64},{56,72},... | collective-permute-start | bytes 405512 | tf_op jit(solution)/shard_map/ppermute | solution.py:219
  80.1 7.9 %collective-permute-start.9 = (f32[264,128]{1,0:T(8,128)S(1)}, f32[264,128]{1,0:T(8,128)S(1)}, u32[]{:S(2)}, u32[]{:S(2)}) collective-permute-start(f32[264,128]{1,0:T(8,128)S(1)} %get-tuple-element.49), channel_id=1, source_target_pairs={{0,16},{8,24},{16,0},{24,8},{32,48},{40,56},{48,32},{56,40},{64,80... | collective-permute-start | bytes 405512 | tf_op jit(solution)/shard_map/ppermute | solution.py:219
  82.0 9.7 %collective-permute-start.10 = (f32[264,128]{1,0:T(8,128)S(1)}, f32[264,128]{1,0:T(8,128)S(1)}, u32[]{:S(2)}, u32[]{:S(2)}) collective-permute-start(f32[264,128]{1,0:T(8,128)S(1)} %get-tuple-element.50), channel_id=1, source_target_pairs={{0,1016},{8,16},{16,8},{24,32},{32,24},{40,48},{48,40},{56,64},{64... | collective-permute-start | bytes 405512 | tf_op jit(solution)/shard_map/ppermute | solution.py:219
  84.8 6.9 %collective-permute-start.11 = (f32[264,128]{1,0:T(8,128)S(1)}, f32[264,128]{1,0:T(8,128)S(1)}, u32[]{:S(2)}, u32[]{:S(2)}) collective-permute-start(f32[264,128]{1,0:T(8,128)S(1)} %get-tuple-element.51), channel_id=1, source_target_pairs={{0,8},{8,0},{16,24},{24,16},{32,40},{40,32},{48,56},{56,48},{64,72... | collective-permute-start | bytes 405512 | tf_op jit(solution)/shard_map/ppermute | solution.py:219

commit v9 on v7

--- a/solution.py
+++ b/solution.py
@@ -85,27 +85,28 @@
     return copies
 
 
-def first_kernel(labels, send, kept, out0, out1, out2, out3, rows, send_here, sems):
-    pairs = [(labels.at[block], kept.at[block]) for block in range(8)]
-    copies = copy_all([(send, send_here)] + pairs, sems)
+def first_kernel(labels, send, rows, cols, mask, kept, plan, mask_kept, *refs):
+    *outs, sums_out, send_here, rows_here, cols_here, plan_here, sems = refs
+    pairs = [(send, send_here), (rows, rows_here), (cols, cols_here)]
+    pairs += [(labels.at[block], kept.at[block]) for block in range(8)]
+    copies = copy_all(pairs + [(mask, mask_kept)], sems)
+    for copy in copies[:3]:
+        copy.wait()
+    for place, entry in enumerate(plan_entries(rows_here, cols_here, send_here)):
+        plan_here[place] = entry
+    plan_copy = pltpu.make_async_copy(plan_here, plan, sems.at[12])
+    plan_copy.start()
     sums = []
     for block in range(8):
-        copies[1 + block].wait()
+        copies[3 + block].wait()
         sums.append(lane_sums(kept[block]))
-    copies[0].wait()
     block_of = lambda offset, within: send_here[0, within, offset]
-    fill_swaps(kept, jnp.concatenate(sums, axis=0), block_of, (out0, out1, out2, out3), rows)
-
-
-def plan_kernel(rows, cols, send, mask, plan, mask_kept, rows_here, cols_here, send_here, sems):
-    copies = copy_all([(rows, rows_here), (cols, cols_here), (send, send_here), (mask, mask_kept)], sems)
-    for copy in copies:
-        copy.wait()
-    for place, entry in enumerate(plan_entries(rows_here, cols_here, send_here)):
-        plan[place] = entry
-
-
-def mass_kernel(sums, in0, in1, in2, in3, plan, parts):
+    fill_swaps(kept, jnp.concatenate(sums, axis=0), block_of, outs, sums_out)
+    copies[11].wait()
+    plan_copy.wait()
+
+
+def mass_kernel(sums, in0, in1, in2, in3, parts):
     received = [ref[2 * SIDE : 2 * SIDE + 2, :] for ref in (in0, in1, in2, in3)]
     partial = jnp.concatenate([sums[...]] + received, axis=0)
     for share in range(8):
@@ -226,33 +227,22 @@
             seed_mask.reshape(8, SIDE),
         )
     ]
-    send_scratch = pltpu.SMEM((1, 2, 4), jnp.int32)
-    source, *outs, rows = pl.pallas_call(
+    plan_shape = jax.ShapeDtypeStruct((72,), jnp.int32)
+    source, plan, mask, *outs, rows = pl.pallas_call(
         first_kernel,
-        out_shape=[own_shape] + sent_shapes,
-        in_specs=[HBM] * 2,
-        out_specs=[VMEM] * 6,
-        scratch_shapes=[send_scratch, pltpu.SemaphoreType.DMA((9,))],
-        compiler_params=PARAMS,
-        cost_estimate=pl.CostEstimate(flops=1 << 20, bytes_accessed=1 << 20, transcendentals=0),
-    )(blocks, send_lists)
-    plan, mask = pl.pallas_call(
-        plan_kernel,
-        out_shape=[
-            jax.ShapeDtypeStruct((72,), jnp.int32),
-            jax.ShapeDtypeStruct((8, SIDE), jnp.int32),
-        ],
-        in_specs=[HBM] * 4,
-        out_specs=[SMEM, VMEM],
+        out_shape=[own_shape, plan_shape, jax.ShapeDtypeStruct((8, SIDE), jnp.int32)] + sent_shapes,
+        in_specs=[HBM] * 5,
+        out_specs=[VMEM] * 8,
         scratch_shapes=[
+            pltpu.SMEM((1, 2, 4), jnp.int32),
             pltpu.SMEM((32,), jnp.int32),
             pltpu.SMEM((32,), jnp.int32),
-            send_scratch,
-            pltpu.SemaphoreType.DMA((4,)),
+            pltpu.SMEM((72,), jnp.int32),
+            pltpu.SemaphoreType.DMA((13,)),
         ],
         compiler_params=PARAMS,
         cost_estimate=pl.CostEstimate(flops=1 << 20, bytes_accessed=1 << 20, transcendentals=0),
-    )(tile_rows, tile_cols, send_lists, mask)
+    )(blocks, send_lists, tile_rows, tile_cols, mask)
     anchor = None
     for iteration in range(ITERS):
         first = iteration == 0
@@ -261,10 +251,10 @@
         parts = pl.pallas_call(
             mass_kernel,
             out_shape=shape(8, 16, SIDE),
-            in_specs=[VMEM] * 6,
+            in_specs=[VMEM] * 5,
             out_specs=VMEM,
             compiler_params=PARAMS,
-        )(rows, *received, plan)
+        )(rows, *received)
         parts = lax.all_to_all(parts, "cls", 0, 0)
         out_shape = [own_shape] * (2 if first else 1)
         out_shape += [shape(8, 8, SIDE)] if last else sent_shapes

time: 114 us -> 114 us (level)
  Pallas kernels: 9.71 us -> 8.28 us
    pallas_call x2 -> x1, Pallas kernels: 3.49 us -> 2.06 us  [on_device(): pl.pallas_call(first_kernel, out_shape=[own_shape, plan_shape, jax.ShapeD...]
  transfers between devices with their start and end apart: 12 -> 12, of which waited for: 3 -> 5; matrix products, arithmetic and copies ran while one was open for 0% -> 0% of each run, Pallas kernels for 1% -> 0%
where the time goes in v9:
time: 114 us; the launch traced here: 112 us
  starting transfers between devices  58.2 us (51%)
  blocking collectives  42.7 us (37%)
  Pallas kernels  8.28 us (7%)
  waiting for transfers between devices  2.85 us (2%)
    ppermute x12, starting transfers between devices, on_device(): received = [lax.ppermute(out, dom, swap) for out, swap in zip(outs, swaps)]  58.2 us
    all_to_all x4, blocking collectives, on_device(): parts = lax.all_to_all(parts, 'cls', 0, 0)  42.7 us
    pallas_call x3, Pallas kernels, on_device(): pl.pallas_call(lambda *refs, first=first, last=last: spread_kernel(first,...  5.09 us
    ppermute x12, waiting for transfers between devices, on_device(): received = [lax.ppermute(out, dom, swap) for out, swap in zip(outs, swaps)]  2.85 us
  transfers between devices with their start and end apart: 12, of which 5 were waited for; matrix products, arithmetic and copies ran while one was open for 0% of the time, Pallas kernels for 0%

profile of v9, /device:TPU:1, one launch (start us, length us, event | category | flops | bytes accessed | tf_op | source)
XLA Modules:
  0.0 112.2 jit_solution(17403322413960820530)
XLA Ops:
  0.0 0.0 copy-start
  0.0 2.1 %shard_map.64 = (f32[8,128,128]{2,1,0:T(8,128)S(1)}, s32[72]{0:T(128)S(1)}, s32[8,128]{1,0:T(8,128)S(1)}, f32[264,128]{1,0:T(8,128)S(1)}, f32[264,128]{1,0:T(8,1...) custom-call(f32[8,128,128]{2,1,0:T(8,128)} %bitcast.4, s32[1,2,4]{2,1,0:T(2,128)} %bitcast.6, ...), custom_call_target="tpu_custom_call" | custom-call | flops 1048576 | bytes 1048576 | tf_op jit(solution)/shard_map/pallas_call | solution.py:231
  2.1 20.2 %collective-permute-start = (f32[264,128]{1,0:T(8,128)S(1)}, f32[264,128]{1,0:T(8,128)S(1)}, u32[]{:S(2)}, u32[]{:S(2)}) collective-permute-start(f32[264,128]{1,0:T(8,128)S(1)} %get-tuple-element.31), channel_id=1, source_target_pairs={{0,1008},{8,1016},{16,32},{24,40},{32,16},{40,24},{48,64},{56,72},... | collective-permute-start | bytes 405512 | tf_op jit(solution)/shard_map/ppermute | solution.py:250
  22.3 1.9 %collective-permute-start.1 = (f32[264,128]{1,0:T(8,128)S(1)}, f32[264,128]{1,0:T(8,128)S(1)}, u32[]{:S(2)}, u32[]{:S(2)}) collective-permute-start(f32[264,128]{1,0:T(8,128)S(1)} %get-tuple-element.32), channel_id=1, source_target_pairs={{0,1016},{8,16},{16,8},{24,32},{32,24},{40,48},{48,40},{56,64},{64... | collective-permute-start | bytes 405512 | tf_op jit(solution)/shard_map/ppermute | solution.py:250
  24.2 1.9 %collective-permute-start.2 = (f32[264,128]{1,0:T(8,128)S(1)}, f32[264,128]{1,0:T(8,128)S(1)}, u32[]{:S(2)}, u32[]{:S(2)}) collective-permute-start(f32[264,128]{1,0:T(8,128)S(1)} %get-tuple-element.33), channel_id=1, source_target_pairs={{0,16},{8,24},{16,0},{24,8},{32,48},{40,56},{48,32},{56,40},{64,80... | collective-permute-start | bytes 405512 | tf_op jit(solution)/shard_map/ppermute | solution.py:250
  26.1 4.0 %collective-permute-start.3 = (f32[264,128]{1,0:T(8,128)S(1)}, f32[264,128]{1,0:T(8,128)S(1)}, u32[]{:S(2)}, u32[]{:S(2)}) collective-permute-start(f32[264,128]{1,0:T(8,128)S(1)} %get-tuple-element.34), channel_id=1, source_target_pairs={{0,8},{8,0},{16,24},{24,16},{32,40},{40,32},{48,56},{56,48},{64,72... | collective-permute-start | bytes 405512 | tf_op jit(solution)/shard_map/ppermute | solution.py:250
  30.1 0.0 collective-permute-done.in0.refs_4_
  30.2 0.0 collective-permute-done.1.in1.refs_5_
  30.2 0.2 collective-permute-done.2.in2.refs_6_
  30.4 0.7 collective-permute-done.3.in3.refs_7_
  31.1 14.3 %all_to_all.20.refs_8_ = f32[8,16,128]{2,1,0:T(8,128)S(1)} all-to-all(f32[8,16,128]{2,1,0:T(8,128)S(1)} %shard_map.65), channel_id=1, replica_groups=mesh['chip'=64,'core'=2,'cls'=8] {'cls'}, dimensions={0} | all-to-all | bytes 131072 | tf_op jit(solution)/shard_map/all_to_all | solution.py:258
  45.4 0.0 copy-done
  45.4 2.1 %shard_map.66 = (f32[8,128,128]{2,1,0:T(8,128)S(1)}, f32[8,128,128]{2,1,0:T(8,128)S(1)}, f32[264,128]{1,0:T(8,128)S(1)}, f32[264,128]{1,0:T(8,128)S(1)}, f32[264...) custom-call(bf16[32,128,128]{2,1,0:T(8,128)(2,1)S(1)} %copy-done, s32[72]{0:T(128)S(1)} %get-tuple-element.28.refs_1_, ...), custom_call_target="tpu_custom_call" | custom-call | tf_op jit(solution)/shard_map/pallas_call | solution.py:261
  47.5 6.7 %collective-permute-start.4 = (f32[264,128]{1,0:T(8,128)S(1)}, f32[264,128]{1,0:T(8,128)S(1)}, u32[]{:S(2)}, u32[]{:S(2)}) collective-permute-start(f32[264,128]{1,0:T(8,128)S(1)} %get-tuple-element.38), channel_id=1, source_target_pairs={{0,1008},{8,1016},{16,32},{24,40},{32,16},{40,24},{48,64},{56,72},... | collective-permute-start | bytes 405512 | tf_op jit(solution)/shard_map/ppermute | solution.py:250
  54.2 1.9 %collective-permute-start.5 = (f32[264,128]{1,0:T(8,128)S(1)}, f32[264,128]{1,0:T(8,128)S(1)}, u32[]{:S(2)}, u32[]{:S(2)}) collective-permute-start(f32[264,128]{1,0:T(8,128)S(1)} %get-tuple-element.39), channel_id=1, source_target_pairs={{0,1016},{8,16},{16,8},{24,32},{32,24},{40,48},{48,40},{56,64},{64... | collective-permute-start | bytes 405512 | tf_op jit(solution)/shard_map/ppermute | solution.py:250
  56.1 2.0 %collective-permute-start.6 = (f32[264,128]{1,0:T(8,128)S(1)}, f32[264,128]{1,0:T(8,128)S(1)}, u32[]{:S(2)}, u32[]{:S(2)}) collective-permute-start(f32[264,128]{1,0:T(8,128)S(1)} %get-tuple-element.40), channel_id=1, source_target_pairs={{0,16},{8,24},{16,0},{24,8},{32,48},{40,56},{48,32},{56,40},{64,80... | collective-permute-start | bytes 405512 | tf_op jit(solution)/shard_map/ppermute | solution.py:250
  58.1 3.9 %collective-permute-start.7 = (f32[264,128]{1,0:T(8,128)S(1)}, f32[264,128]{1,0:T(8,128)S(1)}, u32[]{:S(2)}, u32[]{:S(2)}) collective-permute-start(f32[264,128]{1,0:T(8,128)S(1)} %get-tuple-element.41), channel_id=1, source_target_pairs={{0,8},{8,0},{16,24},{24,16},{32,40},{40,32},{48,56},{56,48},{64,72... | collective-permute-start | bytes 405512 | tf_op jit(solution)/shard_map/ppermute | solution.py:250
  62.1 0.0 collective-permute-done.4.in0.refs_4_
  62.1 0.0 collective-permute-done.5.in1.refs_5_
  62.1 0.0 collective-permute-done.6.in2.refs_6_
  62.1 0.9 collective-permute-done.7.in3.refs_7_
  63.1 9.6 %all_to_all.21.refs_8_ = f32[8,16,128]{2,1,0:T(8,128)S(1)} all-to-all(f32[8,16,128]{2,1,0:T(8,128)S(1)} %shard_map.67), channel_id=1, replica_groups=mesh['chip'=64,'core'=2,'cls'=8] {'cls'}, dimensions={0} | all-to-all | bytes 131072 | tf_op jit(solution)/shard_map/all_to_all | solution.py:258
  72.7 1.5 %shard_map.68 = (f32[8,128,128]{2,1,0:T(8,128)S(1)}, f32[264,128]{1,0:T(8,128)S(1)}, f32[264,128]{1,0:T(8,128)S(1)}, f32[264,128]{1,0:T(8,128)S(1)}, f32[264,128]{1,0:T(8,128)S(1)}, /*index=5*/f32[8,128]{1,0:T(8,128)S(1)}) custom-call(bf16[32,128,128]{2,1,0:T(8,128)(2,1)S(1)} %copy-done, s32[72]{0:T(128)S(1)} %get-tuple-element.28.refs_1_, ...), custom_call_target="tpu_custom_call" | custom-call | tf_op jit(solution)/shard_map/pallas_call | solution.py:261
  74.2 7.7 %collective-permute-start.8 = (f32[264,128]{1,0:T(8,128)S(1)}, f32[264,128]{1,0:T(8,128)S(1)}, u32[]{:S(2)}, u32[]{:S(2)}) collective-permute-start(f32[264,128]{1,0:T(8,128)S(1)} %get-tuple-element.44), channel_id=1, source_target_pairs={{0,1008},{8,1016},{16,32},{24,40},{32,16},{40,24},{48,64},{56,72},... | collective-permute-start | bytes 405512 | tf_op jit(solution)/shard_map/ppermute | solution.py:250
  81.9 1.9 %collective-permute-start.9 = (f32[264,128]{1,0:T(8,128)S(1)}, f32[264,128]{1,0:T(8,128)S(1)}, u32[]{:S(2)}, u32[]{:S(2)}) collective-permute-start(f32[264,128]{1,0:T(8,128)S(1)} %get-tuple-element.45), channel_id=1, source_target_pairs={{0,1016},{8,16},{16,8},{24,32},{32,24},{40,48},{48,40},{56,64},{64... | collective-permute-start | bytes 405512 | tf_op jit(solution)/shard_map/ppermute | solution.py:250
  83.9 1.9 %collective-permute-start.10 = (f32[264,128]{1,0:T(8,128)S(1)}, f32[264,128]{1,0:T(8,128)S(1)}, u32[]{:S(2)}, u32[]{:S(2)}) collective-permute-start(f32[264,128]{1,0:T(8,128)S(1)} %get-tuple-element.46), channel_id=1, source_target_pairs={{0,16},{8,24},{16,0},{24,8},{32,48},{40,56},{48,32},{56,40},{64,80... | collective-permute-start | bytes 405512 | tf_op jit(solution)/shard_map/ppermute | solution.py:250
  85.8 4.0 %collective-permute-start.11 = (f32[264,128]{1,0:T(8,128)S(1)}, f32[264,128]{1,0:T(8,128)S(1)}, u32[]{:S(2)}, u32[]{:S(2)}) collective-permute-start(f32[264,128]{1,0:T(8,128)S(1)} %get-tuple-element.47), channel_id=1, source_target_pairs={{0,8},{8,0},{16,24},{24,16},{32,40},{40,32},{48,56},{56,48},{64,72... | collective-permute-start | bytes 405512 | tf_op jit(solution)/shard_map/ppermute | solution.py:250
  89.8 0.0 collective-permute-done.8.in0.refs_4_
  89.8 0.0 collective-permute-done.9.in1.refs_5_
  89.8 0.6 collective-permute-done.10.in2.refs_6_
  90.4 0.4 collective-permute-done.11.in3.refs_7_
  90.8 9.6 %all_to_all.22.refs_8_ = f32[8,16,128]{2,1,0:T(8,128)S(1)} all-to-all(f32[8,16,128]{2,1,0:T(8,128)S(1)} %shard_map.69), channel_id=1, replica_groups=mesh['chip'=64,'core'=2,'cls'=8] {'cls'}, dimensions={0} | all-to-all | bytes 131072 | tf_op jit(solution)/shard_map/all_to_all | solution.py:258
  100.4 1.5 %shard_map.70 = (f32[8,128,128]{2,1,0:T(8,128)S(1)}, f32[8,8,128]{2,1,0:T(8,128)S(1)}) custom-call(bf16[32,128,128]{2,1,0:T(8,128)(2,1)S(1)} %copy-done, s32[72]{0:T(128)S(1)} %get-tuple-element.28.refs_1_, f32[8,128,128]{2,1,0:T(8,128)S(1)} %get-tuple-element.36.refs_2_, f32[8,128,128]{2,1,0:T(8,128)S(1)} %get-tuple-element.43.refs_3_, ...), custom_call_target="tpu_custom_call" | custom-call | tf_op jit(solution)/shard_map/pallas_call | solution.py:261
  101.9 9.2 %all_to_all.23.parts = f32[8,8,128]{2,1,0:T(8,128)S(1)} all-to-all(f32[8,8,128]{2,1,0:T(8,128)S(1)} %get-tuple-element.50), channel_id=1, replica_groups=mesh['chip'=64,'core'=2,'cls'=8] {'cls'}, dimensions={0} | all-to-all | bytes 65536 | tf_op jit(solution)/shard_map/all_to_all | solution.py:280
  111.1 1.1 shard_map.71
  (3 shorter events, 0.0 us)
Async XLA Ops:
  0.0 45.4 %copy-start = (bf16[32,128,128]{2,1,0:T(8,128)(2,1)S(1)}, bf16[32,128,128]{2,1,0:T(8,128)(2,1)}, u32[]{:S(2)}) copy-start(bf16[32,128,128]{2,1,0:T(8,128)(2,1)} %refs_0_.5) | copy-start | bytes 3145732
  2.1 28.1 %collective-permute-start = (f32[264,128]{1,0:T(8,128)S(1)}, f32[264,128]{1,0:T(8,128)S(1)}, u32[]{:S(2)}, u32[]{:S(2)}) collective-permute-start(f32[264,128]{1,0:T(8,128)S(1)} %get-tuple-element.31), channel_id=1, source_target_pairs={{0,1008},{8,1016},{16,32},{24,40},{32,16},{40,24},{48,64},{56,72},... | collective-permute-start | bytes 405512 | tf_op jit(solution)/shard_map/ppermute | solution.py:250
  22.3 7.9 %collective-permute-start.1 = (f32[264,128]{1,0:T(8,128)S(1)}, f32[264,128]{1,0:T(8,128)S(1)}, u32[]{:S(2)}, u32[]{:S(2)}) collective-permute-start(f32[264,128]{1,0:T(8,128)S(1)} %get-tuple-element.32), channel_id=1, source_target_pairs={{0,1016},{8,16},{16,8},{24,32},{32,24},{40,48},{48,40},{56,64},{64... | collective-permute-start | bytes 405512 | tf_op jit(solution)/shard_map/ppermute | solution.py:250
  24.2 6.2 %collective-permute-start.2 = (f32[264,128]{1,0:T(8,128)S(1)}, f32[264,128]{1,0:T(8,128)S(1)}, u32[]{:S(2)}, u32[]{:S(2)}) collective-permute-start(f32[264,128]{1,0:T(8,128)S(1)} %get-tuple-element.33), channel_id=1, source_target_pairs={{0,16},{8,24},{16,0},{24,8},{32,48},{40,56},{48,32},{56,40},{64,80... | collective-permute-start | bytes 405512 | tf_op jit(solution)/shard_map/ppermute | solution.py:250
  26.1 5.0 %collective-permute-start.3 = (f32[264,128]{1,0:T(8,128)S(1)}, f32[264,128]{1,0:T(8,128)S(1)}, u32[]{:S(2)}, u32[]{:S(2)}) collective-permute-start(f32[264,128]{1,0:T(8,128)S(1)} %get-tuple-element.34), channel_id=1, source_target_pairs={{0,8},{8,0},{16,24},{24,16},{32,40},{40,32},{48,56},{56,48},{64,72... | collective-permute-start | bytes 405512 | tf_op jit(solution)/shard_map/ppermute | solution.py:250
  47.5 14.6 %collective-permute-start.4 = (f32[264,128]{1,0:T(8,128)S(1)}, f32[264,128]{1,0:T(8,128)S(1)}, u32[]{:S(2)}, u32[]{:S(2)}) collective-permute-start(f32[264,128]{1,0:T(8,128)S(1)} %get-tuple-element.38), channel_id=1, source_target_pairs={{0,1008},{8,1016},{16,32},{24,40},{32,16},{40,24},{48,64},{56,72},... | collective-permute-start | bytes 405512 | tf_op jit(solution)/shard_map/ppermute | solution.py:250
  54.2 7.9 %collective-permute-start.5 = (f32[264,128]{1,0:T(8,128)S(1)}, f32[264,128]{1,0:T(8,128)S(1)}, u32[]{:S(2)}, u32[]{:S(2)}) collective-permute-start(f32[264,128]{1,0:T(8,128)S(1)} %get-tuple-element.39), channel_id=1, source_target_pairs={{0,1016},{8,16},{16,8},{24,32},{32,24},{40,48},{48,40},{56,64},{64... | collective-permute-start | bytes 405512 | tf_op jit(solution)/shard_map/ppermute | solution.py:250
  56.1 6.0 %collective-permute-start.6 = (f32[264,128]{1,0:T(8,128)S(1)}, f32[264,128]{1,0:T(8,128)S(1)}, u32[]{:S(2)}, u32[]{:S(2)}) collective-permute-start(f32[264,128]{1,0:T(8,128)S(1)} %get-tuple-element.40), channel_id=1, source_target_pairs={{0,16},{8,24},{16,0},{24,8},{32,48},{40,56},{48,32},{56,40},{64,80... | collective-permute-start | bytes 405512 | tf_op jit(solution)/shard_map/ppermute | solution.py:250
  58.1 4.9 %collective-permute-start.7 = (f32[264,128]{1,0:T(8,128)S(1)}, f32[264,128]{1,0:T(8,128)S(1)}, u32[]{:S(2)}, u32[]{:S(2)}) collective-permute-start(f32[264,128]{1,0:T(8,128)S(1)} %get-tuple-element.41), channel_id=1, source_target_pairs={{0,8},{8,0},{16,24},{24,16},{32,40},{40,32},{48,56},{56,48},{64,72... | collective-permute-start | bytes 405512 | tf_op jit(solution)/shard_map/ppermute | solution.py:250
  74.2 15.6 %collective-permute-start.8 = (f32[264,128]{1,0:T(8,128)S(1)}, f32[264,128]{1,0:T(8,128)S(1)}, u32[]{:S(2)}, u32[]{:S(2)}) collective-permute-start(f32[264,128]{1,0:T(8,128)S(1)} %get-tuple-element.44), channel_id=1, source_target_pairs={{0,1008},{8,1016},{16,32},{24,40},{32,16},{40,24},{48,64},{56,72},... | collective-permute-start | bytes 405512 | tf_op jit(solution)/shard_map/ppermute | solution.py:250
  81.9 7.9 %collective-permute-start.9 = (f32[264,128]{1,0:T(8,128)S(1)}, f32[264,128]{1,0:T(8,128)S(1)}, u32[]{:S(2)}, u32[]{:S(2)}) collective-permute-start(f32[264,128]{1,0:T(8,128)S(1)} %get-tuple-element.45), channel_id=1, source_target_pairs={{0,1016},{8,16},{16,8},{24,32},{32,24},{40,48},{48,40},{56,64},{64... | collective-permute-start | bytes 405512 | tf_op jit(solution)/shard_map/ppermute | solution.py:250
  83.9 6.5 %collective-permute-start.10 = (f32[264,128]{1,0:T(8,128)S(1)}, f32[264,128]{1,0:T(8,128)S(1)}, u32[]{:S(2)}, u32[]{:S(2)}) collective-permute-start(f32[264,128]{1,0:T(8,128)S(1)} %get-tuple-element.46), channel_id=1, source_target_pairs={{0,16},{8,24},{16,0},{24,8},{32,48},{40,56},{48,32},{56,40},{64,80... | collective-permute-start | bytes 405512 | tf_op jit(solution)/shard_map/ppermute | solution.py:250
  85.8 5.0 %collective-permute-start.11 = (f32[264,128]{1,0:T(8,128)S(1)}, f32[264,128]{1,0:T(8,128)S(1)}, u32[]{:S(2)}, u32[]{:S(2)}) collective-permute-start(f32[264,128]{1,0:T(8,128)S(1)} %get-tuple-element.47), channel_id=1, source_target_pairs={{0,8},{8,0},{16,24},{24,16},{32,40},{40,32},{48,56},{56,48},{64,72... | collective-permute-start | bytes 405512 | tf_op jit(solution)/shard_map/ppermute | solution.py:250

commit v10 on v9

--- a/solution.py
+++ b/solution.py
@@ -72,8 +72,8 @@
             out[2 * SIDE + within : 2 * SIDE + within + 1, :] = rows[pl.ds(block, 1), :]
 
 
-def lane_sums(block):
-    return jnp.sum(jnp.transpose(block), axis=0, keepdims=True)
+def class_sums(block):
+    return jnp.sum(block, axis=0, keepdims=True)
 
 
 def copy_all(pairs, sems):
@@ -86,9 +86,9 @@
 
 
 def first_kernel(labels, send, rows, cols, mask, kept, plan, mask_kept, *refs):
-    *outs, sums_out, send_here, rows_here, cols_here, plan_here, sems = refs
+    *outs, sums_out, fetched, send_here, rows_here, cols_here, plan_here, sems = refs
     pairs = [(send, send_here), (rows, rows_here), (cols, cols_here)]
-    pairs += [(labels.at[block], kept.at[block]) for block in range(8)]
+    pairs += [(labels.at[block], fetched.at[block]) for block in range(8)]
     copies = copy_all(pairs + [(mask, mask_kept)], sems)
     for copy in copies[:3]:
         copy.wait()
@@ -99,7 +99,9 @@
     sums = []
     for block in range(8):
         copies[3 + block].wait()
-        sums.append(lane_sums(kept[block]))
+        value = jnp.transpose(fetched[block])
+        kept[block] = value
+        sums.append(class_sums(value))
     block_of = lambda offset, within: send_here[0, within, offset]
     fill_swaps(kept, jnp.concatenate(sums, axis=0), block_of, outs, sums_out)
     copies[11].wait()
@@ -111,12 +113,6 @@
     partial = jnp.concatenate([sums[...]] + received, axis=0)
     for share in range(8):
         parts[share] = partial
-
-
-def scales(total, blocks):
-    scale = CLASSES / total
-    full = jnp.concatenate([scale, jnp.zeros((SIDE - blocks, SIDE), F32)], axis=0)
-    return jnp.transpose(full)
 
 
 def total_of(parts):
@@ -148,32 +144,30 @@
     operand, products, plan_here, plan_sem = refs
     plan_copy = pltpu.make_async_copy(plan, plan_here, plan_sem)
     plan_copy.start()
-    scale = scales(total_of(parts), 16)
+    scale = CLASSES / total_of(parts)
     if first:
-        seeded = jnp.concatenate(
-            [mask[...].astype(F32), jnp.zeros((SIDE - 8, SIDE), F32)], axis=0
-        )
-        seeded = 64.0 * jnp.transpose(seeded)
+        seeded = 64.0 * mask[...].astype(F32)
     for block in range(16):
         if block < 8:
             value = source[block]
         else:
             value = block_at(received[(block - 8) // 2], block % 2)
-        value = value * scale[:, block : block + 1]
+        value = value * scale[block : block + 1, :]
         if first and block < 8:
-            anchor[block] = seeded[:, block : block + 1] * value + 4.0
+            anchor[block] = seeded[block : block + 1, :] * value + 4.0
         high, low = split(value)
         operand[block, :SIDE, :] = high
         operand[block, SIDE:, :] = low
     plan_copy.wait()
     plan = plan_here
     for tile in range(32):
-        weights = tiles[tile]
-        products[tile] = jnp.dot(
-            jnp.concatenate([weights, weights], axis=1),
+        halves = lax.dot_general(
             operand[operand_block(plan, tile)],
+            tiles[tile],
+            (((1,), (1,)), ((), ())),
             preferred_element_type=F32,
         )
+        products[tile] = halves[:SIDE] + halves[SIDE:]
     squared[...] = anchor[...]
     for tile in range(32):
         row = row_block(plan, tile)
@@ -183,7 +177,7 @@
         value = squared[block]
         value = value * value
         squared[block] = value
-        sums.append(lane_sums(value))
+        sums.append(class_sums(value))
     sums = jnp.concatenate(sums, axis=0)
     if last:
         for share in range(8):
@@ -194,10 +188,10 @@
 
 
 def last_kernel(squared, parts, out, scaled, sems):
-    scale = scales(total_of(parts), 8)
+    scale = CLASSES / total_of(parts)
     copies = []
     for block in range(8):
-        scaled[block] = squared[block] * scale[:, block : block + 1]
+        scaled[block] = jnp.transpose(squared[block] * scale[block : block + 1, :])
         copy = pltpu.make_async_copy(scaled.at[block], out.at[block], sems.at[block])
         copy.start()
         copies.append(copy)
@@ -234,6 +228,7 @@
         in_specs=[HBM] * 5,
         out_specs=[VMEM] * 8,
         scratch_shapes=[
+            pltpu.VMEM((8, SIDE, SIDE), F32),
             pltpu.SMEM((1, 2, 4), jnp.int32),
             pltpu.SMEM((32,), jnp.int32),
             pltpu.SMEM((32,), jnp.int32),

time: 114 us -> 113 us (level)
  no operation moved by 1% of the time
where the time goes in v10:
time: 113 us; the launch traced here: 111 us
  starting transfers between devices  58.2 us (52%)
  blocking collectives  42.7 us (38%)
  Pallas kernels  7.19 us (6%)
  waiting for transfers between devices  2.85 us (3%)
    ppermute x12, starting transfers between devices, on_device(): received = [lax.ppermute(out, dom, swap) for out, swap in zip(outs, swaps)]  58.2 us
    all_to_all x4, blocking collectives, on_device(): parts = lax.all_to_all(parts, 'cls', 0, 0)  42.7 us
    pallas_call x3, Pallas kernels, on_device(): pl.pallas_call(lambda *refs, first=first, last=last: spread_kernel(first,...  4.12 us
    ppermute x12, waiting for transfers between devices, on_device(): received = [lax.ppermute(out, dom, swap) for out, swap in zip(outs, swaps)]  2.85 us
  transfers between devices with their start and end apart: 12, of which 5 were waited for; matrix products, arithmetic and copies ran while one was open for 0% of the time, Pallas kernels for 0%

profile of v10, /device:TPU:1, one launch (start us, length us, event | category | flops | bytes accessed | tf_op | source)
XLA Modules:
  0.0 111.2 jit_solution(18284021990394195433)
XLA Ops:
  0.0 0.0 copy-start
  0.0 2.1 %shard_map.64 = (f32[8,128,128]{2,1,0:T(8,128)S(1)}, s32[72]{0:T(128)S(1)}, s32[8,128]{1,0:T(8,128)S(1)}, f32[264,128]{1,0:T(8,128)S(1)}, f32[264,128]{1,0:T(8,1...) custom-call(f32[8,128,128]{2,1,0:T(8,128)} %bitcast.4, s32[1,2,4]{2,1,0:T(2,128)} %bitcast.6, ...), custom_call_target="tpu_custom_call" | custom-call | flops 1048576 | bytes 1048576 | tf_op jit(solution)/shard_map/pallas_call | solution.py:225
  2.1 20.2 %collective-permute-start = (f32[264,128]{1,0:T(8,128)S(1)}, f32[264,128]{1,0:T(8,128)S(1)}, u32[]{:S(2)}, u32[]{:S(2)}) collective-permute-start(f32[264,128]{1,0:T(8,128)S(1)} %get-tuple-element.31), channel_id=1, source_target_pairs={{0,1008},{8,1016},{16,32},{24,40},{32,16},{40,24},{48,64},{56,72},... | collective-permute-start | bytes 405512 | tf_op jit(solution)/shard_map/ppermute | solution.py:245
  22.3 1.9 %collective-permute-start.1 = (f32[264,128]{1,0:T(8,128)S(1)}, f32[264,128]{1,0:T(8,128)S(1)}, u32[]{:S(2)}, u32[]{:S(2)}) collective-permute-start(f32[264,128]{1,0:T(8,128)S(1)} %get-tuple-element.32), channel_id=1, source_target_pairs={{0,1016},{8,16},{16,8},{24,32},{32,24},{40,48},{48,40},{56,64},{64... | collective-permute-start | bytes 405512 | tf_op jit(solution)/shard_map/ppermute | solution.py:245
  24.2 1.9 %collective-permute-start.2 = (f32[264,128]{1,0:T(8,128)S(1)}, f32[264,128]{1,0:T(8,128)S(1)}, u32[]{:S(2)}, u32[]{:S(2)}) collective-permute-start(f32[264,128]{1,0:T(8,128)S(1)} %get-tuple-element.33), channel_id=1, source_target_pairs={{0,16},{8,24},{16,0},{24,8},{32,48},{40,56},{48,32},{56,40},{64,80... | collective-permute-start | bytes 405512 | tf_op jit(solution)/shard_map/ppermute | solution.py:245
  26.1 4.0 %collective-permute-start.3 = (f32[264,128]{1,0:T(8,128)S(1)}, f32[264,128]{1,0:T(8,128)S(1)}, u32[]{:S(2)}, u32[]{:S(2)}) collective-permute-start(f32[264,128]{1,0:T(8,128)S(1)} %get-tuple-element.34), channel_id=1, source_target_pairs={{0,8},{8,0},{16,24},{24,16},{32,40},{40,32},{48,56},{56,48},{64,72... | collective-permute-start | bytes 405512 | tf_op jit(solution)/shard_map/ppermute | solution.py:245
  30.2 0.0 collective-permute-done.in0.refs_4_
  30.2 0.0 collective-permute-done.1.in1.refs_5_
  30.2 0.2 collective-permute-done.2.in2.refs_6_
  30.4 0.7 collective-permute-done.3.in3.refs_7_
  31.1 14.3 %all_to_all.20.refs_8_ = f32[8,16,128]{2,1,0:T(8,128)S(1)} all-to-all(f32[8,16,128]{2,1,0:T(8,128)S(1)} %shard_map.65), channel_id=1, replica_groups=mesh['chip'=64,'core'=2,'cls'=8] {'cls'}, dimensions={0} | all-to-all | bytes 131072 | tf_op jit(solution)/shard_map/all_to_all | solution.py:253
  45.4 0.0 copy-done
  45.4 1.4 %shard_map.66 = (f32[8,128,128]{2,1,0:T(8,128)S(1)}, f32[8,128,128]{2,1,0:T(8,128)S(1)}, f32[264,128]{1,0:T(8,128)S(1)}, f32[264,128]{1,0:T(8,128)S(1)}, f32[264...) custom-call(bf16[32,128,128]{2,1,0:T(8,128)(2,1)S(1)} %copy-done, s32[72]{0:T(128)S(1)} %get-tuple-element.28.refs_1_, ...), custom_call_target="tpu_custom_call" | custom-call | tf_op jit(solution)/shard_map/pallas_call | solution.py:256
  46.8 6.7 %collective-permute-start.4 = (f32[264,128]{1,0:T(8,128)S(1)}, f32[264,128]{1,0:T(8,128)S(1)}, u32[]{:S(2)}, u32[]{:S(2)}) collective-permute-start(f32[264,128]{1,0:T(8,128)S(1)} %get-tuple-element.38), channel_id=1, source_target_pairs={{0,1008},{8,1016},{16,32},{24,40},{32,16},{40,24},{48,64},{56,72},... | collective-permute-start | bytes 405512 | tf_op jit(solution)/shard_map/ppermute | solution.py:245
  53.5 1.9 %collective-permute-start.5 = (f32[264,128]{1,0:T(8,128)S(1)}, f32[264,128]{1,0:T(8,128)S(1)}, u32[]{:S(2)}, u32[]{:S(2)}) collective-permute-start(f32[264,128]{1,0:T(8,128)S(1)} %get-tuple-element.39), channel_id=1, source_target_pairs={{0,1016},{8,16},{16,8},{24,32},{32,24},{40,48},{48,40},{56,64},{64... | collective-permute-start | bytes 405512 | tf_op jit(solution)/shard_map/ppermute | solution.py:245
  55.5 2.0 %collective-permute-start.6 = (f32[264,128]{1,0:T(8,128)S(1)}, f32[264,128]{1,0:T(8,128)S(1)}, u32[]{:S(2)}, u32[]{:S(2)}) collective-permute-start(f32[264,128]{1,0:T(8,128)S(1)} %get-tuple-element.40), channel_id=1, source_target_pairs={{0,16},{8,24},{16,0},{24,8},{32,48},{40,56},{48,32},{56,40},{64,80... | collective-permute-start | bytes 405512 | tf_op jit(solution)/shard_map/ppermute | solution.py:245
  57.5 3.9 %collective-permute-start.7 = (f32[264,128]{1,0:T(8,128)S(1)}, f32[264,128]{1,0:T(8,128)S(1)}, u32[]{:S(2)}, u32[]{:S(2)}) collective-permute-start(f32[264,128]{1,0:T(8,128)S(1)} %get-tuple-element.41), channel_id=1, source_target_pairs={{0,8},{8,0},{16,24},{24,16},{32,40},{40,32},{48,56},{56,48},{64,72... | collective-permute-start | bytes 405512 | tf_op jit(solution)/shard_map/ppermute | solution.py:245
  61.4 0.0 collective-permute-done.4.in0.refs_4_
  61.4 0.0 collective-permute-done.5.in1.refs_5_
  61.5 0.0 collective-permute-done.6.in2.refs_6_
  61.5 0.9 collective-permute-done.7.in3.refs_7_
  62.4 9.6 %all_to_all.21.refs_8_ = f32[8,16,128]{2,1,0:T(8,128)S(1)} all-to-all(f32[8,16,128]{2,1,0:T(8,128)S(1)} %shard_map.67), channel_id=1, replica_groups=mesh['chip'=64,'core'=2,'cls'=8] {'cls'}, dimensions={0} | all-to-all | bytes 131072 | tf_op jit(solution)/shard_map/all_to_all | solution.py:253
  72.0 1.4 %shard_map.68 = (f32[8,128,128]{2,1,0:T(8,128)S(1)}, f32[264,128]{1,0:T(8,128)S(1)}, f32[264,128]{1,0:T(8,128)S(1)}, f32[264,128]{1,0:T(8,128)S(1)}, f32[264,128]{1,0:T(8,128)S(1)}, /*index=5*/f32[8,128]{1,0:T(8,128)S(1)}) custom-call(bf16[32,128,128]{2,1,0:T(8,128)(2,1)S(1)} %copy-done, s32[72]{0:T(128)S(1)} %get-tuple-element.28.refs_1_, ...), custom_call_target="tpu_custom_call" | custom-call | tf_op jit(solution)/shard_map/pallas_call | solution.py:256
  73.4 7.7 %collective-permute-start.8 = (f32[264,128]{1,0:T(8,128)S(1)}, f32[264,128]{1,0:T(8,128)S(1)}, u32[]{:S(2)}, u32[]{:S(2)}) collective-permute-start(f32[264,128]{1,0:T(8,128)S(1)} %get-tuple-element.44), channel_id=1, source_target_pairs={{0,1008},{8,1016},{16,32},{24,40},{32,16},{40,24},{48,64},{56,72},... | collective-permute-start | bytes 405512 | tf_op jit(solution)/shard_map/ppermute | solution.py:245
  81.1 1.9 %collective-permute-start.9 = (f32[264,128]{1,0:T(8,128)S(1)}, f32[264,128]{1,0:T(8,128)S(1)}, u32[]{:S(2)}, u32[]{:S(2)}) collective-permute-start(f32[264,128]{1,0:T(8,128)S(1)} %get-tuple-element.45), channel_id=1, source_target_pairs={{0,1016},{8,16},{16,8},{24,32},{32,24},{40,48},{48,40},{56,64},{64... | collective-permute-start | bytes 405512 | tf_op jit(solution)/shard_map/ppermute | solution.py:245
  83.0 1.9 %collective-permute-start.10 = (f32[264,128]{1,0:T(8,128)S(1)}, f32[264,128]{1,0:T(8,128)S(1)}, u32[]{:S(2)}, u32[]{:S(2)}) collective-permute-start(f32[264,128]{1,0:T(8,128)S(1)} %get-tuple-element.46), channel_id=1, source_target_pairs={{0,16},{8,24},{16,0},{24,8},{32,48},{40,56},{48,32},{56,40},{64,80... | collective-permute-start | bytes 405512 | tf_op jit(solution)/shard_map/ppermute | solution.py:245
  85.0 4.0 %collective-permute-start.11 = (f32[264,128]{1,0:T(8,128)S(1)}, f32[264,128]{1,0:T(8,128)S(1)}, u32[]{:S(2)}, u32[]{:S(2)}) collective-permute-start(f32[264,128]{1,0:T(8,128)S(1)} %get-tuple-element.47), channel_id=1, source_target_pairs={{0,8},{8,0},{16,24},{24,16},{32,40},{40,32},{48,56},{56,48},{64,72... | collective-permute-start | bytes 405512 | tf_op jit(solution)/shard_map/ppermute | solution.py:245
  89.0 0.0 collective-permute-done.8.in0.refs_4_
  89.0 0.0 collective-permute-done.9.in1.refs_5_
  89.0 0.5 collective-permute-done.10.in2.refs_6_
  89.6 0.4 collective-permute-done.11.in3.refs_7_
  90.0 9.6 %all_to_all.22.refs_8_ = f32[8,16,128]{2,1,0:T(8,128)S(1)} all-to-all(f32[8,16,128]{2,1,0:T(8,128)S(1)} %shard_map.69), channel_id=1, replica_groups=mesh['chip'=64,'core'=2,'cls'=8] {'cls'}, dimensions={0} | all-to-all | bytes 131072 | tf_op jit(solution)/shard_map/all_to_all | solution.py:253
  99.6 1.4 %shard_map.70 = (f32[8,128,128]{2,1,0:T(8,128)S(1)}, f32[8,8,128]{2,1,0:T(8,128)S(1)}) custom-call(bf16[32,128,128]{2,1,0:T(8,128)(2,1)S(1)} %copy-done, s32[72]{0:T(128)S(1)} %get-tuple-element.28.refs_1_, f32[8,128,128]{2,1,0:T(8,128)S(1)} %get-tuple-element.36.refs_2_, f32[8,128,128]{2,1,0:T(8,128)S(1)} %get-tuple-element.43.refs_3_, ...), custom_call_target="tpu_custom_call" | custom-call | tf_op jit(solution)/shard_map/pallas_call | solution.py:256
  100.9 9.2 %all_to_all.23.parts = f32[8,8,128]{2,1,0:T(8,128)S(1)} all-to-all(f32[8,8,128]{2,1,0:T(8,128)S(1)} %get-tuple-element.50), channel_id=1, replica_groups=mesh['chip'=64,'core'=2,'cls'=8] {'cls'}, dimensions={0} | all-to-all | bytes 65536 | tf_op jit(solution)/shard_map/all_to_all | solution.py:275
  110.2 1.0 shard_map.71
  (3 shorter events, 0.0 us)
Async XLA Ops:
  0.0 45.4 %copy-start = (bf16[32,128,128]{2,1,0:T(8,128)(2,1)S(1)}, bf16[32,128,128]{2,1,0:T(8,128)(2,1)}, u32[]{:S(2)}) copy-start(bf16[32,128,128]{2,1,0:T(8,128)(2,1)} %refs_0_.5) | copy-start | bytes 3145732
  2.1 28.1 %collective-permute-start = (f32[264,128]{1,0:T(8,128)S(1)}, f32[264,128]{1,0:T(8,128)S(1)}, u32[]{:S(2)}, u32[]{:S(2)}) collective-permute-start(f32[264,128]{1,0:T(8,128)S(1)} %get-tuple-element.31), channel_id=1, source_target_pairs={{0,1008},{8,1016},{16,32},{24,40},{32,16},{40,24},{48,64},{56,72},... | collective-permute-start | bytes 405512 | tf_op jit(solution)/shard_map/ppermute | solution.py:245
  22.3 7.9 %collective-permute-start.1 = (f32[264,128]{1,0:T(8,128)S(1)}, f32[264,128]{1,0:T(8,128)S(1)}, u32[]{:S(2)}, u32[]{:S(2)}) collective-permute-start(f32[264,128]{1,0:T(8,128)S(1)} %get-tuple-element.32), channel_id=1, source_target_pairs={{0,1016},{8,16},{16,8},{24,32},{32,24},{40,48},{48,40},{56,64},{64... | collective-permute-start | bytes 405512 | tf_op jit(solution)/shard_map/ppermute | solution.py:245
  24.2 6.2 %collective-permute-start.2 = (f32[264,128]{1,0:T(8,128)S(1)}, f32[264,128]{1,0:T(8,128)S(1)}, u32[]{:S(2)}, u32[]{:S(2)}) collective-permute-start(f32[264,128]{1,0:T(8,128)S(1)} %get-tuple-element.33), channel_id=1, source_target_pairs={{0,16},{8,24},{16,0},{24,8},{32,48},{40,56},{48,32},{56,40},{64,80... | collective-permute-start | bytes 405512 | tf_op jit(solution)/shard_map/ppermute | solution.py:245
  26.1 5.0 %collective-permute-start.3 = (f32[264,128]{1,0:T(8,128)S(1)}, f32[264,128]{1,0:T(8,128)S(1)}, u32[]{:S(2)}, u32[]{:S(2)}) collective-permute-start(f32[264,128]{1,0:T(8,128)S(1)} %get-tuple-element.34), channel_id=1, source_target_pairs={{0,8},{8,0},{16,24},{24,16},{32,40},{40,32},{48,56},{56,48},{64,72... | collective-permute-start | bytes 405512 | tf_op jit(solution)/shard_map/ppermute | solution.py:245
  46.8 14.6 %collective-permute-start.4 = (f32[264,128]{1,0:T(8,128)S(1)}, f32[264,128]{1,0:T(8,128)S(1)}, u32[]{:S(2)}, u32[]{:S(2)}) collective-permute-start(f32[264,128]{1,0:T(8,128)S(1)} %get-tuple-element.38), channel_id=1, source_target_pairs={{0,1008},{8,1016},{16,32},{24,40},{32,16},{40,24},{48,64},{56,72},... | collective-permute-start | bytes 405512 | tf_op jit(solution)/shard_map/ppermute | solution.py:245
  53.5 7.9 %collective-permute-start.5 = (f32[264,128]{1,0:T(8,128)S(1)}, f32[264,128]{1,0:T(8,128)S(1)}, u32[]{:S(2)}, u32[]{:S(2)}) collective-permute-start(f32[264,128]{1,0:T(8,128)S(1)} %get-tuple-element.39), channel_id=1, source_target_pairs={{0,1016},{8,16},{16,8},{24,32},{32,24},{40,48},{48,40},{56,64},{64... | collective-permute-start | bytes 405512 | tf_op jit(solution)/shard_map/ppermute | solution.py:245
  55.5 6.0 %collective-permute-start.6 = (f32[264,128]{1,0:T(8,128)S(1)}, f32[264,128]{1,0:T(8,128)S(1)}, u32[]{:S(2)}, u32[]{:S(2)}) collective-permute-start(f32[264,128]{1,0:T(8,128)S(1)} %get-tuple-element.40), channel_id=1, source_target_pairs={{0,16},{8,24},{16,0},{24,8},{32,48},{40,56},{48,32},{56,40},{64,80... | collective-permute-start | bytes 405512 | tf_op jit(solution)/shard_map/ppermute | solution.py:245
  57.5 4.9 %collective-permute-start.7 = (f32[264,128]{1,0:T(8,128)S(1)}, f32[264,128]{1,0:T(8,128)S(1)}, u32[]{:S(2)}, u32[]{:S(2)}) collective-permute-start(f32[264,128]{1,0:T(8,128)S(1)} %get-tuple-element.41), channel_id=1, source_target_pairs={{0,8},{8,0},{16,24},{24,16},{32,40},{40,32},{48,56},{56,48},{64,72... | collective-permute-start | bytes 405512 | tf_op jit(solution)/shard_map/ppermute | solution.py:245
  73.4 15.6 %collective-permute-start.8 = (f32[264,128]{1,0:T(8,128)S(1)}, f32[264,128]{1,0:T(8,128)S(1)}, u32[]{:S(2)}, u32[]{:S(2)}) collective-permute-start(f32[264,128]{1,0:T(8,128)S(1)} %get-tuple-element.44), channel_id=1, source_target_pairs={{0,1008},{8,1016},{16,32},{24,40},{32,16},{40,24},{48,64},{56,72},... | collective-permute-start | bytes 405512 | tf_op jit(solution)/shard_map/ppermute | solution.py:245
  81.1 7.9 %collective-permute-start.9 = (f32[264,128]{1,0:T(8,128)S(1)}, f32[264,128]{1,0:T(8,128)S(1)}, u32[]{:S(2)}, u32[]{:S(2)}) collective-permute-start(f32[264,128]{1,0:T(8,128)S(1)} %get-tuple-element.45), channel_id=1, source_target_pairs={{0,1016},{8,16},{16,8},{24,32},{32,24},{40,48},{48,40},{56,64},{64... | collective-permute-start | bytes 405512 | tf_op jit(solution)/shard_map/ppermute | solution.py:245
  83.0 6.5 %collective-permute-start.10 = (f32[264,128]{1,0:T(8,128)S(1)}, f32[264,128]{1,0:T(8,128)S(1)}, u32[]{:S(2)}, u32[]{:S(2)}) collective-permute-start(f32[264,128]{1,0:T(8,128)S(1)} %get-tuple-element.46), channel_id=1, source_target_pairs={{0,16},{8,24},{16,0},{24,8},{32,48},{40,56},{48,32},{56,40},{64,80... | collective-permute-start | bytes 405512 | tf_op jit(solution)/shard_map/ppermute | solution.py:245
  85.0 5.0 %collective-permute-start.11 = (f32[264,128]{1,0:T(8,128)S(1)}, f32[264,128]{1,0:T(8,128)S(1)}, u32[]{:S(2)}, u32[]{:S(2)}) collective-permute-start(f32[264,128]{1,0:T(8,128)S(1)} %get-tuple-element.47), channel_id=1, source_target_pairs={{0,8},{8,0},{16,24},{24,16},{32,40},{40,32},{48,56},{56,48},{64,72... | collective-permute-start | bytes 405512 | tf_op jit(solution)/shard_map/ppermute | solution.py:245

commit v11 on v10

--- a/solution.py
+++ b/solution.py
@@ -90,18 +90,18 @@
     pairs = [(send, send_here), (rows, rows_here), (cols, cols_here)]
     pairs += [(labels.at[block], fetched.at[block]) for block in range(8)]
     copies = copy_all(pairs + [(mask, mask_kept)], sems)
+    sums = []
+    for block in range(8):
+        copies[3 + block].wait()
+        value = jnp.transpose(fetched[block])
+        kept[block] = value
+        sums.append(class_sums(value))
     for copy in copies[:3]:
         copy.wait()
     for place, entry in enumerate(plan_entries(rows_here, cols_here, send_here)):
         plan_here[place] = entry
     plan_copy = pltpu.make_async_copy(plan_here, plan, sems.at[12])
     plan_copy.start()
-    sums = []
-    for block in range(8):
-        copies[3 + block].wait()
-        value = jnp.transpose(fetched[block])
-        kept[block] = value
-        sums.append(class_sums(value))
     block_of = lambda offset, within: send_here[0, within, offset]
     fill_swaps(kept, jnp.concatenate(sums, axis=0), block_of, outs, sums_out)
     copies[11].wait()
@@ -156,18 +156,18 @@
         if first and block < 8:
             anchor[block] = seeded[block : block + 1, :] * value + 4.0
         high, low = split(value)
-        operand[block, :SIDE, :] = high
-        operand[block, SIDE:, :] = low
+        operand[block, :, :SIDE] = high
+        operand[block, :, SIDE:] = low
     plan_copy.wait()
     plan = plan_here
     for tile in range(32):
-        halves = lax.dot_general(
+        weights = tiles[tile]
+        products[tile] = lax.dot_general(
             operand[operand_block(plan, tile)],
-            tiles[tile],
+            jnp.concatenate([weights, weights], axis=1),
             (((1,), (1,)), ((), ())),
             preferred_element_type=F32,
         )
-        products[tile] = halves[:SIDE] + halves[SIDE:]
     squared[...] = anchor[...]
     for tile in range(32):
         row = row_block(plan, tile)
@@ -259,7 +259,7 @@
             in_specs=[VMEM] * 9,
             out_specs=[VMEM] * len(out_shape),
             scratch_shapes=[
-                pltpu.VMEM((16, 2 * SIDE, SIDE), jnp.bfloat16),
+                pltpu.VMEM((16, SIDE, 2 * SIDE), jnp.bfloat16),
                 pltpu.VMEM((32, SIDE, SIDE), F32),
                 pltpu.SMEM((72,), jnp.int32),
                 pltpu.SemaphoreType.DMA,

time: 113 us -> 114 us (level)
  no operation moved by 1% of the time
where the time goes in v11:
time: 114 us; the launch traced here: 112 us
  starting transfers between devices  58.2 us (51%)
  blocking collectives  42.7 us (37%)
  Pallas kernels  7.89 us (7%)
  waiting for transfers between devices  2.85 us (2%)
    ppermute x12, starting transfers between devices, on_device(): received = [lax.ppermute(out, dom, swap) for out, swap in zip(outs, swaps)]  58.2 us
    all_to_all x4, blocking collectives, on_device(): parts = lax.all_to_all(parts, 'cls', 0, 0)  42.7 us
    pallas_call x3, Pallas kernels, on_device(): pl.pallas_call(lambda *refs, first=first, last=last: spread_kernel(first,...  4.15 us
    ppermute x12, waiting for transfers between devices, on_device(): received = [lax.ppermute(out, dom, swap) for out, swap in zip(outs, swaps)]  2.85 us
    pallas_call x1, Pallas kernels, on_device(): pl.pallas_call(first_kernel, out_shape=[own_shape, plan_shape, jax.ShapeD...  2.75 us
  transfers between devices with their start and end apart: 12, of which 5 were waited for; matrix products, arithmetic and copies ran while one was open for 0% of the time, Pallas kernels for 0%

profile of v11, /device:TPU:1, one launch (start us, length us, event | category | flops | bytes accessed | tf_op | source)
XLA Modules:
  0.0 111.8 jit_solution(3737624074782703313)
XLA Ops:
  0.0 0.0 copy-start
  0.0 2.8 %shard_map.64 = (f32[8,128,128]{2,1,0:T(8,128)S(1)}, s32[72]{0:T(128)S(1)}, s32[8,128]{1,0:T(8,128)S(1)}, f32[264,128]{1,0:T(8,128)S(1)}, f32[264,128]{1,0:T(8,1...) custom-call(f32[8,128,128]{2,1,0:T(8,128)} %bitcast.4, s32[1,2,4]{2,1,0:T(2,128)} %bitcast.6, ...), custom_call_target="tpu_custom_call" | custom-call | flops 1048576 | bytes 1048576 | tf_op jit(solution)/shard_map/pallas_call | solution.py:225
  2.8 20.2 %collective-permute-start = (f32[264,128]{1,0:T(8,128)S(1)}, f32[264,128]{1,0:T(8,128)S(1)}, u32[]{:S(2)}, u32[]{:S(2)}) collective-permute-start(f32[264,128]{1,0:T(8,128)S(1)} %get-tuple-element.31), channel_id=1, source_target_pairs={{0,1008},{8,1016},{16,32},{24,40},{32,16},{40,24},{48,64},{56,72},... | collective-permute-start | bytes 405512 | tf_op jit(solution)/shard_map/ppermute | solution.py:245
  22.9 1.9 %collective-permute-start.1 = (f32[264,128]{1,0:T(8,128)S(1)}, f32[264,128]{1,0:T(8,128)S(1)}, u32[]{:S(2)}, u32[]{:S(2)}) collective-permute-start(f32[264,128]{1,0:T(8,128)S(1)} %get-tuple-element.32), channel_id=1, source_target_pairs={{0,1016},{8,16},{16,8},{24,32},{32,24},{40,48},{48,40},{56,64},{64... | collective-permute-start | bytes 405512 | tf_op jit(solution)/shard_map/ppermute | solution.py:245
  24.9 1.9 %collective-permute-start.2 = (f32[264,128]{1,0:T(8,128)S(1)}, f32[264,128]{1,0:T(8,128)S(1)}, u32[]{:S(2)}, u32[]{:S(2)}) collective-permute-start(f32[264,128]{1,0:T(8,128)S(1)} %get-tuple-element.33), channel_id=1, source_target_pairs={{0,16},{8,24},{16,0},{24,8},{32,48},{40,56},{48,32},{56,40},{64,80... | collective-permute-start | bytes 405512 | tf_op jit(solution)/shard_map/ppermute | solution.py:245
  26.8 4.0 %collective-permute-start.3 = (f32[264,128]{1,0:T(8,128)S(1)}, f32[264,128]{1,0:T(8,128)S(1)}, u32[]{:S(2)}, u32[]{:S(2)}) collective-permute-start(f32[264,128]{1,0:T(8,128)S(1)} %get-tuple-element.34), channel_id=1, source_target_pairs={{0,8},{8,0},{16,24},{24,16},{32,40},{40,32},{48,56},{56,48},{64,72... | collective-permute-start | bytes 405512 | tf_op jit(solution)/shard_map/ppermute | solution.py:245
  30.8 0.0 collective-permute-done.in0.refs_4_
  30.8 0.0 collective-permute-done.1.in1.refs_5_
  30.9 0.2 collective-permute-done.2.in2.refs_6_
  31.1 0.7 collective-permute-done.3.in3.refs_7_
  31.8 14.3 %all_to_all.20.refs_8_ = f32[8,16,128]{2,1,0:T(8,128)S(1)} all-to-all(f32[8,16,128]{2,1,0:T(8,128)S(1)} %shard_map.65), channel_id=1, replica_groups=mesh['chip'=64,'core'=2,'cls'=8] {'cls'}, dimensions={0} | all-to-all | bytes 131072 | tf_op jit(solution)/shard_map/all_to_all | solution.py:253
  46.1 0.0 copy-done
  46.1 1.4 %shard_map.66 = (f32[8,128,128]{2,1,0:T(8,128)S(1)}, f32[8,128,128]{2,1,0:T(8,128)S(1)}, f32[264,128]{1,0:T(8,128)S(1)}, f32[264,128]{1,0:T(8,128)S(1)}, f32[264...) custom-call(bf16[32,128,128]{2,1,0:T(8,128)(2,1)S(1)} %copy-done, s32[72]{0:T(128)S(1)} %get-tuple-element.28.refs_1_, ...), custom_call_target="tpu_custom_call" | custom-call | tf_op jit(solution)/shard_map/pallas_call | solution.py:256
  47.5 6.7 %collective-permute-start.4 = (f32[264,128]{1,0:T(8,128)S(1)}, f32[264,128]{1,0:T(8,128)S(1)}, u32[]{:S(2)}, u32[]{:S(2)}) collective-permute-start(f32[264,128]{1,0:T(8,128)S(1)} %get-tuple-element.38), channel_id=1, source_target_pairs={{0,1008},{8,1016},{16,32},{24,40},{32,16},{40,24},{48,64},{56,72},... | collective-permute-start | bytes 405512 | tf_op jit(solution)/shard_map/ppermute | solution.py:245
  54.2 1.9 %collective-permute-start.5 = (f32[264,128]{1,0:T(8,128)S(1)}, f32[264,128]{1,0:T(8,128)S(1)}, u32[]{:S(2)}, u32[]{:S(2)}) collective-permute-start(f32[264,128]{1,0:T(8,128)S(1)} %get-tuple-element.39), channel_id=1, source_target_pairs={{0,1016},{8,16},{16,8},{24,32},{32,24},{40,48},{48,40},{56,64},{64... | collective-permute-start | bytes 405512 | tf_op jit(solution)/shard_map/ppermute | solution.py:245
  56.1 2.0 %collective-permute-start.6 = (f32[264,128]{1,0:T(8,128)S(1)}, f32[264,128]{1,0:T(8,128)S(1)}, u32[]{:S(2)}, u32[]{:S(2)}) collective-permute-start(f32[264,128]{1,0:T(8,128)S(1)} %get-tuple-element.40), channel_id=1, source_target_pairs={{0,16},{8,24},{16,0},{24,8},{32,48},{40,56},{48,32},{56,40},{64,80... | collective-permute-start | bytes 405512 | tf_op jit(solution)/shard_map/ppermute | solution.py:245
  58.1 4.0 %collective-permute-start.7 = (f32[264,128]{1,0:T(8,128)S(1)}, f32[264,128]{1,0:T(8,128)S(1)}, u32[]{:S(2)}, u32[]{:S(2)}) collective-permute-start(f32[264,128]{1,0:T(8,128)S(1)} %get-tuple-element.41), channel_id=1, source_target_pairs={{0,8},{8,0},{16,24},{24,16},{32,40},{40,32},{48,56},{56,48},{64,72... | collective-permute-start | bytes 405512 | tf_op jit(solution)/shard_map/ppermute | solution.py:245
  62.1 0.0 collective-permute-done.4.in0.refs_4_
  62.1 0.0 collective-permute-done.5.in1.refs_5_
  62.1 0.0 collective-permute-done.6.in2.refs_6_
  62.1 0.9 collective-permute-done.7.in3.refs_7_
  63.1 9.6 %all_to_all.21.refs_8_ = f32[8,16,128]{2,1,0:T(8,128)S(1)} all-to-all(f32[8,16,128]{2,1,0:T(8,128)S(1)} %shard_map.67), channel_id=1, replica_groups=mesh['chip'=64,'core'=2,'cls'=8] {'cls'}, dimensions={0} | all-to-all | bytes 131072 | tf_op jit(solution)/shard_map/all_to_all | solution.py:253
  72.7 1.4 %shard_map.68 = (f32[8,128,128]{2,1,0:T(8,128)S(1)}, f32[264,128]{1,0:T(8,128)S(1)}, f32[264,128]{1,0:T(8,128)S(1)}, f32[264,128]{1,0:T(8,128)S(1)}, f32[264,128]{1,0:T(8,128)S(1)}, /*index=5*/f32[8,128]{1,0:T(8,128)S(1)}) custom-call(bf16[32,128,128]{2,1,0:T(8,128)(2,1)S(1)} %copy-done, s32[72]{0:T(128)S(1)} %get-tuple-element.28.refs_1_, ...), custom_call_target="tpu_custom_call" | custom-call | tf_op jit(solution)/shard_map/pallas_call | solution.py:256
  74.1 7.7 %collective-permute-start.8 = (f32[264,128]{1,0:T(8,128)S(1)}, f32[264,128]{1,0:T(8,128)S(1)}, u32[]{:S(2)}, u32[]{:S(2)}) collective-permute-start(f32[264,128]{1,0:T(8,128)S(1)} %get-tuple-element.44), channel_id=1, source_target_pairs={{0,1008},{8,1016},{16,32},{24,40},{32,16},{40,24},{48,64},{56,72},... | collective-permute-start | bytes 405512 | tf_op jit(solution)/shard_map/ppermute | solution.py:245
  81.8 1.9 %collective-permute-start.9 = (f32[264,128]{1,0:T(8,128)S(1)}, f32[264,128]{1,0:T(8,128)S(1)}, u32[]{:S(2)}, u32[]{:S(2)}) collective-permute-start(f32[264,128]{1,0:T(8,128)S(1)} %get-tuple-element.45), channel_id=1, source_target_pairs={{0,1016},{8,16},{16,8},{24,32},{32,24},{40,48},{48,40},{56,64},{64... | collective-permute-start | bytes 405512 | tf_op jit(solution)/shard_map/ppermute | solution.py:245
  83.7 1.9 %collective-permute-start.10 = (f32[264,128]{1,0:T(8,128)S(1)}, f32[264,128]{1,0:T(8,128)S(1)}, u32[]{:S(2)}, u32[]{:S(2)}) collective-permute-start(f32[264,128]{1,0:T(8,128)S(1)} %get-tuple-element.46), channel_id=1, source_target_pairs={{0,16},{8,24},{16,0},{24,8},{32,48},{40,56},{48,32},{56,40},{64,80... | collective-permute-start | bytes 405512 | tf_op jit(solution)/shard_map/ppermute | solution.py:245
  85.7 4.0 %collective-permute-start.11 = (f32[264,128]{1,0:T(8,128)S(1)}, f32[264,128]{1,0:T(8,128)S(1)}, u32[]{:S(2)}, u32[]{:S(2)}) collective-permute-start(f32[264,128]{1,0:T(8,128)S(1)} %get-tuple-element.47), channel_id=1, source_target_pairs={{0,8},{8,0},{16,24},{24,16},{32,40},{40,32},{48,56},{56,48},{64,72... | collective-permute-start | bytes 405512 | tf_op jit(solution)/shard_map/ppermute | solution.py:245
  89.7 0.0 collective-permute-done.8.in0.refs_4_
  89.7 0.0 collective-permute-done.9.in1.refs_5_
  89.7 0.5 collective-permute-done.10.in2.refs_6_
  90.3 0.4 collective-permute-done.11.in3.refs_7_
  90.7 9.6 %all_to_all.22.refs_8_ = f32[8,16,128]{2,1,0:T(8,128)S(1)} all-to-all(f32[8,16,128]{2,1,0:T(8,128)S(1)} %shard_map.69), channel_id=1, replica_groups=mesh['chip'=64,'core'=2,'cls'=8] {'cls'}, dimensions={0} | all-to-all | bytes 131072 | tf_op jit(solution)/shard_map/all_to_all | solution.py:253
  100.3 1.4 %shard_map.70 = (f32[8,128,128]{2,1,0:T(8,128)S(1)}, f32[8,8,128]{2,1,0:T(8,128)S(1)}) custom-call(bf16[32,128,128]{2,1,0:T(8,128)(2,1)S(1)} %copy-done, s32[72]{0:T(128)S(1)} %get-tuple-element.28.refs_1_, f32[8,128,128]{2,1,0:T(8,128)S(1)} %get-tuple-element.36.refs_2_, f32[8,128,128]{2,1,0:T(8,128)S(1)} %get-tuple-element.43.refs_3_, ...), custom_call_target="tpu_custom_call" | custom-call | tf_op jit(solution)/shard_map/pallas_call | solution.py:256
  101.6 9.2 %all_to_all.23.parts = f32[8,8,128]{2,1,0:T(8,128)S(1)} all-to-all(f32[8,8,128]{2,1,0:T(8,128)S(1)} %get-tuple-element.50), channel_id=1, replica_groups=mesh['chip'=64,'core'=2,'cls'=8] {'cls'}, dimensions={0} | all-to-all | bytes 65536 | tf_op jit(solution)/shard_map/all_to_all | solution.py:275
  110.9 1.0 shard_map.71
  (3 shorter events, 0.0 us)
Async XLA Ops:
  0.0 46.1 %copy-start = (bf16[32,128,128]{2,1,0:T(8,128)(2,1)S(1)}, bf16[32,128,128]{2,1,0:T(8,128)(2,1)}, u32[]{:S(2)}) copy-start(bf16[32,128,128]{2,1,0:T(8,128)(2,1)} %refs_0_.5) | copy-start | bytes 3145732
  2.8 28.1 %collective-permute-start = (f32[264,128]{1,0:T(8,128)S(1)}, f32[264,128]{1,0:T(8,128)S(1)}, u32[]{:S(2)}, u32[]{:S(2)}) collective-permute-start(f32[264,128]{1,0:T(8,128)S(1)} %get-tuple-element.31), channel_id=1, source_target_pairs={{0,1008},{8,1016},{16,32},{24,40},{32,16},{40,24},{48,64},{56,72},... | collective-permute-start | bytes 405512 | tf_op jit(solution)/shard_map/ppermute | solution.py:245
  22.9 7.9 %collective-permute-start.1 = (f32[264,128]{1,0:T(8,128)S(1)}, f32[264,128]{1,0:T(8,128)S(1)}, u32[]{:S(2)}, u32[]{:S(2)}) collective-permute-start(f32[264,128]{1,0:T(8,128)S(1)} %get-tuple-element.32), channel_id=1, source_target_pairs={{0,1016},{8,16},{16,8},{24,32},{32,24},{40,48},{48,40},{56,64},{64... | collective-permute-start | bytes 405512 | tf_op jit(solution)/shard_map/ppermute | solution.py:245
  24.9 6.2 %collective-permute-start.2 = (f32[264,128]{1,0:T(8,128)S(1)}, f32[264,128]{1,0:T(8,128)S(1)}, u32[]{:S(2)}, u32[]{:S(2)}) collective-permute-start(f32[264,128]{1,0:T(8,128)S(1)} %get-tuple-element.33), channel_id=1, source_target_pairs={{0,16},{8,24},{16,0},{24,8},{32,48},{40,56},{48,32},{56,40},{64,80... | collective-permute-start | bytes 405512 | tf_op jit(solution)/shard_map/ppermute | solution.py:245
  26.8 5.0 %collective-permute-start.3 = (f32[264,128]{1,0:T(8,128)S(1)}, f32[264,128]{1,0:T(8,128)S(1)}, u32[]{:S(2)}, u32[]{:S(2)}) collective-permute-start(f32[264,128]{1,0:T(8,128)S(1)} %get-tuple-element.34), channel_id=1, source_target_pairs={{0,8},{8,0},{16,24},{24,16},{32,40},{40,32},{48,56},{56,48},{64,72... | collective-permute-start | bytes 405512 | tf_op jit(solution)/shard_map/ppermute | solution.py:245
  47.5 14.6 %collective-permute-start.4 = (f32[264,128]{1,0:T(8,128)S(1)}, f32[264,128]{1,0:T(8,128)S(1)}, u32[]{:S(2)}, u32[]{:S(2)}) collective-permute-start(f32[264,128]{1,0:T(8,128)S(1)} %get-tuple-element.38), channel_id=1, source_target_pairs={{0,1008},{8,1016},{16,32},{24,40},{32,16},{40,24},{48,64},{56,72},... | collective-permute-start | bytes 405512 | tf_op jit(solution)/shard_map/ppermute | solution.py:245
  54.2 7.9 %collective-permute-start.5 = (f32[264,128]{1,0:T(8,128)S(1)}, f32[264,128]{1,0:T(8,128)S(1)}, u32[]{:S(2)}, u32[]{:S(2)}) collective-permute-start(f32[264,128]{1,0:T(8,128)S(1)} %get-tuple-element.39), channel_id=1, source_target_pairs={{0,1016},{8,16},{16,8},{24,32},{32,24},{40,48},{48,40},{56,64},{64... | collective-permute-start | bytes 405512 | tf_op jit(solution)/shard_map/ppermute | solution.py:245
  56.1 6.0 %collective-permute-start.6 = (f32[264,128]{1,0:T(8,128)S(1)}, f32[264,128]{1,0:T(8,128)S(1)}, u32[]{:S(2)}, u32[]{:S(2)}) collective-permute-start(f32[264,128]{1,0:T(8,128)S(1)} %get-tuple-element.40), channel_id=1, source_target_pairs={{0,16},{8,24},{16,0},{24,8},{32,48},{40,56},{48,32},{56,40},{64,80... | collective-permute-start | bytes 405512 | tf_op jit(solution)/shard_map/ppermute | solution.py:245
  58.1 4.9 %collective-permute-start.7 = (f32[264,128]{1,0:T(8,128)S(1)}, f32[264,128]{1,0:T(8,128)S(1)}, u32[]{:S(2)}, u32[]{:S(2)}) collective-permute-start(f32[264,128]{1,0:T(8,128)S(1)} %get-tuple-element.41), channel_id=1, source_target_pairs={{0,8},{8,0},{16,24},{24,16},{32,40},{40,32},{48,56},{56,48},{64,72... | collective-permute-start | bytes 405512 | tf_op jit(solution)/shard_map/ppermute | solution.py:245
  74.1 15.6 %collective-permute-start.8 = (f32[264,128]{1,0:T(8,128)S(1)}, f32[264,128]{1,0:T(8,128)S(1)}, u32[]{:S(2)}, u32[]{:S(2)}) collective-permute-start(f32[264,128]{1,0:T(8,128)S(1)} %get-tuple-element.44), channel_id=1, source_target_pairs={{0,1008},{8,1016},{16,32},{24,40},{32,16},{40,24},{48,64},{56,72},... | collective-permute-start | bytes 405512 | tf_op jit(solution)/shard_map/ppermute | solution.py:245
  81.8 7.9 %collective-permute-start.9 = (f32[264,128]{1,0:T(8,128)S(1)}, f32[264,128]{1,0:T(8,128)S(1)}, u32[]{:S(2)}, u32[]{:S(2)}) collective-permute-start(f32[264,128]{1,0:T(8,128)S(1)} %get-tuple-element.45), channel_id=1, source_target_pairs={{0,1016},{8,16},{16,8},{24,32},{32,24},{40,48},{48,40},{56,64},{64... | collective-permute-start | bytes 405512 | tf_op jit(solution)/shard_map/ppermute | solution.py:245
  83.7 6.5 %collective-permute-start.10 = (f32[264,128]{1,0:T(8,128)S(1)}, f32[264,128]{1,0:T(8,128)S(1)}, u32[]{:S(2)}, u32[]{:S(2)}) collective-permute-start(f32[264,128]{1,0:T(8,128)S(1)} %get-tuple-element.46), channel_id=1, source_target_pairs={{0,16},{8,24},{16,0},{24,8},{32,48},{40,56},{48,32},{56,40},{64,80... | collective-permute-start | bytes 405512 | tf_op jit(solution)/shard_map/ppermute | solution.py:245
  85.7 5.0 %collective-permute-start.11 = (f32[264,128]{1,0:T(8,128)S(1)}, f32[264,128]{1,0:T(8,128)S(1)}, u32[]{:S(2)}, u32[]{:S(2)}) collective-permute-start(f32[264,128]{1,0:T(8,128)S(1)} %get-tuple-element.47), channel_id=1, source_target_pairs={{0,8},{8,0},{16,24},{24,16},{32,40},{40,32},{48,56},{56,48},{64,72... | collective-permute-start | bytes 405512 | tf_op jit(solution)/shard_map/ppermute | solution.py:245

commit v12 on v10

--- a/solution.py
+++ b/solution.py
@@ -29,7 +29,6 @@
 
 def plan_entries(rows, cols, send):
     core = lax.axis_index("core")
-    odd = lax.rem(lax.axis_index("chip"), 2)
     for tile in range(32):
         yield rows[tile]
     for tile in range(32):
@@ -37,7 +36,7 @@
         ghost = jnp.maximum(col - 8, 0)
         offset = shift_right(ghost, 1)
         half = shift_right(offset, 1)
-        pair = jnp.where(lax.rem(offset, 2) == 1, 2 * (half ^ odd), 1 + 2 * (half ^ core))
+        pair = jnp.where(lax.rem(offset, 2) == 1, 2 * half, 1 + 2 * (half ^ core))
         yield jnp.where(col < 8, col, 8 + 2 * pair + lax.rem(ghost, 2))
     for offset in range(4):
         for within in range(2):
@@ -62,9 +61,8 @@
 
 def fill_swaps(source, sums, block_of, outs, rows):
     core = lax.axis_index("core")
-    odd = lax.rem(lax.axis_index("chip"), 2)
     rows[0:8, :] = sums
-    for out, offset in zip(outs, (3 - 2 * odd, 2 - 2 * core, 1 + 2 * odd, 2 * core)):
+    for out, offset in zip(outs, (1, 2 - 2 * core, 3, 2 * core)):
         out[2 * SIDE + 2 :, :] = jnp.zeros((6, SIDE), F32)
         for within in range(2):
             block = block_of(offset, within)
@@ -203,9 +201,9 @@
     dom = ("chip", "core")
     count = 2 * lax.axis_size("chip")
     swaps = [
-        [(i, (i + (2 if i // 2 % 2 else -2)) % count) for i in range(count)],
+        [(i, (i + 2) % count) for i in range(count)],
         [(i, (i + (1 if i % 2 else -1)) % count) for i in range(count)],
-        [(i, (i + (-2 if i // 2 % 2 else 2)) % count) for i in range(count)],
+        [(i, (i - 2) % count) for i in range(count)],
         [(i, i ^ 1) for i in range(count)],
     ]
     send_lists = jnp.transpose(send_lists, (0, 2, 1))

time: 113 us -> 112 us (level)
  transfers between devices with their start and end apart: 12 -> 12, of which waited for: 5 -> 4; matrix products, arithmetic and copies ran while one was open for 0% -> 0% of each run, Pallas kernels for 0% -> 0%
where the time goes in v12:
time: 112 us; the launch traced here: 111 us
  starting transfers between devices  58 us (52%)
  blocking collectives  42.7 us (38%)
  Pallas kernels  7.17 us (6%)
  waiting for transfers between devices  2.84 us (3%)
    ppermute x12, starting transfers between devices, on_device(): received = [lax.ppermute(out, dom, swap) for out, swap in zip(outs, swaps)]  58 us
    all_to_all x4, blocking collectives, on_device(): parts = lax.all_to_all(parts, 'cls', 0, 0)  42.7 us
    pallas_call x3, Pallas kernels, on_device(): pl.pallas_call(lambda *refs, first=first, last=last: spread_kernel(first,...  4.11 us
    ppermute x12, waiting for transfers between devices, on_device(): received = [lax.ppermute(out, dom, swap) for out, swap in zip(outs, swaps)]  2.84 us
  transfers between devices with their start and end apart: 12, of which 4 were waited for; matrix products, arithmetic and copies ran while one was open for 0% of the time, Pallas kernels for 0%

profile of v12, /device:TPU:1, one launch (start us, length us, event | category | flops | bytes accessed | tf_op | source)
XLA Modules:
  0.0 110.9 jit_solution(4603906239384167474)
XLA Ops:
  0.0 0.0 copy-start
  0.0 2.1 %shard_map.64 = (f32[8,128,128]{2,1,0:T(8,128)S(1)}, s32[72]{0:T(128)S(1)}, s32[8,128]{1,0:T(8,128)S(1)}, f32[264,128]{1,0:T(8,128)S(1)}, f32[264,128]{1,0:T(8,1...) custom-call(f32[8,128,128]{2,1,0:T(8,128)} %bitcast.4, s32[1,2,4]{2,1,0:T(2,128)} %bitcast.6, ...), custom_call_target="tpu_custom_call" | custom-call | flops 1048576 | bytes 1048576 | tf_op jit(solution)/shard_map/pallas_call | solution.py:223
  2.1 5.7 %collective-permute-start = (f32[264,128]{1,0:T(8,128)S(1)}, f32[264,128]{1,0:T(8,128)S(1)}, u32[]{:S(2)}, u32[]{:S(2)}) collective-permute-start(f32[264,128]{1,0:T(8,128)S(1)} %get-tuple-element.31), channel_id=1, source_target_pairs={{0,16},{8,24},{16,32},{24,40},{32,48},{40,56},{48,64},{56,72},{64,... | collective-permute-start | bytes 405512 | tf_op jit(solution)/shard_map/ppermute | solution.py:243
  7.8 5.8 %collective-permute-start.1 = (f32[264,128]{1,0:T(8,128)S(1)}, f32[264,128]{1,0:T(8,128)S(1)}, u32[]{:S(2)}, u32[]{:S(2)}) collective-permute-start(f32[264,128]{1,0:T(8,128)S(1)} %get-tuple-element.32), channel_id=1, source_target_pairs={{0,1016},{8,16},{16,8},{24,32},{32,24},{40,48},{48,40},{56,64},{64... | collective-permute-start | bytes 405512 | tf_op jit(solution)/shard_map/ppermute | solution.py:243
  13.6 13.1 %collective-permute-start.2 = (f32[264,128]{1,0:T(8,128)S(1)}, f32[264,128]{1,0:T(8,128)S(1)}, u32[]{:S(2)}, u32[]{:S(2)}) collective-permute-start(f32[264,128]{1,0:T(8,128)S(1)} %get-tuple-element.33), channel_id=1, source_target_pairs={{0,1008},{8,1016},{16,0},{24,8},{32,16},{40,24},{48,32},{56,40},{6... | collective-permute-start | bytes 405512 | tf_op jit(solution)/shard_map/ppermute | solution.py:243
  26.7 3.5 %collective-permute-start.3 = (f32[264,128]{1,0:T(8,128)S(1)}, f32[264,128]{1,0:T(8,128)S(1)}, u32[]{:S(2)}, u32[]{:S(2)}) collective-permute-start(f32[264,128]{1,0:T(8,128)S(1)} %get-tuple-element.34), channel_id=1, source_target_pairs={{0,8},{8,0},{16,24},{24,16},{32,40},{40,32},{48,56},{56,48},{64,72... | collective-permute-start | bytes 405512 | tf_op jit(solution)/shard_map/ppermute | solution.py:243
  30.1 0.0 collective-permute-done.in0.refs_4_
  30.2 0.0 collective-permute-done.1.in1.refs_5_
  30.2 0.0 collective-permute-done.2.in2.refs_6_
  30.2 0.9 collective-permute-done.3.in3.refs_7_
  31.1 14.3 %all_to_all.20.refs_8_ = f32[8,16,128]{2,1,0:T(8,128)S(1)} all-to-all(f32[8,16,128]{2,1,0:T(8,128)S(1)} %shard_map.65), channel_id=1, replica_groups=mesh['chip'=64,'core'=2,'cls'=8] {'cls'}, dimensions={0} | all-to-all | bytes 131072 | tf_op jit(solution)/shard_map/all_to_all | solution.py:251
  45.4 0.0 copy-done
  45.4 1.4 %shard_map.66 = (f32[8,128,128]{2,1,0:T(8,128)S(1)}, f32[8,128,128]{2,1,0:T(8,128)S(1)}, f32[264,128]{1,0:T(8,128)S(1)}, f32[264,128]{1,0:T(8,128)S(1)}, f32[264...) custom-call(bf16[32,128,128]{2,1,0:T(8,128)(2,1)S(1)} %copy-done, s32[72]{0:T(128)S(1)} %get-tuple-element.28.refs_1_, ...), custom_call_target="tpu_custom_call" | custom-call | tf_op jit(solution)/shard_map/pallas_call | solution.py:254
  46.8 1.9 %collective-permute-start.4 = (f32[264,128]{1,0:T(8,128)S(1)}, f32[264,128]{1,0:T(8,128)S(1)}, u32[]{:S(2)}, u32[]{:S(2)}) collective-permute-start(f32[264,128]{1,0:T(8,128)S(1)} %get-tuple-element.38), channel_id=1, source_target_pairs={{0,16},{8,24},{16,32},{24,40},{32,48},{40,56},{48,64},{56,72},{64,... | collective-permute-start | bytes 405512 | tf_op jit(solution)/shard_map/ppermute | solution.py:243
  48.8 3.6 %collective-permute-start.5 = (f32[264,128]{1,0:T(8,128)S(1)}, f32[264,128]{1,0:T(8,128)S(1)}, u32[]{:S(2)}, u32[]{:S(2)}) collective-permute-start(f32[264,128]{1,0:T(8,128)S(1)} %get-tuple-element.39), channel_id=1, source_target_pairs={{0,1016},{8,16},{16,8},{24,32},{32,24},{40,48},{48,40},{56,64},{64... | collective-permute-start | bytes 405512 | tf_op jit(solution)/shard_map/ppermute | solution.py:243
  52.4 7.0 %collective-permute-start.6 = (f32[264,128]{1,0:T(8,128)S(1)}, f32[264,128]{1,0:T(8,128)S(1)}, u32[]{:S(2)}, u32[]{:S(2)}) collective-permute-start(f32[264,128]{1,0:T(8,128)S(1)} %get-tuple-element.40), channel_id=1, source_target_pairs={{0,1008},{8,1016},{16,0},{24,8},{32,16},{40,24},{48,32},{56,40},{6... | collective-permute-start | bytes 405512 | tf_op jit(solution)/shard_map/ppermute | solution.py:243
  59.3 2.3 %collective-permute-start.7 = (f32[264,128]{1,0:T(8,128)S(1)}, f32[264,128]{1,0:T(8,128)S(1)}, u32[]{:S(2)}, u32[]{:S(2)}) collective-permute-start(f32[264,128]{1,0:T(8,128)S(1)} %get-tuple-element.41), channel_id=1, source_target_pairs={{0,8},{8,0},{16,24},{24,16},{32,40},{40,32},{48,56},{56,48},{64,72... | collective-permute-start | bytes 405512 | tf_op jit(solution)/shard_map/ppermute | solution.py:243
  61.7 0.0 collective-permute-done.4.in0.refs_4_
  61.7 0.0 collective-permute-done.5.in1.refs_5_
  61.7 0.5 collective-permute-done.6.in2.refs_6_
  62.2 0.5 collective-permute-done.7.in3.refs_7_
  62.7 9.6 %all_to_all.21.refs_8_ = f32[8,16,128]{2,1,0:T(8,128)S(1)} all-to-all(f32[8,16,128]{2,1,0:T(8,128)S(1)} %shard_map.67), channel_id=1, replica_groups=mesh['chip'=64,'core'=2,'cls'=8] {'cls'}, dimensions={0} | all-to-all | bytes 131072 | tf_op jit(solution)/shard_map/all_to_all | solution.py:251
  72.2 1.4 %shard_map.68 = (f32[8,128,128]{2,1,0:T(8,128)S(1)}, f32[264,128]{1,0:T(8,128)S(1)}, f32[264,128]{1,0:T(8,128)S(1)}, f32[264,128]{1,0:T(8,128)S(1)}, f32[264,128]{1,0:T(8,128)S(1)}, /*index=5*/f32[8,128]{1,0:T(8,128)S(1)}) custom-call(bf16[32,128,128]{2,1,0:T(8,128)(2,1)S(1)} %copy-done, s32[72]{0:T(128)S(1)} %get-tuple-element.28.refs_1_, ...), custom_call_target="tpu_custom_call" | custom-call | tf_op jit(solution)/shard_map/pallas_call | solution.py:254
  73.6 1.9 %collective-permute-start.8 = (f32[264,128]{1,0:T(8,128)S(1)}, f32[264,128]{1,0:T(8,128)S(1)}, u32[]{:S(2)}, u32[]{:S(2)}) collective-permute-start(f32[264,128]{1,0:T(8,128)S(1)} %get-tuple-element.44), channel_id=1, source_target_pairs={{0,16},{8,24},{16,32},{24,40},{32,48},{40,56},{48,64},{56,72},{64,... | collective-permute-start | bytes 405512 | tf_op jit(solution)/shard_map/ppermute | solution.py:243
  75.5 3.1 %collective-permute-start.9 = (f32[264,128]{1,0:T(8,128)S(1)}, f32[264,128]{1,0:T(8,128)S(1)}, u32[]{:S(2)}, u32[]{:S(2)}) collective-permute-start(f32[264,128]{1,0:T(8,128)S(1)} %get-tuple-element.45), channel_id=1, source_target_pairs={{0,1016},{8,16},{16,8},{24,32},{32,24},{40,48},{48,40},{56,64},{64... | collective-permute-start | bytes 405512 | tf_op jit(solution)/shard_map/ppermute | solution.py:243
  78.6 7.1 %collective-permute-start.10 = (f32[264,128]{1,0:T(8,128)S(1)}, f32[264,128]{1,0:T(8,128)S(1)}, u32[]{:S(2)}, u32[]{:S(2)}) collective-permute-start(f32[264,128]{1,0:T(8,128)S(1)} %get-tuple-element.46), channel_id=1, source_target_pairs={{0,1008},{8,1016},{16,0},{24,8},{32,16},{40,24},{48,32},{56,40},{6... | collective-permute-start | bytes 405512 | tf_op jit(solution)/shard_map/ppermute | solution.py:243
  85.7 3.1 %collective-permute-start.11 = (f32[264,128]{1,0:T(8,128)S(1)}, f32[264,128]{1,0:T(8,128)S(1)}, u32[]{:S(2)}, u32[]{:S(2)}) collective-permute-start(f32[264,128]{1,0:T(8,128)S(1)} %get-tuple-element.47), channel_id=1, source_target_pairs={{0,8},{8,0},{16,24},{24,16},{32,40},{40,32},{48,56},{56,48},{64,72... | collective-permute-start | bytes 405512 | tf_op jit(solution)/shard_map/ppermute | solution.py:243
  88.8 0.0 collective-permute-done.8.in0.refs_4_
  88.8 0.0 collective-permute-done.9.in1.refs_5_
  88.8 0.0 collective-permute-done.10.in2.refs_6_
  88.8 0.9 collective-permute-done.11.in3.refs_7_
  89.7 9.5 %all_to_all.22.refs_8_ = f32[8,16,128]{2,1,0:T(8,128)S(1)} all-to-all(f32[8,16,128]{2,1,0:T(8,128)S(1)} %shard_map.69), channel_id=1, replica_groups=mesh['chip'=64,'core'=2,'cls'=8] {'cls'}, dimensions={0} | all-to-all | bytes 131072 | tf_op jit(solution)/shard_map/all_to_all | solution.py:251
  99.2 1.4 %shard_map.70 = (f32[8,128,128]{2,1,0:T(8,128)S(1)}, f32[8,8,128]{2,1,0:T(8,128)S(1)}) custom-call(bf16[32,128,128]{2,1,0:T(8,128)(2,1)S(1)} %copy-done, s32[72]{0:T(128)S(1)} %get-tuple-element.28.refs_1_, f32[8,128,128]{2,1,0:T(8,128)S(1)} %get-tuple-element.36.refs_2_, f32[8,128,128]{2,1,0:T(8,128)S(1)} %get-tuple-element.43.refs_3_, ...), custom_call_target="tpu_custom_call" | custom-call | tf_op jit(solution)/shard_map/pallas_call | solution.py:254
  100.6 9.3 %all_to_all.23.parts = f32[8,8,128]{2,1,0:T(8,128)S(1)} all-to-all(f32[8,8,128]{2,1,0:T(8,128)S(1)} %get-tuple-element.50), channel_id=1, replica_groups=mesh['chip'=64,'core'=2,'cls'=8] {'cls'}, dimensions={0} | all-to-all | bytes 65536 | tf_op jit(solution)/shard_map/all_to_all | solution.py:273
  110.0 1.0 shard_map.71
  (3 shorter events, 0.0 us)
Async XLA Ops:
  0.0 45.4 %copy-start = (bf16[32,128,128]{2,1,0:T(8,128)(2,1)S(1)}, bf16[32,128,128]{2,1,0:T(8,128)(2,1)}, u32[]{:S(2)}) copy-start(bf16[32,128,128]{2,1,0:T(8,128)(2,1)} %refs_0_.5) | copy-start | bytes 3145732
  2.1 28.1 %collective-permute-start = (f32[264,128]{1,0:T(8,128)S(1)}, f32[264,128]{1,0:T(8,128)S(1)}, u32[]{:S(2)}, u32[]{:S(2)}) collective-permute-start(f32[264,128]{1,0:T(8,128)S(1)} %get-tuple-element.31), channel_id=1, source_target_pairs={{0,16},{8,24},{16,32},{24,40},{32,48},{40,56},{48,64},{56,72},{64,... | collective-permute-start | bytes 405512 | tf_op jit(solution)/shard_map/ppermute | solution.py:243
  7.8 22.3 %collective-permute-start.1 = (f32[264,128]{1,0:T(8,128)S(1)}, f32[264,128]{1,0:T(8,128)S(1)}, u32[]{:S(2)}, u32[]{:S(2)}) collective-permute-start(f32[264,128]{1,0:T(8,128)S(1)} %get-tuple-element.32), channel_id=1, source_target_pairs={{0,1016},{8,16},{16,8},{24,32},{32,24},{40,48},{48,40},{56,64},{64... | collective-permute-start | bytes 405512 | tf_op jit(solution)/shard_map/ppermute | solution.py:243
  13.6 16.6 %collective-permute-start.2 = (f32[264,128]{1,0:T(8,128)S(1)}, f32[264,128]{1,0:T(8,128)S(1)}, u32[]{:S(2)}, u32[]{:S(2)}) collective-permute-start(f32[264,128]{1,0:T(8,128)S(1)} %get-tuple-element.33), channel_id=1, source_target_pairs={{0,1008},{8,1016},{16,0},{24,8},{32,16},{40,24},{48,32},{56,40},{6... | collective-permute-start | bytes 405512 | tf_op jit(solution)/shard_map/ppermute | solution.py:243
  26.7 4.5 %collective-permute-start.3 = (f32[264,128]{1,0:T(8,128)S(1)}, f32[264,128]{1,0:T(8,128)S(1)}, u32[]{:S(2)}, u32[]{:S(2)}) collective-permute-start(f32[264,128]{1,0:T(8,128)S(1)} %get-tuple-element.34), channel_id=1, source_target_pairs={{0,8},{8,0},{16,24},{24,16},{32,40},{40,32},{48,56},{56,48},{64,72... | collective-permute-start | bytes 405512 | tf_op jit(solution)/shard_map/ppermute | solution.py:243
  46.8 14.9 %collective-permute-start.4 = (f32[264,128]{1,0:T(8,128)S(1)}, f32[264,128]{1,0:T(8,128)S(1)}, u32[]{:S(2)}, u32[]{:S(2)}) collective-permute-start(f32[264,128]{1,0:T(8,128)S(1)} %get-tuple-element.38), channel_id=1, source_target_pairs={{0,16},{8,24},{16,32},{24,40},{32,48},{40,56},{48,64},{56,72},{64,... | collective-permute-start | bytes 405512 | tf_op jit(solution)/shard_map/ppermute | solution.py:243
  48.8 12.9 %collective-permute-start.5 = (f32[264,128]{1,0:T(8,128)S(1)}, f32[264,128]{1,0:T(8,128)S(1)}, u32[]{:S(2)}, u32[]{:S(2)}) collective-permute-start(f32[264,128]{1,0:T(8,128)S(1)} %get-tuple-element.39), channel_id=1, source_target_pairs={{0,1016},{8,16},{16,8},{24,32},{32,24},{40,48},{48,40},{56,64},{64... | collective-permute-start | bytes 405512 | tf_op jit(solution)/shard_map/ppermute | solution.py:243
  52.4 9.8 %collective-permute-start.6 = (f32[264,128]{1,0:T(8,128)S(1)}, f32[264,128]{1,0:T(8,128)S(1)}, u32[]{:S(2)}, u32[]{:S(2)}) collective-permute-start(f32[264,128]{1,0:T(8,128)S(1)} %get-tuple-element.40), channel_id=1, source_target_pairs={{0,1008},{8,1016},{16,0},{24,8},{32,16},{40,24},{48,32},{56,40},{6... | collective-permute-start | bytes 405512 | tf_op jit(solution)/shard_map/ppermute | solution.py:243
  59.3 3.3 %collective-permute-start.7 = (f32[264,128]{1,0:T(8,128)S(1)}, f32[264,128]{1,0:T(8,128)S(1)}, u32[]{:S(2)}, u32[]{:S(2)}) collective-permute-start(f32[264,128]{1,0:T(8,128)S(1)} %get-tuple-element.41), channel_id=1, source_target_pairs={{0,8},{8,0},{16,24},{24,16},{32,40},{40,32},{48,56},{56,48},{64,72... | collective-permute-start | bytes 405512 | tf_op jit(solution)/shard_map/ppermute | solution.py:243
  73.6 15.1 %collective-permute-start.8 = (f32[264,128]{1,0:T(8,128)S(1)}, f32[264,128]{1,0:T(8,128)S(1)}, u32[]{:S(2)}, u32[]{:S(2)}) collective-permute-start(f32[264,128]{1,0:T(8,128)S(1)} %get-tuple-element.44), channel_id=1, source_target_pairs={{0,16},{8,24},{16,32},{24,40},{32,48},{40,56},{48,64},{56,72},{64,... | collective-permute-start | bytes 405512 | tf_op jit(solution)/shard_map/ppermute | solution.py:243
  75.5 13.2 %collective-permute-start.9 = (f32[264,128]{1,0:T(8,128)S(1)}, f32[264,128]{1,0:T(8,128)S(1)}, u32[]{:S(2)}, u32[]{:S(2)}) collective-permute-start(f32[264,128]{1,0:T(8,128)S(1)} %get-tuple-element.45), channel_id=1, source_target_pairs={{0,1016},{8,16},{16,8},{24,32},{32,24},{40,48},{48,40},{56,64},{64... | collective-permute-start | bytes 405512 | tf_op jit(solution)/shard_map/ppermute | solution.py:243
  78.6 10.2 %collective-permute-start.10 = (f32[264,128]{1,0:T(8,128)S(1)}, f32[264,128]{1,0:T(8,128)S(1)}, u32[]{:S(2)}, u32[]{:S(2)}) collective-permute-start(f32[264,128]{1,0:T(8,128)S(1)} %get-tuple-element.46), channel_id=1, source_target_pairs={{0,1008},{8,1016},{16,0},{24,8},{32,16},{40,24},{48,32},{56,40},{6... | collective-permute-start | bytes 405512 | tf_op jit(solution)/shard_map/ppermute | solution.py:243
  85.7 4.0 %collective-permute-start.11 = (f32[264,128]{1,0:T(8,128)S(1)}, f32[264,128]{1,0:T(8,128)S(1)}, u32[]{:S(2)}, u32[]{:S(2)}) collective-permute-start(f32[264,128]{1,0:T(8,128)S(1)} %get-tuple-element.47), channel_id=1, source_target_pairs={{0,8},{8,0},{16,24},{24,16},{32,40},{40,32},{48,56},{56,48},{64,72... | collective-permute-start | bytes 405512 | tf_op jit(solution)/shard_map/ppermute | solution.py:243

commit v13 on v12

--- a/solution.py
+++ b/solution.py
@@ -36,7 +36,7 @@
         ghost = jnp.maximum(col - 8, 0)
         offset = shift_right(ghost, 1)
         half = shift_right(offset, 1)
-        pair = jnp.where(lax.rem(offset, 2) == 1, 2 * half, 1 + 2 * (half ^ core))
+        pair = jnp.where(lax.rem(offset, 2) == 1, 2 * (half ^ core), 1 + 2 * (half ^ core))
         yield jnp.where(col < 8, col, 8 + 2 * pair + lax.rem(ghost, 2))
     for offset in range(4):
         for within in range(2):
@@ -62,7 +62,7 @@
 def fill_swaps(source, sums, block_of, outs, rows):
     core = lax.axis_index("core")
     rows[0:8, :] = sums
-    for out, offset in zip(outs, (1, 2 - 2 * core, 3, 2 * core)):
+    for out, offset in zip(outs, (1 + 2 * core, 2 - 2 * core, 3 - 2 * core, 2 * core)):
         out[2 * SIDE + 2 :, :] = jnp.zeros((6, SIDE), F32)
         for within in range(2):
             block = block_of(offset, within)
@@ -201,9 +201,9 @@
     dom = ("chip", "core")
     count = 2 * lax.axis_size("chip")
     swaps = [
-        [(i, (i + 2) % count) for i in range(count)],
+        [(i, (i + (-2 if i % 2 else 2)) % count) for i in range(count)],
         [(i, (i + (1 if i % 2 else -1)) % count) for i in range(count)],
-        [(i, (i - 2) % count) for i in range(count)],
+        [(i, (i + (2 if i % 2 else -2)) % count) for i in range(count)],
         [(i, i ^ 1) for i in range(count)],
     ]
     send_lists = jnp.transpose(send_lists, (0, 2, 1))

time: 112 us -> 111 us (level)
  starting transfers between devices: 58 us -> 53.8 us
  waiting for transfers between devices: 2.84 us -> 6.44 us
    ppermute x12, starting transfers between devices: 58 us -> 53.8 us  [on_device(): received = [lax.ppermute(out, dom, swap) for out, swap in zip(outs, swaps)]]
    ppermute x12, waiting for transfers between devices: 2.84 us -> 6.44 us  [on_device(): received = [lax.ppermute(out, dom, swap) for out, swap in zip(outs, swaps)]]
  transfers between devices with their start and end apart: 12 -> 12, of which waited for: 4 -> 3; matrix products, arithmetic and copies ran while one was open for 0% -> 0% of each run, Pallas kernels for 0% -> 0%
where the time goes in v13:
time: 111 us
  starting transfers between devices  53.8 us (48%)
  blocking collectives  43.2 us (39%)
  Pallas kernels  7.17 us (6%)
  waiting for transfers between devices  6.44 us (6%)
    ppermute x12, starting transfers between devices, on_device(): received = [lax.ppermute(out, dom, swap) for out, swap in zip(outs, swaps)]  53.8 us
    all_to_all x4, blocking collectives, on_device(): parts = lax.all_to_all(parts, 'cls', 0, 0)  43.2 us
    ppermute x12, waiting for transfers between devices, on_device(): received = [lax.ppermute(out, dom, swap) for out, swap in zip(outs, swaps)]  6.44 us
    pallas_call x3, Pallas kernels, on_device(): pl.pallas_call(lambda *refs, first=first, last=last: spread_kernel(first,...  4.12 us
  transfers between devices with their start and end apart: 12, of which 3 were waited for; matrix products, arithmetic and copies ran while one was open for 0% of the time, Pallas kernels for 0%

profile of v13, /device:TPU:1, one launch (start us, length us, event | category | flops | bytes accessed | tf_op | source)
XLA Modules:
  0.0 110.7 jit_solution(14776410266695882373)
XLA Ops:
  0.0 0.0 copy-start
  0.0 2.1 %shard_map.64 = (f32[8,128,128]{2,1,0:T(8,128)S(1)}, s32[72]{0:T(128)S(1)}, s32[8,128]{1,0:T(8,128)S(1)}, f32[264,128]{1,0:T(8,128)S(1)}, f32[264,128]{1,0:T(8,1...) custom-call(f32[8,128,128]{2,1,0:T(8,128)} %bitcast.4, s32[1,2,4]{2,1,0:T(2,128)} %bitcast.6, ...), custom_call_target="tpu_custom_call" | custom-call | flops 1048576 | bytes 1048576 | tf_op jit(solution)/shard_map/pallas_call | solution.py:223
  2.1 20.2 %collective-permute-start = (f32[264,128]{1,0:T(8,128)S(1)}, f32[264,128]{1,0:T(8,128)S(1)}, u32[]{:S(2)}, u32[]{:S(2)}) collective-permute-start(f32[264,128]{1,0:T(8,128)S(1)} %get-tuple-element.31), channel_id=1, source_target_pairs={{0,16},{8,1016},{16,32},{24,8},{32,48},{40,24},{48,64},{56,40},{64... | collective-permute-start | bytes 405512 | tf_op jit(solution)/shard_map/ppermute | solution.py:243
  22.3 1.9 %collective-permute-start.1 = (f32[264,128]{1,0:T(8,128)S(1)}, f32[264,128]{1,0:T(8,128)S(1)}, u32[]{:S(2)}, u32[]{:S(2)}) collective-permute-start(f32[264,128]{1,0:T(8,128)S(1)} %get-tuple-element.32), channel_id=1, source_target_pairs={{0,1016},{8,16},{16,8},{24,32},{32,24},{40,48},{48,40},{56,64},{64... | collective-permute-start | bytes 405512 | tf_op jit(solution)/shard_map/ppermute | solution.py:243
  24.2 1.9 %collective-permute-start.2 = (f32[264,128]{1,0:T(8,128)S(1)}, f32[264,128]{1,0:T(8,128)S(1)}, u32[]{:S(2)}, u32[]{:S(2)}) collective-permute-start(f32[264,128]{1,0:T(8,128)S(1)} %get-tuple-element.33), channel_id=1, source_target_pairs={{0,1008},{8,24},{16,0},{24,40},{32,16},{40,56},{48,32},{56,72},{64... | collective-permute-start | bytes 405512 | tf_op jit(solution)/shard_map/ppermute | solution.py:243
  26.1 3.1 %collective-permute-start.3 = (f32[264,128]{1,0:T(8,128)S(1)}, f32[264,128]{1,0:T(8,128)S(1)}, u32[]{:S(2)}, u32[]{:S(2)}) collective-permute-start(f32[264,128]{1,0:T(8,128)S(1)} %get-tuple-element.34), channel_id=1, source_target_pairs={{0,8},{8,0},{16,24},{24,16},{32,40},{40,32},{48,56},{56,48},{64,72... | collective-permute-start | bytes 405512 | tf_op jit(solution)/shard_map/ppermute | solution.py:243
  29.3 0.0 collective-permute-done.in0.refs_4_
  29.3 0.0 collective-permute-done.1.in1.refs_5_
  29.3 4.0 %collective-permute-done.2.in2.refs_6_ = f32[264,128]{1,0:T(8,128)S(1)} collective-permute-done((f32[264,128]{1,0:T(8,128)S(1)}, f32[264,128]{1,0:T(8,128)S(1)}, u32[]{:S(2)}, u32[]{:S(2)}) %collective-permute-start.2) | collective-permute-done | bytes 135200 | tf_op jit(solution)/shard_map/ppermute | solution.py:243
  33.3 0.0 collective-permute-done.3.in3.refs_7_
  33.3 14.3 %all_to_all.20.refs_8_ = f32[8,16,128]{2,1,0:T(8,128)S(1)} all-to-all(f32[8,16,128]{2,1,0:T(8,128)S(1)} %shard_map.65), channel_id=1, replica_groups=mesh['chip'=64,'core'=2,'cls'=8] {'cls'}, dimensions={0} | all-to-all | bytes 131072 | tf_op jit(solution)/shard_map/all_to_all | solution.py:251
  47.6 0.0 copy-done
  47.6 1.4 %shard_map.66 = (f32[8,128,128]{2,1,0:T(8,128)S(1)}, f32[8,128,128]{2,1,0:T(8,128)S(1)}, f32[264,128]{1,0:T(8,128)S(1)}, f32[264,128]{1,0:T(8,128)S(1)}, f32[264...) custom-call(bf16[32,128,128]{2,1,0:T(8,128)(2,1)S(1)} %copy-done, s32[72]{0:T(128)S(1)} %get-tuple-element.28.refs_1_, ...), custom_call_target="tpu_custom_call" | custom-call | tf_op jit(solution)/shard_map/pallas_call | solution.py:254
  49.0 2.8 %collective-permute-start.4 = (f32[264,128]{1,0:T(8,128)S(1)}, f32[264,128]{1,0:T(8,128)S(1)}, u32[]{:S(2)}, u32[]{:S(2)}) collective-permute-start(f32[264,128]{1,0:T(8,128)S(1)} %get-tuple-element.38), channel_id=1, source_target_pairs={{0,16},{8,1016},{16,32},{24,8},{32,48},{40,24},{48,64},{56,40},{64... | collective-permute-start | bytes 405512 | tf_op jit(solution)/shard_map/ppermute | solution.py:243
  51.8 2.3 %collective-permute-start.5 = (f32[264,128]{1,0:T(8,128)S(1)}, f32[264,128]{1,0:T(8,128)S(1)}, u32[]{:S(2)}, u32[]{:S(2)}) collective-permute-start(f32[264,128]{1,0:T(8,128)S(1)} %get-tuple-element.39), channel_id=1, source_target_pairs={{0,1016},{8,16},{16,8},{24,32},{32,24},{40,48},{48,40},{56,64},{64... | collective-permute-start | bytes 405512 | tf_op jit(solution)/shard_map/ppermute | solution.py:243
  54.1 2.1 %collective-permute-start.6 = (f32[264,128]{1,0:T(8,128)S(1)}, f32[264,128]{1,0:T(8,128)S(1)}, u32[]{:S(2)}, u32[]{:S(2)}) collective-permute-start(f32[264,128]{1,0:T(8,128)S(1)} %get-tuple-element.40), channel_id=1, source_target_pairs={{0,1008},{8,24},{16,0},{24,40},{32,16},{40,56},{48,32},{56,72},{64... | collective-permute-start | bytes 405512 | tf_op jit(solution)/shard_map/ppermute | solution.py:243
  56.2 5.4 %collective-permute-start.7 = (f32[264,128]{1,0:T(8,128)S(1)}, f32[264,128]{1,0:T(8,128)S(1)}, u32[]{:S(2)}, u32[]{:S(2)}) collective-permute-start(f32[264,128]{1,0:T(8,128)S(1)} %get-tuple-element.41), channel_id=1, source_target_pairs={{0,8},{8,0},{16,24},{24,16},{32,40},{40,32},{48,56},{56,48},{64,72... | collective-permute-start | bytes 405512 | tf_op jit(solution)/shard_map/ppermute | solution.py:243
  61.7 0.0 collective-permute-done.4.in0.refs_4_
  61.7 0.0 collective-permute-done.5.in1.refs_5_
  61.7 1.5 %collective-permute-done.6.in2.refs_6_ = f32[264,128]{1,0:T(8,128)S(1)} collective-permute-done((f32[264,128]{1,0:T(8,128)S(1)}, f32[264,128]{1,0:T(8,128)S(1)}, u32[]{:S(2)}, u32[]{:S(2)}) %collective-permute-start.6) | collective-permute-done | bytes 135200 | tf_op jit(solution)/shard_map/ppermute | solution.py:243
  63.2 0.0 collective-permute-done.7.in3.refs_7_
  63.2 10.0 %all_to_all.21.refs_8_ = f32[8,16,128]{2,1,0:T(8,128)S(1)} all-to-all(f32[8,16,128]{2,1,0:T(8,128)S(1)} %shard_map.67), channel_id=1, replica_groups=mesh['chip'=64,'core'=2,'cls'=8] {'cls'}, dimensions={0} | all-to-all | bytes 131072 | tf_op jit(solution)/shard_map/all_to_all | solution.py:251
  73.2 1.4 %shard_map.68 = (f32[8,128,128]{2,1,0:T(8,128)S(1)}, f32[264,128]{1,0:T(8,128)S(1)}, f32[264,128]{1,0:T(8,128)S(1)}, f32[264,128]{1,0:T(8,128)S(1)}, f32[264,128]{1,0:T(8,128)S(1)}, /*index=5*/f32[8,128]{1,0:T(8,128)S(1)}) custom-call(bf16[32,128,128]{2,1,0:T(8,128)(2,1)S(1)} %copy-done, s32[72]{0:T(128)S(1)} %get-tuple-element.28.refs_1_, ...), custom_call_target="tpu_custom_call" | custom-call | tf_op jit(solution)/shard_map/pallas_call | solution.py:254
  74.6 2.9 %collective-permute-start.8 = (f32[264,128]{1,0:T(8,128)S(1)}, f32[264,128]{1,0:T(8,128)S(1)}, u32[]{:S(2)}, u32[]{:S(2)}) collective-permute-start(f32[264,128]{1,0:T(8,128)S(1)} %get-tuple-element.44), channel_id=1, source_target_pairs={{0,16},{8,1016},{16,32},{24,8},{32,48},{40,24},{48,64},{56,40},{64... | collective-permute-start | bytes 405512 | tf_op jit(solution)/shard_map/ppermute | solution.py:243
  77.5 1.9 %collective-permute-start.9 = (f32[264,128]{1,0:T(8,128)S(1)}, f32[264,128]{1,0:T(8,128)S(1)}, u32[]{:S(2)}, u32[]{:S(2)}) collective-permute-start(f32[264,128]{1,0:T(8,128)S(1)} %get-tuple-element.45), channel_id=1, source_target_pairs={{0,1016},{8,16},{16,8},{24,32},{32,24},{40,48},{48,40},{56,64},{64... | collective-permute-start | bytes 405512 | tf_op jit(solution)/shard_map/ppermute | solution.py:243
  79.5 2.3 %collective-permute-start.10 = (f32[264,128]{1,0:T(8,128)S(1)}, f32[264,128]{1,0:T(8,128)S(1)}, u32[]{:S(2)}, u32[]{:S(2)}) collective-permute-start(f32[264,128]{1,0:T(8,128)S(1)} %get-tuple-element.46), channel_id=1, source_target_pairs={{0,1008},{8,24},{16,0},{24,40},{32,16},{40,56},{48,32},{56,72},{64... | collective-permute-start | bytes 405512 | tf_op jit(solution)/shard_map/ppermute | solution.py:243
  81.8 6.8 %collective-permute-start.11 = (f32[264,128]{1,0:T(8,128)S(1)}, f32[264,128]{1,0:T(8,128)S(1)}, u32[]{:S(2)}, u32[]{:S(2)}) collective-permute-start(f32[264,128]{1,0:T(8,128)S(1)} %get-tuple-element.47), channel_id=1, source_target_pairs={{0,8},{8,0},{16,24},{24,16},{32,40},{40,32},{48,56},{56,48},{64,72... | collective-permute-start | bytes 405512 | tf_op jit(solution)/shard_map/ppermute | solution.py:243
  88.6 0.0 collective-permute-done.8.in0.refs_4_
  88.6 0.0 collective-permute-done.9.in1.refs_5_
  88.6 0.0 collective-permute-done.10.in2.refs_6_
  88.6 0.9 collective-permute-done.11.in3.refs_7_
  89.6 9.5 %all_to_all.22.refs_8_ = f32[8,16,128]{2,1,0:T(8,128)S(1)} all-to-all(f32[8,16,128]{2,1,0:T(8,128)S(1)} %shard_map.69), channel_id=1, replica_groups=mesh['chip'=64,'core'=2,'cls'=8] {'cls'}, dimensions={0} | all-to-all | bytes 131072 | tf_op jit(solution)/shard_map/all_to_all | solution.py:251
  99.1 1.4 %shard_map.70 = (f32[8,128,128]{2,1,0:T(8,128)S(1)}, f32[8,8,128]{2,1,0:T(8,128)S(1)}) custom-call(bf16[32,128,128]{2,1,0:T(8,128)(2,1)S(1)} %copy-done, s32[72]{0:T(128)S(1)} %get-tuple-element.28.refs_1_, f32[8,128,128]{2,1,0:T(8,128)S(1)} %get-tuple-element.36.refs_2_, f32[8,128,128]{2,1,0:T(8,128)S(1)} %get-tuple-element.43.refs_3_, ...), custom_call_target="tpu_custom_call" | custom-call | tf_op jit(solution)/shard_map/pallas_call | solution.py:254
  100.4 9.3 %all_to_all.23.parts = f32[8,8,128]{2,1,0:T(8,128)S(1)} all-to-all(f32[8,8,128]{2,1,0:T(8,128)S(1)} %get-tuple-element.50), channel_id=1, replica_groups=mesh['chip'=64,'core'=2,'cls'=8] {'cls'}, dimensions={0} | all-to-all | bytes 65536 | tf_op jit(solution)/shard_map/all_to_all | solution.py:273
  109.8 1.0 shard_map.71
  (3 shorter events, 0.0 us)
Async XLA Ops:
  0.0 47.6 %copy-start = (bf16[32,128,128]{2,1,0:T(8,128)(2,1)S(1)}, bf16[32,128,128]{2,1,0:T(8,128)(2,1)}, u32[]{:S(2)}) copy-start(bf16[32,128,128]{2,1,0:T(8,128)(2,1)} %refs_0_.5) | copy-start | bytes 3145732
  2.1 27.2 %collective-permute-start = (f32[264,128]{1,0:T(8,128)S(1)}, f32[264,128]{1,0:T(8,128)S(1)}, u32[]{:S(2)}, u32[]{:S(2)}) collective-permute-start(f32[264,128]{1,0:T(8,128)S(1)} %get-tuple-element.31), channel_id=1, source_target_pairs={{0,16},{8,1016},{16,32},{24,8},{32,48},{40,24},{48,64},{56,40},{64... | collective-permute-start | bytes 405512 | tf_op jit(solution)/shard_map/ppermute | solution.py:243
  22.3 7.0 %collective-permute-start.1 = (f32[264,128]{1,0:T(8,128)S(1)}, f32[264,128]{1,0:T(8,128)S(1)}, u32[]{:S(2)}, u32[]{:S(2)}) collective-permute-start(f32[264,128]{1,0:T(8,128)S(1)} %get-tuple-element.32), channel_id=1, source_target_pairs={{0,1016},{8,16},{16,8},{24,32},{32,24},{40,48},{48,40},{56,64},{64... | collective-permute-start | bytes 405512 | tf_op jit(solution)/shard_map/ppermute | solution.py:243
  24.2 9.1 %collective-permute-start.2 = (f32[264,128]{1,0:T(8,128)S(1)}, f32[264,128]{1,0:T(8,128)S(1)}, u32[]{:S(2)}, u32[]{:S(2)}) collective-permute-start(f32[264,128]{1,0:T(8,128)S(1)} %get-tuple-element.33), channel_id=1, source_target_pairs={{0,1008},{8,24},{16,0},{24,40},{32,16},{40,56},{48,32},{56,72},{64... | collective-permute-start | bytes 405512 | tf_op jit(solution)/shard_map/ppermute | solution.py:243
  26.1 7.2 %collective-permute-start.3 = (f32[264,128]{1,0:T(8,128)S(1)}, f32[264,128]{1,0:T(8,128)S(1)}, u32[]{:S(2)}, u32[]{:S(2)}) collective-permute-start(f32[264,128]{1,0:T(8,128)S(1)} %get-tuple-element.34), channel_id=1, source_target_pairs={{0,8},{8,0},{16,24},{24,16},{32,40},{40,32},{48,56},{56,48},{64,72... | collective-permute-start | bytes 405512 | tf_op jit(solution)/shard_map/ppermute | solution.py:243
  49.0 12.7 %collective-permute-start.4 = (f32[264,128]{1,0:T(8,128)S(1)}, f32[264,128]{1,0:T(8,128)S(1)}, u32[]{:S(2)}, u32[]{:S(2)}) collective-permute-start(f32[264,128]{1,0:T(8,128)S(1)} %get-tuple-element.38), channel_id=1, source_target_pairs={{0,16},{8,1016},{16,32},{24,8},{32,48},{40,24},{48,64},{56,40},{64... | collective-permute-start | bytes 405512 | tf_op jit(solution)/shard_map/ppermute | solution.py:243
  51.8 9.9 %collective-permute-start.5 = (f32[264,128]{1,0:T(8,128)S(1)}, f32[264,128]{1,0:T(8,128)S(1)}, u32[]{:S(2)}, u32[]{:S(2)}) collective-permute-start(f32[264,128]{1,0:T(8,128)S(1)} %get-tuple-element.39), channel_id=1, source_target_pairs={{0,1016},{8,16},{16,8},{24,32},{32,24},{40,48},{48,40},{56,64},{64... | collective-permute-start | bytes 405512 | tf_op jit(solution)/shard_map/ppermute | solution.py:243
  54.1 9.1 %collective-permute-start.6 = (f32[264,128]{1,0:T(8,128)S(1)}, f32[264,128]{1,0:T(8,128)S(1)}, u32[]{:S(2)}, u32[]{:S(2)}) collective-permute-start(f32[264,128]{1,0:T(8,128)S(1)} %get-tuple-element.40), channel_id=1, source_target_pairs={{0,1008},{8,24},{16,0},{24,40},{32,16},{40,56},{48,32},{56,72},{64... | collective-permute-start | bytes 405512 | tf_op jit(solution)/shard_map/ppermute | solution.py:243
  56.2 7.0 %collective-permute-start.7 = (f32[264,128]{1,0:T(8,128)S(1)}, f32[264,128]{1,0:T(8,128)S(1)}, u32[]{:S(2)}, u32[]{:S(2)}) collective-permute-start(f32[264,128]{1,0:T(8,128)S(1)} %get-tuple-element.41), channel_id=1, source_target_pairs={{0,8},{8,0},{16,24},{24,16},{32,40},{40,32},{48,56},{56,48},{64,72... | collective-permute-start | bytes 405512 | tf_op jit(solution)/shard_map/ppermute | solution.py:243
  74.6 14.0 %collective-permute-start.8 = (f32[264,128]{1,0:T(8,128)S(1)}, f32[264,128]{1,0:T(8,128)S(1)}, u32[]{:S(2)}, u32[]{:S(2)}) collective-permute-start(f32[264,128]{1,0:T(8,128)S(1)} %get-tuple-element.44), channel_id=1, source_target_pairs={{0,16},{8,1016},{16,32},{24,8},{32,48},{40,24},{48,64},{56,40},{64... | collective-permute-start | bytes 405512 | tf_op jit(solution)/shard_map/ppermute | solution.py:243
  77.5 11.1 %collective-permute-start.9 = (f32[264,128]{1,0:T(8,128)S(1)}, f32[264,128]{1,0:T(8,128)S(1)}, u32[]{:S(2)}, u32[]{:S(2)}) collective-permute-start(f32[264,128]{1,0:T(8,128)S(1)} %get-tuple-element.45), channel_id=1, source_target_pairs={{0,1016},{8,16},{16,8},{24,32},{32,24},{40,48},{48,40},{56,64},{64... | collective-permute-start | bytes 405512 | tf_op jit(solution)/shard_map/ppermute | solution.py:243
  79.5 9.1 %collective-permute-start.10 = (f32[264,128]{1,0:T(8,128)S(1)}, f32[264,128]{1,0:T(8,128)S(1)}, u32[]{:S(2)}, u32[]{:S(2)}) collective-permute-start(f32[264,128]{1,0:T(8,128)S(1)} %get-tuple-element.46), channel_id=1, source_target_pairs={{0,1008},{8,24},{16,0},{24,40},{32,16},{40,56},{48,32},{56,72},{64... | collective-permute-start | bytes 405512 | tf_op jit(solution)/shard_map/ppermute | solution.py:243
  81.8 7.7 %collective-permute-start.11 = (f32[264,128]{1,0:T(8,128)S(1)}, f32[264,128]{1,0:T(8,128)S(1)}, u32[]{:S(2)}, u32[]{:S(2)}) collective-permute-start(f32[264,128]{1,0:T(8,128)S(1)} %get-tuple-element.47), channel_id=1, source_target_pairs={{0,8},{8,0},{16,24},{24,16},{32,40},{40,32},{48,56},{56,48},{64,72... | collective-permute-start | bytes 405512 | tf_op jit(solution)/shard_map/ppermute | solution.py:243

commit v14 on v13

--- a/solution.py
+++ b/solution.py
@@ -27,10 +27,8 @@
     return lax.shift_right_logical(value, by)
 
 
-def plan_entries(rows, cols, send):
+def plan_entries(cols, send):
     core = lax.axis_index("core")
-    for tile in range(32):
-        yield rows[tile]
     for tile in range(32):
         col = cols[tile]
         ghost = jnp.maximum(col - 8, 0)
@@ -43,16 +41,12 @@
             yield send[0, within, offset]
 
 
-def row_block(plan, tile):
+def operand_block(plan, tile):
     return plan[tile]
 
 
-def operand_block(plan, tile):
-    return plan[32 + tile]
-
-
 def sent_block(plan, offset, within):
-    return plan[64 + 2 * offset + within]
+    return plan[32 + 2 * offset + within]
 
 
 def block_at(ref, place):
@@ -83,25 +77,26 @@
     return copies
 
 
-def first_kernel(labels, send, rows, cols, mask, kept, plan, mask_kept, *refs):
-    *outs, sums_out, fetched, send_here, rows_here, cols_here, plan_here, sems = refs
-    pairs = [(send, send_here), (rows, rows_here), (cols, cols_here)]
+def first_kernel(labels, send, rows, cols, mask, kept, plan, rows_kept, mask_kept, *refs):
+    *outs, sums_out, fetched, send_here, cols_here, plan_here, sems = refs
+    pairs = [(send, send_here), (cols, cols_here)]
     pairs += [(labels.at[block], fetched.at[block]) for block in range(8)]
-    copies = copy_all(pairs + [(mask, mask_kept)], sems)
-    for copy in copies[:3]:
+    copies = copy_all(pairs + [(mask, mask_kept), (rows, rows_kept)], sems)
+    for copy in copies[:2]:
         copy.wait()
-    for place, entry in enumerate(plan_entries(rows_here, cols_here, send_here)):
+    for place, entry in enumerate(plan_entries(cols_here, send_here)):
         plan_here[place] = entry
     plan_copy = pltpu.make_async_copy(plan_here, plan, sems.at[12])
     plan_copy.start()
     sums = []
     for block in range(8):
-        copies[3 + block].wait()
+        copies[2 + block].wait()
         value = jnp.transpose(fetched[block])
         kept[block] = value
         sums.append(class_sums(value))
     block_of = lambda offset, within: send_here[0, within, offset]
     fill_swaps(kept, jnp.concatenate(sums, axis=0), block_of, outs, sums_out)
+    copies[10].wait()
     copies[11].wait()
     plan_copy.wait()
 
@@ -128,10 +123,10 @@
 
 def spread_kernel(first, last, *refs):
     refs = list(refs)
-    tiles, plan, mask, source = refs[:4]
-    received = refs[4:8]
-    parts = refs[8]
-    refs = refs[9:]
+    tiles, plan, rows, mask, source = refs[:5]
+    received = refs[5:9]
+    parts = refs[9]
+    refs = refs[10:]
     anchor = refs.pop(0) if first else mask
     squared = refs.pop(0)
     if last:
@@ -139,9 +134,8 @@
     else:
         *outs, rows_out = refs[:5]
         refs = refs[5:]
-    operand, products, plan_here, plan_sem = refs
-    plan_copy = pltpu.make_async_copy(plan, plan_here, plan_sem)
-    plan_copy.start()
+    operand, products, plan_here, rows_here, sems = refs
+    copies = copy_all([(plan, plan_here), (rows, rows_here)], sems)
     scale = CLASSES / total_of(parts)
     if first:
         seeded = 64.0 * mask[...].astype(F32)
@@ -156,7 +150,8 @@
         high, low = split(value)
         operand[block, :SIDE, :] = high
         operand[block, SIDE:, :] = low
-    plan_copy.wait()
+    for copy in copies:
+        copy.wait()
     plan = plan_here
     for tile in range(32):
         halves = lax.dot_general(
@@ -168,7 +163,7 @@
         products[tile] = halves[:SIDE] + halves[SIDE:]
     squared[...] = anchor[...]
     for tile in range(32):
-        row = row_block(plan, tile)
+        row = rows_here[tile]
         squared[row] = squared[row] + products[tile]
     sums = []
     for block in range(8):
@@ -219,18 +214,18 @@
             seed_mask.reshape(8, SIDE),
         )
     ]
-    plan_shape = jax.ShapeDtypeStruct((72,), jnp.int32)
-    source, plan, mask, *outs, rows = pl.pallas_call(
+    plan_shape = jax.ShapeDtypeStruct((40,), jnp.int32)
+    tile_shape = jax.ShapeDtypeStruct((32,), jnp.int32)
+    source, plan, tile_rows, mask, *outs, rows = pl.pallas_call(
         first_kernel,
-        out_shape=[own_shape, plan_shape, jax.ShapeDtypeStruct((8, SIDE), jnp.int32)] + sent_shapes,
+        out_shape=[own_shape, plan_shape, tile_shape, jax.ShapeDtypeStruct((8, SIDE), jnp.int32)] + sent_shapes,
         in_specs=[HBM] * 5,
-        out_specs=[VMEM] * 8,
+        out_specs=[VMEM] * 9,
         scratch_shapes=[
             pltpu.VMEM((8, SIDE, SIDE), F32),
             pltpu.SMEM((1, 2, 4), jnp.int32),
             pltpu.SMEM((32,), jnp.int32),
-            pltpu.SMEM((32,), jnp.int32),
-            pltpu.SMEM((72,), jnp.int32),
+            pltpu.SMEM((40,), jnp.int32),
             pltpu.SemaphoreType.DMA((13,)),
         ],
         compiler_params=PARAMS,
@@ -254,16 +249,17 @@
         results = pl.pallas_call(
             lambda *refs, first=first, last=last: spread_kernel(first, last, *refs),
             out_shape=out_shape,
-            in_specs=[VMEM] * 9,
+            in_specs=[VMEM] * 10,
             out_specs=[VMEM] * len(out_shape),
             scratch_shapes=[
                 pltpu.VMEM((16, 2 * SIDE, SIDE), jnp.bfloat16),
                 pltpu.VMEM((32, SIDE, SIDE), F32),
-                pltpu.SMEM((72,), jnp.int32),
-                pltpu.SemaphoreType.DMA,
+                pltpu.SMEM((40,), jnp.int32),
+                pltpu.SMEM((32,), jnp.int32),
+                pltpu.SemaphoreType.DMA((2,)),
             ],
             compiler_params=PARAMS,
-        )(tiles, plan, mask if first else anchor, source, *received, parts)
+        )(tiles, plan, tile_rows, mask if first else anchor, source, *received, parts)
         if first:
             anchor, *results = results
         if last:

time: 111 us -> 111 us (level)
  no operation moved by 1% of the time
where the time goes in v14:
time: 111 us
  starting transfers between devices  53.7 us (48%)
  blocking collectives  43.2 us (39%)
  Pallas kernels  7.13 us (6%)
  waiting for transfers between devices  6.44 us (6%)
    ppermute x12, starting transfers between devices, on_device(): received = [lax.ppermute(out, dom, swap) for out, swap in zip(outs, swaps)]  53.7 us
    all_to_all x4, blocking collectives, on_device(): parts = lax.all_to_all(parts, 'cls', 0, 0)  43.2 us
    ppermute x12, waiting for transfers between devices, on_device(): received = [lax.ppermute(out, dom, swap) for out, swap in zip(outs, swaps)]  6.44 us
    pallas_call x3, Pallas kernels, on_device(): pl.pallas_call(lambda *refs, first=first, last=last: spread_kernel(first,...  4.11 us
  transfers between devices with their start and end apart: 12, of which 3 were waited for; matrix products, arithmetic and copies ran while one was open for 0% of the time, Pallas kernels for 0%

profile of v14, /device:TPU:1, one launch (start us, length us, event | category | flops | bytes accessed | tf_op | source)
XLA Modules:
  0.0 110.7 jit_solution(1298964997782283764)
XLA Ops:
  0.0 0.0 copy-start
  0.0 2.0 %shard_map.64 = (f32[8,128,128]{2,1,0:T(8,128)S(1)}, s32[40]{0:T(128)S(1)}, s32[32]{0:T(128)S(1)}, s32[8,128]{1,0:T(8,128)S(1)}, f32[264,128]{1,0:T(8,128)S(1)},...) custom-call(f32[8,128,128]{2,1,0:T(8,128)} %bitcast.4, ...), custom_call_target="tpu_custom_call" | custom-call | flops 1048576 | bytes 1048576 | tf_op jit(solution)/shard_map/pallas_call | solution.py:219
  2.1 20.2 %collective-permute-start = (f32[264,128]{1,0:T(8,128)S(1)}, f32[264,128]{1,0:T(8,128)S(1)}, u32[]{:S(2)}, u32[]{:S(2)}) collective-permute-start(f32[264,128]{1,0:T(8,128)S(1)} %get-tuple-element.33), channel_id=1, source_target_pairs={{0,16},{8,1016},{16,32},{24,8},{32,48},{40,24},{48,64},{56,40},{64... | collective-permute-start | bytes 405512 | tf_op jit(solution)/shard_map/ppermute | solution.py:238
  22.2 1.9 %collective-permute-start.1 = (f32[264,128]{1,0:T(8,128)S(1)}, f32[264,128]{1,0:T(8,128)S(1)}, u32[]{:S(2)}, u32[]{:S(2)}) collective-permute-start(f32[264,128]{1,0:T(8,128)S(1)} %get-tuple-element.34), channel_id=1, source_target_pairs={{0,1016},{8,16},{16,8},{24,32},{32,24},{40,48},{48,40},{56,64},{64... | collective-permute-start | bytes 405512 | tf_op jit(solution)/shard_map/ppermute | solution.py:238
  24.2 1.9 %collective-permute-start.2 = (f32[264,128]{1,0:T(8,128)S(1)}, f32[264,128]{1,0:T(8,128)S(1)}, u32[]{:S(2)}, u32[]{:S(2)}) collective-permute-start(f32[264,128]{1,0:T(8,128)S(1)} %get-tuple-element.35), channel_id=1, source_target_pairs={{0,1008},{8,24},{16,0},{24,40},{32,16},{40,56},{48,32},{56,72},{64... | collective-permute-start | bytes 405512 | tf_op jit(solution)/shard_map/ppermute | solution.py:238
  26.1 3.1 %collective-permute-start.3 = (f32[264,128]{1,0:T(8,128)S(1)}, f32[264,128]{1,0:T(8,128)S(1)}, u32[]{:S(2)}, u32[]{:S(2)}) collective-permute-start(f32[264,128]{1,0:T(8,128)S(1)} %get-tuple-element.36), channel_id=1, source_target_pairs={{0,8},{8,0},{16,24},{24,16},{32,40},{40,32},{48,56},{56,48},{64,72... | collective-permute-start | bytes 405512 | tf_op jit(solution)/shard_map/ppermute | solution.py:238
  29.2 0.0 collective-permute-done.in0.refs_5_
  29.2 0.0 collective-permute-done.1.in1.refs_6_
  29.2 4.0 %collective-permute-done.2.in2.refs_7_ = f32[264,128]{1,0:T(8,128)S(1)} collective-permute-done((f32[264,128]{1,0:T(8,128)S(1)}, f32[264,128]{1,0:T(8,128)S(1)}, u32[]{:S(2)}, u32[]{:S(2)}) %collective-permute-start.2) | collective-permute-done | bytes 135200 | tf_op jit(solution)/shard_map/ppermute | solution.py:238
  33.2 0.0 collective-permute-done.3.in3.refs_8_
  33.3 14.3 %all_to_all.20.refs_9_ = f32[8,16,128]{2,1,0:T(8,128)S(1)} all-to-all(f32[8,16,128]{2,1,0:T(8,128)S(1)} %shard_map.65), channel_id=1, replica_groups=mesh['chip'=64,'core'=2,'cls'=8] {'cls'}, dimensions={0} | all-to-all | bytes 131072 | tf_op jit(solution)/shard_map/all_to_all | solution.py:246
  47.6 0.0 copy-done
  47.6 1.4 %shard_map.66 = (f32[8,128,128]{2,1,0:T(8,128)S(1)}, f32[8,128,128]{2,1,0:T(8,128)S(1)}, f32[264,128]{1,0:T(8,128)S(1)}, f32[264,128]{1,0:T(8,128)S(1)}, f32[264...) custom-call(bf16[32,128,128]{2,1,0:T(8,128)(2,1)S(1)} %copy-done, s32[40]{0:T(128)S(1)} %get-tuple-element.29.refs_1_, ...), custom_call_target="tpu_custom_call" | custom-call | tf_op jit(solution)/shard_map/pallas_call | solution.py:249
  48.9 2.8 %collective-permute-start.4 = (f32[264,128]{1,0:T(8,128)S(1)}, f32[264,128]{1,0:T(8,128)S(1)}, u32[]{:S(2)}, u32[]{:S(2)}) collective-permute-start(f32[264,128]{1,0:T(8,128)S(1)} %get-tuple-element.40), channel_id=1, source_target_pairs={{0,16},{8,1016},{16,32},{24,8},{32,48},{40,24},{48,64},{56,40},{64... | collective-permute-start | bytes 405512 | tf_op jit(solution)/shard_map/ppermute | solution.py:238
  51.7 2.3 %collective-permute-start.5 = (f32[264,128]{1,0:T(8,128)S(1)}, f32[264,128]{1,0:T(8,128)S(1)}, u32[]{:S(2)}, u32[]{:S(2)}) collective-permute-start(f32[264,128]{1,0:T(8,128)S(1)} %get-tuple-element.41), channel_id=1, source_target_pairs={{0,1016},{8,16},{16,8},{24,32},{32,24},{40,48},{48,40},{56,64},{64... | collective-permute-start | bytes 405512 | tf_op jit(solution)/shard_map/ppermute | solution.py:238
  54.1 2.1 %collective-permute-start.6 = (f32[264,128]{1,0:T(8,128)S(1)}, f32[264,128]{1,0:T(8,128)S(1)}, u32[]{:S(2)}, u32[]{:S(2)}) collective-permute-start(f32[264,128]{1,0:T(8,128)S(1)} %get-tuple-element.42), channel_id=1, source_target_pairs={{0,1008},{8,24},{16,0},{24,40},{32,16},{40,56},{48,32},{56,72},{64... | collective-permute-start | bytes 405512 | tf_op jit(solution)/shard_map/ppermute | solution.py:238
  56.2 5.4 %collective-permute-start.7 = (f32[264,128]{1,0:T(8,128)S(1)}, f32[264,128]{1,0:T(8,128)S(1)}, u32[]{:S(2)}, u32[]{:S(2)}) collective-permute-start(f32[264,128]{1,0:T(8,128)S(1)} %get-tuple-element.43), channel_id=1, source_target_pairs={{0,8},{8,0},{16,24},{24,16},{32,40},{40,32},{48,56},{56,48},{64,72... | collective-permute-start | bytes 405512 | tf_op jit(solution)/shard_map/ppermute | solution.py:238
  61.6 0.0 collective-permute-done.4.in0.refs_5_
  61.6 0.0 collective-permute-done.5.in1.refs_6_
  61.6 1.5 %collective-permute-done.6.in2.refs_7_ = f32[264,128]{1,0:T(8,128)S(1)} collective-permute-done((f32[264,128]{1,0:T(8,128)S(1)}, f32[264,128]{1,0:T(8,128)S(1)}, u32[]{:S(2)}, u32[]{:S(2)}) %collective-permute-start.6) | collective-permute-done | bytes 135200 | tf_op jit(solution)/shard_map/ppermute | solution.py:238
  63.1 0.0 collective-permute-done.7.in3.refs_8_
  63.1 10.0 %all_to_all.21.refs_9_ = f32[8,16,128]{2,1,0:T(8,128)S(1)} all-to-all(f32[8,16,128]{2,1,0:T(8,128)S(1)} %shard_map.67), channel_id=1, replica_groups=mesh['chip'=64,'core'=2,'cls'=8] {'cls'}, dimensions={0} | all-to-all | bytes 131072 | tf_op jit(solution)/shard_map/all_to_all | solution.py:246
  73.2 1.4 %shard_map.68 = (f32[8,128,128]{2,1,0:T(8,128)S(1)}, f32[264,128]{1,0:T(8,128)S(1)}, f32[264,128]{1,0:T(8,128)S(1)}, f32[264,128]{1,0:T(8,128)S(1)}, f32[264,128]{1,0:T(8,128)S(1)}, /*index=5*/f32[8,128]{1,0:T(8,128)S(1)}) custom-call(bf16[32,128,128]{2,1,0:T(8,128)(2,1)S(1)} %copy-done, s32[40]{0:T(128)S(1)} %get-tuple-element.29.refs_1_, ...), custom_call_target="tpu_custom_call" | custom-call | tf_op jit(solution)/shard_map/pallas_call | solution.py:249
  74.6 2.9 %collective-permute-start.8 = (f32[264,128]{1,0:T(8,128)S(1)}, f32[264,128]{1,0:T(8,128)S(1)}, u32[]{:S(2)}, u32[]{:S(2)}) collective-permute-start(f32[264,128]{1,0:T(8,128)S(1)} %get-tuple-element.46), channel_id=1, source_target_pairs={{0,16},{8,1016},{16,32},{24,8},{32,48},{40,24},{48,64},{56,40},{64... | collective-permute-start | bytes 405512 | tf_op jit(solution)/shard_map/ppermute | solution.py:238
  77.5 1.9 %collective-permute-start.9 = (f32[264,128]{1,0:T(8,128)S(1)}, f32[264,128]{1,0:T(8,128)S(1)}, u32[]{:S(2)}, u32[]{:S(2)}) collective-permute-start(f32[264,128]{1,0:T(8,128)S(1)} %get-tuple-element.47), channel_id=1, source_target_pairs={{0,1016},{8,16},{16,8},{24,32},{32,24},{40,48},{48,40},{56,64},{64... | collective-permute-start | bytes 405512 | tf_op jit(solution)/shard_map/ppermute | solution.py:238
  79.4 2.3 %collective-permute-start.10 = (f32[264,128]{1,0:T(8,128)S(1)}, f32[264,128]{1,0:T(8,128)S(1)}, u32[]{:S(2)}, u32[]{:S(2)}) collective-permute-start(f32[264,128]{1,0:T(8,128)S(1)} %get-tuple-element.48), channel_id=1, source_target_pairs={{0,1008},{8,24},{16,0},{24,40},{32,16},{40,56},{48,32},{56,72},{64... | collective-permute-start | bytes 405512 | tf_op jit(solution)/shard_map/ppermute | solution.py:238
  81.8 6.7 %collective-permute-start.11 = (f32[264,128]{1,0:T(8,128)S(1)}, f32[264,128]{1,0:T(8,128)S(1)}, u32[]{:S(2)}, u32[]{:S(2)}) collective-permute-start(f32[264,128]{1,0:T(8,128)S(1)} %get-tuple-element.49), channel_id=1, source_target_pairs={{0,8},{8,0},{16,24},{24,16},{32,40},{40,32},{48,56},{56,48},{64,72... | collective-permute-start | bytes 405512 | tf_op jit(solution)/shard_map/ppermute | solution.py:238
  88.5 0.0 collective-permute-done.8.in0.refs_5_
  88.5 0.0 collective-permute-done.9.in1.refs_6_
  88.6 0.0 collective-permute-done.10.in2.refs_7_
  88.6 0.9 collective-permute-done.11.in3.refs_8_
  89.5 9.5 %all_to_all.22.refs_9_ = f32[8,16,128]{2,1,0:T(8,128)S(1)} all-to-all(f32[8,16,128]{2,1,0:T(8,128)S(1)} %shard_map.69), channel_id=1, replica_groups=mesh['chip'=64,'core'=2,'cls'=8] {'cls'}, dimensions={0} | all-to-all | bytes 131072 | tf_op jit(solution)/shard_map/all_to_all | solution.py:246
  99.0 1.4 %shard_map.70 = (f32[8,128,128]{2,1,0:T(8,128)S(1)}, f32[8,8,128]{2,1,0:T(8,128)S(1)}) custom-call(bf16[32,128,128]{2,1,0:T(8,128)(2,1)S(1)} %copy-done, s32[40]{0:T(128)S(1)} %get-tuple-element.29.refs_1_, s32[32]{0:T(128)S(1)} %get-tuple-element.30.refs_2_, f32[8,128,128]{2,1,0:T(8,128)S(1)} %get-tuple-element.38.refs_3_, ...), custom_call_target="tpu_custom_call" | custom-call | tf_op jit(solution)/shard_map/pallas_call | solution.py:249
  100.4 9.3 %all_to_all.23.parts = f32[8,8,128]{2,1,0:T(8,128)S(1)} all-to-all(f32[8,8,128]{2,1,0:T(8,128)S(1)} %get-tuple-element.52), channel_id=1, replica_groups=mesh['chip'=64,'core'=2,'cls'=8] {'cls'}, dimensions={0} | all-to-all | bytes 65536 | tf_op jit(solution)/shard_map/all_to_all | solution.py:269
  109.7 1.0 shard_map.71
  (3 shorter events, 0.0 us)
Async XLA Ops:
  0.0 47.6 %copy-start = (bf16[32,128,128]{2,1,0:T(8,128)(2,1)S(1)}, bf16[32,128,128]{2,1,0:T(8,128)(2,1)}, u32[]{:S(2)}) copy-start(bf16[32,128,128]{2,1,0:T(8,128)(2,1)} %refs_0_.5) | copy-start | bytes 3145732
  2.1 27.2 %collective-permute-start = (f32[264,128]{1,0:T(8,128)S(1)}, f32[264,128]{1,0:T(8,128)S(1)}, u32[]{:S(2)}, u32[]{:S(2)}) collective-permute-start(f32[264,128]{1,0:T(8,128)S(1)} %get-tuple-element.33), channel_id=1, source_target_pairs={{0,16},{8,1016},{16,32},{24,8},{32,48},{40,24},{48,64},{56,40},{64... | collective-permute-start | bytes 405512 | tf_op jit(solution)/shard_map/ppermute | solution.py:238
  22.2 7.0 %collective-permute-start.1 = (f32[264,128]{1,0:T(8,128)S(1)}, f32[264,128]{1,0:T(8,128)S(1)}, u32[]{:S(2)}, u32[]{:S(2)}) collective-permute-start(f32[264,128]{1,0:T(8,128)S(1)} %get-tuple-element.34), channel_id=1, source_target_pairs={{0,1016},{8,16},{16,8},{24,32},{32,24},{40,48},{48,40},{56,64},{64... | collective-permute-start | bytes 405512 | tf_op jit(solution)/shard_map/ppermute | solution.py:238
  24.2 9.1 %collective-permute-start.2 = (f32[264,128]{1,0:T(8,128)S(1)}, f32[264,128]{1,0:T(8,128)S(1)}, u32[]{:S(2)}, u32[]{:S(2)}) collective-permute-start(f32[264,128]{1,0:T(8,128)S(1)} %get-tuple-element.35), channel_id=1, source_target_pairs={{0,1008},{8,24},{16,0},{24,40},{32,16},{40,56},{48,32},{56,72},{64... | collective-permute-start | bytes 405512 | tf_op jit(solution)/shard_map/ppermute | solution.py:238
  26.1 7.2 %collective-permute-start.3 = (f32[264,128]{1,0:T(8,128)S(1)}, f32[264,128]{1,0:T(8,128)S(1)}, u32[]{:S(2)}, u32[]{:S(2)}) collective-permute-start(f32[264,128]{1,0:T(8,128)S(1)} %get-tuple-element.36), channel_id=1, source_target_pairs={{0,8},{8,0},{16,24},{24,16},{32,40},{40,32},{48,56},{56,48},{64,72... | collective-permute-start | bytes 405512 | tf_op jit(solution)/shard_map/ppermute | solution.py:238
  48.9 12.7 %collective-permute-start.4 = (f32[264,128]{1,0:T(8,128)S(1)}, f32[264,128]{1,0:T(8,128)S(1)}, u32[]{:S(2)}, u32[]{:S(2)}) collective-permute-start(f32[264,128]{1,0:T(8,128)S(1)} %get-tuple-element.40), channel_id=1, source_target_pairs={{0,16},{8,1016},{16,32},{24,8},{32,48},{40,24},{48,64},{56,40},{64... | collective-permute-start | bytes 405512 | tf_op jit(solution)/shard_map/ppermute | solution.py:238
  51.7 9.9 %collective-permute-start.5 = (f32[264,128]{1,0:T(8,128)S(1)}, f32[264,128]{1,0:T(8,128)S(1)}, u32[]{:S(2)}, u32[]{:S(2)}) collective-permute-start(f32[264,128]{1,0:T(8,128)S(1)} %get-tuple-element.41), channel_id=1, source_target_pairs={{0,1016},{8,16},{16,8},{24,32},{32,24},{40,48},{48,40},{56,64},{64... | collective-permute-start | bytes 405512 | tf_op jit(solution)/shard_map/ppermute | solution.py:238
  54.1 9.1 %collective-permute-start.6 = (f32[264,128]{1,0:T(8,128)S(1)}, f32[264,128]{1,0:T(8,128)S(1)}, u32[]{:S(2)}, u32[]{:S(2)}) collective-permute-start(f32[264,128]{1,0:T(8,128)S(1)} %get-tuple-element.42), channel_id=1, source_target_pairs={{0,1008},{8,24},{16,0},{24,40},{32,16},{40,56},{48,32},{56,72},{64... | collective-permute-start | bytes 405512 | tf_op jit(solution)/shard_map/ppermute | solution.py:238
  56.2 7.0 %collective-permute-start.7 = (f32[264,128]{1,0:T(8,128)S(1)}, f32[264,128]{1,0:T(8,128)S(1)}, u32[]{:S(2)}, u32[]{:S(2)}) collective-permute-start(f32[264,128]{1,0:T(8,128)S(1)} %get-tuple-element.43), channel_id=1, source_target_pairs={{0,8},{8,0},{16,24},{24,16},{32,40},{40,32},{48,56},{56,48},{64,72... | collective-permute-start | bytes 405512 | tf_op jit(solution)/shard_map/ppermute | solution.py:238
  74.6 14.0 %collective-permute-start.8 = (f32[264,128]{1,0:T(8,128)S(1)}, f32[264,128]{1,0:T(8,128)S(1)}, u32[]{:S(2)}, u32[]{:S(2)}) collective-permute-start(f32[264,128]{1,0:T(8,128)S(1)} %get-tuple-element.46), channel_id=1, source_target_pairs={{0,16},{8,1016},{16,32},{24,8},{32,48},{40,24},{48,64},{56,40},{64... | collective-permute-start | bytes 405512 | tf_op jit(solution)/shard_map/ppermute | solution.py:238
  77.5 11.1 %collective-permute-start.9 = (f32[264,128]{1,0:T(8,128)S(1)}, f32[264,128]{1,0:T(8,128)S(1)}, u32[]{:S(2)}, u32[]{:S(2)}) collective-permute-start(f32[264,128]{1,0:T(8,128)S(1)} %get-tuple-element.47), channel_id=1, source_target_pairs={{0,1016},{8,16},{16,8},{24,32},{32,24},{40,48},{48,40},{56,64},{64... | collective-permute-start | bytes 405512 | tf_op jit(solution)/shard_map/ppermute | solution.py:238
  79.4 9.1 %collective-permute-start.10 = (f32[264,128]{1,0:T(8,128)S(1)}, f32[264,128]{1,0:T(8,128)S(1)}, u32[]{:S(2)}, u32[]{:S(2)}) collective-permute-start(f32[264,128]{1,0:T(8,128)S(1)} %get-tuple-element.48), channel_id=1, source_target_pairs={{0,1008},{8,24},{16,0},{24,40},{32,16},{40,56},{48,32},{56,72},{64... | collective-permute-start | bytes 405512 | tf_op jit(solution)/shard_map/ppermute | solution.py:238
  81.8 7.7 %collective-permute-start.11 = (f32[264,128]{1,0:T(8,128)S(1)}, f32[264,128]{1,0:T(8,128)S(1)}, u32[]{:S(2)}, u32[]{:S(2)}) collective-permute-start(f32[264,128]{1,0:T(8,128)S(1)} %get-tuple-element.49), channel_id=1, source_target_pairs={{0,8},{8,0},{16,24},{24,16},{32,40},{40,32},{48,56},{56,48},{64,72... | collective-permute-start | bytes 405512 | tf_op jit(solution)/shard_map/ppermute | solution.py:238
